TPU v7x, 32 devices: a whole 2x2x4 slice. The times are simulated.
32 devices in a mesh: stream: 4 (over y, core), span: 8 (over z, x).
Axes of the slice: x: 2, y: 2, z: 4, core: 2. Of those that a mesh axis runs over, the one named last changes fastest.
Arguments:
- velocity_modes: bfloat16 [8, 64, 10, 3, 128], P('stream', 'span'), may hold values from -6 to 6
- cell_weight: float32 [8, 64, 10], P('stream', 'span'), may hold values from 0.001 to 0.01
Outputs:
- convection: float32 [128, 128, 128], replicated
All inputs are finite; a program needn't handle non-finite values.
Results may differ from a plain program's by a relative error of at most 0.0085.
Values may be sent and summed in bfloat16 or wider, within the bound.
No kernel may reach another device: no remote copies, remote signals or barrier semaphores. Data moves between devices by JAX's collectives and lax.ppermute only.
A program may use at most 64 MiB of HBM per device.

v0:
```python
import jax
import jax.numpy as jnp
from jax import lax
from jax.sharding import PartitionSpec as P


def with_halo(cells, sides, width):
    for axis, dim in sides:
        count = lax.axis_size(axis)
        ends = count - 1
        head = lax.slice_in_dim(cells, 0, width, axis=dim)
        tail = lax.slice_in_dim(cells, cells.shape[dim] - width, cells.shape[dim], axis=dim)
        cells = jnp.concatenate(
            [
                lax.ppermute(tail, axis, [(i, (i + 1) % count) for i in range(ends)]),
                cells,
                lax.ppermute(head, axis, [((i + 1) % count, i) for i in range(ends)]),
            ],
            axis=dim,
        )
    return cells


def gradient(padded):
    core_x = padded[:, 2:-2]
    deriv_x = (8.0 * (core_x[3:-1] - core_x[1:-3]) - (core_x[4:] - core_x[:-4])) / 12.0
    core_y = padded[2:-2]
    deriv_y = (8.0 * (core_y[:, 3:-1] - core_y[:, 1:-3]) - (core_y[:, 4:] - core_y[:, :-4])) / 12.0
    center = padded[2:-2, 2:-2]
    vertical = jnp.pad(center, ((0, 0), (0, 0), (1, 1), (0, 0), (0, 0)))
    deriv_z = 0.5 * (vertical[:, :, 2:] - vertical[:, :, :-2])
    return jnp.stack([deriv_x, deriv_y, deriv_z])


def shards(velocity_modes, cell_weight):
    padded = with_halo(velocity_modes, (("stream", 0), ("span", 1)), 2)
    grads = gradient(padded.astype(jnp.float32))
    width = velocity_modes.shape[-1]
    cells = velocity_modes.shape[0] * velocity_modes.shape[1] * velocity_modes.shape[2]
    phi_half = velocity_modes.reshape(cells, 3, width)
    grad_cells = grads.reshape(3, cells, 3, width)
    grad_high = grad_cells.astype(jnp.bfloat16)
    grad_low = (grad_cells - grad_high.astype(jnp.float32)).astype(jnp.bfloat16)
    weight_cells = cell_weight.reshape(cells)
    test_count = width * width // width
    block_size = min(8, test_count)
    turns = test_count // block_size

    def one_block(turn_index, result):
        test_start = turn_index * block_size
        phi_test = lax.dynamic_slice_in_dim(phi_half, test_start, block_size, 2)
        quad = jnp.einsum("cbi,acbk->acik", phi_test, grad_high, preferred_element_type=jnp.float32)
        quad = quad + jnp.einsum(
            "cbi,acbk->acik", phi_test, grad_low, preferred_element_type=jnp.float32
        )
        quad = (quad * weight_cells[None, :, None, None]).astype(jnp.bfloat16)
        block_terms = jnp.einsum(
            "caj,acik->ijk", phi_half, quad, preferred_element_type=jnp.float32
        )
        return lax.dynamic_update_slice_in_dim(
            result, block_terms, (turn_index * block_size).astype(jnp.int32), 0
        )

    result = jnp.zeros((test_count, width, width), jnp.float32)
    result = lax.fori_loop(0, turns, one_block, result)
    whole = lax.psum(result.reshape(test_count * width, width), ("stream", "span"))
    return whole.reshape(width, width, width)


def solution(mesh):
    placed = (P("stream", "span", None, None, None), P("stream", "span", None))
    return jax.shard_map(shards, mesh=mesh, in_specs=placed, out_specs=P(), check_vma=False)
```

profile of v0, /device:TPU:1, one launch (start us, length us, event | category | flops | bytes accessed | tf_op | source)
XLA Modules:
  0.0 281.7 jit_solution(5334257990387182939)
XLA Ops:
  6.5 4.5 %collective-permute-start = (bf16[2,8,10,3,128]{4,1,3,2,0:T(8,128)(2,1)}, bf16[2,8,10,3,128]{4,1,3,2,0:T(8,128)(2,1)S(1)}, u32[]{:S(2)}, u32[]{:S(2)}) collective-permute-start(bf16[2,8,10,3,128]{4,1,3,2,0:T(8,128)(2,1)} %param.4), channel_id=1, source_target_pairs={{0,8},{8,16},{16,24},{1,9},{9,17},{17,25},{2,10},{10,18},{18,26},{... | collective-permute-start | bytes 368648 | tf_op jit(solution)/shard_map/ppermute | solution.py:15
  11.1 1.9 collective-permute-start.1
  13.3 0.9 constant_dynamic-update-slice_fusion.2
  14.2 3.3 %collective-permute-done.1 = bf16[2,8,10,3,128]{4,1,3,2,0:T(8,128)(2,1)S(1)} collective-permute-done((bf16[2,8,10,3,128]{4,1,3,2,0:T(8,128)(2,1)}, bf16[2,8,10,3,128]{4,1,3,2,0:T(8,128)(2,1)S(1)}, u32[]{:S(2)}, u32[]{:S(2)}) %collective-permute-start.1) | collective-permute-done | bytes 122912 | tf_op jit(solution)/shard_map/ppermute | solution.py:17
  17.6 3.1 %collective-permute-start.2 = (bf16[6,2,10,3,128]{4,1,3,2,0:T(2,128)(2,1)S(1)}, bf16[6,2,10,3,128]{4,1,3,2,0:T(2,128)(2,1)S(1)}, u32[]{:S(2)}, u32[]{:S(2)}) collective-permute-start(bf16[6,2,10,3,128]{4,1,3,2,0:T(2,128)(2,1)S(1)} %get-tuple-element.130), channel_id=1, source_target_pairs={{0,1},{1,2},{2,3},{3,4},{4,5},{5,6},{6,7},{8,9},{9,10},{10,11},{11... | collective-permute-start | bytes 276488 | tf_op jit(solution)/shard_map/ppermute | solution.py:15
  20.8 1.3 collective-permute-start.3
  22.1 0.9 copy.8
  23.9 2.2 collective-permute-done.3
  27.5 4.5 %broadcast_in_dim.3.clone = f32[128,128,128]{2,1,0:T(8,128)} broadcast(f32[]{:T(128)} %constant.37.clone.1), dimensions={} | broadcast | bytes 8388612 | tf_op jit(solution)/shard_map/broadcast_in_dim | solution.py:64
  31.9 55.6 %while.14 = (s32[]{:T(128)}, f32[128,128,128]{2,1,0:T(8,128)}, bf16[160,3,128]{2,0,1:T(8,128)(2,1)S(1)}, bf16[3,160,3,128]{3,2,1,0:T(4,128)(2,1)S(1)}, bf16[3,16...) while((s32[]{:T(128)}, f32[128,128,128]{2,1,0:T(8,128)}, ...), condition=%wide.wide.region_1.2_spmd, body=%wide.wide.region_0.1_spmd.sunk | while | flops 133201928 | bytes 11377443 | solution.py:65
  33.2 1.2 convolution_bitcast_fusion.3
  34.6 0.8 constant_dynamic-update-slice_fusion.6
  36.7 1.2 convolution_bitcast_fusion.3
  38.1 0.8 constant_dynamic-update-slice_fusion.6
  40.2 1.2 convolution_bitcast_fusion.3
  43.6 1.2 convolution_bitcast_fusion.3
  45.0 0.8 constant_dynamic-update-slice_fusion.6
  47.1 1.2 convolution_bitcast_fusion.3
  48.5 0.8 constant_dynamic-update-slice_fusion.6
  50.6 1.2 convolution_bitcast_fusion.3
  54.1 1.2 convolution_bitcast_fusion.3
  57.5 1.2 convolution_bitcast_fusion.3
  61.0 1.2 convolution_bitcast_fusion.3
  64.5 1.2 convolution_bitcast_fusion.3
  67.9 1.2 convolution_bitcast_fusion.3
  71.4 1.2 convolution_bitcast_fusion.3
  74.9 1.2 convolution_bitcast_fusion.3
  78.4 1.2 convolution_bitcast_fusion.3
  81.8 1.2 convolution_bitcast_fusion.3
  85.3 1.2 convolution_bitcast_fusion.3
  87.5 179.5 %all-reduce.3.cloned.1.call-done = f32[128,128,128]{2,1,0:T(8,128)} async-done(((f32[128,128,128]{2,1,0:T(8,128)}), f32[128,128,128]{2,1,0:T(8,128)}) %all-reduce.3.cloned.1.call-update) | async-done | bytes 8388624 | tf_op jit(solution)/shard_map/psum | solution.py:66
  267.0 7.9 %copy.73 = f32[128,128,128]{2,1,0:T(8,128)} copy(f32[128,128,128]{2,1,0:T(8,128)} %all-reduce.3.cloned.1.call-done) | data formatting | bytes 16777216
  (93 shorter events, 35.9 us)
Async XLA Ops:
  6.5 260.5 %all-reduce.3.cloned.1.call-start = ((), (), s32[]{:S(2)}) async-start(), calls=%async_computation | async-start | bytes 16777216 | tf_op jit(solution)/shard_map/psum | solution.py:66
  6.5 6.7 %collective-permute-start = (bf16[2,8,10,3,128]{4,1,3,2,0:T(8,128)(2,1)}, bf16[2,8,10,3,128]{4,1,3,2,0:T(8,128)(2,1)S(1)}, u32[]{:S(2)}, u32[]{:S(2)}) collective-permute-start(bf16[2,8,10,3,128]{4,1,3,2,0:T(8,128)(2,1)} %param.4), channel_id=1, source_target_pairs={{0,8},{8,16},{16,24},{1,9},{9,17},{17,25},{2,10},{10,18},{18,26},{... | collective-permute-start | bytes 368648 | tf_op jit(solution)/shard_map/ppermute | solution.py:15
  11.1 6.4 %collective-permute-start.1 = (bf16[2,8,10,3,128]{4,1,3,2,0:T(8,128)(2,1)}, bf16[2,8,10,3,128]{4,1,3,2,0:T(8,128)(2,1)S(1)}, u32[]{:S(2)}, u32[]{:S(2)}) collective-permute-start(bf16[2,8,10,3,128]{4,1,3,2,0:T(8,128)(2,1)} %param.4), channel_id=1, source_target_pairs={{8,0},{16,8},{24,16},{9,1},{17,9},{25,17},{10,2},{18,10},{26,18},{... | collective-permute-start | bytes 368648 | tf_op jit(solution)/shard_map/ppermute | solution.py:17
  17.6 6.2 %collective-permute-start.2 = (bf16[6,2,10,3,128]{4,1,3,2,0:T(2,128)(2,1)S(1)}, bf16[6,2,10,3,128]{4,1,3,2,0:T(2,128)(2,1)S(1)}, u32[]{:S(2)}, u32[]{:S(2)}) collective-permute-start(bf16[6,2,10,3,128]{4,1,3,2,0:T(2,128)(2,1)S(1)} %get-tuple-element.130), channel_id=1, source_target_pairs={{0,1},{1,2},{2,3},{3,4},{4,5},{5,6},{6,7},{8,9},{9,10},{10,11},{11... | collective-permute-start | bytes 276488 | tf_op jit(solution)/shard_map/ppermute | solution.py:15
  20.8 5.3 %collective-permute-start.3 = (bf16[6,2,10,3,128]{4,1,3,2,0:T(2,128)(2,1)S(1)}, bf16[6,2,10,3,128]{4,1,3,2,0:T(2,128)(2,1)S(1)}, u32[]{:S(2)}, u32[]{:S(2)}) collective-permute-start(bf16[6,2,10,3,128]{4,1,3,2,0:T(2,128)(2,1)S(1)} %get-tuple-element.131), channel_id=1, source_target_pairs={{1,0},{2,1},{3,2},{4,3},{5,4},{6,5},{7,6},{9,8},{10,9},{11,10},{12... | collective-permute-start | bytes 276488 | tf_op jit(solution)/shard_map/ppermute | solution.py:17
Sparse Core Ops, SparseCore 0:
  87.7 179.3 all-reduce.2
where the time goes:
time: 283 us; the launch traced here: 282 us
  waiting for transfers between devices  185 us (65%)
  matrix products  36.9 us (13%)
  local copies, waits for them, and re-layouts  33.7 us (12%)
  between operations  13.5 us (5%)
  starting transfers between devices  10.9 us (4%)
    psum x1, waiting for transfers between devices, shards(): lax.psum(result.reshape(test_count * width, width), ('stream', 'span'))  179 us
    dot_general x16, matrix products, one_block(): jnp.einsum('caj,acik->ijk', phi_half, quad, preferred_element_type=jnp.fl...  18.4 us
    dynamic_update_slice x32, local copies, waits for them, and re-layouts, one_block(): lax.dynamic_update_slice_in_dim(result, block_terms, (turn_index * block_...  16.6 us
    unnamed x4, local copies, waits for them, and re-layouts  9.77 us
    dot_general x16, matrix products, one_block(): jnp.einsum('cbi,acbk->acik', phi_test, grad_high, preferred_element_type=...  9.23 us
    dot_general x16, matrix products, one_block(): jnp.einsum('cbi,acbk->acik', phi_test, grad_low, preferred_element_type=j...  9.22 us
    ppermute x2, starting transfers between devices, with_halo(): lax.ppermute(tail, axis, [(i, (i + 1) % count) for i in range(ends)])  7.65 us
  transfers between devices with their start and end apart: 5, of which 4 were waited for; matrix products, arithmetic and copies ran while one was open for 1% of the time, Pallas kernels for 0%

commit v1 on v0

v1 whole, which is shorter than its diff:
```python
import jax
import jax.numpy as jnp
from jax import lax
from jax.sharding import PartitionSpec as P


def with_halo(cells, axis, dim, width):
    count = lax.axis_size(axis)
    ends = count - 1
    head = lax.slice_in_dim(cells, 0, width, axis=dim)
    tail = lax.slice_in_dim(cells, cells.shape[dim] - width, cells.shape[dim], axis=dim)
    return jnp.concatenate(
        [
            lax.ppermute(tail, axis, [(i, i + 1) for i in range(ends)]),
            cells,
            lax.ppermute(head, axis, [(i + 1, i) for i in range(ends)]),
        ],
        axis=dim,
    )


def gradient(padded):
    core_x = padded[:, 2:-2]
    deriv_x = (8.0 * (core_x[3:-1] - core_x[1:-3]) - (core_x[4:] - core_x[:-4])) / 12.0
    core_y = padded[2:-2]
    deriv_y = (8.0 * (core_y[:, 3:-1] - core_y[:, 1:-3]) - (core_y[:, 4:] - core_y[:, :-4])) / 12.0
    center = padded[2:-2, 2:-2]
    vertical = jnp.pad(center, ((0, 0), (0, 0), (1, 1), (0, 0), (0, 0)))
    deriv_z = 0.5 * (vertical[:, :, 2:] - vertical[:, :, :-2])
    return jnp.stack([deriv_x, deriv_y, deriv_z])


def shards(velocity_modes, cell_weight):
    streams = lax.axis_size("stream")
    me = lax.axis_index("stream")
    width = velocity_modes.shape[-1]
    wide = with_halo(velocity_modes, "span", 1, 2)
    block = lax.all_gather(wide, "stream", axis=0, tiled=True)
    weight = lax.all_gather(cell_weight, "stream", axis=0, tiled=True)
    padded = jnp.pad(block.astype(jnp.float32), ((2, 2), (0, 0), (0, 0), (0, 0), (0, 0)))
    center = block[:, 2:-2]
    cells = center.shape[0] * center.shape[1] * center.shape[2]
    grads = gradient(padded).reshape(3, cells, 3, width)
    phi = center.reshape(cells, 3, width)
    weighted = phi.astype(jnp.float32) * weight.reshape(cells, 1, 1)
    share = width // streams
    own = lax.dynamic_slice_in_dim(weighted, me * share, share, 2)
    turn = min(8, share)

    def one_block(step, result):
        mine = lax.dynamic_slice_in_dim(own, step * turn, turn, 2)
        quad = sum(
            mine[None, :, b, :, None] * grads[:, :, b, None, :] for b in range(3)
        ).astype(jnp.bfloat16)
        terms = jnp.einsum("caj,acik->ijk", phi, quad, preferred_element_type=jnp.float32)
        return lax.dynamic_update_slice_in_dim(
            result, terms.astype(jnp.bfloat16), step * turn, 0
        )

    result = jnp.zeros((share, width, width), jnp.bfloat16)
    result = lax.fori_loop(0, share // turn, one_block, result)
    rows = result.reshape(share * width, width)
    mine = lax.psum_scatter(rows, "span", scatter_dimension=0, tiled=True)
    whole = lax.all_gather(mine, ("stream", "span"), axis=0, tiled=True)
    return whole.astype(jnp.float32).reshape(width, width, width)


def solution(mesh):
    placed = (P("stream", "span", None, None, None), P("stream", "span", None))
    return jax.shard_map(shards, mesh=mesh, in_specs=placed, out_specs=P(), check_vma=False)
```

time: 283 us -> 210 us (0.74)
  waiting for transfers between devices: 185 us -> 131 us
  matrix products: 36.9 us -> 7.29 us
  blocking collectives: 0 us -> 16 us
  other arithmetic: 1.12 us -> 13.7 us
  local copies, waits for them, and re-layouts: 33.7 us -> 22.4 us
  starting transfers between devices: 10.9 us -> 5.28 us
    psum x1 -> x0, waiting for transfers between devices: 179 us -> none  [shards(): lax.psum(result.reshape(test_count * width, width), ('stream', 'span'))]
    all_gather x0 -> x1, waiting for transfers between devices: none -> 66.6 us  [shards(): whole = lax.all_gather(mine, ('stream', 'span'), axis=0, tiled=True)]
    reduce_scatter x0 -> x1, waiting for transfers between devices: none -> 64.4 us  [shards(): mine = lax.psum_scatter(rows, 'span', scatter_dimension=0, tiled=True)]
    dot_general x48 -> x4, matrix products: 36.9 us -> 7.29 us  [one_block(): jnp.einsum('caj,acik->ijk', phi, quad, preferred_element_type=jnp.float32)]
    all_gather x0 -> x2, blocking collectives: none -> 16 us  [the longest x1 9.79 us: shards(): block = lax.all_gather(wide, 'stream', axis=0, tiled=True)]
    dynamic_update_slice x32 -> x8, local copies, waits for them, and re-layouts: 16.6 us -> 3.62 us  [one_block(): lax.dynamic_update_slice_in_dim(result, terms.astype(jnp.bfloat16), step...]
    unnamed x4, local copies, waits for them, and re-layouts: 9.77 us -> 0.01 us
    reshape x0 -> x1, other arithmetic: none -> 6.65 us  [shards(): return whole.astype(jnp.float32).reshape(width, width, width)]
  transfers between devices with their start and end apart: 5 -> 4, of which waited for: 4 -> 2; matrix products, arithmetic and copies ran while one was open for 1% -> 0% of each run, Pallas kernels for 0% -> 0%
where the time goes in v1:
time: 210 us; the launch traced here: 209 us
  waiting for transfers between devices  131 us (62%)
  local copies, waits for them, and re-layouts  22.4 us (11%)
  blocking collectives  16 us (8%)
  other arithmetic  13.7 us (7%)
  between operations  13.5 us (6%)
  matrix products  7.29 us (3%)
  starting transfers between devices  5.28 us (3%)
    all_gather x1, waiting for transfers between devices, shards(): whole = lax.all_gather(mine, ('stream', 'span'), axis=0, tiled=True)  66.6 us
    reduce_scatter x1, waiting for transfers between devices, shards(): mine = lax.psum_scatter(rows, 'span', scatter_dimension=0, tiled=True)  64.4 us
    all_gather x1, blocking collectives, shards(): block = lax.all_gather(wide, 'stream', axis=0, tiled=True)  9.79 us
    dot_general x4, matrix products, one_block(): jnp.einsum('caj,acik->ijk', phi, quad, preferred_element_type=jnp.float32)  7.29 us
    reshape x1, other arithmetic, shards(): return whole.astype(jnp.float32).reshape(width, width, width)  6.65 us
    all_gather x1, blocking collectives, shards(): weight = lax.all_gather(cell_weight, 'stream', axis=0, tiled=True)  6.17 us
    while x2, local copies, waits for them, and re-layouts, shards(): result = lax.fori_loop(0, share // turn, one_block, result)  5.29 us
  transfers between devices with their start and end apart: 4, of which 2 were waited for; matrix products, arithmetic and copies ran while one was open for 0% of the time, Pallas kernels for 0%

profile of v1, /device:TPU:1, one launch (start us, length us, event | category | flops | bytes accessed | tf_op | source)
XLA Modules:
  0.0 209.2 jit_solution(3219193497266629802)
XLA Ops:
  6.5 1.0 fusion.15
  7.6 3.9 %collective-permute-start = (bf16[2,2,10,3,128]{4,1,3,2,0:T(2,128)(2,1)S(1)}, bf16[2,2,10,3,128]{4,1,3,2,0:T(2,128)(2,1)S(1)}, u32[]{:S(2)}, u32[]{:S(2)}) collective-permute-start(bf16[2,2,10,3,128]{4,1,3,2,0:T(2,128)(2,1)S(1)} %get-tuple-element.133), channel_id=1, source_target_pairs={{0,1},{1,2},{2,3},{3,4},{4,5},{5,6},{6,7},{8,9},{9,10},{10,11},{11... | collective-permute-start | bytes 92168 | tf_op jit(solution)/shard_map/ppermute | solution.py:14
  11.5 1.3 collective-permute-start.1
  12.8 6.2 %all_gather.10 = f32[8,8,10]{2,1,0:T(8,128)S(1)} all-gather(f32[2,8,10]{2,1,0:T(8,128)} %param.5), channel_id=1, replica_groups=mesh['stream'=4,'span'=8] {'stream'}, dimensions={0}, use_global_device_ids=true | all-gather | bytes 3200 | tf_op jit(solution)/shard_map/all_gather | solution.py:39
  19.2 1.0 pad_maximum_fusion.1
  20.2 9.8 %all_gather.9 = bf16[8,12,10,3,128]{4,1,3,2,0:T(8,128)(2,1)S(1)} all-gather(bf16[2,12,10,3,128]{4,1,3,2,0:T(8,128)(2,1)S(1)} %pad_maximum_fusion.1), channel_id=1, replica_groups=mesh['stream'=4,'span'=8] {'stream'}, dimensions={0}, use_global_device_ids=true | all-gather | bytes 921600 | tf_op jit(solution)/shard_map/all_gather | solution.py:38
  30.5 1.1 copy.15
  31.5 1.3 reshape.24
  32.9 1.2 convert_multiply_fusion
  34.1 2.2 %copy.19 = f32[640,3,32]{0,2,1:T(8,128)} copy(f32[640,3,32]{2,0,1:T(8,128)} %convert_multiply_fusion) | data formatting | bytes 491520 | tf_op jit(solution)/shard_map/while | solution.py:61
  36.6 1.0 stack.14
  37.7 1.5 fusion.10
  39.6 1.5 copy.17
  41.1 1.0 stack.13
  42.1 3.0 %pad_maximum_fusion = f32[3,640,3,128]{3,1,2,0:T(8,128)} fusion(f32[1,640,3,128]{3,1,2,0:T(8,128)S(1)} %copy-done, f32[1,640,3,128]{3,1,2,0:T(8,128)} %stack.13, f32[1,640,3,128]{3,1,2,0:T(8,128)S(1)} %stack.12), kind=kLoop, calls=%fused_computation.17 | loop fusion | flops 1474560 | bytes 5898240 | tf_op jit(solution)/shard_map/stack | solution.py:30
  45.1 3.1 %copy.20 = f32[3,640,3,128]{1,3,0,2:T(8,128)S(1)} copy(f32[3,640,3,128]{3,1,2,0:T(8,128)} %pad_maximum_fusion) | data formatting | bytes 5898240 | tf_op jit(solution)/shard_map/while | solution.py:61
  48.2 1.2 broadcast_in_dim.3.clone
  49.4 15.3 %while.13 = (s32[]{:T(128)}, bf16[32,128,128]{2,1,0:T(8,128)(2,1)}, f32[640,3,32]{0,2,1:T(8,128)}, f32[3,640,3,128]{1,3,0,2:T(8,128)S(1)}, bf16[640,3,128]{2,0,1...) while((s32[]{:T(128)}, bf16[32,128,128]{2,1,0:T(8,128)(2,1)}, ...), condition=%wide.region_1.2_spmd, body=%wide.region_0.1_spmd.sunk | while | flops 515244032 | bytes 12800223 | solution.py:61
  49.4 0.8 dynamic-slice_bitcast_fusion.4
  50.5 1.8 fusion.19
  52.5 0.7 constant_dynamic-update-slice_fusion.2
  53.2 0.8 dynamic-slice_bitcast_fusion.4
  54.3 1.8 fusion.19
  57.1 0.8 dynamic-slice_bitcast_fusion.4
  58.1 1.8 fusion.19
  60.1 0.7 constant_dynamic-update-slice_fusion.2
  60.9 0.8 dynamic-slice_bitcast_fusion.4
  62.0 1.8 fusion.19
  64.0 0.7 constant_dynamic-update-slice_fusion.2
  64.8 64.4 %reduce-scatter.2.cloned.1.call-done = bf16[512,128]{1,0:T(8,128)(2,1)} async-done(((bf16[4096,128]{1,0:T(8,128)(2,1)}), bf16[512,128]{1,0:T(8,128)(2,1)}) %reduce-scatter.2.cloned.1.call-update) | async-done | bytes 131088 | tf_op jit(solution)/shard_map/reduce_scatter | solution.py:63
  129.2 66.6 %all-gather.2.cloned.1.call-done = bf16[16384,128]{1,0:T(8,128)(2,1)} async-done(((bf16[512,128]{1,0:T(8,128)(2,1)}), bf16[16384,128]{1,0:T(8,128)(2,1)}) %all-gather.2.cloned.1.call-update) | async-done | bytes 4194320 | tf_op jit(solution)/shard_map/all_gather | solution.py:64
  195.7 6.7 %convert.1 = f32[128,128,128]{2,1,0:T(8,128)} convert(bf16[128,128,128]{2,1,0:T(8,128)(2,1)} %bitcast.45) | non-fusion elementwise | flops 2097152 | bytes 12582912 | tf_op jit(solution)/shard_map/reshape | solution.py:65
  (35 shorter events, 3.8 us)
Async XLA Ops:
  6.5 122.6 %reduce-scatter.2.cloned.1.call-start = ((), (), s32[]{:S(2)}) async-start(), calls=%async_computation.1 | async-start | bytes 1179648 | tf_op jit(solution)/shard_map/reduce_scatter | solution.py:63
  7.6 11.6 %collective-permute-start = (bf16[2,2,10,3,128]{4,1,3,2,0:T(2,128)(2,1)S(1)}, bf16[2,2,10,3,128]{4,1,3,2,0:T(2,128)(2,1)S(1)}, u32[]{:S(2)}, u32[]{:S(2)}) collective-permute-start(bf16[2,2,10,3,128]{4,1,3,2,0:T(2,128)(2,1)S(1)} %get-tuple-element.133), channel_id=1, source_target_pairs={{0,1},{1,2},{2,3},{3,4},{4,5},{5,6},{6,7},{8,9},{9,10},{10,11},{11... | collective-permute-start | bytes 92168 | tf_op jit(solution)/shard_map/ppermute | solution.py:14
  11.5 7.6 %collective-permute-start.1 = (bf16[2,2,10,3,128]{4,1,3,2,0:T(2,128)(2,1)S(1)}, bf16[2,2,10,3,128]{4,1,3,2,0:T(2,128)(2,1)S(1)}, u32[]{:S(2)}, u32[]{:S(2)}) collective-permute-start(bf16[2,2,10,3,128]{4,1,3,2,0:T(2,128)(2,1)S(1)} %get-tuple-element.134), channel_id=1, source_target_pairs={{1,0},{2,1},{3,2},{4,3},{5,4},{6,5},{7,6},{9,8},{10,9},{11,10},{12... | collective-permute-start | bytes 92168 | tf_op jit(solution)/shard_map/ppermute | solution.py:16
  32.9 3.4 %copy-start.1 = (bf16[640,3,128]{2,0,1:T(8,128)(2,1)}, bf16[640,3,128]{2,0,1:T(8,128)(2,1)S(1)}, u32[]{:S(2)}) copy-start(bf16[640,3,128]{2,0,1:T(8,128)(2,1)S(1)} %reshape.24) | copy-start | bytes 1474564
  39.4 2.7 %copy-start = (f32[1,640,3,128]{3,1,2,0:T(8,128)S(1)}, f32[1,640,3,128]{3,1,2,0:T(8,128)}, u32[]{:S(2)}) copy-start(f32[1,640,3,128]{3,1,2,0:T(8,128)} %stack.14) | copy-start | bytes 2949124
  49.4 1.1 copy-start.2
  53.2 1.1 copy-start.2
  57.1 1.1 copy-start.2
  60.9 1.1 copy-start.2
  64.7 131.0 %all-gather.2.cloned.1.call-start = ((), (), s32[]{:S(2)}) async-start(), calls=%async_computation.2 | async-start | bytes 4325376 | tf_op jit(solution)/shard_map/all_gather | solution.py:64
Sparse Core Ops, SparseCore 0:
  64.8 64.2 reduce-scatter.1
  132.6 63.1 all-gather.1

commit v2 on v1

--- a/solution.py
+++ b/solution.py
@@ -60,8 +60,11 @@
     result = jnp.zeros((share, width, width), jnp.bfloat16)
     result = lax.fori_loop(0, share // turn, one_block, result)
     rows = result.reshape(share * width, width)
-    mine = lax.psum_scatter(rows, "span", scatter_dimension=0, tiled=True)
-    whole = lax.all_gather(mine, ("stream", "span"), axis=0, tiled=True)
+    spans = lax.axis_size("span")
+    pieces = lax.all_to_all(rows.reshape(spans, -1, width), "span", 0, 0)
+    mine = jnp.sum(pieces.astype(jnp.float32), axis=0).astype(jnp.bfloat16)
+    slab = lax.all_gather(mine, "span", axis=0, tiled=True)
+    whole = lax.all_gather(slab, "stream", axis=0, tiled=True)
     return whole.astype(jnp.float32).reshape(width, width, width)
 
 

time: 210 us -> 187 us (0.89)
  waiting for transfers between devices: 131 us -> 75.2 us
  blocking collectives: 16 us -> 48 us
    reduce_scatter x1 -> x0, waiting for transfers between devices: 64.4 us -> none  [shards(): mine = lax.psum_scatter(rows, 'span', scatter_dimension=0, tiled=True)]
    all_to_all x0 -> x1, blocking collectives: none -> 32.1 us  [shards(): pieces = lax.all_to_all(rows.reshape(spans, -1, width), 'span', 0, 0)]
    all_gather x1 -> x2, waiting for transfers between devices: 66.6 us -> 75.2 us  [the longest x1 38.9 us: shards(): slab = lax.all_gather(mine, 'span', axis=0, tiled=True)]
where the time goes in v2:
time: 187 us; the launch traced here: 186 us
  waiting for transfers between devices  75.2 us (40%)
  blocking collectives  48 us (26%)
  local copies, waits for them, and re-layouts  22.4 us (12%)
  other arithmetic  14.5 us (8%)
  between operations  13.5 us (7%)
  matrix products  7.29 us (4%)
  starting transfers between devices  5.28 us (3%)
    all_gather x1, waiting for transfers between devices, shards(): slab = lax.all_gather(mine, 'span', axis=0, tiled=True)  38.9 us
    all_gather x1, waiting for transfers between devices, shards(): whole = lax.all_gather(slab, 'stream', axis=0, tiled=True)  36.2 us
    all_to_all x1, blocking collectives, shards(): pieces = lax.all_to_all(rows.reshape(spans, -1, width), 'span', 0, 0)  32.1 us
    all_gather x1, blocking collectives, shards(): block = lax.all_gather(wide, 'stream', axis=0, tiled=True)  9.79 us
    dot_general x4, matrix products, one_block(): jnp.einsum('caj,acik->ijk', phi, quad, preferred_element_type=jnp.float32)  7.29 us
    reshape x1, other arithmetic, shards(): return whole.astype(jnp.float32).reshape(width, width, width)  6.65 us
    all_gather x1, blocking collectives, shards(): weight = lax.all_gather(cell_weight, 'stream', axis=0, tiled=True)  6.17 us
    while x2, local copies, waits for them, and re-layouts, shards(): result = lax.fori_loop(0, share // turn, one_block, result)  5.29 us
  transfers between devices with their start and end apart: 4, of which 2 were waited for; matrix products, arithmetic and copies ran while one was open for 0% of the time, Pallas kernels for 0%

profile of v2, /device:TPU:1, one launch (start us, length us, event | category | flops | bytes accessed | tf_op | source)
XLA Modules:
  0.0 186.3 jit_solution(12334042549596957455)
XLA Ops:
  6.5 1.0 fusion.15
  7.6 3.9 %collective-permute-start = (bf16[2,2,10,3,128]{4,1,3,2,0:T(2,128)(2,1)S(1)}, bf16[2,2,10,3,128]{4,1,3,2,0:T(2,128)(2,1)S(1)}, u32[]{:S(2)}, u32[]{:S(2)}) collective-permute-start(bf16[2,2,10,3,128]{4,1,3,2,0:T(2,128)(2,1)S(1)} %get-tuple-element.133), channel_id=1, source_target_pairs={{0,1},{1,2},{2,3},{3,4},{4,5},{5,6},{6,7},{8,9},{9,10},{10,11},{11... | collective-permute-start | bytes 92168 | tf_op jit(solution)/shard_map/ppermute | solution.py:14
  11.5 1.3 collective-permute-start.1
  12.8 6.2 %all_gather.13 = f32[8,8,10]{2,1,0:T(8,128)S(1)} all-gather(f32[2,8,10]{2,1,0:T(8,128)} %param.5), channel_id=1, replica_groups=mesh['stream'=4,'span'=8] {'stream'}, dimensions={0}, use_global_device_ids=true | all-gather | bytes 3200 | tf_op jit(solution)/shard_map/all_gather | solution.py:39
  19.2 1.0 pad_maximum_fusion.1
  20.2 9.8 %all_gather.12 = bf16[8,12,10,3,128]{4,1,3,2,0:T(8,128)(2,1)S(1)} all-gather(bf16[2,12,10,3,128]{4,1,3,2,0:T(8,128)(2,1)S(1)} %pad_maximum_fusion.1), channel_id=1, replica_groups=mesh['stream'=4,'span'=8] {'stream'}, dimensions={0}, use_global_device_ids=true | all-gather | bytes 921600 | tf_op jit(solution)/shard_map/all_gather | solution.py:38
  30.5 1.1 copy.15
  31.5 1.3 reshape.21
  32.9 1.2 convert_multiply_fusion
  34.1 2.2 %copy.19 = f32[640,3,32]{0,2,1:T(8,128)} copy(f32[640,3,32]{2,0,1:T(8,128)} %convert_multiply_fusion) | data formatting | bytes 491520 | tf_op jit(solution)/shard_map/while | solution.py:61
  36.6 1.0 stack.14
  37.7 1.5 fusion.10
  39.6 1.5 copy.17
  41.1 1.0 stack.13
  42.1 3.0 %pad_maximum_fusion = f32[3,640,3,128]{3,1,2,0:T(8,128)} fusion(f32[1,640,3,128]{3,1,2,0:T(8,128)S(1)} %copy-done, f32[1,640,3,128]{3,1,2,0:T(8,128)} %stack.13, f32[1,640,3,128]{3,1,2,0:T(8,128)S(1)} %stack.12), kind=kLoop, calls=%fused_computation.17 | loop fusion | flops 1474560 | bytes 5898240 | tf_op jit(solution)/shard_map/stack | solution.py:30
  45.1 3.1 %copy.20 = f32[3,640,3,128]{1,3,0,2:T(8,128)S(1)} copy(f32[3,640,3,128]{3,1,2,0:T(8,128)} %pad_maximum_fusion) | data formatting | bytes 5898240 | tf_op jit(solution)/shard_map/while | solution.py:61
  48.2 1.2 broadcast_in_dim.3.clone
  49.4 15.3 %while.13 = (s32[]{:T(128)}, bf16[32,128,128]{2,1,0:T(8,128)(2,1)}, f32[640,3,32]{0,2,1:T(8,128)}, f32[3,640,3,128]{1,3,0,2:T(8,128)S(1)}, bf16[640,3,128]{2,0,1...) while((s32[]{:T(128)}, bf16[32,128,128]{2,1,0:T(8,128)(2,1)}, ...), condition=%wide.region_1.2_spmd, body=%wide.region_0.1_spmd.sunk | while | flops 515244032 | bytes 12800223 | solution.py:61
  49.4 0.8 dynamic-slice_bitcast_fusion.4
  50.5 1.8 fusion.19
  52.5 0.7 constant_dynamic-update-slice_fusion.2
  53.2 0.8 dynamic-slice_bitcast_fusion.4
  54.3 1.8 fusion.19
  57.1 0.8 dynamic-slice_bitcast_fusion.4
  58.1 1.8 fusion.19
  60.9 0.8 dynamic-slice_bitcast_fusion.4
  62.0 1.8 fusion.19
  64.7 32.1 %all_to_all.5 = bf16[8,512,128]{2,1,0:T(8,128)(2,1)S(1)} all-to-all(bf16[8,512,128]{2,1,0:T(8,128)(2,1)} %bitcast.46), channel_id=1, replica_groups=mesh['stream'=4,'span'=8] {'span'}, dimensions={0} | all-to-all | bytes 2097152 | tf_op jit(solution)/shard_map/all_to_all | solution.py:64
  96.8 0.8 reduce_sum.12
  97.7 38.9 %all-gather.3.cloned.1.call-done = bf16[4096,128]{1,0:T(8,128)(2,1)} async-done(((bf16[512,128]{1,0:T(8,128)(2,1)}), bf16[4096,128]{1,0:T(8,128)(2,1)}) %all-gather.3.cloned.1.call-update) | async-done | bytes 1048592 | tf_op jit(solution)/shard_map/all_gather | solution.py:66
  136.6 36.2 %all-gather.5.cloned.1.call-done = bf16[16384,128]{1,0:T(8,128)(2,1)} async-done(((bf16[4096,128]{1,0:T(8,128)(2,1)}), bf16[16384,128]{1,0:T(8,128)(2,1)}) %all-gather.5.cloned.1.call-update) | async-done | bytes 4194320 | tf_op jit(solution)/shard_map/all_gather | solution.py:67
  172.8 6.7 %convert.2 = f32[128,128,128]{2,1,0:T(8,128)} convert(bf16[128,128,128]{2,1,0:T(8,128)(2,1)} %bitcast.45) | non-fusion elementwise | flops 2097152 | bytes 12582912 | tf_op jit(solution)/shard_map/reshape | solution.py:68
  (37 shorter events, 5.2 us)
Async XLA Ops:
  6.5 130.1 %all-gather.3.cloned.1.call-start = ((), (), s32[]{:S(2)}) async-start(), calls=%async_computation.1 | async-start | bytes 1179648 | tf_op jit(solution)/shard_map/all_gather | solution.py:66
  7.6 11.6 %collective-permute-start = (bf16[2,2,10,3,128]{4,1,3,2,0:T(2,128)(2,1)S(1)}, bf16[2,2,10,3,128]{4,1,3,2,0:T(2,128)(2,1)S(1)}, u32[]{:S(2)}, u32[]{:S(2)}) collective-permute-start(bf16[2,2,10,3,128]{4,1,3,2,0:T(2,128)(2,1)S(1)} %get-tuple-element.133), channel_id=1, source_target_pairs={{0,1},{1,2},{2,3},{3,4},{4,5},{5,6},{6,7},{8,9},{9,10},{10,11},{11... | collective-permute-start | bytes 92168 | tf_op jit(solution)/shard_map/ppermute | solution.py:14
  11.5 7.6 %collective-permute-start.1 = (bf16[2,2,10,3,128]{4,1,3,2,0:T(2,128)(2,1)S(1)}, bf16[2,2,10,3,128]{4,1,3,2,0:T(2,128)(2,1)S(1)}, u32[]{:S(2)}, u32[]{:S(2)}) collective-permute-start(bf16[2,2,10,3,128]{4,1,3,2,0:T(2,128)(2,1)S(1)} %get-tuple-element.134), channel_id=1, source_target_pairs={{1,0},{2,1},{3,2},{4,3},{5,4},{6,5},{7,6},{9,8},{10,9},{11,10},{12... | collective-permute-start | bytes 92168 | tf_op jit(solution)/shard_map/ppermute | solution.py:16
  32.9 3.4 %copy-start.1 = (bf16[640,3,128]{2,0,1:T(8,128)(2,1)}, bf16[640,3,128]{2,0,1:T(8,128)(2,1)S(1)}, u32[]{:S(2)}) copy-start(bf16[640,3,128]{2,0,1:T(8,128)(2,1)S(1)} %reshape.21) | copy-start | bytes 1474564
  39.4 2.7 %copy-start = (f32[1,640,3,128]{3,1,2,0:T(8,128)S(1)}, f32[1,640,3,128]{3,1,2,0:T(8,128)}, u32[]{:S(2)}) copy-start(f32[1,640,3,128]{3,1,2,0:T(8,128)} %stack.14) | copy-start | bytes 2949124
  49.4 1.1 copy-start.2
  53.2 1.1 copy-start.2
  57.1 1.1 copy-start.2
  60.9 1.1 copy-start.2
  97.6 75.2 %all-gather.5.cloned.1.call-start = ((), (), s32[]{:S(2)}) async-start(), calls=%async_computation.2 | async-start | bytes 5242880 | tf_op jit(solution)/shard_map/all_gather | solution.py:67
Sparse Core Ops, SparseCore 0:
  97.7 38.8 all-gather.2
  138.2 34.6 all-gather.4

commit v3 on v1

v3 whole, which is shorter than its diff:
```python
import functools

import jax
import jax.numpy as jnp
from jax import lax
from jax.experimental import pallas as pl
from jax.experimental.pallas import tpu as pltpu
from jax.sharding import Mesh, PartitionSpec as P

STREAM = ("row", "core")
SPAN = ("deck", "side")
PLANE = ("row", "core", "side")
LANES = 128


def shift_pairs(axis, by):
    count = lax.axis_size(axis)
    return [(i, i + by) for i in range(count) if 0 <= i + by < count]


def rotate(value, axis, by=1):
    count = lax.axis_size(axis)
    return lax.ppermute(value, axis, [(i, (i + by) % count) for i in range(count)])


def terms_kernel(sizes, place_ref, cells_ref, weight_ref, out_ref, grad, own, phi, quad, total):
    layers, height, across, share, chunk = sizes
    width = LANES
    shift = lax.rem(width - place_ref[0] * share, width)

    def one_layer(x, _):
        def cell(layer, z, b, first=2):
            return cells_ref[layer, z, b, first : first + across, :]

        before = [(jnp.maximum(x - s, 0), (x >= s).astype(jnp.float32)) for s in (1, 2)]
        after = [
            (jnp.minimum(x + s, layers - 1), (x < layers - s).astype(jnp.float32)) for s in (1, 2)
        ]
        for z in range(height):
            at = pl.ds(pl.multiple_of((x * height + z) * across, across), across)
            weight = weight_ref[x, z]
            for b in range(3):
                here = cell(x, z, b)
                near = cell(after[0][0], z, b) * after[0][1] - cell(before[0][0], z, b) * before[0][1]
                far = cell(after[1][0], z, b) * after[1][1] - cell(before[1][0], z, b) * before[1][1]
                grad[0, b, at, :] = (8.0 * near - far) * (1.0 / 12.0)
                near = cell(x, z, b, 3) - cell(x, z, b, 1)
                far = cell(x, z, b, 4) - cell(x, z, b, 0)
                grad[1, b, at, :] = (8.0 * near - far) * (1.0 / 12.0)
                if z == 0:
                    grad[2, b, at, :] = 0.5 * cell(x, z + 1, b)
                elif z == height - 1:
                    grad[2, b, at, :] = -0.5 * cell(x, z - 1, b)
                else:
                    grad[2, b, at, :] = 0.5 * (cell(x, z + 1, b) - cell(x, z - 1, b))
                own[b, at, :] = pltpu.roll(here * weight, shift, 1)
                phi[b, at, :] = here
        return 0

    lax.fori_loop(0, layers, one_layer, 0)
    total[...] = jnp.zeros_like(total)
    rows = 16

    def one_chunk(turn, _):
        start = pl.multiple_of(turn * chunk, chunk)
        turned = jnp.concatenate(
            [phi[a, pl.ds(start, chunk), :].T.astype(jnp.bfloat16) for a in range(3)], axis=1
        )
        for pair in range(share // 2):
            for r in range(chunk // rows):
                at = pl.ds(pl.multiple_of(start + r * rows, rows), rows)
                mine = [own[b, at, :] for b in range(3)]
                for half in range(2):
                    lane = 2 * pair + half
                    spread = [
                        jnp.broadcast_to(mine[b][:, lane : lane + 1], (rows, width))
                        for b in range(3)
                    ]
                    for a in range(3):
                        value = spread[0] * grad[a, 0, at, :]
                        value = value + spread[1] * grad[a, 1, at, :]
                        value = value + spread[2] * grad[a, 2, at, :]
                        quad[
                            a * chunk + r * rows : a * chunk + (r + 1) * rows,
                            half * width : (half + 1) * width,
                        ] = value.astype(jnp.bfloat16)
            total[pair] += jnp.dot(turned, quad[...], preferred_element_type=jnp.float32)
        return 0

    lax.fori_loop(0, layers * height * across // chunk, one_chunk, 0)
    for pair in range(share // 2):
        for half in range(2):
            i = 2 * pair + half
            out_ref[i * width : (i + 1) * width, :] = total[
                pair, :, half * width : (half + 1) * width
            ].astype(jnp.bfloat16)


def plane_terms(place, cells, weight, share):
    layers, height, _, padded, width = cells.shape
    across = padded - 4
    count = layers * height * across
    chunk = next(c for c in (256, 128, 64, 32, 16) if count % c == 0)
    kernel = functools.partial(terms_kernel, (layers, height, across, share, chunk))
    flops = 2 * share * width * width * count * 3
    return pl.pallas_call(
        kernel,
        out_shape=jax.ShapeDtypeStruct((share * width, width), jnp.bfloat16),
        in_specs=[
            pl.BlockSpec(memory_space=pltpu.SMEM),
            pl.BlockSpec(memory_space=pltpu.VMEM),
            pl.BlockSpec(memory_space=pltpu.VMEM),
        ],
        out_specs=pl.BlockSpec(memory_space=pltpu.VMEM),
        scratch_shapes=[
            pltpu.VMEM((3, 3, count, width), jnp.float32),
            pltpu.VMEM((3, count, width), jnp.float32),
            pltpu.VMEM((3, count, width), jnp.float32),
            pltpu.VMEM((3 * chunk, 2 * width), jnp.bfloat16),
            pltpu.VMEM((share // 2, width, 2 * width), jnp.float32),
        ],
        compiler_params=pltpu.CompilerParams(vmem_limit_bytes=56 * 2**20),
        cost_estimate=pl.CostEstimate(flops=flops, bytes_accessed=2**22, transcendentals=0),
    )(place, cells, weight)


def pack(velocity, weight):
    x, y, z, comps, width = velocity.shape
    rows = velocity.transpose(0, 2, 3, 1, 4).reshape(x * z * comps * y, width)
    columns = weight.transpose(1, 0, 2).reshape(y, x * z)
    parts = []
    for _ in range(3):
        part = columns.astype(jnp.bfloat16)
        columns = columns - part.astype(jnp.float32)
        parts.append(part)
    tile = jnp.concatenate(parts, axis=1)
    tile = jnp.pad(tile, ((0, 0), (0, width - tile.shape[1])))
    return jnp.concatenate([rows, tile], axis=0)


def unpack(packed, shape):
    x, y, z, comps, width = shape
    streams = packed.shape[0] // 2
    cells = x * z * comps * y
    block = packed[:, :cells].reshape(streams, 2, x, z, comps, y, width)
    block = block.transpose(0, 2, 3, 4, 1, 5, 6).reshape(streams * x, z, comps, 2 * y, width)
    tile = packed[:, cells:, : 3 * x * z].astype(jnp.float32).reshape(streams, 2, y, 3, x, z)
    weight = tile.sum(axis=3).transpose(0, 3, 4, 1, 2).reshape(streams * x, z, 2 * y)
    return block, weight


def spread_all(piece):
    rows = lax.axis_size("row")
    half = piece.shape[0] // 2
    got = {(0, 0): piece}
    got[(0, 1)] = rotate(piece, "side")
    for r in range(1, rows):
        got[(r, 0)] = rotate(piece, "row", r)
    for r in range(1, rows):
        got[(r, 1)] = (
            rotate(got[(0, 1)][:half], "row", r),
            rotate(got[(r, 0)][half:], "side"),
        )
    out = {}
    for (r, s), value in got.items():
        out[(r, 0, s)] = value
        out[(r, 1, s)] = jax.tree.map(lambda v: rotate(v, "core"), value)
    return out


def shards(velocity_modes, cell_weight):
    shape = velocity_modes.shape
    width = shape[-1]
    rows, decks = lax.axis_size("row"), lax.axis_size("deck")
    members = rows * 4
    share = width // members
    row, core, side = (lax.axis_index(a) for a in PLANE)
    place = (row * 2 + core) * 2 + side

    packed = lax.all_gather(pack(velocity_modes, cell_weight), PLANE, axis=0, tiled=False)
    block, weight = unpack(packed, shape)
    below = lax.ppermute(block[..., -2:, :], "deck", shift_pairs("deck", 1))
    above = lax.ppermute(block[..., :2, :], "deck", shift_pairs("deck", -1))
    cells = jnp.concatenate([below, block, above], axis=3).astype(jnp.float32)
    spread_weight = jnp.broadcast_to(weight[..., None], weight.shape + (width,))
    terms = plane_terms(place.reshape(1).astype(jnp.int32), cells, spread_weight, share)

    parts = lax.all_to_all(terms.reshape(decks, -1, width), "deck", 0, 0)
    mine = jnp.sum(parts.astype(jnp.float32), axis=0).astype(jnp.bfloat16)
    piece = lax.all_gather(mine, "deck", axis=0, tiled=True)

    result = jnp.zeros((members * share * width, width), jnp.float32)
    for (r, c, s), value in spread_all(piece).items():
        source = (lax.rem(row - r + rows, rows) * 2 + lax.rem(core + c, 2)) * 2 + lax.rem(side + s, 2)
        start = source * share * width
        for part in value if isinstance(value, tuple) else (value,):
            result = lax.dynamic_update_slice(result, part.astype(jnp.float32), (start, 0))
            start = start + part.shape[0]
    return result.reshape(width, width, width)


def solution(mesh):
    streams, spans = (mesh.shape[name] for name in ("stream", "span"))
    split = Mesh(mesh.devices.reshape(streams // 2, 2, spans // 2, 2), STREAM + SPAN)
    placed = (P(STREAM, SPAN, None, None, None), P(STREAM, SPAN, None))
    return jax.shard_map(shards, mesh=split, in_specs=placed, out_specs=P(), check_vma=False)
```

time: 210 us -> 115 us (0.55)
  waiting for transfers between devices: 131 us -> 7.87 us
  blocking collectives: 16 us -> 52 us
  starting transfers between devices: 5.28 us -> 25.2 us
  Pallas kernels: 0 us -> 18.5 us
  local copies, waits for them, and re-layouts: 22.4 us -> 6.58 us
  between operations: 13.5 us -> 0.21 us
  other arithmetic: 13.7 us -> 4.2 us
  matrix products: 7.29 us -> 0 us
    all_gather x1 -> x0, waiting for transfers between devices: 66.6 us -> none  [shards(): whole = lax.all_gather(mine, ('stream', 'span'), axis=0, tiled=True)]
    reduce_scatter x1 -> x0, waiting for transfers between devices: 64.4 us -> none  [shards(): mine = lax.psum_scatter(rows, 'span', scatter_dimension=0, tiled=True)]
    ppermute x2 -> x11, starting transfers between devices: 5.24 us -> 25.2 us  [the longest x9 20.7 us: rotate(): lax.ppermute(value, axis, [(i, (i + by) % count) for i in range(count)])]
    pallas_call x0 -> x1, Pallas kernels: none -> 18.5 us  [plane_terms(): pl.pallas_call(kernel, out_shape=jax.ShapeDtypeStruct((share * width, wid...]
    all_gather x2, blocking collectives: 16 us -> 34.4 us  [the longest x1 21.6 us: shards(): lax.all_gather(pack(velocity_modes, cell_weight), PLANE, axis=0, tiled=Fa...]
    all_to_all x0 -> x1, blocking collectives: none -> 17.6 us  [shards(): parts = lax.all_to_all(terms.reshape(decks, -1, width), 'deck', 0, 0)]
    ppermute x2 -> x11, waiting for transfers between devices: 0.01 us -> 7.87 us  [the longest x1 4.26 us: shards(): above = lax.ppermute(block[..., :2, :], 'deck', shift_pairs('deck', -1))]
    dot_general x4 -> x0, matrix products: 7.29 us -> none  [one_block(): jnp.einsum('caj,acik->ijk', phi, quad, preferred_element_type=jnp.float32)]
  transfers between devices with their start and end apart: 4 -> 11, of which waited for: 2 -> 4; matrix products, arithmetic and copies ran while one was open for 0% -> 1% of each run, Pallas kernels for 0% -> 0%
where the time goes in v3:
time: 115 us
  blocking collectives  52 us (45%)
  starting transfers between devices  25.2 us (22%)
  Pallas kernels  18.5 us (16%)
  waiting for transfers between devices  7.87 us (7%)
  local copies, waits for them, and re-layouts  6.58 us (6%)
  other arithmetic  4.2 us (4%)
    all_gather x1, blocking collectives, shards(): lax.all_gather(pack(velocity_modes, cell_weight), PLANE, axis=0, tiled=Fa...  21.6 us
    ppermute x9, starting transfers between devices, rotate(): lax.ppermute(value, axis, [(i, (i + by) % count) for i in range(count)])  20.7 us
    pallas_call x1, Pallas kernels, plane_terms(): pl.pallas_call(kernel, out_shape=jax.ShapeDtypeStruct((share * width, wid...  18.5 us
    all_to_all x1, blocking collectives, shards(): parts = lax.all_to_all(terms.reshape(decks, -1, width), 'deck', 0, 0)  17.6 us
    all_gather x1, blocking collectives, shards(): piece = lax.all_gather(mine, 'deck', axis=0, tiled=True)  12.8 us
    ppermute x1, waiting for transfers between devices, shards(): above = lax.ppermute(block[..., :2, :], 'deck', shift_pairs('deck', -1))  4.26 us
    unnamed x2, local copies, waits for them, and re-layouts  3.39 us
    ppermute x1, starting transfers between devices, shards(): below = lax.ppermute(block[..., -2:, :], 'deck', shift_pairs('deck', 1))  3.21 us
  transfers between devices with their start and end apart: 11, of which 4 were waited for; matrix products, arithmetic and copies ran while one was open for 1% of the time, Pallas kernels for 0%

profile of v3, /device:TPU:1, one launch (start us, length us, event | category | flops | bytes accessed | tf_op | source)
XLA Modules:
  0.0 114.6 jit_solution(506521152471463136)
XLA Ops:
  0.0 0.7 copy.6
  0.7 0.1 reshape.30
  0.8 0.1 fusion.5
  0.9 0.9 pad_maximum_fusion
  1.8 21.6 %all-gather = bf16[3904,128]{1,0:T(8,128)(2,1)S(1)} all-gather(bf16[488,128]{1,0:T(8,128)(2,1)S(1)} %pad_maximum_fusion), channel_id=2, replica_groups=mesh['row'=2,'core'=2,'deck'=4,'side'=2] {'row','core','side'}, dimensions={0}, use_global_device_ids=true | all-gather | bytes 1124352 | tf_op jit(solution)/shard_map/all_gather | solution.py:180
  23.5 0.2 copy.7
  23.7 0.2 fusion.6
  23.9 3.2 %collective-permute-start = (bf16[8,10,3,2,128]{4,3,2,1,0:T(2,128)(2,1)S(1)}, bf16[8,10,3,2,128]{4,3,2,1,0:T(2,128)(2,1)S(1)}, u32[]{:S(2)}, u32[]{:S(2)}) collective-permute-start(bf16[8,10,3,2,128]{4,3,2,1,0:T(2,128)(2,1)S(1)} %get-tuple-element.5), channel_id=1, source_target_pairs={{0,2},{2,4},{4,6},{1,3},{3,5},{5,7},{8,10},{10,12},{12,14},{9,11},... | collective-permute-start | bytes 368648 | tf_op jit(solution)/shard_map/ppermute | solution.py:182
  27.1 1.3 %collective-permute-start.1 = (bf16[8,10,3,2,128]{4,3,2,1,0:T(2,128)(2,1)S(1)}, bf16[8,10,3,2,128]{4,3,2,1,0:T(2,128)(2,1)S(1)}, u32[]{:S(2)}, u32[]{:S(2)}) collective-permute-start(bf16[8,10,3,2,128]{4,3,2,1,0:T(2,128)(2,1)S(1)} %get-tuple-element.6), channel_id=1, source_target_pairs={{2,0},{4,2},{6,4},{3,1},{5,3},{7,5},{10,8},{12,10},{14,12},{11,9},... | collective-permute-start | bytes 368648 | tf_op jit(solution)/shard_map/ppermute | solution.py:183
  28.4 0.2 reshape.38
  28.6 0.1 reduce_sum.21
  28.8 0.1 copy.9
  28.9 1.1 collective-permute-done
  30.0 4.3 %collective-permute-done.1 = bf16[8,10,3,2,128]{4,3,2,1,0:T(2,128)(2,1)S(1)} collective-permute-done((bf16[8,10,3,2,128]{4,3,2,1,0:T(2,128)(2,1)S(1)}, bf16[8,10,3,2,128]{4,3,2,1,0:T(2,128)(2,1)S(1)}, u32[]{:S(2)}, u32[]{:S(2)}) %collective-permute-start.1) | collective-permute-done | bytes 122912 | tf_op jit(solution)/shard_map/ppermute | solution.py:183
  34.3 2.4 %maximum_convert_fusion.cells_ref = f32[8,10,3,20,128]{4,3,2,1,0:T(8,128)} fusion(bf16[8,10,3,2,128]{4,3,2,1,0:T(2,128)(2,1)S(1)} %collective-permute-done.1, bf16[8,10,3,16,128]{4,3,2,1,0:T(8,128)(2,1)S(1)} %bitcast.15, bf16[8,10,3,2,128]{4,3,2,1,0:T(2,128)(2,1)S(1)} %collective-permute-done), kind=kLoop, calls=%fused_computation | loop fusion | flops 3686400 | bytes 3686400 | tf_op jit(solution)/shard_map/convert_element_type | solution.py:184
  36.6 1.1 broadcast_in_dim.12.weight_ref
  37.7 18.5 %shard_map.28 = bf16[2048,128]{1,0:T(8,128)(2,1)} custom-call(s32[1]{0:T(128)} %bitcast.place_ref, f32[8,10,3,20,128]{4,3,2,1,0:T(8,128)} %maximum_convert_fusion.cells_ref, f32[8,10,16,128]{3,2,1,0:T(8,128)} %broadcast_in_dim.12.weight_ref), custom_call_target="tpu_custom_call" | custom-call | flops 2013265920 | bytes 4194304 | tf_op jit(solution)/shard_map/pallas_call | solution.py:106
  56.2 17.6 %all_to_all.5 = bf16[4,512,128]{2,1,0:T(8,128)(2,1)S(1)} all-to-all(bf16[4,512,128]{2,1,0:T(8,128)(2,1)} %bitcast.19), channel_id=1, replica_groups=mesh['row'=2,'core'=2,'deck'=4,'side'=2] {'deck'}, dimensions={0} | all-to-all | bytes 1048576 | tf_op jit(solution)/shard_map/all_to_all | solution.py:188
  73.8 0.1 reduce_sum.22
  73.9 12.8 %all_gather.11 = bf16[2048,128]{1,0:T(8,128)(2,1)S(1)} all-gather(bf16[512,128]{1,0:T(8,128)(2,1)S(1)} %reduce_sum.22), channel_id=1, replica_groups=mesh['row'=2,'core'=2,'deck'=4,'side'=2] {'deck'}, dimensions={0}, use_global_device_ids=true | all-gather | bytes 655360 | tf_op jit(solution)/shard_map/all_gather | solution.py:190
  86.6 0.1 collective-permute-start.3
  86.7 1.5 %collective-permute-start.5 = (bf16[2048,128]{1,0:T(8,128)(2,1)S(1)}, bf16[2048,128]{1,0:T(8,128)(2,1)S(1)}, u32[]{:S(2)}, u32[]{:S(2)}) collective-permute-start(bf16[2048,128]{1,0:T(8,128)(2,1)S(1)} %all_gather.11), channel_id=1, source_target_pairs={{0,16},{16,0},{1,17},{17,1},{2,18},{18,2},{3,19},{19,3},{4,20},{20... | collective-permute-start | bytes 1572872 | tf_op jit(solution)/shard_map/ppermute | solution.py:23
  88.2 5.0 %collective-permute-start.2 = (bf16[2048,128]{1,0:T(8,128)(2,1)S(1)}, bf16[2048,128]{1,0:T(8,128)(2,1)S(1)}, u32[]{:S(2)}, u32[]{:S(2)}) collective-permute-start(bf16[2048,128]{1,0:T(8,128)(2,1)S(1)} %all_gather.11), channel_id=1, source_target_pairs={{0,8},{8,0},{1,9},{9,1},{2,10},{10,2},{3,11},{11,3},{4,12},{12,4},... | collective-permute-start | bytes 1572872 | tf_op jit(solution)/shard_map/ppermute | solution.py:23
  93.2 0.6 broadcast_in_dim.10
  93.9 1.7 %collective-permute-done.3 = bf16[2048,128]{1,0:T(8,128)(2,1)S(1)} collective-permute-done((bf16[2048,128]{1,0:T(8,128)(2,1)S(1)}, bf16[2048,128]{1,0:T(8,128)(2,1)S(1)}, u32[]{:S(2)}, u32[]{:S(2)}) %collective-permute-start.3) | collective-permute-done | bytes 524320 | tf_op jit(solution)/shard_map/ppermute | solution.py:23
  95.6 0.4 collective-permute-start.7
  96.1 1.3 %collective-permute-start.8 = (bf16[1024,128]{1,0:T(8,128)(2,1)S(1)}, bf16[1024,128]{1,0:T(8,128)(2,1)S(1)}, u32[]{:S(2)}, u32[]{:S(2)}) collective-permute-start(bf16[1024,128]{1,0:T(8,128)(2,1)S(1)} %slice.29), channel_id=1, source_target_pairs={{0,1},{1,0},{2,3},{3,2},{4,5},{5,4},{6,7},{7,6},{8,9},{9,8},{10,11... | collective-permute-start | bytes 786440 | tf_op jit(solution)/shard_map/ppermute | solution.py:23
  97.3 8.3 %collective-permute-start.4 = (bf16[2048,128]{1,0:T(8,128)(2,1)S(1)}, bf16[2048,128]{1,0:T(8,128)(2,1)S(1)}, u32[]{:S(2)}, u32[]{:S(2)}) collective-permute-start(bf16[2048,128]{1,0:T(8,128)(2,1)S(1)} %collective-permute-done.3), channel_id=1, source_target_pairs={{0,8},{8,0},{1,9},{9,1},{2,10},{10,2},{3,11},{11,3},{4,12},{12,4},... | collective-permute-start | bytes 1572872 | tf_op jit(solution)/shard_map/ppermute | solution.py:23
  105.8 3.3 %collective-permute-start.9 = (bf16[1024,128]{1,0:T(8,128)(2,1)S(1)}, bf16[1024,128]{1,0:T(8,128)(2,1)S(1)}, u32[]{:S(2)}, u32[]{:S(2)}) collective-permute-start(bf16[1024,128]{1,0:T(8,128)(2,1)S(1)} %collective-permute-done.7), channel_id=1, source_target_pairs={{0,8},{8,0},{1,9},{9,1},{2,10},{10,2},{3,11},{11,3},{4,12},{12,4},... | collective-permute-start | bytes 786440 | tf_op jit(solution)/shard_map/ppermute | solution.py:23
  109.1 0.9 collective-permute-start.10
  110.4 0.7 collective-permute-done.10
  111.2 3.4 %copy-done = f32[16384,128]{1,0:T(8,128)} copy-done((f32[16384,128]{1,0:T(8,128)}, f32[16384,128]{1,0:T(8,128)S(1)}, u32[]{:S(2)}) %copy-start) | copy-done | bytes 8388632
  (25 shorter events, 0.8 us)
Async XLA Ops:
  23.9 6.1 %collective-permute-start = (bf16[8,10,3,2,128]{4,3,2,1,0:T(2,128)(2,1)S(1)}, bf16[8,10,3,2,128]{4,3,2,1,0:T(2,128)(2,1)S(1)}, u32[]{:S(2)}, u32[]{:S(2)}) collective-permute-start(bf16[8,10,3,2,128]{4,3,2,1,0:T(2,128)(2,1)S(1)} %get-tuple-element.5), channel_id=1, source_target_pairs={{0,2},{2,4},{4,6},{1,3},{3,5},{5,7},{8,10},{10,12},{12,14},{9,11},... | collective-permute-start | bytes 368648 | tf_op jit(solution)/shard_map/ppermute | solution.py:182
  27.1 7.2 %collective-permute-start.1 = (bf16[8,10,3,2,128]{4,3,2,1,0:T(2,128)(2,1)S(1)}, bf16[8,10,3,2,128]{4,3,2,1,0:T(2,128)(2,1)S(1)}, u32[]{:S(2)}, u32[]{:S(2)}) collective-permute-start(bf16[8,10,3,2,128]{4,3,2,1,0:T(2,128)(2,1)S(1)} %get-tuple-element.6), channel_id=1, source_target_pairs={{2,0},{4,2},{6,4},{3,1},{5,3},{7,5},{10,8},{12,10},{14,12},{11,9},... | collective-permute-start | bytes 368648 | tf_op jit(solution)/shard_map/ppermute | solution.py:183
  86.6 9.0 %collective-permute-start.3 = (bf16[2048,128]{1,0:T(8,128)(2,1)S(1)}, bf16[2048,128]{1,0:T(8,128)(2,1)S(1)}, u32[]{:S(2)}, u32[]{:S(2)}) collective-permute-start(bf16[2048,128]{1,0:T(8,128)(2,1)S(1)} %all_gather.11), channel_id=1, source_target_pairs={{0,1},{1,0},{2,3},{3,2},{4,5},{5,4},{6,7},{7,6},{8,9},{9,8},{10,11... | collective-permute-start | bytes 1572872 | tf_op jit(solution)/shard_map/ppermute | solution.py:23
  86.7 9.3 %collective-permute-start.5 = (bf16[2048,128]{1,0:T(8,128)(2,1)S(1)}, bf16[2048,128]{1,0:T(8,128)(2,1)S(1)}, u32[]{:S(2)}, u32[]{:S(2)}) collective-permute-start(bf16[2048,128]{1,0:T(8,128)(2,1)S(1)} %all_gather.11), channel_id=1, source_target_pairs={{0,16},{16,0},{1,17},{17,1},{2,18},{18,2},{3,19},{19,3},{4,20},{20... | collective-permute-start | bytes 1572872 | tf_op jit(solution)/shard_map/ppermute | solution.py:23
  88.2 17.4 %collective-permute-start.2 = (bf16[2048,128]{1,0:T(8,128)(2,1)S(1)}, bf16[2048,128]{1,0:T(8,128)(2,1)S(1)}, u32[]{:S(2)}, u32[]{:S(2)}) collective-permute-start(bf16[2048,128]{1,0:T(8,128)(2,1)S(1)} %all_gather.11), channel_id=1, source_target_pairs={{0,8},{8,0},{1,9},{9,1},{2,10},{10,2},{3,11},{11,3},{4,12},{12,4},... | collective-permute-start | bytes 1572872 | tf_op jit(solution)/shard_map/ppermute | solution.py:23
  95.6 10.2 %collective-permute-start.7 = (bf16[1024,128]{1,0:T(8,128)(2,1)S(1)}, bf16[1024,128]{1,0:T(8,128)(2,1)S(1)}, u32[]{:S(2)}, u32[]{:S(2)}) collective-permute-start(bf16[1024,128]{1,0:T(8,128)(2,1)S(1)} %slice.28), channel_id=1, source_target_pairs={{0,16},{16,0},{1,17},{17,1},{2,18},{18,2},{3,19},{19,3},{4,20},{20... | collective-permute-start | bytes 786440 | tf_op jit(solution)/shard_map/ppermute | solution.py:23
  96.1 13.0 %collective-permute-start.8 = (bf16[1024,128]{1,0:T(8,128)(2,1)S(1)}, bf16[1024,128]{1,0:T(8,128)(2,1)S(1)}, u32[]{:S(2)}, u32[]{:S(2)}) collective-permute-start(bf16[1024,128]{1,0:T(8,128)(2,1)S(1)} %slice.29), channel_id=1, source_target_pairs={{0,1},{1,0},{2,3},{3,2},{4,5},{5,4},{6,7},{7,6},{8,9},{9,8},{10,11... | collective-permute-start | bytes 786440 | tf_op jit(solution)/shard_map/ppermute | solution.py:23
  97.3 12.6 %collective-permute-start.4 = (bf16[2048,128]{1,0:T(8,128)(2,1)S(1)}, bf16[2048,128]{1,0:T(8,128)(2,1)S(1)}, u32[]{:S(2)}, u32[]{:S(2)}) collective-permute-start(bf16[2048,128]{1,0:T(8,128)(2,1)S(1)} %collective-permute-done.3), channel_id=1, source_target_pairs={{0,8},{8,0},{1,9},{9,1},{2,10},{10,2},{3,11},{11,3},{4,12},{12,4},... | collective-permute-start | bytes 1572872 | tf_op jit(solution)/shard_map/ppermute | solution.py:23
  105.6 4.5 %collective-permute-start.6 = (bf16[2048,128]{1,0:T(8,128)(2,1)S(1)}, bf16[2048,128]{1,0:T(8,128)(2,1)S(1)}, u32[]{:S(2)}, u32[]{:S(2)}) collective-permute-start(bf16[2048,128]{1,0:T(8,128)(2,1)S(1)} %collective-permute-done.5), channel_id=1, source_target_pairs={{0,8},{8,0},{1,9},{9,1},{2,10},{10,2},{3,11},{11,3},{4,12},{12,4},... | collective-permute-start | bytes 1572872 | tf_op jit(solution)/shard_map/ppermute | solution.py:23
  105.8 4.5 %collective-permute-start.9 = (bf16[1024,128]{1,0:T(8,128)(2,1)S(1)}, bf16[1024,128]{1,0:T(8,128)(2,1)S(1)}, u32[]{:S(2)}, u32[]{:S(2)}) collective-permute-start(bf16[1024,128]{1,0:T(8,128)(2,1)S(1)} %collective-permute-done.7), channel_id=1, source_target_pairs={{0,8},{8,0},{1,9},{9,1},{2,10},{10,2},{3,11},{11,3},{4,12},{12,4},... | collective-permute-start | bytes 786440 | tf_op jit(solution)/shard_map/ppermute | solution.py:23
  109.1 2.0 %collective-permute-start.10 = (bf16[1024,128]{1,0:T(8,128)(2,1)S(1)}, bf16[1024,128]{1,0:T(8,128)(2,1)S(1)}, u32[]{:S(2)}, u32[]{:S(2)}) collective-permute-start(bf16[1024,128]{1,0:T(8,128)(2,1)S(1)} %collective-permute-done.8), channel_id=1, source_target_pairs={{0,8},{8,0},{1,9},{9,1},{2,10},{10,2},{3,11},{11,3},{4,12},{12,4},... | collective-permute-start | bytes 786440 | tf_op jit(solution)/shard_map/ppermute | solution.py:23
  111.2 3.4 %copy-start = (f32[16384,128]{1,0:T(8,128)}, f32[16384,128]{1,0:T(8,128)S(1)}, u32[]{:S(2)}) copy-start(f32[16384,128]{1,0:T(8,128)S(1)} %convert_dynamic-update-slice_fusion.6) | copy-start | bytes 25165828

commit v4 on v1

v4 whole, which is shorter than its diff:
```python
import functools

import jax
import jax.numpy as jnp
from jax import lax
from jax.experimental import pallas as pl
from jax.experimental.pallas import tpu as pltpu
from jax.sharding import Mesh, PartitionSpec as P

STREAM = ("row", "core")
SPAN = ("deck", "side")
DIAGONAL = ("row", "side")
WEIGHT_PARTS = 3
VMEM_LIMIT = 56 * 2**20


def rotate(value, axis, by=1):
    count = lax.axis_size(axis)
    return lax.ppermute(value, axis, [(i, (i + by) % count) for i in range(count)])


def terms_kernel(sizes, place_ref, *refs):
    layers, height, across, width, share, members = sizes
    pieces, out_ref = refs[:members], refs[members]
    field, grad, own, tall, turned, quad, total = refs[members + 1 :]
    cells = layers * height * across
    slab = 2 * cells
    depth = quad.shape[1]
    streams = members // 2
    shift = place_ref[0]

    for n, piece in enumerate(pieces):
        field[place_ref[1 + n]] = piece[...].astype(jnp.float32)

    index = lax.broadcasted_iota(jnp.int32, (across, width), 0)

    def column(b):
        return slice(b * width, (b + 1) * width)

    def one_stream(s, _):
        def layer_at(layer, side):
            at = s * layers + layer
            inside = ((at >= 0) & (at < streams * layers)).astype(jnp.float32)
            at = jnp.clip(at, 0, streams * layers - 1)
            return lax.div(at, layers) * 2 + side, lax.rem(at, layers), inside

        for side in range(2):
            member = 2 * s + side
            tile = field[member, cells + 2 * layers * height :, 0:width]
            weights = tile
            for part in range(1, WEIGHT_PARTS):
                weights = weights + pltpu.roll(tile, width - part * layers * height, 1)
            for layer in range(layers):
                beside = {step: layer_at(layer + step, side) for step in (-2, -1, 1, 2)}
                for z in range(height):
                    line = layer * height + z
                    row = line * across
                    rows = slice(row, row + across)
                    at = pl.ds(pl.multiple_of(member * cells + row, across), across)
                    weight = jnp.broadcast_to(weights[:, line : line + 1], (across, width))
                    first = cells + 2 * line
                    base = first // across * across
                    for b in range(3):
                        here = field[member, rows, column(b)]
                        along = {}
                        for step, (m, l, inside) in beside.items():
                            start = pl.multiple_of((l * height + z) * across, across)
                            along[step] = field[m, pl.ds(start, across), column(b)] * inside
                        value = 8.0 * (along[1] - along[-1]) - (along[2] - along[-2])
                        grad[0, at, column(b)] = value * (1.0 / 12.0)

                        outer = field[member, base : base + across, column(b)]
                        if side == 0:
                            prev = pltpu.roll(outer, (across - 2 - (first - base)) % across, 0)
                            after = field[member + 1, rows, column(b)]
                        else:
                            prev = field[member - 1, rows, column(b)]
                            after = pltpu.roll(outer, (across - (first - base)) % across, 0)
                        near = pltpu.roll(jnp.where(index < 1, after, here), across - 1, 0)
                        near = near - pltpu.roll(jnp.where(index >= across - 1, prev, here), 1, 0)
                        far = pltpu.roll(jnp.where(index < 2, after, here), across - 2, 0)
                        far = far - pltpu.roll(jnp.where(index >= across - 2, prev, here), 2, 0)
                        grad[1, at, column(b)] = (8.0 * near - far) * (1.0 / 12.0)

                        value = jnp.zeros_like(here)
                        if z < height - 1:
                            value = field[member, row + across : row + 2 * across, column(b)]
                        if z > 0:
                            value = value - field[member, row - across : row, column(b)]
                        grad[2, at, column(b)] = 0.5 * value
                        own[at, column(b)] = pltpu.roll(here * weight, shift, 1)
            for a in range(3):
                start = a * slab + side * cells
                tall[start : start + cells, :] = field[member, :cells, column(a)]
        if depth > 3 * slab:
            tall[3 * slab :, :] = jnp.zeros((depth - 3 * slab, width), jnp.float32)
        turned[s] = tall[...].T.astype(jnp.bfloat16)
        return 0

    lax.fori_loop(0, streams, one_stream, 0)
    total[...] = jnp.zeros_like(total)
    if depth > 3 * slab:
        quad[:, 3 * slab :, :] = jnp.zeros((2, depth - 3 * slab, 2 * width), jnp.bfloat16)
    rows = 16

    def one_slab(s, _):
        for pair in range(share // 2):
            for r in range(slab // rows):
                at = pl.ds(pl.multiple_of(s * slab + r * rows, rows), rows)
                mine = [own[at, column(b)] for b in range(3)]
                for half in range(2):
                    lane = 2 * pair + half
                    spread = [
                        jnp.broadcast_to(mine[b][:, lane : lane + 1], (rows, width))
                        for b in range(3)
                    ]
                    for a in range(3):
                        value = spread[0] * grad[a, at, column(0)]
                        value = value + spread[1] * grad[a, at, column(1)]
                        value = value + spread[2] * grad[a, at, column(2)]
                        start = a * slab + r * rows
                        quad[pair % 2, start : start + rows, column(half)] = value.astype(
                            jnp.bfloat16
                        )
            total[pair] += jnp.dot(
                turned[s], quad[pair % 2], preferred_element_type=jnp.float32
            )
        return 0

    lax.fori_loop(0, streams, one_slab, 0)
    for pair in range(share // 2):
        for half in range(2):
            start = (2 * pair + half) * width
            out_ref[start : start + width, :] = total[pair, :, column(half)].astype(jnp.bfloat16)


def plane_terms(place, pieces, shape, share):
    layers, across, height, comps, width = shape
    members = len(pieces)
    cells = layers * height * across
    count = members * cells
    depth = pl.cdiv(3 * 2 * cells, 256) * 256
    sizes = (layers, height, across, width, share, members)
    vmem = pl.BlockSpec(memory_space=pltpu.VMEM)
    return pl.pallas_call(
        functools.partial(terms_kernel, sizes),
        out_shape=jax.ShapeDtypeStruct((share * width, width), jnp.bfloat16),
        in_specs=[pl.BlockSpec(memory_space=pltpu.SMEM)] + [vmem] * members,
        out_specs=vmem,
        scratch_shapes=[
            pltpu.VMEM((members,) + pieces[0].shape, jnp.float32),
            pltpu.VMEM((3, count, comps * width), jnp.float32),
            pltpu.VMEM((count, comps * width), jnp.float32),
            pltpu.VMEM((depth, width), jnp.float32),
            pltpu.VMEM((members // 2, width, depth), jnp.bfloat16),
            pltpu.VMEM((2, depth, 2 * width), jnp.bfloat16),
            pltpu.VMEM((share // 2, width, 2 * width), jnp.float32),
        ],
        compiler_params=pltpu.CompilerParams(vmem_limit_bytes=VMEM_LIMIT),
        cost_estimate=pl.CostEstimate(
            flops=2 * share * width * width * count * 3, bytes_accessed=2**22, transcendentals=0
        ),
    )(place, *pieces)


def place_kernel(pieces, given, start_ref, *refs):
    out_ref, wide, sems = refs[pieces + given :]
    copies = []
    done = 0
    for n, piece in enumerate(refs[:pieces]):
        rows = piece.shape[0]
        here = wide.at[done : done + rows]
        here[...] = piece[...].astype(jnp.float32)
        to = pl.ds(pl.multiple_of(start_ref[n], rows), rows)
        copies.append(pltpu.make_async_copy(here, out_ref.at[to], sems.at[n]))
        copies[-1].start()
        done += rows
    for copy in copies:
        copy.wait()


def put(result, total_rows, pieces, starts):
    width = pieces[0].shape[1]
    given = [] if result is None else [result]
    rows = sum(piece.shape[0] for piece in pieces)
    vmem, anywhere = (pl.BlockSpec(memory_space=m) for m in (pltpu.VMEM, pl.ANY))
    return pl.pallas_call(
        functools.partial(place_kernel, len(pieces), len(given)),
        out_shape=jax.ShapeDtypeStruct((total_rows, width), jnp.float32),
        in_specs=[pl.BlockSpec(memory_space=pltpu.SMEM)]
        + [vmem] * len(pieces)
        + [anywhere] * len(given),
        out_specs=anywhere,
        scratch_shapes=[
            pltpu.VMEM((rows, width), jnp.float32),
            pltpu.SemaphoreType.DMA((len(pieces),)),
        ],
        input_output_aliases={1 + len(pieces): 0} if given else {},
        compiler_params=pltpu.CompilerParams(vmem_limit_bytes=VMEM_LIMIT),
        cost_estimate=pl.CostEstimate(
            flops=0, bytes_accessed=6 * rows * width, transcendentals=0
        ),
    )(jnp.stack(starts).astype(jnp.int32), *pieces, *given)


def pack(velocity, weight):
    x, y, z, comps, width = velocity.shape
    side = lax.axis_index("side")
    decks = lax.axis_size("deck")
    edge = jnp.where(side == 1, velocity[:, y - 2 :], velocity[:, :2])
    joints = [(2 * d + 1, 2 * d + 2) for d in range(decks - 1)]
    outer = lax.ppermute(edge, SPAN, joints + [(j, i) for i, j in joints])
    columns = weight.transpose(1, 0, 2).reshape(y, x * z)
    parts = []
    for _ in range(WEIGHT_PARTS):
        part = lax.reduce_precision(columns, 8, 7)
        columns = columns - part
        parts.append(part.astype(jnp.bfloat16))
    tile = jnp.concatenate(parts, axis=1)
    tile = jnp.pad(tile, ((0, 0), (0, comps * width - tile.shape[1])))
    rows = [v.transpose(0, 2, 1, 3, 4).reshape(-1, comps * width) for v in (velocity, outer)]
    return jnp.concatenate(rows + [tile], axis=0)


def spread_small(piece):
    rows = lax.axis_size("row")
    got = {(0, 0): piece, (0, 1): rotate(piece, "side")}
    for r in range(1, rows):
        got[(r, 0)] = rotate(piece, "row", r)
        pairs = [
            (2 * i + s, 2 * ((i + r) % rows) + 1 - s) for i in range(rows) for s in range(2)
        ]
        got[(r, 1)] = lax.ppermute(piece, DIAGONAL, pairs)
    out = {}
    for (r, s), value in got.items():
        out[(r, 0, s)] = value
        out[(r, 1, s)] = rotate(value, "core")
    return out


def spread_all(piece):
    rows = lax.axis_size("row")
    half = piece.shape[0] // 2
    got = {(0, 0): (piece,), (0, 1): (rotate(piece, "side"),)}
    for r in range(1, rows):
        got[(r, 0)] = (rotate(piece, "row", r),)
    for r in range(1, rows):
        got[(r, 1)] = (
            rotate(got[(0, 1)][0][:half], "row", r),
            rotate(got[(r, 0)][0][half:], "side"),
        )
    out = {}
    for (r, s), value in got.items():
        out[(r, 0, s)] = value
        out[(r, 1, s)] = tuple(rotate(v, "core") for v in value)
    return out


def shards(velocity_modes, cell_weight):
    shape = velocity_modes.shape
    width = shape[-1]
    rows, decks = lax.axis_size("row"), lax.axis_size("deck")
    members = rows * 4
    share = width // members
    row, core, side = (lax.axis_index(a) for a in ("row", "core", "side"))

    def member(r, c, s):
        return (lax.rem(row - r + rows, rows) * 2 + lax.rem(core + c, 2)) * 2 + lax.rem(side + s, 2)

    pieces = spread_small(pack(velocity_modes, cell_weight))
    shift = lax.rem(width - member(0, 0, 0) * share, width)
    place = jnp.stack([shift] + [member(*offsets) for offsets in pieces]).astype(jnp.int32)
    terms = plane_terms(place, list(pieces.values()), shape, share)

    parts = lax.all_to_all(terms.reshape(decks, -1, width), "deck", 0, 0)
    mine = jnp.sum(parts.astype(jnp.float32), axis=0).astype(jnp.bfloat16)
    piece = lax.all_gather(mine, "deck", axis=0, tiled=True)

    result = None
    block = share * width
    got = spread_all(piece)
    for s, r in sorted({(s, r) for r, _, s in got}):
        values, starts = [], []
        for c in range(2):
            start = member(r, c, s) * block
            for value in got[(r, c, s)]:
                values.append(value)
                starts.append(start)
                start = start + value.shape[0]
        result = put(result, members * block, values, starts)
    return result.reshape(width, width, width)


def solution(mesh):
    streams, spans = (mesh.shape[name] for name in ("stream", "span"))
    split = Mesh(mesh.devices.reshape(streams // 2, 2, spans // 2, 2), STREAM + SPAN)
    placed = (P(STREAM, SPAN, None, None, None), P(STREAM, SPAN, None))
    return jax.shard_map(shards, mesh=split, in_specs=placed, out_specs=P(), check_vma=False)
```

time: 210 us -> 114 us (0.54)
  waiting for transfers between devices: 131 us -> 7.76 us
  Pallas kernels: 0 us -> 31.2 us
  starting transfers between devices: 5.28 us -> 33.6 us
  local copies, waits for them, and re-layouts: 22.4 us -> 6.3 us
  blocking collectives: 16 us -> 30.4 us
  between operations: 13.5 us -> 0.2 us
  other arithmetic: 13.7 us -> 4.69 us
  matrix products: 7.29 us -> 0 us
    all_gather x1 -> x0, waiting for transfers between devices: 66.6 us -> none  [shards(): whole = lax.all_gather(mine, ('stream', 'span'), axis=0, tiled=True)]
    reduce_scatter x1 -> x0, waiting for transfers between devices: 64.4 us -> none  [shards(): mine = lax.psum_scatter(rows, 'span', scatter_dimension=0, tiled=True)]
    pallas_call x0 -> x5, Pallas kernels: none -> 31.2 us  [the longest x1 20.8 us: plane_terms(): pl.pallas_call(functools.partial(terms_kernel, sizes), out_shape=jax.Shap...]
    ppermute x2 -> x17, starting transfers between devices: 5.24 us -> 33.6 us  [the longest x15 32.9 us: rotate(): lax.ppermute(value, axis, [(i, (i + by) % count) for i in range(count)])]
    all_to_all x0 -> x1, blocking collectives: none -> 17.6 us  [shards(): parts = lax.all_to_all(terms.reshape(decks, -1, width), 'deck', 0, 0)]
    ppermute x2 -> x17, waiting for transfers between devices: 0.01 us -> 7.76 us  [the longest x15 7.75 us: rotate(): lax.ppermute(value, axis, [(i, (i + by) % count) for i in range(count)])]
    dot_general x4 -> x0, matrix products: 7.29 us -> none  [one_block(): jnp.einsum('caj,acik->ijk', phi, quad, preferred_element_type=jnp.float32)]
    reshape x1 -> x0, other arithmetic: 6.65 us -> none  [shards(): return whole.astype(jnp.float32).reshape(width, width, width)]
  transfers between devices with their start and end apart: 4 -> 17, of which waited for: 2 -> 3; matrix products, arithmetic and copies ran while one was open for 0% -> 5% of each run, Pallas kernels for 0% -> 7%
where the time goes in v4:
time: 114 us
  starting transfers between devices  33.6 us (29%)
  Pallas kernels  31.2 us (27%)
  blocking collectives  30.4 us (27%)
  waiting for transfers between devices  7.76 us (7%)
  local copies, waits for them, and re-layouts  6.3 us (6%)
  other arithmetic  4.69 us (4%)
    ppermute x15, starting transfers between devices, rotate(): lax.ppermute(value, axis, [(i, (i + by) % count) for i in range(count)])  32.9 us
    pallas_call x1, Pallas kernels, plane_terms(): pl.pallas_call(functools.partial(terms_kernel, sizes), out_shape=jax.Shap...  20.8 us
    all_to_all x1, blocking collectives, shards(): parts = lax.all_to_all(terms.reshape(decks, -1, width), 'deck', 0, 0)  17.6 us
    all_gather x1, blocking collectives, shards(): piece = lax.all_gather(mine, 'deck', axis=0, tiled=True)  12.7 us
    pallas_call x4, Pallas kernels, put(): pl.pallas_call(functools.partial(place_kernel, len(pieces), len(given)),...  10.4 us
    ppermute x15, waiting for transfers between devices, rotate(): lax.ppermute(value, axis, [(i, (i + by) % count) for i in range(count)])  7.75 us
    unnamed x31, local copies, waits for them, and re-layouts  3.35 us
    another operation x4, other arithmetic, put(): jnp.stack(starts).astype(jnp.int32)  2.57 us
  transfers between devices with their start and end apart: 17, of which 3 were waited for; matrix products, arithmetic and copies ran while one was open for 5% of the time, Pallas kernels for 7%

profile of v4, /device:TPU:1, one launch (start us, length us, event | category | flops | bytes accessed | tf_op | source)
XLA Modules:
  0.0 114.1 jit_solution(1932909772419281485)
XLA Ops:
  0.0 1.0 broadcast_select_fusion
  1.0 0.7 collective-permute-start
  1.7 0.7 copy.9
  2.6 0.9 pad_maximum_fusion.refs_0_
  3.6 6.1 %collective-permute-start.2 = (bf16[208,384]{1,0:T(8,128)(2,1)S(1)}, bf16[208,384]{1,0:T(8,128)(2,1)S(1)}, u32[]{:S(2)}, u32[]{:S(2)}) collective-permute-start(bf16[208,384]{1,0:T(8,128)(2,1)S(1)} %pad_maximum_fusion.refs_0_), channel_id=1, source_target_pairs={{0,1},{1,0},{2,3},{3,2},{4,5},{5,4},{6,7},{7,6},{8,9},{9,8},{10,11... | collective-permute-start | bytes 479240 | tf_op jit(solution)/shard_map/ppermute | solution.py:19
  9.6 1.2 %collective-permute-start.4 = (bf16[208,384]{1,0:T(8,128)(2,1)S(1)}, bf16[208,384]{1,0:T(8,128)(2,1)S(1)}, u32[]{:S(2)}, u32[]{:S(2)}) collective-permute-start(bf16[208,384]{1,0:T(8,128)(2,1)S(1)} %pad_maximum_fusion.refs_0_), channel_id=1, source_target_pairs={{0,16},{16,0},{1,17},{17,1},{2,18},{18,2},{3,19},{19,3},{4,20},{20... | collective-permute-start | bytes 479240 | tf_op jit(solution)/shard_map/ppermute | solution.py:19
  10.9 2.4 %collective-permute-start.1 = (bf16[208,384]{1,0:T(8,128)(2,1)S(1)}, bf16[208,384]{1,0:T(8,128)(2,1)S(1)}, u32[]{:S(2)}, u32[]{:S(2)}) collective-permute-start(bf16[208,384]{1,0:T(8,128)(2,1)S(1)} %pad_maximum_fusion.refs_0_), channel_id=1, source_target_pairs={{0,8},{8,0},{1,9},{9,1},{2,10},{10,2},{3,11},{11,3},{4,12},{12,4},... | collective-permute-start | bytes 479240 | tf_op jit(solution)/shard_map/ppermute | solution.py:19
  13.3 2.8 %collective-permute-start.3 = (bf16[208,384]{1,0:T(8,128)(2,1)S(1)}, bf16[208,384]{1,0:T(8,128)(2,1)S(1)}, u32[]{:S(2)}, u32[]{:S(2)}) collective-permute-start(bf16[208,384]{1,0:T(8,128)(2,1)S(1)} %collective-permute-done.2.refs_2_), channel_id=1, source_target_pairs={{0,8},{8,0},{1,9},{9,1},{2,10},{10,2},{3,11},{11,3},{4,12},{12,4},... | collective-permute-start | bytes 479240 | tf_op jit(solution)/shard_map/ppermute | solution.py:19
  16.1 4.1 %collective-permute-start.5 = (bf16[208,384]{1,0:T(8,128)(2,1)S(1)}, bf16[208,384]{1,0:T(8,128)(2,1)S(1)}, u32[]{:S(2)}, u32[]{:S(2)}) collective-permute-start(bf16[208,384]{1,0:T(8,128)(2,1)S(1)} %collective-permute-done.4.refs_4_), channel_id=1, source_target_pairs={{0,8},{8,0},{1,9},{9,1},{2,10},{10,2},{3,11},{11,3},{4,12},{12,4},... | collective-permute-start | bytes 479240 | tf_op jit(solution)/shard_map/ppermute | solution.py:19
  21.9 0.7 copy-done.14
  22.5 20.8 %shard_map.28 = bf16[2048,128]{1,0:T(8,128)(2,1)} custom-call(s32[9]{0:T(128)} %stack.86.place_ref, bf16[208,384]{1,0:T(8,128)(2,1)} %copy-done.7, bf16[208,384]{1,0:T(8,128)(2,1)} %copy-done.11, bf16[208,384]{1,0:T(8,128)(2,1)} %copy-done.8, bf16[208,384]{1,0:T(8,128)(2,1)} %copy-done.12, bf16[208,384]{1,0:T(8,128)(2,1)} %copy-done.9, ...), custom_call_target="tpu_custom_call" | custom-call | flops 2013265920 | bytes 4194304 | tf_op jit(solution)/shard_map/pallas_call | solution.py:145
  43.3 17.6 %all_to_all.5 = bf16[4,512,128]{2,1,0:T(8,128)(2,1)S(1)} all-to-all(bf16[4,512,128]{2,1,0:T(8,128)(2,1)} %bitcast.31), channel_id=1, replica_groups=mesh['row'=2,'core'=2,'deck'=4,'side'=2] {'deck'}, dimensions={0} | all-to-all | bytes 1048576 | tf_op jit(solution)/shard_map/all_to_all | solution.py:275
  61.1 12.7 %all_gather.3.refs_0_ = bf16[2048,128]{1,0:T(8,128)(2,1)S(1)} all-gather(bf16[512,128]{1,0:T(8,128)(2,1)S(1)} %reduce_sum.12), channel_id=1, replica_groups=mesh['row'=2,'core'=2,'deck'=4,'side'=2] {'deck'}, dimensions={0}, use_global_device_ids=true | all-gather | bytes 655360 | tf_op jit(solution)/shard_map/all_gather | solution.py:277
  73.8 1.2 %collective-permute-start.8 = (bf16[2048,128]{1,0:T(8,128)(2,1)S(1)}, bf16[2048,128]{1,0:T(8,128)(2,1)S(1)}, u32[]{:S(2)}, u32[]{:S(2)}) collective-permute-start(bf16[2048,128]{1,0:T(8,128)(2,1)S(1)} %all_gather.3.refs_0_), channel_id=1, source_target_pairs={{0,1},{1,0},{2,3},{3,2},{4,5},{5,4},{6,7},{7,6},{8,9},{9,8},{10,11... | collective-permute-start | bytes 1572872 | tf_op jit(solution)/shard_map/ppermute | solution.py:19
  75.0 0.7 collective-permute-start.10
  75.8 7.0 %collective-permute-done.8.refs_0_ = bf16[2048,128]{1,0:T(8,128)(2,1)S(1)} collective-permute-done((bf16[2048,128]{1,0:T(8,128)(2,1)S(1)}, bf16[2048,128]{1,0:T(8,128)(2,1)S(1)}, u32[]{:S(2)}, u32[]{:S(2)}) %collective-permute-start.8) | collective-permute-done | bytes 524320 | tf_op jit(solution)/shard_map/ppermute | solution.py:19
  82.8 0.8 slice.16
  83.6 0.7 collective-permute-start.9
  84.3 0.8 slice.17
  85.1 1.2 %collective-permute-start.11 = (bf16[1024,128]{1,0:T(8,128)(2,1)}, bf16[1024,128]{1,0:T(8,128)(2,1)}, u32[]{:S(2)}, u32[]{:S(2)}) collective-permute-start(bf16[1024,128]{1,0:T(8,128)(2,1)} %slice.17), channel_id=1, source_target_pairs={{0,1},{1,0},{2,3},{3,2},{4,5},{5,4},{6,7},{7,6},{8,9},{9,8},{10,11... | collective-permute-start | bytes 786440 | tf_op jit(solution)/shard_map/ppermute | solution.py:19
  86.3 6.2 %collective-permute-start.16 = (bf16[2048,128]{1,0:T(8,128)(2,1)S(1)}, bf16[2048,128]{1,0:T(8,128)(2,1)S(1)}, u32[]{:S(2)}, u32[]{:S(2)}) collective-permute-start(bf16[2048,128]{1,0:T(8,128)(2,1)S(1)} %all_gather.3.refs_0_), channel_id=1, source_target_pairs={{0,8},{8,0},{1,9},{9,1},{2,10},{10,2},{3,11},{11,3},{4,12},{12,4},... | collective-permute-start | bytes 1572872 | tf_op jit(solution)/shard_map/ppermute | solution.py:19
  93.1 0.7 pad_add_fusion.3.start_ref
  93.7 1.8 %collective-permute-start.12 = (bf16[1024,128]{1,0:T(8,128)(2,1)S(1)}, bf16[1024,128]{1,0:T(8,128)(2,1)}, u32[]{:S(2)}, u32[]{:S(2)}) collective-permute-start(bf16[1024,128]{1,0:T(8,128)(2,1)S(1)} %collective-permute-done.9.refs_0_), channel_id=1, source_target_pairs={{0,8},{8,0},{1,9},{9,1},{2,10},{10,2},{3,11},{11,3},{4,12},{12,4},... | collective-permute-start | bytes 786440 | tf_op jit(solution)/shard_map/ppermute | solution.py:19
  95.5 3.7 %collective-permute-start.13 = (bf16[1024,128]{1,0:T(8,128)(2,1)}, bf16[1024,128]{1,0:T(8,128)(2,1)}, u32[]{:S(2)}, u32[]{:S(2)}) collective-permute-start(bf16[1024,128]{1,0:T(8,128)(2,1)} %collective-permute-done.11.refs_1_), channel_id=1, source_target_pairs={{0,8},{8,0},{1,9},{9,1},{2,10},{10,2},{3,11},{11,3},{4,12},{12,4},... | collective-permute-start | bytes 786440 | tf_op jit(solution)/shard_map/ppermute | solution.py:19
  100.5 0.7 pad_add_fusion.start_ref
  101.2 0.8 copy-done.5
  102.0 2.6 %shard_map.29.refs_2_ = f32[16384,128]{1,0:T(8,128)} custom-call(s32[2]{0:T(128)} %pad_add_fusion.3.start_ref, bf16[2048,128]{1,0:T(8,128)(2,1)} %copy-done, bf16[2048,128]{1,0:T(8,128)(2,1)} %copy-done.5), custom_call_target="tpu_custom_call" | custom-call | bytes 3145728 | tf_op jit(solution)/shard_map/pallas_call | solution.py:187
  104.6 0.8 copy-done.4
  105.4 2.6 %shard_map.30.refs_2_ = f32[16384,128]{1,0:T(8,128)} custom-call(s32[2]{0:T(128)} %pad_add_fusion.2.start_ref, bf16[2048,128]{1,0:T(8,128)(2,1)} %copy-done.2, bf16[2048,128]{1,0:T(8,128)(2,1)} %copy-done.4, f32[16384,128]{1,0:T(8,128)} %shard_map.29.refs_2_), custom_call_target="tpu_custom_call", output_to_operand_aliasing={{}: (3, {})} | custom-call | bytes 3145728 | tf_op jit(solution)/shard_map/pallas_call | solution.py:187
  108.1 0.8 copy-done.3
  108.9 2.6 %shard_map.31.refs_4_ = f32[16384,128]{1,0:T(8,128)} custom-call(s32[2]{0:T(128)} %pad_add_fusion.1.start_ref, bf16[2048,128]{1,0:T(8,128)(2,1)} %copy-done.1, bf16[2048,128]{1,0:T(8,128)(2,1)} %copy-done.3, f32[16384,128]{1,0:T(8,128)} %shard_map.30.refs_2_), custom_call_target="tpu_custom_call", output_to_operand_aliasing={{}: (3, {})} | custom-call | bytes 3145728 | tf_op jit(solution)/shard_map/pallas_call | solution.py:187
  111.5 2.6 %shard_map.32 = f32[16384,128]{1,0:T(8,128)} custom-call(s32[4]{0:T(128)} %pad_add_fusion.start_ref, bf16[1024,128]{1,0:T(8,128)(2,1)} %copy-done.6, bf16[1024,128]{1,0:T(8,128)(2,1)} %collective-permute-done.11.refs_1_, bf16[1024,128]{1,0:T(8,128)(2,1)} %collective-permute-done.12.refs_2_, ...), custom_call_target="tpu_custom_call", output_to_operand_aliasing={{}: (5, {})} | custom-call | bytes 3145728 | tf_op jit(solution)/shard_map/pallas_call | solution.py:187
  (55 shorter events, 3.7 us)
Async XLA Ops:
  1.0 1.6 %collective-permute-start = (bf16[2,2,10,3,128]{4,1,3,2,0:T(2,128)(2,1)S(1)}, bf16[2,2,10,3,128]{4,1,3,2,0:T(2,128)(2,1)S(1)}, u32[]{:S(2)}, u32[]{:S(2)}) collective-permute-start(bf16[2,2,10,3,128]{4,1,3,2,0:T(2,128)(2,1)S(1)} %broadcast_select_fusion), channel_id=1, source_target_pairs={{1,2},{3,4},{5,6},{2,1},{4,3},{6,5},{9,10},{11,12},{13,14},{10,9},... | collective-permute-start | bytes 92168 | tf_op jit(solution)/shard_map/ppermute | solution.py:212
  3.5 18.1 %copy-start.7 = (bf16[208,384]{1,0:T(8,128)(2,1)}, bf16[208,384]{1,0:T(8,128)(2,1)S(1)}, u32[]{:S(2)}) copy-start(bf16[208,384]{1,0:T(8,128)(2,1)S(1)} %pad_maximum_fusion.refs_0_) | copy-start | bytes 479236
  3.6 9.7 %collective-permute-start.2 = (bf16[208,384]{1,0:T(8,128)(2,1)S(1)}, bf16[208,384]{1,0:T(8,128)(2,1)S(1)}, u32[]{:S(2)}, u32[]{:S(2)}) collective-permute-start(bf16[208,384]{1,0:T(8,128)(2,1)S(1)} %pad_maximum_fusion.refs_0_), channel_id=1, source_target_pairs={{0,1},{1,0},{2,3},{3,2},{4,5},{5,4},{6,7},{7,6},{8,9},{9,8},{10,11... | collective-permute-start | bytes 479240 | tf_op jit(solution)/shard_map/ppermute | solution.py:19
  9.6 6.5 %collective-permute-start.4 = (bf16[208,384]{1,0:T(8,128)(2,1)S(1)}, bf16[208,384]{1,0:T(8,128)(2,1)S(1)}, u32[]{:S(2)}, u32[]{:S(2)}) collective-permute-start(bf16[208,384]{1,0:T(8,128)(2,1)S(1)} %pad_maximum_fusion.refs_0_), channel_id=1, source_target_pairs={{0,16},{16,0},{1,17},{17,1},{2,18},{18,2},{3,19},{19,3},{4,20},{20... | collective-permute-start | bytes 479240 | tf_op jit(solution)/shard_map/ppermute | solution.py:19
  10.9 9.3 %collective-permute-start.6 = (bf16[208,384]{1,0:T(8,128)(2,1)S(1)}, bf16[208,384]{1,0:T(8,128)(2,1)S(1)}, u32[]{:S(2)}, u32[]{:S(2)}) collective-permute-start(bf16[208,384]{1,0:T(8,128)(2,1)S(1)} %pad_maximum_fusion.refs_0_), channel_id=1, source_target_pairs={{0,17},{1,16},{16,1},{17,0},{2,19},{3,18},{18,3},{19,2},{4,21},{5,... | collective-permute-start | bytes 479240 | tf_op jit(solution)/shard_map/ppermute | solution.py:233
  10.9 10.0 %collective-permute-start.1 = (bf16[208,384]{1,0:T(8,128)(2,1)S(1)}, bf16[208,384]{1,0:T(8,128)(2,1)S(1)}, u32[]{:S(2)}, u32[]{:S(2)}) collective-permute-start(bf16[208,384]{1,0:T(8,128)(2,1)S(1)} %pad_maximum_fusion.refs_0_), channel_id=1, source_target_pairs={{0,8},{8,0},{1,9},{9,1},{2,10},{10,2},{3,11},{11,3},{4,12},{12,4},... | collective-permute-start | bytes 479240 | tf_op jit(solution)/shard_map/ppermute | solution.py:19
  13.3 8.3 %copy-start.8 = (bf16[208,384]{1,0:T(8,128)(2,1)}, bf16[208,384]{1,0:T(8,128)(2,1)S(1)}, u32[]{:S(2)}) copy-start(bf16[208,384]{1,0:T(8,128)(2,1)S(1)} %collective-permute-done.2.refs_2_) | copy-start | bytes 479236
  13.3 7.6 %collective-permute-start.3 = (bf16[208,384]{1,0:T(8,128)(2,1)S(1)}, bf16[208,384]{1,0:T(8,128)(2,1)S(1)}, u32[]{:S(2)}, u32[]{:S(2)}) collective-permute-start(bf16[208,384]{1,0:T(8,128)(2,1)S(1)} %collective-permute-done.2.refs_2_), channel_id=1, source_target_pairs={{0,8},{8,0},{1,9},{9,1},{2,10},{10,2},{3,11},{11,3},{4,12},{12,4},... | collective-permute-start | bytes 479240 | tf_op jit(solution)/shard_map/ppermute | solution.py:19
  16.1 5.5 %copy-start.9 = (bf16[208,384]{1,0:T(8,128)(2,1)}, bf16[208,384]{1,0:T(8,128)(2,1)S(1)}, u32[]{:S(2)}) copy-start(bf16[208,384]{1,0:T(8,128)(2,1)S(1)} %collective-permute-done.4.refs_4_) | copy-start | bytes 479236
  16.1 5.1 %collective-permute-start.5 = (bf16[208,384]{1,0:T(8,128)(2,1)S(1)}, bf16[208,384]{1,0:T(8,128)(2,1)S(1)}, u32[]{:S(2)}, u32[]{:S(2)}) collective-permute-start(bf16[208,384]{1,0:T(8,128)(2,1)S(1)} %collective-permute-done.4.refs_4_), channel_id=1, source_target_pairs={{0,8},{8,0},{1,9},{9,1},{2,10},{10,2},{3,11},{11,3},{4,12},{12,4},... | collective-permute-start | bytes 479240 | tf_op jit(solution)/shard_map/ppermute | solution.py:19
  20.2 1.4 %copy-start.10 = (bf16[208,384]{1,0:T(8,128)(2,1)}, bf16[208,384]{1,0:T(8,128)(2,1)S(1)}, u32[]{:S(2)}) copy-start(bf16[208,384]{1,0:T(8,128)(2,1)S(1)} %collective-permute-done.6.refs_6_) | copy-start | bytes 479236
  20.2 1.4 %collective-permute-start.7 = (bf16[208,384]{1,0:T(8,128)(2,1)S(1)}, bf16[208,384]{1,0:T(8,128)(2,1)S(1)}, u32[]{:S(2)}, u32[]{:S(2)}) collective-permute-start(bf16[208,384]{1,0:T(8,128)(2,1)S(1)} %collective-permute-done.6.refs_6_), channel_id=1, source_target_pairs={{0,8},{8,0},{1,9},{9,1},{2,10},{10,2},{3,11},{11,3},{4,12},{12,4},... | collective-permute-start | bytes 479240 | tf_op jit(solution)/shard_map/ppermute | solution.py:19
  20.9 0.7 copy-start.11
  20.9 0.7 copy-start.12
  21.2 0.7 copy-start.13
  21.9 0.7 copy-start.14
  73.8 27.4 %copy-start = (bf16[2048,128]{1,0:T(8,128)(2,1)}, bf16[2048,128]{1,0:T(8,128)(2,1)S(1)}, u32[]{:S(2)}) copy-start(bf16[2048,128]{1,0:T(8,128)(2,1)S(1)} %all_gather.3.refs_0_) | copy-start | bytes 1572868
  73.8 9.0 %collective-permute-start.8 = (bf16[2048,128]{1,0:T(8,128)(2,1)S(1)}, bf16[2048,128]{1,0:T(8,128)(2,1)S(1)}, u32[]{:S(2)}, u32[]{:S(2)}) collective-permute-start(bf16[2048,128]{1,0:T(8,128)(2,1)S(1)} %all_gather.3.refs_0_), channel_id=1, source_target_pairs={{0,1},{1,0},{2,3},{3,2},{4,5},{5,4},{6,7},{7,6},{8,9},{9,8},{10,11... | collective-permute-start | bytes 1572872 | tf_op jit(solution)/shard_map/ppermute | solution.py:19
  75.0 9.3 %collective-permute-start.10 = (bf16[2048,128]{1,0:T(8,128)(2,1)S(1)}, bf16[2048,128]{1,0:T(8,128)(2,1)S(1)}, u32[]{:S(2)}, u32[]{:S(2)}) collective-permute-start(bf16[2048,128]{1,0:T(8,128)(2,1)S(1)} %all_gather.3.refs_0_), channel_id=1, source_target_pairs={{0,16},{16,0},{1,17},{17,1},{2,18},{18,2},{3,19},{19,3},{4,20},{20... | collective-permute-start | bytes 1572872 | tf_op jit(solution)/shard_map/ppermute | solution.py:19
  82.8 25.2 %copy-start.1 = (bf16[2048,128]{1,0:T(8,128)(2,1)}, bf16[2048,128]{1,0:T(8,128)(2,1)S(1)}, u32[]{:S(2)}) copy-start(bf16[2048,128]{1,0:T(8,128)(2,1)S(1)} %collective-permute-done.8.refs_0_) | copy-start | bytes 1572868
  83.6 10.1 %collective-permute-start.9 = (bf16[1024,128]{1,0:T(8,128)(2,1)}, bf16[1024,128]{1,0:T(8,128)(2,1)S(1)}, u32[]{:S(2)}, u32[]{:S(2)}) collective-permute-start(bf16[1024,128]{1,0:T(8,128)(2,1)} %slice.16), channel_id=1, source_target_pairs={{0,16},{16,0},{1,17},{17,1},{2,18},{18,2},{3,19},{19,3},{4,20},{20... | collective-permute-start | bytes 786440 | tf_op jit(solution)/shard_map/ppermute | solution.py:19
  84.3 20.3 %copy-start.2 = (bf16[2048,128]{1,0:T(8,128)(2,1)}, bf16[2048,128]{1,0:T(8,128)(2,1)S(1)}, u32[]{:S(2)}) copy-start(bf16[2048,128]{1,0:T(8,128)(2,1)S(1)} %collective-permute-done.10.refs_0_) | copy-start | bytes 1572868
  85.1 10.4 %collective-permute-start.11 = (bf16[1024,128]{1,0:T(8,128)(2,1)}, bf16[1024,128]{1,0:T(8,128)(2,1)}, u32[]{:S(2)}, u32[]{:S(2)}) collective-permute-start(bf16[1024,128]{1,0:T(8,128)(2,1)} %slice.17), channel_id=1, source_target_pairs={{0,1},{1,0},{2,3},{3,2},{4,5},{5,4},{6,7},{7,6},{8,9},{9,8},{10,11... | collective-permute-start | bytes 786440 | tf_op jit(solution)/shard_map/ppermute | solution.py:19
  86.3 14.8 %collective-permute-start.16 = (bf16[2048,128]{1,0:T(8,128)(2,1)S(1)}, bf16[2048,128]{1,0:T(8,128)(2,1)S(1)}, u32[]{:S(2)}, u32[]{:S(2)}) collective-permute-start(bf16[2048,128]{1,0:T(8,128)(2,1)S(1)} %all_gather.3.refs_0_), channel_id=1, source_target_pairs={{0,8},{8,0},{1,9},{9,1},{2,10},{10,2},{3,11},{11,3},{4,12},{12,4},... | collective-permute-start | bytes 1572872 | tf_op jit(solution)/shard_map/ppermute | solution.py:19
  92.6 12.0 %collective-permute-start.15 = (bf16[2048,128]{1,0:T(8,128)(2,1)S(1)}, bf16[2048,128]{1,0:T(8,128)(2,1)S(1)}, u32[]{:S(2)}, u32[]{:S(2)}) collective-permute-start(bf16[2048,128]{1,0:T(8,128)(2,1)S(1)} %collective-permute-done.10.refs_0_), channel_id=1, source_target_pairs={{0,8},{8,0},{1,9},{9,1},{2,10},{10,2},{3,11},{11,3},{4,12},{12,4},... | collective-permute-start | bytes 1572872 | tf_op jit(solution)/shard_map/ppermute | solution.py:19
  92.6 15.5 %collective-permute-start.14 = (bf16[2048,128]{1,0:T(8,128)(2,1)S(1)}, bf16[2048,128]{1,0:T(8,128)(2,1)S(1)}, u32[]{:S(2)}, u32[]{:S(2)}) collective-permute-start(bf16[2048,128]{1,0:T(8,128)(2,1)S(1)} %collective-permute-done.8.refs_0_), channel_id=1, source_target_pairs={{0,8},{8,0},{1,9},{9,1},{2,10},{10,2},{3,11},{11,3},{4,12},{12,4},... | collective-permute-start | bytes 1572872 | tf_op jit(solution)/shard_map/ppermute | solution.py:19
  93.7 17.8 %copy-start.6 = (bf16[1024,128]{1,0:T(8,128)(2,1)}, bf16[1024,128]{1,0:T(8,128)(2,1)S(1)}, u32[]{:S(2)}) copy-start(bf16[1024,128]{1,0:T(8,128)(2,1)S(1)} %collective-permute-done.9.refs_0_) | copy-start | bytes 786436
  93.7 17.7 %collective-permute-start.12 = (bf16[1024,128]{1,0:T(8,128)(2,1)S(1)}, bf16[1024,128]{1,0:T(8,128)(2,1)}, u32[]{:S(2)}, u32[]{:S(2)}) collective-permute-start(bf16[1024,128]{1,0:T(8,128)(2,1)S(1)} %collective-permute-done.9.refs_0_), channel_id=1, source_target_pairs={{0,8},{8,0},{1,9},{9,1},{2,10},{10,2},{3,11},{11,3},{4,12},{12,4},... | collective-permute-start | bytes 786440 | tf_op jit(solution)/shard_map/ppermute | solution.py:19
  95.5 16.0 %collective-permute-start.13 = (bf16[1024,128]{1,0:T(8,128)(2,1)}, bf16[1024,128]{1,0:T(8,128)(2,1)}, u32[]{:S(2)}, u32[]{:S(2)}) collective-permute-start(bf16[1024,128]{1,0:T(8,128)(2,1)} %collective-permute-done.11.refs_1_), channel_id=1, source_target_pairs={{0,8},{8,0},{1,9},{9,1},{2,10},{10,2},{3,11},{11,3},{4,12},{12,4},... | collective-permute-start | bytes 786440 | tf_op jit(solution)/shard_map/ppermute | solution.py:19
  101.2 0.8 copy-start.5
  104.6 0.8 copy-start.4
  108.0 0.8 copy-start.3

commit v5 on v4

v5 whole, which is shorter than its diff:
```python
import functools

import jax
import jax.numpy as jnp
from jax import lax
from jax.experimental import pallas as pl
from jax.experimental.pallas import tpu as pltpu
from jax.sharding import Mesh, PartitionSpec as P

STREAM = ("row", "core")
SPAN = ("deck", "side")
DIAGONAL = ("row", "side")
WEIGHT_PARTS = 3
VMEM_LIMIT = 56 * 2**20
LANES = 128
CHUNKS = 2
TURNED = (((1,), (1,)), ((), ()))


def rotate(value, axis, by=1):
    count = lax.axis_size(axis)
    return lax.ppermute(value, axis, [(i, (i + by) % count) for i in range(count)])


def transposed(value):
    rows = value.shape[1]
    row, column = (lax.broadcasted_iota(jnp.int32, (rows, rows), d) for d in range(2))
    eye = (row == column).astype(jnp.bfloat16)
    return lax.dot_general(eye, value, TURNED, preferred_element_type=jnp.float32)


def terms_kernel(sizes, place_ref, *refs):
    layers, height, across, width, share, members, outs = sizes
    pieces, out_refs = refs[:members], refs[members : members + outs]
    field, flat, grad, phi, phi_wide, grad_turned, own, quad = refs[members + outs :]
    cells = layers * height * across
    count = members * cells
    streams = members // 2
    span = grad.shape[1]
    together = span // (2 * cells)

    for n, piece in enumerate(pieces):
        field[place_ref[2 + n]] = piece[...].astype(jnp.float32)

    index = lax.broadcasted_iota(jnp.int32, (across, width), 0)

    def column(b):
        return slice(b * width, (b + 1) * width)

    def one_stream(s, group):
        def layer_at(layer, side):
            at = s * layers + layer
            inside = ((at >= 0) & (at < streams * layers)).astype(jnp.float32)
            at = jnp.clip(at, 0, streams * layers - 1)
            return lax.div(at, layers) * 2 + side, lax.rem(at, layers), inside

        for side in range(2):
            member = 2 * s + side
            tile = field[member, cells + 2 * layers * height :, 0:width]
            weights = tile
            for part in range(1, WEIGHT_PARTS):
                weights = weights + pltpu.roll(tile, width - part * layers * height, 1)
            for layer in range(layers):
                beside = {step: layer_at(layer + step, side) for step in (-2, -1, 1, 2)}
                for z in range(height):
                    line = layer * height + z
                    row = line * across
                    rows = slice(row, row + across)
                    at = (s - group * together) * 2 + side
                    at = pl.ds(pl.multiple_of(at * cells + row, across), across)
                    weight = jnp.broadcast_to(weights[:, line : line + 1], (across, width))
                    twelfth, half = weight * (1.0 / 12.0), weight * 0.5
                    first = cells + 2 * line
                    base = first // across * across
                    for b in range(3):
                        here = field[member, rows, column(b)]
                        along = {}
                        for step, (m, l, inside) in beside.items():
                            start = pl.multiple_of((l * height + z) * across, across)
                            along[step] = field[m, pl.ds(start, across), column(b)] * inside
                        value = 8.0 * (along[1] - along[-1]) - (along[2] - along[-2])
                        grad[0, at, column(b)] = value * twelfth

                        outer = field[member, base : base + across, column(b)]
                        if side == 0:
                            prev = pltpu.roll(outer, (across - 2 - (first - base)) % across, 0)
                            after = field[member + 1, rows, column(b)]
                        else:
                            prev = field[member - 1, rows, column(b)]
                            after = pltpu.roll(outer, (across - (first - base)) % across, 0)
                        near = pltpu.roll(jnp.where(index < 1, after, here), across - 1, 0)
                        near = near - pltpu.roll(jnp.where(index >= across - 1, prev, here), 1, 0)
                        far = pltpu.roll(jnp.where(index < 2, after, here), across - 2, 0)
                        far = far - pltpu.roll(jnp.where(index >= across - 2, prev, here), 2, 0)
                        grad[1, at, column(b)] = (8.0 * near - far) * twelfth

                        value = jnp.zeros_like(here)
                        if z < height - 1:
                            value = field[member, row + across : row + 2 * across, column(b)]
                        if z > 0:
                            value = value - field[member, row - across : row, column(b)]
                        grad[2, at, column(b)] = value * half
                        flat[at, column(b)] = here
        return group

    def one_group(group, _):
        lax.fori_loop(group * together, (group + 1) * together, one_stream, group)
        start = pl.multiple_of(group * span, LANES)
        lanes = pl.ds(start, span)
        for b in range(3):
            value = transposed(flat[:, column(b)].astype(jnp.bfloat16))
            phi_wide[b, :, lanes] = value
            phi[:, pl.ds(pl.multiple_of(b * count + start, LANES), span)] = value.astype(jnp.bfloat16)
            for a in range(3):
                value = transposed(grad[a, :, column(b)].astype(jnp.bfloat16))
                grad_turned[a, b, :, lanes] = value.astype(jnp.bfloat16)
        return 0

    lax.fori_loop(0, streams // together, one_group, 0)

    rows = 16
    for i in range(share):
        mode = place_ref[0] + lax.rem(i + place_ref[1], share)
        for b in range(3):
            row = phi_wide[b, pl.ds(mode, 1), :]
            own[b, i] = jnp.broadcast_to(row, (rows, count)).astype(jnp.bfloat16)

    for pair in range(share // 2):
        for a in range(3):
            for start in range(0, count, LANES):
                lanes = slice(start, start + LANES)
                spread = [[own[b, 2 * pair + h, :, lanes] for b in range(3)] for h in range(2)]
                for k in range(0, width, rows):
                    slope = [grad_turned[a, b, k : k + rows, lanes] for b in range(3)]
                    for h in range(2):
                        value = spread[h][0] * slope[0]
                        value = value + spread[h][1] * slope[1]
                        value = value + spread[h][2] * slope[2]
                        quad[
                            pair % 2,
                            h * width + k : h * width + k + rows,
                            a * count + start : a * count + start + LANES,
                        ] = value
        total = lax.dot_general(
            phi[...], quad[pair % 2], TURNED, preferred_element_type=jnp.float32
        )
        for h in range(2):
            start = (2 * pair + h) * width
            out_ref = out_refs[start * outs // (share * width)]
            start = start % (share * width // outs)
            out_ref[start : start + width, :] = total[:, column(h)].astype(out_ref.dtype)


def plane_terms(place, pieces, shape, share, outs):
    layers, across, height, comps, width = shape
    members = len(pieces)
    cells = layers * height * across
    count = members * cells
    span = next(n * 2 * cells for n in (1, 2, 4, members // 2) if n * 2 * cells % LANES == 0)
    sizes = (layers, height, across, width, share, members, outs)
    vmem = pl.BlockSpec(memory_space=pltpu.VMEM)
    dtypes = [jnp.float32 if outs > 1 and n == 0 else jnp.bfloat16 for n in range(outs)]
    return pl.pallas_call(
        functools.partial(terms_kernel, sizes),
        out_shape=[jax.ShapeDtypeStruct((share * width // outs, width), t) for t in dtypes],
        in_specs=[pl.BlockSpec(memory_space=pltpu.SMEM)] + [vmem] * members,
        out_specs=[vmem] * outs,
        scratch_shapes=[
            pltpu.VMEM((members,) + pieces[0].shape, jnp.float32),
            pltpu.VMEM((span, comps * width), jnp.float32),
            pltpu.VMEM((3, span, comps * width), jnp.float32),
            pltpu.VMEM((width, 3 * count), jnp.bfloat16),
            pltpu.VMEM((3, width, count), jnp.float32),
            pltpu.VMEM((3, 3, width, count), jnp.bfloat16),
            pltpu.VMEM((3, share, 16, count), jnp.bfloat16),
            pltpu.VMEM((min(2, share // 2), 2 * width, 3 * count), jnp.bfloat16),
        ],
        compiler_params=pltpu.CompilerParams(vmem_limit_bytes=VMEM_LIMIT),
        cost_estimate=pl.CostEstimate(
            flops=2 * share * width * width * count * 3, bytes_accessed=2**22, transcendentals=0
        ),
    )(place, *pieces)


def place_kernel(runs, pieces, given, start_ref, *refs):
    out_ref, wide, sems = refs[pieces + given :]
    copies = []
    done = 0
    for n, (piece, first, rows) in enumerate(runs):
        here = wide.at[done : done + rows]
        here[...] = refs[piece][first : first + rows, :].astype(jnp.float32)
        to = pl.ds(pl.multiple_of(start_ref[n], rows), rows)
        copies.append(pltpu.make_async_copy(here, out_ref.at[to], sems.at[n]))
        copies[-1].start()
        done += rows
    for copy in copies:
        copy.wait()


def put(result, total_rows, values, starts):
    pieces = list({id(value): value for value, _, _ in values}.values())
    place = {id(piece): n for n, piece in enumerate(pieces)}
    runs = [(place[id(value)], first, rows) for value, first, rows in values]
    width = pieces[0].shape[1]
    given = [] if result is None else [result]
    rows = sum(run[2] for run in runs)
    vmem, anywhere = (pl.BlockSpec(memory_space=m) for m in (pltpu.VMEM, pl.ANY))
    return pl.pallas_call(
        functools.partial(place_kernel, runs, len(pieces), len(given)),
        out_shape=jax.ShapeDtypeStruct((total_rows, width), jnp.float32),
        in_specs=[pl.BlockSpec(memory_space=pltpu.SMEM)]
        + [vmem] * len(pieces)
        + [anywhere] * len(given),
        out_specs=anywhere,
        scratch_shapes=[
            pltpu.VMEM((rows, width), jnp.float32),
            pltpu.SemaphoreType.DMA((len(runs),)),
        ],
        input_output_aliases={1 + len(pieces): 0} if given else {},
        compiler_params=pltpu.CompilerParams(vmem_limit_bytes=VMEM_LIMIT),
        cost_estimate=pl.CostEstimate(
            flops=0, bytes_accessed=6 * rows * width, transcendentals=0
        ),
    )(jnp.stack(starts).astype(jnp.int32), *pieces, *given)


def pack(velocity, weight):
    x, y, z, comps, width = velocity.shape
    side = lax.axis_index("side")
    decks = lax.axis_size("deck")
    edge = jnp.where(side == 1, velocity[:, y - 2 :], velocity[:, :2])
    joints = [(2 * d + 1, 2 * d + 2) for d in range(decks - 1)]
    outer = lax.ppermute(edge, SPAN, joints + [(j, i) for i, j in joints])
    columns = weight.transpose(1, 0, 2).reshape(y, x * z)
    parts = []
    for _ in range(WEIGHT_PARTS):
        part = lax.reduce_precision(columns, 8, 7)
        columns = columns - part
        parts.append(part.astype(jnp.bfloat16))
    tile = jnp.concatenate(parts, axis=1)
    tile = jnp.pad(tile, ((0, 0), (0, comps * width - tile.shape[1])))
    rows = [v.transpose(0, 2, 1, 3, 4).reshape(-1, comps * width) for v in (velocity, outer)]
    return jnp.concatenate(rows + [tile], axis=0)


def spread_small(piece):
    rows = lax.axis_size("row")
    got = {(0, 0): piece, (0, 1): rotate(piece, "side")}
    for r in range(1, rows):
        got[(r, 0)] = rotate(piece, "row", r)
        pairs = [
            (2 * i + s, 2 * ((i + r) % rows) + 1 - s) for i in range(rows) for s in range(2)
        ]
        got[(r, 1)] = lax.ppermute(piece, DIAGONAL, pairs)
    out = {}
    for (r, s), value in got.items():
        out[(r, 0, s)] = value
        out[(r, 1, s)] = rotate(value, "core")
    return out


def sum_over_decks(terms, decks):
    if len(terms) > 1:
        parts = [terms[0]] + [rotate(terms[r], "deck", r) for r in range(1, decks)]
    else:
        width = terms[0].shape[1]
        parts = list(lax.all_to_all(terms[0].reshape(decks, -1, width), "deck", 0, 0))
    return sum(part.astype(jnp.float32) for part in parts).astype(jnp.bfloat16)


def shards(velocity_modes, cell_weight):
    shape = velocity_modes.shape
    width = shape[-1]
    rows, decks = lax.axis_size("row"), lax.axis_size("deck")
    members = rows * 4
    share = width // members
    part = share // CHUNKS
    row, core, side, deck = (lax.axis_index(a) for a in ("row", "core", "side", "deck"))
    outs = decks if part % (2 * decks) == 0 else 1

    def member(r, c, s):
        return (lax.rem(row - r + rows, rows) * 2 + lax.rem(core + c, 2)) * 2 + lax.rem(side + s, 2)

    pieces = spread_small(pack(velocity_modes, cell_weight))
    sources = [member(*offsets) for offsets in pieces]
    first = deck * (part // decks) if outs > 1 else jnp.zeros_like(deck)
    terms = []
    for n in range(CHUNKS):
        start = member(0, 0, 0) * share + n * part
        place = jnp.stack([start, first] + sources).astype(jnp.int32)
        terms.append(plane_terms(place, list(pieces.values()), shape, part, outs))

    block = part * width
    line = block // decks
    result = None

    def put_all(result, n, chosen):
        values, starts = [], []
        for (r, c, s), value in chosen:
            start = (member(r, c, s) * CHUNKS + n) * block
            for d in range(decks):
                values.append((value, d * line, line))
                starts.append(start + lax.rem(deck - d + decks, decks) * line)
        return put(result, members * share * width, values, starts)

    waiting = []
    for n in range(CHUNKS):
        mine = sum_over_decks(terms[n], decks)
        piece = jnp.concatenate([mine] + [rotate(mine, "deck", r) for r in range(1, decks)], axis=0)
        across = rotate(piece, "side")
        along = [rotate(piece, "row", r) for r in range(1, rows)]
        near = [((0, 0, 0), piece), ((0, 0, 1), across)]
        near += [((r, 0, 0), v) for r, v in enumerate(along, 1)]
        if n == 0:
            diagonal = [rotate(across, "row", r) for r in range(1, rows)]
        else:
            along, result = lax.optimization_barrier((along, put_all(result, *waiting.pop(0))))
            diagonal = [rotate(v, "side") for v in along]
        near_core = [((r, 1, s), rotate(v, "core")) for (r, _, s), v in near]
        waiting.append((n, near + near_core))
        far = [((r, 0, 1), v) for r, v in enumerate(diagonal, 1)]
        if n == CHUNKS - 1:
            for group in waiting:
                result = put_all(result, *group)
            waiting = []
            far_values, result = lax.optimization_barrier(([v for _, v in far], result))
            far = [(o, v) for (o, _), v in zip(far, far_values)]
        far_core = [((r, 1, s), rotate(v, "core")) for (r, _, s), v in far]
        waiting.append((n, far + far_core))
    for group in waiting:
        result = put_all(result, *group)
    return result.reshape(width, width, width)


def solution(mesh):
    streams, spans = (mesh.shape[name] for name in ("stream", "span"))
    split = Mesh(mesh.devices.reshape(streams // 2, 2, spans // 2, 2), STREAM + SPAN)
    placed = (P(STREAM, SPAN, None, None, None), P(STREAM, SPAN, None))
    return jax.shard_map(shards, mesh=split, in_specs=placed, out_specs=P(), check_vma=False)
```

time: 114 us -> 110 us (0.965)
  blocking collectives: 30.4 us -> 0 us
  starting transfers between devices: 33.6 us -> 52.1 us
  local copies, waits for them, and re-layouts: 6.3 us -> 9.19 us
  waiting for transfers between devices: 7.76 us -> 9.99 us
  Pallas kernels: 31.2 us -> 33.4 us
    ppermute x15 -> x32, starting transfers between devices: 32.9 us -> 51.5 us  [rotate(): lax.ppermute(value, axis, [(i, (i + by) % count) for i in range(count)])]
    all_to_all x1 -> x0, blocking collectives: 17.6 us -> none  [shards(): parts = lax.all_to_all(terms.reshape(decks, -1, width), 'deck', 0, 0)]
    all_gather x1 -> x0, blocking collectives: 12.7 us -> none  [shards(): piece = lax.all_gather(mine, 'deck', axis=0, tiled=True)]
    another operation x1 -> x6, local copies, waits for them, and re-layouts: 0.61 us -> 3.94 us  [the longest x4 2.68 us: put(): jnp.stack(starts).astype(jnp.int32)]
    another operation x4 -> x0, other arithmetic: 2.57 us -> none  [put(): jnp.stack(starts).astype(jnp.int32)]
    pallas_call x5 -> x6, Pallas kernels: 31.2 us -> 33.4 us  [the longest x2 22.9 us: plane_terms(): pl.pallas_call(functools.partial(terms_kernel, sizes), out_shape=[jax.Sha...]
    ppermute x15 -> x32, waiting for transfers between devices: 7.75 us -> 9.98 us  [rotate(): lax.ppermute(value, axis, [(i, (i + by) % count) for i in range(count)])]
    convert_element_type x0 -> x2, other arithmetic: none -> 1.88 us  [sum_over_decks(): sum((part.astype(jnp.float32) for part in parts)).astype(jnp.bfloat16)]
  transfers between devices with their start and end apart: 17 -> 34, of which waited for: 3 -> 7; matrix products, arithmetic and copies ran while one was open for 5% -> 5% of each run, Pallas kernels for 7% -> 18%
where the time goes in v5:
time: 110 us; the launch traced here: 109 us
  starting transfers between devices  52.1 us (47%)
  Pallas kernels  33.4 us (30%)
  waiting for transfers between devices  9.99 us (9%)
  local copies, waits for them, and re-layouts  9.19 us (8%)
  other arithmetic  3.95 us (4%)
    ppermute x32, starting transfers between devices, rotate(): lax.ppermute(value, axis, [(i, (i + by) % count) for i in range(count)])  51.5 us
    pallas_call x2, Pallas kernels, plane_terms(): pl.pallas_call(functools.partial(terms_kernel, sizes), out_shape=[jax.Sha...  22.9 us
    pallas_call x4, Pallas kernels, put(): pl.pallas_call(functools.partial(place_kernel, runs, len(pieces), len(giv...  10.6 us
    ppermute x32, waiting for transfers between devices, rotate(): lax.ppermute(value, axis, [(i, (i + by) % count) for i in range(count)])  9.98 us
    unnamed x47, local copies, waits for them, and re-layouts  4.45 us
    another operation x4, local copies, waits for them, and re-layouts, put(): jnp.stack(starts).astype(jnp.int32)  2.68 us
  transfers between devices with their start and end apart: 34, of which 7 were waited for; matrix products, arithmetic and copies ran while one was open for 5% of the time, Pallas kernels for 18%

profile of v5, /device:TPU:1, one launch (start us, length us, event | category | flops | bytes accessed | tf_op | source)
XLA Modules:
  0.0 109.1 jit_solution(11935952683323632659)
XLA Ops:
  0.0 1.0 broadcast_select_fusion
  2.6 0.9 pad_maximum_fusion.2.refs_0_
  3.6 6.1 %collective-permute-start.2 = (bf16[208,384]{1,0:T(8,128)(2,1)S(1)}, bf16[208,384]{1,0:T(8,128)(2,1)S(1)}, u32[]{:S(2)}, u32[]{:S(2)}) collective-permute-start(bf16[208,384]{1,0:T(8,128)(2,1)S(1)} %pad_maximum_fusion.2.refs_0_), channel_id=1, source_target_pairs={{0,1},{1,0},{2,3},{3,2},{4,5},{5,4},{6,7},{7,6},{8,9},{9,8},{10,11... | collective-permute-start | bytes 479240 | tf_op jit(solution)/shard_map/ppermute | solution.py:22
  9.6 1.2 %collective-permute-start.4 = (bf16[208,384]{1,0:T(8,128)(2,1)S(1)}, bf16[208,384]{1,0:T(8,128)(2,1)S(1)}, u32[]{:S(2)}, u32[]{:S(2)}) collective-permute-start(bf16[208,384]{1,0:T(8,128)(2,1)S(1)} %pad_maximum_fusion.2.refs_0_), channel_id=1, source_target_pairs={{0,16},{16,0},{1,17},{17,1},{2,18},{18,2},{3,19},{19,3},{4,20},{20... | collective-permute-start | bytes 479240 | tf_op jit(solution)/shard_map/ppermute | solution.py:22
  10.9 2.4 %collective-permute-start.1 = (bf16[208,384]{1,0:T(8,128)(2,1)S(1)}, bf16[208,384]{1,0:T(8,128)(2,1)S(1)}, u32[]{:S(2)}, u32[]{:S(2)}) collective-permute-start(bf16[208,384]{1,0:T(8,128)(2,1)S(1)} %pad_maximum_fusion.2.refs_0_), channel_id=1, source_target_pairs={{0,8},{8,0},{1,9},{9,1},{2,10},{10,2},{3,11},{11,3},{4,12},{12,4},... | collective-permute-start | bytes 479240 | tf_op jit(solution)/shard_map/ppermute | solution.py:22
  13.3 2.8 %collective-permute-start.3 = (bf16[208,384]{1,0:T(8,128)(2,1)S(1)}, bf16[208,384]{1,0:T(8,128)(2,1)S(1)}, u32[]{:S(2)}, u32[]{:S(2)}) collective-permute-start(bf16[208,384]{1,0:T(8,128)(2,1)S(1)} %collective-permute-done.2.refs_2_), channel_id=1, source_target_pairs={{0,8},{8,0},{1,9},{9,1},{2,10},{10,2},{3,11},{11,3},{4,12},{12,4},... | collective-permute-start | bytes 479240 | tf_op jit(solution)/shard_map/ppermute | solution.py:22
  16.1 4.1 %collective-permute-start.5 = (bf16[208,384]{1,0:T(8,128)(2,1)S(1)}, bf16[208,384]{1,0:T(8,128)(2,1)S(1)}, u32[]{:S(2)}, u32[]{:S(2)}) collective-permute-start(bf16[208,384]{1,0:T(8,128)(2,1)S(1)} %collective-permute-done.4.refs_4_), channel_id=1, source_target_pairs={{0,8},{8,0},{1,9},{9,1},{2,10},{10,2},{3,11},{11,3},{4,12},{12,4},... | collective-permute-start | bytes 479240 | tf_op jit(solution)/shard_map/ppermute | solution.py:22
  22.5 11.4 %shard_map.29 = (f32[256,128]{1,0:T(8,128)}, bf16[256,128]{1,0:T(8,128)(2,1)}, bf16[256,128]{1,0:T(8,128)(2,1)}, bf16[256,128]{1,0:T(8,128)(2,1)}) custom-call(s32[10]{0:T(128)} %stack.298.place_ref, bf16[208,384]{1,0:T(8,128)(2,1)} %copy-done.15, bf16[208,384]{1,0:T(8,128)(2,1)} %copy-done.19, bf16[208,384]{1,0:T(8,128)(2,1)} %copy-done.16, ...), custom_call_target="tpu_custom_call" | custom-call | flops 1006632960 | bytes 4194304 | tf_op jit(solution)/shard_map/pallas_call | solution.py:163
  34.0 1.3 %collective-permute-start.15 = (bf16[256,128]{1,0:T(8,128)(2,1)}, bf16[256,128]{1,0:T(8,128)(2,1)S(1)}, u32[]{:S(2)}, u32[]{:S(2)}) collective-permute-start(bf16[256,128]{1,0:T(8,128)(2,1)} %get-tuple-element.22), channel_id=1, source_target_pairs={{0,2},{2,4},{4,6},{6,0},{1,3},{3,5},{5,7},{7,1},{8,10},{10,12},{12... | collective-permute-start | bytes 196616 | tf_op jit(solution)/shard_map/ppermute | solution.py:22
  35.3 1.2 %collective-permute-start.16 = (bf16[256,128]{1,0:T(8,128)(2,1)}, bf16[256,128]{1,0:T(8,128)(2,1)S(1)}, u32[]{:S(2)}, u32[]{:S(2)}) collective-permute-start(bf16[256,128]{1,0:T(8,128)(2,1)} %get-tuple-element.23), channel_id=1, source_target_pairs={{0,4},{2,6},{4,0},{6,2},{1,5},{3,7},{5,1},{7,3},{8,12},{10,14},{12... | collective-permute-start | bytes 196616 | tf_op jit(solution)/shard_map/ppermute | solution.py:22
  36.5 2.2 %collective-permute-start.17 = (bf16[256,128]{1,0:T(8,128)(2,1)}, bf16[256,128]{1,0:T(8,128)(2,1)S(1)}, u32[]{:S(2)}, u32[]{:S(2)}) collective-permute-start(bf16[256,128]{1,0:T(8,128)(2,1)} %get-tuple-element.24), channel_id=1, source_target_pairs={{0,6},{2,0},{4,2},{6,4},{1,7},{3,1},{5,3},{7,5},{8,14},{10,8},{12,... | collective-permute-start | bytes 196616 | tf_op jit(solution)/shard_map/ppermute | solution.py:22
  39.3 3.5 %collective-permute-done.16 = bf16[256,128]{1,0:T(8,128)(2,1)S(1)} collective-permute-done((bf16[256,128]{1,0:T(8,128)(2,1)}, bf16[256,128]{1,0:T(8,128)(2,1)S(1)}, u32[]{:S(2)}, u32[]{:S(2)}) %collective-permute-start.16) | collective-permute-done | bytes 65568 | tf_op jit(solution)/shard_map/ppermute | solution.py:22
  42.8 0.9 add_convert_fusion
  43.7 1.7 %collective-permute-start.18 = (bf16[256,128]{1,0:T(8,128)(2,1)S(1)}, bf16[256,128]{1,0:T(8,128)(2,1)S(1)}, u32[]{:S(2)}, u32[]{:S(2)}) collective-permute-start(bf16[256,128]{1,0:T(8,128)(2,1)S(1)} %add_convert_fusion), channel_id=1, source_target_pairs={{0,2},{2,4},{4,6},{6,0},{1,3},{3,5},{5,7},{7,1},{8,10},{10,12},{12... | collective-permute-start | bytes 196616 | tf_op jit(solution)/shard_map/ppermute | solution.py:22
  45.8 1.8 %collective-permute-start.20 = (bf16[256,128]{1,0:T(8,128)(2,1)S(1)}, bf16[256,128]{1,0:T(8,128)(2,1)S(1)}, u32[]{:S(2)}, u32[]{:S(2)}) collective-permute-start(bf16[256,128]{1,0:T(8,128)(2,1)S(1)} %add_convert_fusion), channel_id=1, source_target_pairs={{0,6},{2,0},{4,2},{6,4},{1,7},{3,1},{5,3},{7,5},{8,14},{10,8},{12,... | collective-permute-start | bytes 196616 | tf_op jit(solution)/shard_map/ppermute | solution.py:22
  47.6 11.4 %shard_map.28 = (f32[256,128]{1,0:T(8,128)}, bf16[256,128]{1,0:T(8,128)(2,1)}, bf16[256,128]{1,0:T(8,128)(2,1)}, bf16[256,128]{1,0:T(8,128)(2,1)}) custom-call(s32[10]{0:T(128)} %stack.271.place_ref, bf16[208,384]{1,0:T(8,128)(2,1)} %copy-done.15, bf16[208,384]{1,0:T(8,128)(2,1)} %copy-done.19, bf16[208,384]{1,0:T(8,128)(2,1)} %copy-done.16, ...), custom_call_target="tpu_custom_call" | custom-call | flops 1006632960 | bytes 4194304 | tf_op jit(solution)/shard_map/pallas_call | solution.py:163
  59.1 1.4 %collective-permute-start.10 = (bf16[256,128]{1,0:T(8,128)(2,1)}, bf16[256,128]{1,0:T(8,128)(2,1)S(1)}, u32[]{:S(2)}, u32[]{:S(2)}) collective-permute-start(bf16[256,128]{1,0:T(8,128)(2,1)} %get-tuple-element.20), channel_id=1, source_target_pairs={{0,6},{2,0},{4,2},{6,4},{1,7},{3,1},{5,3},{7,5},{8,14},{10,8},{12,... | collective-permute-start | bytes 196616 | tf_op jit(solution)/shard_map/ppermute | solution.py:22
  62.6 3.1 %collective-permute-start.23 = (bf16[1024,128]{1,0:T(8,128)(2,1)S(1)}, bf16[1024,128]{1,0:T(8,128)(2,1)S(1)}, u32[]{:S(2)}, u32[]{:S(2)}) collective-permute-start(bf16[1024,128]{1,0:T(8,128)(2,1)S(1)} %pad_maximum_fusion.1.refs_0_), channel_id=1, source_target_pairs={{0,8},{8,0},{1,9},{9,1},{2,10},{10,2},{3,11},{11,3},{4,12},{12,4},... | collective-permute-start | bytes 786440 | tf_op jit(solution)/shard_map/ppermute | solution.py:22
  65.7 1.1 %collective-permute-done.9 = bf16[256,128]{1,0:T(8,128)(2,1)S(1)} collective-permute-done((bf16[256,128]{1,0:T(8,128)(2,1)}, bf16[256,128]{1,0:T(8,128)(2,1)S(1)}, u32[]{:S(2)}, u32[]{:S(2)}) %collective-permute-start.9) | collective-permute-done | bytes 65568 | tf_op jit(solution)/shard_map/ppermute | solution.py:22
  66.8 0.9 add_convert_fusion.1
  67.8 1.2 %collective-permute-start.11 = (bf16[256,128]{1,0:T(8,128)(2,1)S(1)}, bf16[256,128]{1,0:T(8,128)(2,1)S(1)}, u32[]{:S(2)}, u32[]{:S(2)}) collective-permute-start(bf16[256,128]{1,0:T(8,128)(2,1)S(1)} %add_convert_fusion.1), channel_id=1, source_target_pairs={{0,2},{2,4},{4,6},{6,0},{1,3},{3,5},{5,7},{7,1},{8,10},{10,12},{12... | collective-permute-start | bytes 196616 | tf_op jit(solution)/shard_map/ppermute | solution.py:22
  68.9 2.5 %collective-permute-start.12 = (bf16[256,128]{1,0:T(8,128)(2,1)S(1)}, bf16[256,128]{1,0:T(8,128)(2,1)S(1)}, u32[]{:S(2)}, u32[]{:S(2)}) collective-permute-start(bf16[256,128]{1,0:T(8,128)(2,1)S(1)} %add_convert_fusion.1), channel_id=1, source_target_pairs={{0,4},{2,6},{4,0},{6,2},{1,5},{3,7},{5,1},{7,3},{8,12},{10,14},{12... | collective-permute-start | bytes 196616 | tf_op jit(solution)/shard_map/ppermute | solution.py:22
  71.4 1.4 %collective-permute-done.11 = bf16[256,128]{1,0:T(8,128)(2,1)S(1)} collective-permute-done((bf16[256,128]{1,0:T(8,128)(2,1)S(1)}, bf16[256,128]{1,0:T(8,128)(2,1)S(1)}, u32[]{:S(2)}, u32[]{:S(2)}) %collective-permute-start.11) | collective-permute-done | bytes 65568 | tf_op jit(solution)/shard_map/ppermute | solution.py:22
  72.8 1.4 %collective-permute-start.13 = (bf16[256,128]{1,0:T(8,128)(2,1)S(1)}, bf16[256,128]{1,0:T(8,128)(2,1)S(1)}, u32[]{:S(2)}, u32[]{:S(2)}) collective-permute-start(bf16[256,128]{1,0:T(8,128)(2,1)S(1)} %add_convert_fusion.1), channel_id=1, source_target_pairs={{0,6},{2,0},{4,2},{6,4},{1,7},{3,1},{5,3},{7,5},{8,14},{10,8},{12,... | collective-permute-start | bytes 196616 | tf_op jit(solution)/shard_map/ppermute | solution.py:22
  74.2 2.7 %collective-permute-done.13 = bf16[256,128]{1,0:T(8,128)(2,1)S(1)} collective-permute-done((bf16[256,128]{1,0:T(8,128)(2,1)S(1)}, bf16[256,128]{1,0:T(8,128)(2,1)S(1)}, u32[]{:S(2)}, u32[]{:S(2)}) %collective-permute-start.13) | collective-permute-done | bytes 65568 | tf_op jit(solution)/shard_map/ppermute | solution.py:22
  78.8 5.5 %collective-permute-start.24 = (bf16[1024,128]{1,0:T(8,128)(2,1)S(1)}, bf16[1024,128]{1,0:T(8,128)(2,1)S(1)}, u32[]{:S(2)}, u32[]{:S(2)}) collective-permute-start(bf16[1024,128]{1,0:T(8,128)(2,1)S(1)} %collective-permute-done.21.refs_1_), channel_id=1, source_target_pairs={{0,8},{8,0},{1,9},{9,1},{2,10},{10,2},{3,11},{11,3},{4,12},{12,4},... | collective-permute-start | bytes 786440 | tf_op jit(solution)/shard_map/ppermute | solution.py:22
  85.1 3.5 %collective-permute-start.28 = (bf16[1024,128]{1,0:T(8,128)(2,1)S(1)}, bf16[1024,128]{1,0:T(8,128)(2,1)S(1)}, u32[]{:S(2)}, u32[]{:S(2)}) collective-permute-start(bf16[1024,128]{1,0:T(8,128)(2,1)S(1)} %pad_maximum_fusion.refs_0_), channel_id=1, source_target_pairs={{0,8},{8,0},{1,9},{9,1},{2,10},{10,2},{3,11},{11,3},{4,12},{12,4},... | collective-permute-start | bytes 786440 | tf_op jit(solution)/shard_map/ppermute | solution.py:22
  89.1 2.3 %collective-permute-start.32 = (bf16[1024,128]{1,0:T(8,128)(2,1)S(1)}, bf16[1024,128]{1,0:T(8,128)(2,1)S(1)}, u32[]{:S(2)}, u32[]{:S(2)}) collective-permute-start(bf16[1024,128]{1,0:T(8,128)(2,1)S(1)} %collective-permute-done.31.refs_0_), channel_id=1, source_target_pairs={{0,8},{8,0},{1,9},{9,1},{2,10},{10,2},{3,11},{11,3},{4,12},{12,4},... | collective-permute-start | bytes 786440 | tf_op jit(solution)/shard_map/ppermute | solution.py:22
  92.1 3.2 %shard_map.30.refs_2_ = f32[16384,128]{1,0:T(8,128)} custom-call(s32[24]{0:T(128)} %stack.296.start_ref, bf16[1024,128]{1,0:T(8,128)(2,1)} %copy-done.1, bf16[1024,128]{1,0:T(8,128)(2,1)} %copy-done.11, bf16[1024,128]{1,0:T(8,128)(2,1)} %copy-done.12, bf16[1024,128]{1,0:T(8,128)(2,1)} %copy-done.13, bf16[1024,128]{1,0:T(8,128)(2,1)} %copy-done.14, ...), custom_call_target="tpu_custom_call" | custom-call | bytes 4718592 | tf_op jit(solution)/shard_map/pallas_call | solution.py:208
  97.7 2.1 %shard_map.31.refs_6_ = f32[16384,128]{1,0:T(8,128)} custom-call(s32[8]{0:T(128)} %stack.332.start_ref, bf16[1024,128]{1,0:T(8,128)(2,1)} %copy-done.4, bf16[1024,128]{1,0:T(8,128)(2,1)} %copy-done.9, f32[16384,128]{1,0:T(8,128)} %shard_map.30.refs_2_), custom_call_target="tpu_custom_call", output_to_operand_aliasing={{}: (3, {})} | custom-call | bytes 1572864 | tf_op jit(solution)/shard_map/pallas_call | solution.py:208
  101.3 3.2 %shard_map.32.refs_2_ = f32[16384,128]{1,0:T(8,128)} custom-call(s32[24]{0:T(128)} %stack.323.start_ref, bf16[1024,128]{1,0:T(8,128)(2,1)} %copy-done, bf16[1024,128]{1,0:T(8,128)(2,1)} %copy-done.3, bf16[1024,128]{1,0:T(8,128)(2,1)} %copy-done.2, bf16[1024,128]{1,0:T(8,128)(2,1)} %copy-done.6, ...), custom_call_target="tpu_custom_call", output_to_operand_aliasing={{}: (7, {})} | custom-call | bytes 4718592 | tf_op jit(solution)/shard_map/pallas_call | solution.py:208
  106.9 2.1 %shard_map.33 = f32[16384,128]{1,0:T(8,128)} custom-call(s32[8]{0:T(128)} %stack.260.start_ref, bf16[1024,128]{1,0:T(8,128)(2,1)} %copy-done.5, bf16[1024,128]{1,0:T(8,128)(2,1)} %copy-done.10, f32[16384,128]{1,0:T(8,128)} %shard_map.32.refs_2_), custom_call_target="tpu_custom_call", output_to_operand_aliasing={{}: (3, {})} | custom-call | bytes 1572864 | tf_op jit(solution)/shard_map/pallas_call | solution.py:208
  (106 shorter events, 17.0 us)
Async XLA Ops:
  3.6 9.7 %collective-permute-start.2 = (bf16[208,384]{1,0:T(8,128)(2,1)S(1)}, bf16[208,384]{1,0:T(8,128)(2,1)S(1)}, u32[]{:S(2)}, u32[]{:S(2)}) collective-permute-start(bf16[208,384]{1,0:T(8,128)(2,1)S(1)} %pad_maximum_fusion.2.refs_0_), channel_id=1, source_target_pairs={{0,1},{1,0},{2,3},{3,2},{4,5},{5,4},{6,7},{7,6},{8,9},{9,8},{10,11... | collective-permute-start | bytes 479240 | tf_op jit(solution)/shard_map/ppermute | solution.py:22
  9.6 6.5 %collective-permute-start.4 = (bf16[208,384]{1,0:T(8,128)(2,1)S(1)}, bf16[208,384]{1,0:T(8,128)(2,1)S(1)}, u32[]{:S(2)}, u32[]{:S(2)}) collective-permute-start(bf16[208,384]{1,0:T(8,128)(2,1)S(1)} %pad_maximum_fusion.2.refs_0_), channel_id=1, source_target_pairs={{0,16},{16,0},{1,17},{17,1},{2,18},{18,2},{3,19},{19,3},{4,20},{20... | collective-permute-start | bytes 479240 | tf_op jit(solution)/shard_map/ppermute | solution.py:22
  10.9 9.3 %collective-permute-start.6 = (bf16[208,384]{1,0:T(8,128)(2,1)S(1)}, bf16[208,384]{1,0:T(8,128)(2,1)S(1)}, u32[]{:S(2)}, u32[]{:S(2)}) collective-permute-start(bf16[208,384]{1,0:T(8,128)(2,1)S(1)} %pad_maximum_fusion.2.refs_0_), channel_id=1, source_target_pairs={{0,17},{1,16},{16,1},{17,0},{2,19},{3,18},{18,3},{19,2},{4,21},{5,... | collective-permute-start | bytes 479240 | tf_op jit(solution)/shard_map/ppermute | solution.py:254
  10.9 10.0 %collective-permute-start.1 = (bf16[208,384]{1,0:T(8,128)(2,1)S(1)}, bf16[208,384]{1,0:T(8,128)(2,1)S(1)}, u32[]{:S(2)}, u32[]{:S(2)}) collective-permute-start(bf16[208,384]{1,0:T(8,128)(2,1)S(1)} %pad_maximum_fusion.2.refs_0_), channel_id=1, source_target_pairs={{0,8},{8,0},{1,9},{9,1},{2,10},{10,2},{3,11},{11,3},{4,12},{12,4},... | collective-permute-start | bytes 479240 | tf_op jit(solution)/shard_map/ppermute | solution.py:22
  13.3 7.7 %collective-permute-start.3 = (bf16[208,384]{1,0:T(8,128)(2,1)S(1)}, bf16[208,384]{1,0:T(8,128)(2,1)S(1)}, u32[]{:S(2)}, u32[]{:S(2)}) collective-permute-start(bf16[208,384]{1,0:T(8,128)(2,1)S(1)} %collective-permute-done.2.refs_2_), channel_id=1, source_target_pairs={{0,8},{8,0},{1,9},{9,1},{2,10},{10,2},{3,11},{11,3},{4,12},{12,4},... | collective-permute-start | bytes 479240 | tf_op jit(solution)/shard_map/ppermute | solution.py:22
  16.1 5.1 %collective-permute-start.5 = (bf16[208,384]{1,0:T(8,128)(2,1)S(1)}, bf16[208,384]{1,0:T(8,128)(2,1)S(1)}, u32[]{:S(2)}, u32[]{:S(2)}) collective-permute-start(bf16[208,384]{1,0:T(8,128)(2,1)S(1)} %collective-permute-done.4.refs_4_), channel_id=1, source_target_pairs={{0,8},{8,0},{1,9},{9,1},{2,10},{10,2},{3,11},{11,3},{4,12},{12,4},... | collective-permute-start | bytes 479240 | tf_op jit(solution)/shard_map/ppermute | solution.py:22
  34.0 5.3 %collective-permute-start.15 = (bf16[256,128]{1,0:T(8,128)(2,1)}, bf16[256,128]{1,0:T(8,128)(2,1)S(1)}, u32[]{:S(2)}, u32[]{:S(2)}) collective-permute-start(bf16[256,128]{1,0:T(8,128)(2,1)} %get-tuple-element.22), channel_id=1, source_target_pairs={{0,2},{2,4},{4,6},{6,0},{1,3},{3,5},{5,7},{7,1},{8,10},{10,12},{12... | collective-permute-start | bytes 196616 | tf_op jit(solution)/shard_map/ppermute | solution.py:22
  35.3 7.5 %collective-permute-start.16 = (bf16[256,128]{1,0:T(8,128)(2,1)}, bf16[256,128]{1,0:T(8,128)(2,1)S(1)}, u32[]{:S(2)}, u32[]{:S(2)}) collective-permute-start(bf16[256,128]{1,0:T(8,128)(2,1)} %get-tuple-element.23), channel_id=1, source_target_pairs={{0,4},{2,6},{4,0},{6,2},{1,5},{3,7},{5,1},{7,3},{8,12},{10,14},{12... | collective-permute-start | bytes 196616 | tf_op jit(solution)/shard_map/ppermute | solution.py:22
  36.5 6.3 %collective-permute-start.17 = (bf16[256,128]{1,0:T(8,128)(2,1)}, bf16[256,128]{1,0:T(8,128)(2,1)S(1)}, u32[]{:S(2)}, u32[]{:S(2)}) collective-permute-start(bf16[256,128]{1,0:T(8,128)(2,1)} %get-tuple-element.24), channel_id=1, source_target_pairs={{0,6},{2,0},{4,2},{6,4},{1,7},{3,1},{5,3},{7,5},{8,14},{10,8},{12,... | collective-permute-start | bytes 196616 | tf_op jit(solution)/shard_map/ppermute | solution.py:22
  43.7 16.8 %collective-permute-start.18 = (bf16[256,128]{1,0:T(8,128)(2,1)S(1)}, bf16[256,128]{1,0:T(8,128)(2,1)S(1)}, u32[]{:S(2)}, u32[]{:S(2)}) collective-permute-start(bf16[256,128]{1,0:T(8,128)(2,1)S(1)} %add_convert_fusion), channel_id=1, source_target_pairs={{0,2},{2,4},{4,6},{6,0},{1,3},{3,5},{5,7},{7,1},{8,10},{10,12},{12... | collective-permute-start | bytes 196616 | tf_op jit(solution)/shard_map/ppermute | solution.py:22
  45.5 16.0 %collective-permute-start.19 = (bf16[256,128]{1,0:T(8,128)(2,1)S(1)}, bf16[256,128]{1,0:T(8,128)(2,1)S(1)}, u32[]{:S(2)}, u32[]{:S(2)}) collective-permute-start(bf16[256,128]{1,0:T(8,128)(2,1)S(1)} %add_convert_fusion), channel_id=1, source_target_pairs={{0,4},{2,6},{4,0},{6,2},{1,5},{3,7},{5,1},{7,3},{8,12},{10,14},{12... | collective-permute-start | bytes 196616 | tf_op jit(solution)/shard_map/ppermute | solution.py:22
  45.8 15.6 %collective-permute-start.20 = (bf16[256,128]{1,0:T(8,128)(2,1)S(1)}, bf16[256,128]{1,0:T(8,128)(2,1)S(1)}, u32[]{:S(2)}, u32[]{:S(2)}) collective-permute-start(bf16[256,128]{1,0:T(8,128)(2,1)S(1)} %add_convert_fusion), channel_id=1, source_target_pairs={{0,6},{2,0},{4,2},{6,4},{1,7},{3,1},{5,3},{7,5},{8,14},{10,8},{12,... | collective-permute-start | bytes 196616 | tf_op jit(solution)/shard_map/ppermute | solution.py:22
  59.1 3.5 %collective-permute-start.10 = (bf16[256,128]{1,0:T(8,128)(2,1)}, bf16[256,128]{1,0:T(8,128)(2,1)S(1)}, u32[]{:S(2)}, u32[]{:S(2)}) collective-permute-start(bf16[256,128]{1,0:T(8,128)(2,1)} %get-tuple-element.20), channel_id=1, source_target_pairs={{0,6},{2,0},{4,2},{6,4},{1,7},{3,1},{5,3},{7,5},{8,14},{10,8},{12,... | collective-permute-start | bytes 196616 | tf_op jit(solution)/shard_map/ppermute | solution.py:22
  60.4 5.3 %collective-permute-start.8 = (bf16[256,128]{1,0:T(8,128)(2,1)}, bf16[256,128]{1,0:T(8,128)(2,1)S(1)}, u32[]{:S(2)}, u32[]{:S(2)}) collective-permute-start(bf16[256,128]{1,0:T(8,128)(2,1)} %get-tuple-element.18), channel_id=1, source_target_pairs={{0,2},{2,4},{4,6},{6,0},{1,3},{3,5},{5,7},{7,1},{8,10},{10,12},{12... | collective-permute-start | bytes 196616 | tf_op jit(solution)/shard_map/ppermute | solution.py:22
  60.5 6.3 %collective-permute-start.9 = (bf16[256,128]{1,0:T(8,128)(2,1)}, bf16[256,128]{1,0:T(8,128)(2,1)S(1)}, u32[]{:S(2)}, u32[]{:S(2)}) collective-permute-start(bf16[256,128]{1,0:T(8,128)(2,1)} %get-tuple-element.19), channel_id=1, source_target_pairs={{0,4},{2,6},{4,0},{6,2},{1,5},{3,7},{5,1},{7,3},{8,12},{10,14},{12... | collective-permute-start | bytes 196616 | tf_op jit(solution)/shard_map/ppermute | solution.py:22
  61.4 16.5 %collective-permute-start.21 = (bf16[1024,128]{1,0:T(8,128)(2,1)S(1)}, bf16[1024,128]{1,0:T(8,128)(2,1)S(1)}, u32[]{:S(2)}, u32[]{:S(2)}) collective-permute-start(bf16[1024,128]{1,0:T(8,128)(2,1)S(1)} %pad_maximum_fusion.1.refs_0_), channel_id=1, source_target_pairs={{0,1},{1,0},{2,3},{3,2},{4,5},{5,4},{6,7},{7,6},{8,9},{9,8},{10,11... | collective-permute-start | bytes 786440 | tf_op jit(solution)/shard_map/ppermute | solution.py:22
  61.9 16.9 %collective-permute-start.22 = (bf16[1024,128]{1,0:T(8,128)(2,1)S(1)}, bf16[1024,128]{1,0:T(8,128)(2,1)S(1)}, u32[]{:S(2)}, u32[]{:S(2)}) collective-permute-start(bf16[1024,128]{1,0:T(8,128)(2,1)S(1)} %pad_maximum_fusion.1.refs_0_), channel_id=1, source_target_pairs={{0,16},{16,0},{1,17},{17,1},{2,18},{18,2},{3,19},{19,3},{4,20},{20... | collective-permute-start | bytes 786440 | tf_op jit(solution)/shard_map/ppermute | solution.py:22
  62.6 21.7 %collective-permute-start.23 = (bf16[1024,128]{1,0:T(8,128)(2,1)S(1)}, bf16[1024,128]{1,0:T(8,128)(2,1)S(1)}, u32[]{:S(2)}, u32[]{:S(2)}) collective-permute-start(bf16[1024,128]{1,0:T(8,128)(2,1)S(1)} %pad_maximum_fusion.1.refs_0_), channel_id=1, source_target_pairs={{0,8},{8,0},{1,9},{9,1},{2,10},{10,2},{3,11},{11,3},{4,12},{12,4},... | collective-permute-start | bytes 786440 | tf_op jit(solution)/shard_map/ppermute | solution.py:22
  67.8 5.1 %collective-permute-start.11 = (bf16[256,128]{1,0:T(8,128)(2,1)S(1)}, bf16[256,128]{1,0:T(8,128)(2,1)S(1)}, u32[]{:S(2)}, u32[]{:S(2)}) collective-permute-start(bf16[256,128]{1,0:T(8,128)(2,1)S(1)} %add_convert_fusion.1), channel_id=1, source_target_pairs={{0,2},{2,4},{4,6},{6,0},{1,3},{3,5},{5,7},{7,1},{8,10},{10,12},{12... | collective-permute-start | bytes 196616 | tf_op jit(solution)/shard_map/ppermute | solution.py:22
  68.9 5.3 %collective-permute-start.12 = (bf16[256,128]{1,0:T(8,128)(2,1)S(1)}, bf16[256,128]{1,0:T(8,128)(2,1)S(1)}, u32[]{:S(2)}, u32[]{:S(2)}) collective-permute-start(bf16[256,128]{1,0:T(8,128)(2,1)S(1)} %add_convert_fusion.1), channel_id=1, source_target_pairs={{0,4},{2,6},{4,0},{6,2},{1,5},{3,7},{5,1},{7,3},{8,12},{10,14},{12... | collective-permute-start | bytes 196616 | tf_op jit(solution)/shard_map/ppermute | solution.py:22
  72.8 4.2 %collective-permute-start.13 = (bf16[256,128]{1,0:T(8,128)(2,1)S(1)}, bf16[256,128]{1,0:T(8,128)(2,1)S(1)}, u32[]{:S(2)}, u32[]{:S(2)}) collective-permute-start(bf16[256,128]{1,0:T(8,128)(2,1)S(1)} %add_convert_fusion.1), channel_id=1, source_target_pairs={{0,6},{2,0},{4,2},{6,4},{1,7},{3,1},{5,3},{7,5},{8,14},{10,8},{12,... | collective-permute-start | bytes 196616 | tf_op jit(solution)/shard_map/ppermute | solution.py:22
  77.0 8.1 %collective-permute-start.14 = (bf16[1024,128]{1,0:T(8,128)(2,1)S(1)}, bf16[1024,128]{1,0:T(8,128)(2,1)S(1)}, u32[]{:S(2)}, u32[]{:S(2)}) collective-permute-start(bf16[1024,128]{1,0:T(8,128)(2,1)S(1)} %pad_maximum_fusion.refs_0_), channel_id=1, source_target_pairs={{0,16},{16,0},{1,17},{17,1},{2,18},{18,2},{3,19},{19,3},{4,20},{20... | collective-permute-start | bytes 786440 | tf_op jit(solution)/shard_map/ppermute | solution.py:22
  77.8 10.8 %collective-permute-start.27 = (bf16[1024,128]{1,0:T(8,128)(2,1)S(1)}, bf16[1024,128]{1,0:T(8,128)(2,1)S(1)}, u32[]{:S(2)}, u32[]{:S(2)}) collective-permute-start(bf16[1024,128]{1,0:T(8,128)(2,1)S(1)} %pad_maximum_fusion.refs_0_), channel_id=1, source_target_pairs={{0,1},{1,0},{2,3},{3,2},{4,5},{5,4},{6,7},{7,6},{8,9},{9,8},{10,11... | collective-permute-start | bytes 786440 | tf_op jit(solution)/shard_map/ppermute | solution.py:22
  77.9 11.1 %collective-permute-start.31 = (bf16[1024,128]{1,0:T(8,128)(2,1)S(1)}, bf16[1024,128]{1,0:T(8,128)(2,1)S(1)}, u32[]{:S(2)}, u32[]{:S(2)}) collective-permute-start(bf16[1024,128]{1,0:T(8,128)(2,1)S(1)} %collective-permute-done.21.refs_1_), channel_id=1, source_target_pairs={{0,16},{16,0},{1,17},{17,1},{2,18},{18,2},{3,19},{19,3},{4,20},{20... | collective-permute-start | bytes 786440 | tf_op jit(solution)/shard_map/ppermute | solution.py:22
  78.8 12.6 %collective-permute-start.24 = (bf16[1024,128]{1,0:T(8,128)(2,1)S(1)}, bf16[1024,128]{1,0:T(8,128)(2,1)S(1)}, u32[]{:S(2)}, u32[]{:S(2)}) collective-permute-start(bf16[1024,128]{1,0:T(8,128)(2,1)S(1)} %collective-permute-done.21.refs_1_), channel_id=1, source_target_pairs={{0,8},{8,0},{1,9},{9,1},{2,10},{10,2},{3,11},{11,3},{4,12},{12,4},... | collective-permute-start | bytes 786440 | tf_op jit(solution)/shard_map/ppermute | solution.py:22
  84.3 7.2 %collective-permute-start.25 = (bf16[1024,128]{1,0:T(8,128)(2,1)S(1)}, bf16[1024,128]{1,0:T(8,128)(2,1)}, u32[]{:S(2)}, u32[]{:S(2)}) collective-permute-start(bf16[1024,128]{1,0:T(8,128)(2,1)S(1)} %collective-permute-done.22.refs_2_), channel_id=1, source_target_pairs={{0,8},{8,0},{1,9},{9,1},{2,10},{10,2},{3,11},{11,3},{4,12},{12,4},... | collective-permute-start | bytes 786440 | tf_op jit(solution)/shard_map/ppermute | solution.py:22
  85.1 14.7 %collective-permute-start.28 = (bf16[1024,128]{1,0:T(8,128)(2,1)S(1)}, bf16[1024,128]{1,0:T(8,128)(2,1)S(1)}, u32[]{:S(2)}, u32[]{:S(2)}) collective-permute-start(bf16[1024,128]{1,0:T(8,128)(2,1)S(1)} %pad_maximum_fusion.refs_0_), channel_id=1, source_target_pairs={{0,8},{8,0},{1,9},{9,1},{2,10},{10,2},{3,11},{11,3},{4,12},{12,4},... | collective-permute-start | bytes 786440 | tf_op jit(solution)/shard_map/ppermute | solution.py:22
  88.6 11.3 %collective-permute-start.29 = (bf16[1024,128]{1,0:T(8,128)(2,1)S(1)}, bf16[1024,128]{1,0:T(8,128)(2,1)S(1)}, u32[]{:S(2)}, u32[]{:S(2)}) collective-permute-start(bf16[1024,128]{1,0:T(8,128)(2,1)S(1)} %collective-permute-done.27.refs_1_), channel_id=1, source_target_pairs={{0,8},{8,0},{1,9},{9,1},{2,10},{10,2},{3,11},{11,3},{4,12},{12,4},... | collective-permute-start | bytes 786440 | tf_op jit(solution)/shard_map/ppermute | solution.py:22
  89.1 7.9 %collective-permute-start.32 = (bf16[1024,128]{1,0:T(8,128)(2,1)S(1)}, bf16[1024,128]{1,0:T(8,128)(2,1)S(1)}, u32[]{:S(2)}, u32[]{:S(2)}) collective-permute-start(bf16[1024,128]{1,0:T(8,128)(2,1)S(1)} %collective-permute-done.31.refs_0_), channel_id=1, source_target_pairs={{0,8},{8,0},{1,9},{9,1},{2,10},{10,2},{3,11},{11,3},{4,12},{12,4},... | collective-permute-start | bytes 786440 | tf_op jit(solution)/shard_map/ppermute | solution.py:22
  91.4 8.5 %collective-permute-start.30 = (bf16[1024,128]{1,0:T(8,128)(2,1)S(1)}, bf16[1024,128]{1,0:T(8,128)(2,1)S(1)}, u32[]{:S(2)}, u32[]{:S(2)}) collective-permute-start(bf16[1024,128]{1,0:T(8,128)(2,1)S(1)} %collective-permute-done.14.refs_2_), channel_id=1, source_target_pairs={{0,8},{8,0},{1,9},{9,1},{2,10},{10,2},{3,11},{11,3},{4,12},{12,4},... | collective-permute-start | bytes 786440 | tf_op jit(solution)/shard_map/ppermute | solution.py:22
  95.3 9.2 %collective-permute-start.26 = (bf16[1024,128]{1,0:T(8,128)(2,1)S(1)}, bf16[1024,128]{1,0:T(8,128)(2,1)S(1)}, u32[]{:S(2)}, u32[]{:S(2)}) collective-permute-start(bf16[1024,128]{1,0:T(8,128)(2,1)S(1)} %collective-permute-done.14.refs_2_), channel_id=1, source_target_pairs={{0,1},{1,0},{2,3},{3,2},{4,5},{5,4},{6,7},{7,6},{8,9},{9,8},{10,11... | collective-permute-start | bytes 786440 | tf_op jit(solution)/shard_map/ppermute | solution.py:22
  104.6 1.6 %collective-permute-start.33 = (bf16[1024,128]{1,0:T(8,128)(2,1)S(1)}, bf16[1024,128]{1,0:T(8,128)(2,1)S(1)}, u32[]{:S(2)}, u32[]{:S(2)}) collective-permute-start(bf16[1024,128]{1,0:T(8,128)(2,1)S(1)} %collective-permute-done.26.refs_0_), channel_id=1, source_target_pairs={{0,8},{8,0},{1,9},{9,1},{2,10},{10,2},{3,11},{11,3},{4,12},{12,4},... | collective-permute-start | bytes 786440 | tf_op jit(solution)/shard_map/ppermute | solution.py:22
  (25 other events, 165.0 us)

commit v6 on v1

v6 whole, which is shorter than its diff:
```python
import functools
import math

import jax
import jax.numpy as jnp
from jax import lax
from jax.experimental import pallas as pl
from jax.experimental.pallas import tpu as pltpu
from jax.sharding import Mesh, PartitionSpec as P

STREAM = ("row", "core")
SPAN = ("deck", "side")
DIAGONAL = ("row", "side")
WEIGHT_PARTS = 3
LANES = 128
TILE = 16
CHUNKS = 2
TURNED = (((1,), (1,)), ((), ()))


def rotate(value, axis, by=1):
    count = lax.axis_size(axis)
    return lax.ppermute(value, axis, [(i, (i + by) % count) for i in range(count)])


def member(where, rows, offsets):
    r, c, s = offsets
    row = lax.rem(where[0] - r + rows, rows)
    return (row * 2 + lax.rem(where[1] + c, 2)) * 2 + lax.rem(where[2] + s, 2)


def grant(shapes, slack=6 * 2**20):
    total = slack
    for shape, dtype in shapes:
        *outer, rows, columns = shape
        size = jnp.dtype(dtype).itemsize
        rows, columns = pl.cdiv(rows, TILE) * TILE, pl.cdiv(columns, LANES) * LANES
        total += math.prod(outer) * rows * columns * size
    return total


def terms_kernel(sizes, offsets, where_ref, *refs):
    layers, height, across, width, share, chunk, rows, decks, outs = sizes
    members = len(offsets)
    blocks, edges = refs[:members], refs[members : 2 * members]
    out_refs = refs[2 * members : 2 * members + outs]
    field, edge, source, turned, phi, own, even, odd, total = refs[2 * members + outs :]
    slab = layers * height * across
    count = members * slab
    span = source.shape[2]
    group_layers = span // (2 * height * across)

    for n in range(members):
        at = member(where_ref, rows, offsets[n])
        field[at] = blocks[n][...].astype(jnp.float32)
        edge[at] = edges[n][...].astype(jnp.float32)

    index = lax.broadcasted_iota(jnp.int32, (across, width), 0)
    line_rows = 2 * height
    weight_row = edge.shape[2] - across

    def one_layer(x, first_layer):
        stream, layer = lax.div(x, layers), lax.rem(x, layers)

        def layer_at(step, side):
            at = x + step
            inside = ((at >= 0) & (at < members // 2 * layers)).astype(jnp.float32)
            at = jnp.clip(at, 0, members // 2 * layers - 1)
            return lax.div(at, layers) * 2 + side, lax.rem(at, layers), inside

        for side in range(2):
            here_at = 2 * stream + side
            tile = edge[here_at, layer, weight_row:, 0:width]
            weights = tile
            for part in range(1, WEIGHT_PARTS):
                weights = weights + pltpu.roll(tile, width - part * height, 1)
            beside = {step: layer_at(step, side) for step in (-2, -1, 1, 2)}
            for z in range(height):
                at = ((x - first_layer) * 2 + side) * height + z
                at = pl.ds(pl.multiple_of(at * across, across), across)
                weight = jnp.broadcast_to(weights[:, z : z + 1], (across, width))
                twelfth, half = weight * (1.0 / 12.0), weight * 0.5
                base = 2 * z // across * across
                for b in range(3):
                    here = field[here_at, layer, z, b]
                    source[0, b, at, :] = here
                    along = {
                        step: field[m, l, z, b] * inside for step, (m, l, inside) in beside.items()
                    }
                    value = 8.0 * (along[1] - along[-1]) - (along[2] - along[-2])
                    source[1, b, at, :] = value * twelfth

                    outer = edge[here_at, layer, base : base + across, b * width : (b + 1) * width]
                    beyond = field[here_at + 1 - 2 * side, layer, z, b]
                    if side == 0:
                        prev = pltpu.roll(outer, (across - 2 - (2 * z - base)) % across, 0)
                        after = beyond
                    else:
                        prev = beyond
                        after = pltpu.roll(outer, (across - (2 * z - base)) % across, 0)
                    near = pltpu.roll(jnp.where(index < 1, after, here), across - 1, 0)
                    near = near - pltpu.roll(jnp.where(index >= across - 1, prev, here), 1, 0)
                    far = pltpu.roll(jnp.where(index < 2, after, here), across - 2, 0)
                    far = far - pltpu.roll(jnp.where(index >= across - 2, prev, here), 2, 0)
                    source[2, b, at, :] = (8.0 * near - far) * twelfth

                    value = jnp.zeros_like(here)
                    if z < height - 1:
                        value = field[here_at, layer, z + 1, b]
                    if z > 0:
                        value = value - field[here_at, layer, z - 1, b]
                    source[3, b, at, :] = value * half
        return first_layer

    tall = width + share * TILE
    row, column = (lax.broadcasted_iota(jnp.int32, (tall, width), d) for d in range(2))
    mode = lax.div(row - width, TILE) + (
        where_ref[3] * (share // decks) if outs > 1 else 0
    )
    mode = jnp.where(mode >= share, mode - share, mode)
    mode = mode + (member(where_ref, rows, (0, 0, 0)) * CHUNKS + chunk) * share
    pick = (column == jnp.where(row < width, row, mode)).astype(jnp.bfloat16)
    eye = pick[:width]

    def one_group(group, _):
        first_layer = group * group_layers
        lax.fori_loop(first_layer, first_layer + group_layers, one_layer, first_layer)
        lanes = pl.ds(pl.multiple_of(group * span, LANES), span)

        def turn_phi(b, _):
            value = source[0, b].astype(jnp.bfloat16)
            value = lax.dot_general(pick, value, TURNED, preferred_element_type=jnp.float32)
            value = value.astype(jnp.bfloat16)
            phi[b, :, lanes] = value[:width]
            own[b, :, lanes] = value[width:]
            return 0

        def turn_slope(unit, _):
            a, b = lax.div(unit, 3), lax.rem(unit, 3)
            value = source[1 + a, b].astype(jnp.bfloat16)
            value = lax.dot_general(eye, value, TURNED, preferred_element_type=jnp.float32)
            turned[a, b, :, lanes] = value.astype(jnp.bfloat16)
            return 0

        lax.fori_loop(0, 3, turn_phi, 0)
        lax.fori_loop(0, 9, turn_slope, 0)
        return 0

    lax.fori_loop(0, count // span, one_group, 0)

    def build(unit, quad):
        pair, a = lax.div(unit, 3), lax.rem(unit, 3)
        for start in range(0, count, LANES):
            lanes = slice(start, start + LANES)
            spread = [
                [
                    own[b, pl.ds(pl.multiple_of((2 * pair + h) * TILE, TILE), TILE), lanes]
                    for b in range(3)
                ]
                for h in range(2)
            ]
            for k in range(0, width, TILE):
                slope = [turned[a, b, k : k + TILE, lanes] for b in range(3)]
                for h in range(2):
                    value = spread[h][0] * slope[0]
                    value = value + spread[h][1] * slope[1]
                    value = value + spread[h][2] * slope[2]
                    quad[h * width + k : h * width + k + TILE, lanes] = value

    def contract(unit, quad):
        pair, a = lax.div(unit, 3), lax.rem(unit, 3)
        total[pair] += lax.dot_general(
            phi[a], quad[...], TURNED, preferred_element_type=jnp.float32
        )

    units = share // 2 * 3
    total[...] = jnp.zeros_like(total)
    odd[...] = jnp.zeros_like(odd)

    def two_units(turn, _):
        contract(jnp.maximum(2 * turn - 1, 0), odd)
        build(2 * turn, even)
        contract(2 * turn, even)
        build(2 * turn + 1, odd)
        return 0

    lax.fori_loop(0, units // 2, two_units, 0)
    if units % 2:
        contract(units - 2, odd)
        build(units - 1, even)
        contract(units - 1, even)
    else:
        contract(units - 1, odd)
    for pair in range(share // 2):
        for h in range(2):
            start = (2 * pair + h) * width
            out_ref = out_refs[start * outs // (share * width)]
            start = start % (share * width // outs)
            out_ref[start : start + width, :] = total[pair, :, h * width : (h + 1) * width].astype(
                out_ref.dtype
            )


def plane_terms(where, blocks, edges, offsets, chunk, share, rows, decks, outs):
    layers, height, comps, across, width = blocks[0].shape
    members = len(blocks)
    slab = layers * height * across
    count = members * slab
    span = next(n * 2 * slab for n in (1, 2, 4, members // 2) if n * 2 * slab % LANES == 0)
    sizes = (layers, height, across, width, share, chunk, rows, decks, outs)
    vmem = pl.BlockSpec(memory_space=pltpu.VMEM)
    dtypes = [jnp.float32 if outs > 1 and n == 0 else jnp.bfloat16 for n in range(outs)]
    results = [((share * width // outs, width), t) for t in dtypes]
    scratch = [
        ((members,) + blocks[0].shape, jnp.float32),
        ((members,) + edges[0].shape, jnp.float32),
        ((4, comps, span, width), jnp.float32),
        ((3, comps, width, count), jnp.bfloat16),
        ((3, width, count), jnp.bfloat16),
        ((3, share * TILE, count), jnp.bfloat16),
        ((2 * width, count), jnp.bfloat16),
        ((2 * width, count), jnp.bfloat16),
        ((share // 2, width, 2 * width), jnp.float32),
    ]
    inputs = [(v.shape, v.dtype) for v in blocks + edges]
    return pl.pallas_call(
        functools.partial(terms_kernel, sizes, offsets),
        out_shape=[jax.ShapeDtypeStruct(*result) for result in results],
        in_specs=[pl.BlockSpec(memory_space=pltpu.SMEM)] + [vmem] * (2 * members),
        out_specs=[vmem] * outs,
        scratch_shapes=[pltpu.VMEM(*shape) for shape in scratch],
        compiler_params=pltpu.CompilerParams(vmem_limit_bytes=grant(results + scratch + inputs)),
        cost_estimate=pl.CostEstimate(
            flops=2 * share * width * width * count * 3, bytes_accessed=2**22, transcendentals=0
        ),
    )(where, *blocks, *edges)


def place_kernel(plan, pieces, given, where_ref, *refs):
    rows, decks, line, block, runs = plan
    out_ref, wide, sems = refs[pieces + given :]
    step = math.gcd(line, LANES)
    copies = []
    for n, (piece, offsets, chunk, d) in enumerate(runs):
        done = n * line

        def widen(k, _):
            at = pl.multiple_of(k * step, step)
            wide[pl.ds(done + at, step), :] = refs[piece][pl.ds(d * line + at, step), :].astype(
                jnp.float32
            )
            return 0

        lax.fori_loop(0, line // step, widen, 0)
        start = (member(where_ref, rows, offsets) * CHUNKS + chunk) * block
        start = start + lax.rem(where_ref[3] - d + decks, decks) * line
        to = pl.ds(pl.multiple_of(start, line), line)
        copies.append(
            pltpu.make_async_copy(wide.at[done : done + line], out_ref.at[to], sems.at[n])
        )
        copies[-1].start()
    for copy in copies:
        copy.wait()


def put(where, result, total_rows, rows, decks, chosen):
    values = [value for _, _, value in chosen]
    block, width = values[0].shape
    line = block // decks
    runs = [
        (n, offsets, chunk, d) for n, (chunk, offsets, _) in enumerate(chosen) for d in range(decks)
    ]
    given = [] if result is None else [result]
    vmem, anywhere = (pl.BlockSpec(memory_space=m) for m in (pltpu.VMEM, pl.ANY))
    wide = ((len(runs) * line, width), jnp.float32)
    return pl.pallas_call(
        functools.partial(place_kernel, (rows, decks, line, block, runs), len(values), len(given)),
        out_shape=jax.ShapeDtypeStruct((total_rows, width), jnp.float32),
        in_specs=[pl.BlockSpec(memory_space=pltpu.SMEM)]
        + [vmem] * len(values)
        + [anywhere] * len(given),
        out_specs=anywhere,
        scratch_shapes=[pltpu.VMEM(*wide), pltpu.SemaphoreType.DMA((len(runs),))],
        input_output_aliases={1 + len(values): 0} if given else {},
        compiler_params=pltpu.CompilerParams(
            vmem_limit_bytes=grant([wide] + [(v.shape, v.dtype) for v in values], 2**21)
        ),
        cost_estimate=pl.CostEstimate(
            flops=0, bytes_accessed=6 * wide[0][0] * width, transcendentals=0
        ),
    )(where, *values, *given)


def edge_piece(cells, weight):
    layers, height, comps, across, width = cells.shape
    decks = lax.axis_size("deck")
    outer = jnp.where(lax.axis_index("side") == 1, cells[..., across - 2 :, :], cells[..., :2, :])
    joints = [(2 * d + 1, 2 * d + 2) for d in range(decks - 1)]
    outer = lax.ppermute(outer, SPAN, joints + [(j, i) for i, j in joints])
    outer = outer.transpose(0, 1, 3, 2, 4).reshape(layers, 2 * height, comps * width)
    columns = weight.transpose(0, 1, 2)
    parts = []
    for _ in range(WEIGHT_PARTS):
        part = lax.reduce_precision(columns, 8, 7)
        columns = columns - part
        parts.append(part.astype(jnp.bfloat16))
    tile = jnp.concatenate(parts, axis=2)
    total = pl.cdiv(2 * height + across, TILE) * TILE
    outer = jnp.pad(outer, ((0, 0), (0, total - across - 2 * height), (0, 0)))
    tile = jnp.pad(tile, ((0, 0), (0, 0), (0, comps * width - tile.shape[2])))
    return jnp.concatenate([outer, tile], axis=1)


def spread_small(piece):
    rows = lax.axis_size("row")
    got = {(0, 0): piece, (0, 1): rotate(piece, "side")}
    for r in range(1, rows):
        got[(r, 0)] = rotate(piece, "row", r)
        pairs = [(2 * i + s, 2 * ((i + r) % rows) + 1 - s) for i in range(rows) for s in range(2)]
        got[(r, 1)] = lax.ppermute(piece, DIAGONAL, pairs)
    out = {}
    for (r, s), value in got.items():
        out[(r, 0, s)] = value
        out[(r, 1, s)] = rotate(value, "core")
    return out


def sum_over_decks(terms, decks):
    if len(terms) > 1:
        parts = [terms[0]] + [rotate(terms[r], "deck", r) for r in range(1, decks)]
    else:
        width = terms[0].shape[1]
        parts = list(lax.all_to_all(terms[0].reshape(decks, -1, width), "deck", 0, 0))
    return sum(part.astype(jnp.float32) for part in parts).astype(jnp.bfloat16)


def shards(velocity_modes, cell_weight):
    width = velocity_modes.shape[-1]
    rows, decks = lax.axis_size("row"), lax.axis_size("deck")
    members = rows * 4
    share = width // members // CHUNKS
    where = jnp.stack([lax.axis_index(a) for a in ("row", "core", "side", "deck")]).astype(jnp.int32)
    outs = decks if share % (2 * decks) == 0 else 1

    cells = velocity_modes.transpose(0, 2, 3, 1, 4)
    blocks = spread_small(cells)
    edges = spread_small(edge_piece(cells, cell_weight))
    offsets = list(blocks)
    blocks, edges = ([d[o] for o in offsets] for d in (blocks, edges))
    terms = [
        plane_terms(where, blocks, edges, offsets, n, share, rows, decks, outs)
        for n in range(CHUNKS)
    ]

    def put_all(result, chosen):
        return put(where, result, width * width, rows, decks, chosen)

    result = None
    waiting = []
    for n in range(CHUNKS):
        mine = sum_over_decks(terms[n], decks)
        piece = jnp.concatenate([mine] + [rotate(mine, "deck", r) for r in range(1, decks)], axis=0)
        across = rotate(piece, "side")
        along = [rotate(piece, "row", r) for r in range(1, rows)]
        near = [(n, (0, 0, 0), piece), (n, (0, 0, 1), across)]
        near += [(n, (r, 0, 0), v) for r, v in enumerate(along, 1)]
        if n == 0:
            diagonal = [rotate(across, "row", r) for r in range(1, rows)]
        else:
            result = put_all(result, waiting.pop(0))
            along, result = lax.optimization_barrier((along, result))
            diagonal = [rotate(v, "side") for v in along]
        near += [(n, (r, 1, s), rotate(v, "core")) for _, (r, _, s), v in near]
        waiting.append(near)
        if n == CHUNKS - 1:
            result = put_all(result, waiting.pop(0))
            diagonal, result = lax.optimization_barrier((diagonal, result))
        far = [(n, (r, 0, 1), v) for r, v in enumerate(diagonal, 1)]
        far_core = [(n, (r, 1, 1), rotate(v, "core")) for r, v in enumerate(diagonal, 1)]
        if n == CHUNKS - 1:
            waiting[-1] += far
            waiting.append(far_core)
        else:
            waiting.append(far + far_core)
    for chosen in waiting:
        result = put_all(result, chosen)
    return result.reshape(width, width, width)


def solution(mesh):
    streams, spans = (mesh.shape[name] for name in ("stream", "span"))
    split = Mesh(mesh.devices.reshape(streams // 2, 2, spans // 2, 2), STREAM + SPAN)
    placed = (P(STREAM, SPAN, None, None, None), P(STREAM, SPAN, None))
    return jax.shard_map(shards, mesh=split, in_specs=placed, out_specs=P(), check_vma=False)
```

time: 210 us -> 106 us (0.50)
  waiting for transfers between devices: 131 us -> 12.8 us
  starting transfers between devices: 5.28 us -> 54.3 us
  Pallas kernels: 0 us -> 36 us
  local copies, waits for them, and re-layouts: 22.4 us -> 0.95 us
  blocking collectives: 16 us -> 0 us
  between operations: 13.5 us -> 0.15 us
  other arithmetic: 13.7 us -> 2.01 us
  matrix products: 7.29 us -> 0 us
    all_gather x1 -> x0, waiting for transfers between devices: 66.6 us -> none  [shards(): whole = lax.all_gather(mine, ('stream', 'span'), axis=0, tiled=True)]
    reduce_scatter x1 -> x0, waiting for transfers between devices: 64.4 us -> none  [shards(): mine = lax.psum_scatter(rows, 'span', scatter_dimension=0, tiled=True)]
    ppermute x2 -> x41, starting transfers between devices: 5.24 us -> 54.3 us  [the longest x38 53.6 us: rotate(): lax.ppermute(value, axis, [(i, (i + by) % count) for i in range(count)])]
    pallas_call x0 -> x6, Pallas kernels: none -> 36 us  [the longest x2 28 us: plane_terms(): pl.pallas_call(functools.partial(terms_kernel, sizes, offsets), out_shape...]
    all_gather x2 -> x0, blocking collectives: 16 us -> none  [the longest x1 9.79 us: shards(): block = lax.all_gather(wide, 'stream', axis=0, tiled=True)]
    ppermute x2 -> x41, waiting for transfers between devices: 0.01 us -> 12.8 us  [the longest x38 12.8 us: rotate(): lax.ppermute(value, axis, [(i, (i + by) % count) for i in range(count)])]
    dot_general x4 -> x0, matrix products: 7.29 us -> none  [one_block(): jnp.einsum('caj,acik->ijk', phi, quad, preferred_element_type=jnp.float32)]
    reshape x1 -> x0, other arithmetic: 6.65 us -> none  [shards(): return whole.astype(jnp.float32).reshape(width, width, width)]
  transfers between devices with their start and end apart: 4 -> 41, of which waited for: 2 -> 10; matrix products, arithmetic and copies ran while one was open for 0% -> 1% of each run, Pallas kernels for 0% -> 19%
where the time goes in v6:
time: 106 us
  starting transfers between devices  54.3 us (51%)
  Pallas kernels  36 us (34%)
  waiting for transfers between devices  12.8 us (12%)
  other arithmetic  2.01 us (2%)
    ppermute x38, starting transfers between devices, rotate(): lax.ppermute(value, axis, [(i, (i + by) % count) for i in range(count)])  53.6 us
    pallas_call x2, Pallas kernels, plane_terms(): pl.pallas_call(functools.partial(terms_kernel, sizes, offsets), out_shape...  28 us
    ppermute x38, waiting for transfers between devices, rotate(): lax.ppermute(value, axis, [(i, (i + by) % count) for i in range(count)])  12.8 us
    pallas_call x4, Pallas kernels, put(): pl.pallas_call(functools.partial(place_kernel, (rows, decks, line, block,...  8.02 us
  transfers between devices with their start and end apart: 41, of which 10 were waited for; matrix products, arithmetic and copies ran while one was open for 1% of the time, Pallas kernels for 19%

profile of v6, /device:TPU:1, one launch (start us, length us, event | category | flops | bytes accessed | tf_op | source)
XLA Modules:
  0.0 106.3 jit_solution(5092067577100624825)
XLA Ops:
  0.0 1.0 broadcast_select_fusion
  2.6 6.2 %collective-permute-start.9 = (bf16[2,32,384]{2,1,0:T(8,128)(2,1)S(1)}, bf16[2,32,384]{2,1,0:T(8,128)(2,1)S(1)}, u32[]{:S(2)}, u32[]{:S(2)}) collective-permute-start(bf16[2,32,384]{2,1,0:T(8,128)(2,1)S(1)} %fusion.1.refs_8_), channel_id=1, source_target_pairs={{0,1},{1,0},{2,3},{3,2},{4,5},{5,4},{6,7},{7,6},{8,9},{9,8},{10,11... | collective-permute-start | bytes 147464 | tf_op jit(solution)/shard_map/ppermute | solution.py:23
  8.7 1.2 %collective-permute-start.11 = (bf16[2,32,384]{2,1,0:T(8,128)(2,1)S(1)}, bf16[2,32,384]{2,1,0:T(8,128)(2,1)S(1)}, u32[]{:S(2)}, u32[]{:S(2)}) collective-permute-start(bf16[2,32,384]{2,1,0:T(8,128)(2,1)S(1)} %fusion.1.refs_8_), channel_id=1, source_target_pairs={{0,16},{16,0},{1,17},{17,1},{2,18},{18,2},{3,19},{19,3},{4,20},{20... | collective-permute-start | bytes 147464 | tf_op jit(solution)/shard_map/ppermute | solution.py:23
  10.0 1.4 %collective-permute-start.1 = (bf16[2,10,3,8,128]{4,3,2,1,0:T(8,128)(2,1)}, bf16[2,10,3,8,128]{4,3,2,1,0:T(8,128)(2,1)S(1)}, u32[]{:S(2)}, u32[]{:S(2)}) collective-permute-start(bf16[2,10,3,8,128]{4,3,2,1,0:T(8,128)(2,1)} %bitcast.8), channel_id=1, source_target_pairs={{0,1},{1,0},{2,3},{3,2},{4,5},{5,4},{6,7},{7,6},{8,9},{9,8},{10,11... | collective-permute-start | bytes 368648 | tf_op jit(solution)/shard_map/ppermute | solution.py:23
  11.4 1.2 %collective-permute-start.3 = (bf16[2,10,3,8,128]{4,3,2,1,0:T(8,128)(2,1)}, bf16[2,10,3,8,128]{4,3,2,1,0:T(8,128)(2,1)S(1)}, u32[]{:S(2)}, u32[]{:S(2)}) collective-permute-start(bf16[2,10,3,8,128]{4,3,2,1,0:T(8,128)(2,1)} %bitcast.9), channel_id=1, source_target_pairs={{0,16},{16,0},{1,17},{17,1},{2,18},{18,2},{3,19},{19,3},{4,20},{20... | collective-permute-start | bytes 368648 | tf_op jit(solution)/shard_map/ppermute | solution.py:23
  12.7 3.3 %collective-permute-start = (bf16[2,10,3,8,128]{4,3,2,1,0:T(8,128)(2,1)}, bf16[2,10,3,8,128]{4,3,2,1,0:T(8,128)(2,1)S(1)}, u32[]{:S(2)}, u32[]{:S(2)}) collective-permute-start(bf16[2,10,3,8,128]{4,3,2,1,0:T(8,128)(2,1)} %bitcast.11), channel_id=1, source_target_pairs={{0,8},{8,0},{1,9},{9,1},{2,10},{10,2},{3,11},{11,3},{4,12},{12,4},... | collective-permute-start | bytes 368648 | tf_op jit(solution)/shard_map/ppermute | solution.py:23
  15.9 1.9 %collective-permute-start.8 = (bf16[2,32,384]{2,1,0:T(8,128)(2,1)S(1)}, bf16[2,32,384]{2,1,0:T(8,128)(2,1)S(1)}, u32[]{:S(2)}, u32[]{:S(2)}) collective-permute-start(bf16[2,32,384]{2,1,0:T(8,128)(2,1)S(1)} %fusion.1.refs_8_), channel_id=1, source_target_pairs={{0,8},{8,0},{1,9},{9,1},{2,10},{10,2},{3,11},{11,3},{4,12},{12,4},... | collective-permute-start | bytes 147464 | tf_op jit(solution)/shard_map/ppermute | solution.py:23
  20.1 1.7 %collective-permute-start.6 = (bf16[2,10,3,8,128]{4,3,2,1,0:T(8,128)(2,1)S(1)}, bf16[2,10,3,8,128]{4,3,2,1,0:T(8,128)(2,1)S(1)}, u32[]{:S(2)}, u32[]{:S(2)}) collective-permute-start(bf16[2,10,3,8,128]{4,3,2,1,0:T(8,128)(2,1)S(1)} %collective-permute-done.5.refs_6_), channel_id=1, source_target_pairs={{0,8},{8,0},{1,9},{9,1},{2,10},{10,2},{3,11},{11,3},{4,12},{12,4},... | collective-permute-start | bytes 368648 | tf_op jit(solution)/shard_map/ppermute | solution.py:23
  24.2 14.0 %shard_map.29 = (f32[256,128]{1,0:T(8,128)S(1)}, bf16[256,128]{1,0:T(8,128)(2,1)S(1)}, bf16[256,128]{1,0:T(8,128)(2,1)S(1)}, bf16[256,128]{1,0:T(8,128)(2,1)S(1)}) custom-call(s32[4]{0:T(128)S(1)} %pad_add_fusion.where_ref, bf16[2,10,3,8,128]{4,3,2,1,0:T(8,128)(2,1)S(1)} %bitcast.12, bf16[2,10,3,8,128]{4,3,2,1,0:T(8,128)(2,1)S(1)} %collective-permute-done.refs_1_, ...), custom_call_target="tpu_custom_call" | custom-call | flops 1006632960 | bytes 4194304 | tf_op jit(solution)/shard_map/pallas_call | solution.py:226
  38.2 1.4 %collective-permute-start.22 = (bf16[256,128]{1,0:T(8,128)(2,1)S(1)}, bf16[256,128]{1,0:T(8,128)(2,1)S(1)}, u32[]{:S(2)}, u32[]{:S(2)}) collective-permute-start(bf16[256,128]{1,0:T(8,128)(2,1)S(1)} %get-tuple-element.22), channel_id=1, source_target_pairs={{0,2},{2,4},{4,6},{6,0},{1,3},{3,5},{5,7},{7,1},{8,10},{10,12},{12... | collective-permute-start | bytes 196616 | tf_op jit(solution)/shard_map/ppermute | solution.py:23
  39.5 1.1 %collective-permute-start.23 = (bf16[256,128]{1,0:T(8,128)(2,1)S(1)}, bf16[256,128]{1,0:T(8,128)(2,1)S(1)}, u32[]{:S(2)}, u32[]{:S(2)}) collective-permute-start(bf16[256,128]{1,0:T(8,128)(2,1)S(1)} %get-tuple-element.23), channel_id=1, source_target_pairs={{0,4},{2,6},{4,0},{6,2},{1,5},{3,7},{5,1},{7,3},{8,12},{10,14},{12... | collective-permute-start | bytes 196616 | tf_op jit(solution)/shard_map/ppermute | solution.py:23
  40.6 2.3 %collective-permute-start.24 = (bf16[256,128]{1,0:T(8,128)(2,1)S(1)}, bf16[256,128]{1,0:T(8,128)(2,1)S(1)}, u32[]{:S(2)}, u32[]{:S(2)}) collective-permute-start(bf16[256,128]{1,0:T(8,128)(2,1)S(1)} %get-tuple-element.24), channel_id=1, source_target_pairs={{0,6},{2,0},{4,2},{6,4},{1,7},{3,1},{5,3},{7,5},{8,14},{10,8},{12,... | collective-permute-start | bytes 196616 | tf_op jit(solution)/shard_map/ppermute | solution.py:23
  43.2 3.7 %collective-permute-done.23 = bf16[256,128]{1,0:T(8,128)(2,1)S(1)} collective-permute-done((bf16[256,128]{1,0:T(8,128)(2,1)S(1)}, bf16[256,128]{1,0:T(8,128)(2,1)S(1)}, u32[]{:S(2)}, u32[]{:S(2)}) %collective-permute-start.23) | collective-permute-done | bytes 65568 | tf_op jit(solution)/shard_map/ppermute | solution.py:23
  46.9 1.7 %collective-permute-start.25 = (bf16[256,128]{1,0:T(8,128)(2,1)S(1)}, bf16[256,128]{1,0:T(8,128)(2,1)S(1)}, u32[]{:S(2)}, u32[]{:S(2)}) collective-permute-start(bf16[256,128]{1,0:T(8,128)(2,1)S(1)} %add_convert_fusion), channel_id=1, source_target_pairs={{0,2},{2,4},{4,6},{6,0},{1,3},{3,5},{5,7},{7,1},{8,10},{10,12},{12... | collective-permute-start | bytes 196616 | tf_op jit(solution)/shard_map/ppermute | solution.py:23
  49.0 1.8 %collective-permute-start.27 = (bf16[256,128]{1,0:T(8,128)(2,1)S(1)}, bf16[256,128]{1,0:T(8,128)(2,1)S(1)}, u32[]{:S(2)}, u32[]{:S(2)}) collective-permute-start(bf16[256,128]{1,0:T(8,128)(2,1)S(1)} %add_convert_fusion), channel_id=1, source_target_pairs={{0,6},{2,0},{4,2},{6,4},{1,7},{3,1},{5,3},{7,5},{8,14},{10,8},{12,... | collective-permute-start | bytes 196616 | tf_op jit(solution)/shard_map/ppermute | solution.py:23
  50.8 14.0 %shard_map.28 = (f32[256,128]{1,0:T(8,128)S(1)}, bf16[256,128]{1,0:T(8,128)(2,1)S(1)}, bf16[256,128]{1,0:T(8,128)(2,1)S(1)}, bf16[256,128]{1,0:T(8,128)(2,1)S(1)}) custom-call(s32[4]{0:T(128)S(1)} %pad_add_fusion.where_ref, bf16[2,10,3,8,128]{4,3,2,1,0:T(8,128)(2,1)S(1)} %bitcast.13, bf16[2,10,3,8,128]{4,3,2,1,0:T(8,128)(2,1)S(1)} %collective-permute-done.refs_1_, ...), custom_call_target="tpu_custom_call" | custom-call | flops 1006632960 | bytes 4194304 | tf_op jit(solution)/shard_map/pallas_call | solution.py:226
  64.8 1.7 %collective-permute-start.16 = (bf16[256,128]{1,0:T(8,128)(2,1)S(1)}, bf16[256,128]{1,0:T(8,128)(2,1)S(1)}, u32[]{:S(2)}, u32[]{:S(2)}) collective-permute-start(bf16[256,128]{1,0:T(8,128)(2,1)S(1)} %get-tuple-element.19), channel_id=1, source_target_pairs={{0,4},{2,6},{4,0},{6,2},{1,5},{3,7},{5,1},{7,3},{8,12},{10,14},{12... | collective-permute-start | bytes 196616 | tf_op jit(solution)/shard_map/ppermute | solution.py:23
  66.5 1.6 %collective-permute-start.17 = (bf16[256,128]{1,0:T(8,128)(2,1)S(1)}, bf16[256,128]{1,0:T(8,128)(2,1)S(1)}, u32[]{:S(2)}, u32[]{:S(2)}) collective-permute-start(bf16[256,128]{1,0:T(8,128)(2,1)S(1)} %get-tuple-element.20), channel_id=1, source_target_pairs={{0,6},{2,0},{4,2},{6,4},{1,7},{3,1},{5,3},{7,5},{8,14},{10,8},{12,... | collective-permute-start | bytes 196616 | tf_op jit(solution)/shard_map/ppermute | solution.py:23
  70.5 3.2 %collective-permute-start.18 = (bf16[256,128]{1,0:T(8,128)(2,1)S(1)}, bf16[256,128]{1,0:T(8,128)(2,1)S(1)}, u32[]{:S(2)}, u32[]{:S(2)}) collective-permute-start(bf16[256,128]{1,0:T(8,128)(2,1)S(1)} %add_convert_fusion.1), channel_id=1, source_target_pairs={{0,2},{2,4},{4,6},{6,0},{1,3},{3,5},{5,7},{7,1},{8,10},{10,12},{12... | collective-permute-start | bytes 196616 | tf_op jit(solution)/shard_map/ppermute | solution.py:23
  73.6 1.3 %collective-permute-start.19 = (bf16[256,128]{1,0:T(8,128)(2,1)S(1)}, bf16[256,128]{1,0:T(8,128)(2,1)S(1)}, u32[]{:S(2)}, u32[]{:S(2)}) collective-permute-start(bf16[256,128]{1,0:T(8,128)(2,1)S(1)} %add_convert_fusion.1), channel_id=1, source_target_pairs={{0,4},{2,6},{4,0},{6,2},{1,5},{3,7},{5,1},{7,3},{8,12},{10,14},{12... | collective-permute-start | bytes 196616 | tf_op jit(solution)/shard_map/ppermute | solution.py:23
  76.3 4.0 %collective-permute-start.30 = (bf16[1024,128]{1,0:T(8,128)(2,1)S(1)}, bf16[1024,128]{1,0:T(8,128)(2,1)S(1)}, u32[]{:S(2)}, u32[]{:S(2)}) collective-permute-start(bf16[1024,128]{1,0:T(8,128)(2,1)S(1)} %pad_maximum_fusion.1.refs_0_), channel_id=1, source_target_pairs={{0,8},{8,0},{1,9},{9,1},{2,10},{10,2},{3,11},{11,3},{4,12},{12,4},... | collective-permute-start | bytes 786440 | tf_op jit(solution)/shard_map/ppermute | solution.py:23
  80.3 1.0 collective-permute-start.34
  81.2 1.7 %collective-permute-start.32 = (bf16[1024,128]{1,0:T(8,128)(2,1)S(1)}, bf16[1024,128]{1,0:T(8,128)(2,1)S(1)}, u32[]{:S(2)}, u32[]{:S(2)}) collective-permute-start(bf16[1024,128]{1,0:T(8,128)(2,1)S(1)} %collective-permute-done.29.refs_2_), channel_id=1, source_target_pairs={{0,8},{8,0},{1,9},{9,1},{2,10},{10,2},{3,11},{11,3},{4,12},{12,4},... | collective-permute-start | bytes 786440 | tf_op jit(solution)/shard_map/ppermute | solution.py:23
  84.0 2.7 %collective-permute-done.34.refs_0_ = bf16[1024,128]{1,0:T(8,128)(2,1)S(1)} collective-permute-done((bf16[1024,128]{1,0:T(8,128)(2,1)S(1)}, bf16[1024,128]{1,0:T(8,128)(2,1)S(1)}, u32[]{:S(2)}, u32[]{:S(2)}) %collective-permute-start.34) | collective-permute-done | bytes 262176 | tf_op jit(solution)/shard_map/ppermute | solution.py:23
  86.7 4.3 %collective-permute-start.35 = (bf16[1024,128]{1,0:T(8,128)(2,1)S(1)}, bf16[1024,128]{1,0:T(8,128)(2,1)S(1)}, u32[]{:S(2)}, u32[]{:S(2)}) collective-permute-start(bf16[1024,128]{1,0:T(8,128)(2,1)S(1)} %collective-permute-done.34.refs_0_), channel_id=1, source_target_pairs={{0,8},{8,0},{1,9},{9,1},{2,10},{10,2},{3,11},{11,3},{4,12},{12,4},... | collective-permute-start | bytes 786440 | tf_op jit(solution)/shard_map/ppermute | solution.py:23
  91.0 2.4 %shard_map.30.refs_2_ = f32[16384,128]{1,0:T(8,128)} custom-call(s32[4]{0:T(128)S(1)} %pad_add_fusion.where_ref, bf16[1024,128]{1,0:T(8,128)(2,1)S(1)} %pad_maximum_fusion.1.refs_0_, bf16[1024,128]{1,0:T(8,128)(2,1)S(1)} %collective-permute-done.28.refs_1_, bf16[1024,128]{1,0:T(8,128)(2,1)S(1)} %collective-permute-done.29.refs_2_, ...), custom_call_target="tpu_custom_call" | custom-call | bytes 4718592 | tf_op jit(solution)/shard_map/pallas_call | solution.py:276
  93.9 1.4 %collective-permute-start.38 = (bf16[1024,128]{1,0:T(8,128)(2,1)S(1)}, bf16[1024,128]{1,0:T(8,128)(2,1)S(1)}, u32[]{:S(2)}, u32[]{:S(2)}) collective-permute-start(bf16[1024,128]{1,0:T(8,128)(2,1)S(1)} %pad_maximum_fusion.refs_0_), channel_id=1, source_target_pairs={{0,8},{8,0},{1,9},{9,1},{2,10},{10,2},{3,11},{11,3},{4,12},{12,4},... | collective-permute-start | bytes 786440 | tf_op jit(solution)/shard_map/ppermute | solution.py:23
  95.8 1.6 %shard_map.31.refs_7_ = f32[16384,128]{1,0:T(8,128)} custom-call(s32[4]{0:T(128)S(1)} %pad_add_fusion.where_ref, bf16[1024,128]{1,0:T(8,128)(2,1)S(1)} %collective-permute-done.34.refs_0_, bf16[1024,128]{1,0:T(8,128)(2,1)S(1)} %collective-permute-done.35.refs_1_, f32[16384,128]{1,0:T(8,128)} %shard_map.30.refs_2_), custom_call_target="tpu_custom_call", output_to_operand_aliasing={{}: (3, {})} | custom-call | bytes 1572864 | tf_op jit(solution)/shard_map/pallas_call | solution.py:276
  97.4 2.7 %collective-permute-done.33.refs_6_ = bf16[1024,128]{1,0:T(8,128)(2,1)S(1)} collective-permute-done((bf16[1024,128]{1,0:T(8,128)(2,1)S(1)}, bf16[1024,128]{1,0:T(8,128)(2,1)S(1)}, u32[]{:S(2)}, u32[]{:S(2)}) %collective-permute-start.33) | collective-permute-done | bytes 262176 | tf_op jit(solution)/shard_map/ppermute | solution.py:23
  100.1 2.1 %collective-permute-start.36 = (bf16[1024,128]{1,0:T(8,128)(2,1)S(1)}, bf16[1024,128]{1,0:T(8,128)(2,1)S(1)}, u32[]{:S(2)}, u32[]{:S(2)}) collective-permute-start(bf16[1024,128]{1,0:T(8,128)(2,1)S(1)} %collective-permute-done.33.refs_6_), channel_id=1, source_target_pairs={{0,8},{8,0},{1,9},{9,1},{2,10},{10,2},{3,11},{11,3},{4,12},{12,4},... | collective-permute-start | bytes 786440 | tf_op jit(solution)/shard_map/ppermute | solution.py:23
  102.2 2.6 %shard_map.32.refs_1_ = f32[16384,128]{1,0:T(8,128)} custom-call(s32[4]{0:T(128)S(1)} %pad_add_fusion.where_ref, bf16[1024,128]{1,0:T(8,128)(2,1)S(1)} %pad_maximum_fusion.refs_0_, bf16[1024,128]{1,0:T(8,128)(2,1)S(1)} %collective-permute-done.37.refs_1_, bf16[1024,128]{1,0:T(8,128)(2,1)S(1)} %collective-permute-done.21.refs_2_, ...), custom_call_target="tpu_custom_call", output_to_operand_aliasing={{}: (8, {})} | custom-call | bytes 5505024 | tf_op jit(solution)/shard_map/pallas_call | solution.py:276
  104.9 1.4 %shard_map.33 = f32[16384,128]{1,0:T(8,128)} custom-call(s32[4]{0:T(128)S(1)} %pad_add_fusion.where_ref, bf16[1024,128]{1,0:T(8,128)(2,1)S(1)} %collective-permute-done.36.refs_0_, f32[16384,128]{1,0:T(8,128)} %shard_map.32.refs_1_), custom_call_target="tpu_custom_call", output_to_operand_aliasing={{}: (2, {})} | custom-call | bytes 786432 | tf_op jit(solution)/shard_map/pallas_call | solution.py:276
  (69 shorter events, 12.6 us)
Async XLA Ops:
  2.6 10.1 %collective-permute-start.9 = (bf16[2,32,384]{2,1,0:T(8,128)(2,1)S(1)}, bf16[2,32,384]{2,1,0:T(8,128)(2,1)S(1)}, u32[]{:S(2)}, u32[]{:S(2)}) collective-permute-start(bf16[2,32,384]{2,1,0:T(8,128)(2,1)S(1)} %fusion.1.refs_8_), channel_id=1, source_target_pairs={{0,1},{1,0},{2,3},{3,2},{4,5},{5,4},{6,7},{7,6},{8,9},{9,8},{10,11... | collective-permute-start | bytes 147464 | tf_op jit(solution)/shard_map/ppermute | solution.py:23
  10.0 6.0 %collective-permute-start.13 = (bf16[2,32,384]{2,1,0:T(8,128)(2,1)S(1)}, bf16[2,32,384]{2,1,0:T(8,128)(2,1)S(1)}, u32[]{:S(2)}, u32[]{:S(2)}) collective-permute-start(bf16[2,32,384]{2,1,0:T(8,128)(2,1)S(1)} %fusion.1.refs_8_), channel_id=1, source_target_pairs={{0,17},{1,16},{16,1},{17,0},{2,19},{3,18},{18,3},{19,2},{4,21},{5,... | collective-permute-start | bytes 147464 | tf_op jit(solution)/shard_map/ppermute | solution.py:320
  10.0 9.1 %collective-permute-start.1 = (bf16[2,10,3,8,128]{4,3,2,1,0:T(8,128)(2,1)}, bf16[2,10,3,8,128]{4,3,2,1,0:T(8,128)(2,1)S(1)}, u32[]{:S(2)}, u32[]{:S(2)}) collective-permute-start(bf16[2,10,3,8,128]{4,3,2,1,0:T(8,128)(2,1)} %bitcast.8), channel_id=1, source_target_pairs={{0,1},{1,0},{2,3},{3,2},{4,5},{5,4},{6,7},{7,6},{8,9},{9,8},{10,11... | collective-permute-start | bytes 368648 | tf_op jit(solution)/shard_map/ppermute | solution.py:23
  11.4 7.9 %collective-permute-start.3 = (bf16[2,10,3,8,128]{4,3,2,1,0:T(8,128)(2,1)}, bf16[2,10,3,8,128]{4,3,2,1,0:T(8,128)(2,1)S(1)}, u32[]{:S(2)}, u32[]{:S(2)}) collective-permute-start(bf16[2,10,3,8,128]{4,3,2,1,0:T(8,128)(2,1)} %bitcast.9), channel_id=1, source_target_pairs={{0,16},{16,0},{1,17},{17,1},{2,18},{18,2},{3,19},{19,3},{4,20},{20... | collective-permute-start | bytes 368648 | tf_op jit(solution)/shard_map/ppermute | solution.py:23
  12.6 7.5 %collective-permute-start.5 = (bf16[2,10,3,8,128]{4,3,2,1,0:T(8,128)(2,1)}, bf16[2,10,3,8,128]{4,3,2,1,0:T(8,128)(2,1)S(1)}, u32[]{:S(2)}, u32[]{:S(2)}) collective-permute-start(bf16[2,10,3,8,128]{4,3,2,1,0:T(8,128)(2,1)} %bitcast.10), channel_id=1, source_target_pairs={{0,17},{1,16},{16,1},{17,0},{2,19},{3,18},{18,3},{19,2},{4,21},{5,... | collective-permute-start | bytes 368648 | tf_op jit(solution)/shard_map/ppermute | solution.py:320
  12.7 9.2 %collective-permute-start = (bf16[2,10,3,8,128]{4,3,2,1,0:T(8,128)(2,1)}, bf16[2,10,3,8,128]{4,3,2,1,0:T(8,128)(2,1)S(1)}, u32[]{:S(2)}, u32[]{:S(2)}) collective-permute-start(bf16[2,10,3,8,128]{4,3,2,1,0:T(8,128)(2,1)} %bitcast.11), channel_id=1, source_target_pairs={{0,8},{8,0},{1,9},{9,1},{2,10},{10,2},{3,11},{11,3},{4,12},{12,4},... | collective-permute-start | bytes 368648 | tf_op jit(solution)/shard_map/ppermute | solution.py:23
  19.1 4.2 %collective-permute-start.2 = (bf16[2,10,3,8,128]{4,3,2,1,0:T(8,128)(2,1)S(1)}, bf16[2,10,3,8,128]{4,3,2,1,0:T(8,128)(2,1)S(1)}, u32[]{:S(2)}, u32[]{:S(2)}) collective-permute-start(bf16[2,10,3,8,128]{4,3,2,1,0:T(8,128)(2,1)S(1)} %collective-permute-done.1.refs_2_), channel_id=1, source_target_pairs={{0,8},{8,0},{1,9},{9,1},{2,10},{10,2},{3,11},{11,3},{4,12},{12,4},... | collective-permute-start | bytes 368648 | tf_op jit(solution)/shard_map/ppermute | solution.py:23
  38.2 5.0 %collective-permute-start.22 = (bf16[256,128]{1,0:T(8,128)(2,1)S(1)}, bf16[256,128]{1,0:T(8,128)(2,1)S(1)}, u32[]{:S(2)}, u32[]{:S(2)}) collective-permute-start(bf16[256,128]{1,0:T(8,128)(2,1)S(1)} %get-tuple-element.22), channel_id=1, source_target_pairs={{0,2},{2,4},{4,6},{6,0},{1,3},{3,5},{5,7},{7,1},{8,10},{10,12},{12... | collective-permute-start | bytes 196616 | tf_op jit(solution)/shard_map/ppermute | solution.py:23
  39.5 7.3 %collective-permute-start.23 = (bf16[256,128]{1,0:T(8,128)(2,1)S(1)}, bf16[256,128]{1,0:T(8,128)(2,1)S(1)}, u32[]{:S(2)}, u32[]{:S(2)}) collective-permute-start(bf16[256,128]{1,0:T(8,128)(2,1)S(1)} %get-tuple-element.23), channel_id=1, source_target_pairs={{0,4},{2,6},{4,0},{6,2},{1,5},{3,7},{5,1},{7,3},{8,12},{10,14},{12... | collective-permute-start | bytes 196616 | tf_op jit(solution)/shard_map/ppermute | solution.py:23
  40.6 6.2 %collective-permute-start.24 = (bf16[256,128]{1,0:T(8,128)(2,1)S(1)}, bf16[256,128]{1,0:T(8,128)(2,1)S(1)}, u32[]{:S(2)}, u32[]{:S(2)}) collective-permute-start(bf16[256,128]{1,0:T(8,128)(2,1)S(1)} %get-tuple-element.24), channel_id=1, source_target_pairs={{0,6},{2,0},{4,2},{6,4},{1,7},{3,1},{5,3},{7,5},{8,14},{10,8},{12,... | collective-permute-start | bytes 196616 | tf_op jit(solution)/shard_map/ppermute | solution.py:23
  46.9 19.6 %collective-permute-start.25 = (bf16[256,128]{1,0:T(8,128)(2,1)S(1)}, bf16[256,128]{1,0:T(8,128)(2,1)S(1)}, u32[]{:S(2)}, u32[]{:S(2)}) collective-permute-start(bf16[256,128]{1,0:T(8,128)(2,1)S(1)} %add_convert_fusion), channel_id=1, source_target_pairs={{0,2},{2,4},{4,6},{6,0},{1,3},{3,5},{5,7},{7,1},{8,10},{10,12},{12... | collective-permute-start | bytes 196616 | tf_op jit(solution)/shard_map/ppermute | solution.py:23
  48.6 19.5 %collective-permute-start.26 = (bf16[256,128]{1,0:T(8,128)(2,1)S(1)}, bf16[256,128]{1,0:T(8,128)(2,1)S(1)}, u32[]{:S(2)}, u32[]{:S(2)}) collective-permute-start(bf16[256,128]{1,0:T(8,128)(2,1)S(1)} %add_convert_fusion), channel_id=1, source_target_pairs={{0,4},{2,6},{4,0},{6,2},{1,5},{3,7},{5,1},{7,3},{8,12},{10,14},{12... | collective-permute-start | bytes 196616 | tf_op jit(solution)/shard_map/ppermute | solution.py:23
  49.0 19.1 %collective-permute-start.27 = (bf16[256,128]{1,0:T(8,128)(2,1)S(1)}, bf16[256,128]{1,0:T(8,128)(2,1)S(1)}, u32[]{:S(2)}, u32[]{:S(2)}) collective-permute-start(bf16[256,128]{1,0:T(8,128)(2,1)S(1)} %add_convert_fusion), channel_id=1, source_target_pairs={{0,6},{2,0},{4,2},{6,4},{1,7},{3,1},{5,3},{7,5},{8,14},{10,8},{12,... | collective-permute-start | bytes 196616 | tf_op jit(solution)/shard_map/ppermute | solution.py:23
  64.8 5.0 %collective-permute-start.15 = (bf16[256,128]{1,0:T(8,128)(2,1)S(1)}, bf16[256,128]{1,0:T(8,128)(2,1)S(1)}, u32[]{:S(2)}, u32[]{:S(2)}) collective-permute-start(bf16[256,128]{1,0:T(8,128)(2,1)S(1)} %get-tuple-element.18), channel_id=1, source_target_pairs={{0,2},{2,4},{4,6},{6,0},{1,3},{3,5},{5,7},{7,1},{8,10},{10,12},{12... | collective-permute-start | bytes 196616 | tf_op jit(solution)/shard_map/ppermute | solution.py:23
  64.8 4.9 %collective-permute-start.16 = (bf16[256,128]{1,0:T(8,128)(2,1)S(1)}, bf16[256,128]{1,0:T(8,128)(2,1)S(1)}, u32[]{:S(2)}, u32[]{:S(2)}) collective-permute-start(bf16[256,128]{1,0:T(8,128)(2,1)S(1)} %get-tuple-element.19), channel_id=1, source_target_pairs={{0,4},{2,6},{4,0},{6,2},{1,5},{3,7},{5,1},{7,3},{8,12},{10,14},{12... | collective-permute-start | bytes 196616 | tf_op jit(solution)/shard_map/ppermute | solution.py:23
  68.1 12.1 %collective-permute-start.28 = (bf16[1024,128]{1,0:T(8,128)(2,1)S(1)}, bf16[1024,128]{1,0:T(8,128)(2,1)S(1)}, u32[]{:S(2)}, u32[]{:S(2)}) collective-permute-start(bf16[1024,128]{1,0:T(8,128)(2,1)S(1)} %pad_maximum_fusion.1.refs_0_), channel_id=1, source_target_pairs={{0,1},{1,0},{2,3},{3,2},{4,5},{5,4},{6,7},{7,6},{8,9},{9,8},{10,11... | collective-permute-start | bytes 786440 | tf_op jit(solution)/shard_map/ppermute | solution.py:23
  68.5 12.7 %collective-permute-start.29 = (bf16[1024,128]{1,0:T(8,128)(2,1)S(1)}, bf16[1024,128]{1,0:T(8,128)(2,1)S(1)}, u32[]{:S(2)}, u32[]{:S(2)}) collective-permute-start(bf16[1024,128]{1,0:T(8,128)(2,1)S(1)} %pad_maximum_fusion.1.refs_0_), channel_id=1, source_target_pairs={{0,16},{16,0},{1,17},{17,1},{2,18},{18,2},{3,19},{19,3},{4,20},{20... | collective-permute-start | bytes 786440 | tf_op jit(solution)/shard_map/ppermute | solution.py:23
  70.5 5.8 %collective-permute-start.18 = (bf16[256,128]{1,0:T(8,128)(2,1)S(1)}, bf16[256,128]{1,0:T(8,128)(2,1)S(1)}, u32[]{:S(2)}, u32[]{:S(2)}) collective-permute-start(bf16[256,128]{1,0:T(8,128)(2,1)S(1)} %add_convert_fusion.1), channel_id=1, source_target_pairs={{0,2},{2,4},{4,6},{6,0},{1,3},{3,5},{5,7},{7,1},{8,10},{10,12},{12... | collective-permute-start | bytes 196616 | tf_op jit(solution)/shard_map/ppermute | solution.py:23
  73.6 6.6 %collective-permute-start.19 = (bf16[256,128]{1,0:T(8,128)(2,1)S(1)}, bf16[256,128]{1,0:T(8,128)(2,1)S(1)}, u32[]{:S(2)}, u32[]{:S(2)}) collective-permute-start(bf16[256,128]{1,0:T(8,128)(2,1)S(1)} %add_convert_fusion.1), channel_id=1, source_target_pairs={{0,4},{2,6},{4,0},{6,2},{1,5},{3,7},{5,1},{7,3},{8,12},{10,14},{12... | collective-permute-start | bytes 196616 | tf_op jit(solution)/shard_map/ppermute | solution.py:23
  74.9 8.0 %collective-permute-start.20 = (bf16[256,128]{1,0:T(8,128)(2,1)S(1)}, bf16[256,128]{1,0:T(8,128)(2,1)S(1)}, u32[]{:S(2)}, u32[]{:S(2)}) collective-permute-start(bf16[256,128]{1,0:T(8,128)(2,1)S(1)} %add_convert_fusion.1), channel_id=1, source_target_pairs={{0,6},{2,0},{4,2},{6,4},{1,7},{3,1},{5,3},{7,5},{8,14},{10,8},{12,... | collective-permute-start | bytes 196616 | tf_op jit(solution)/shard_map/ppermute | solution.py:23
  76.3 7.3 %collective-permute-start.30 = (bf16[1024,128]{1,0:T(8,128)(2,1)S(1)}, bf16[1024,128]{1,0:T(8,128)(2,1)S(1)}, u32[]{:S(2)}, u32[]{:S(2)}) collective-permute-start(bf16[1024,128]{1,0:T(8,128)(2,1)S(1)} %pad_maximum_fusion.1.refs_0_), channel_id=1, source_target_pairs={{0,8},{8,0},{1,9},{9,1},{2,10},{10,2},{3,11},{11,3},{4,12},{12,4},... | collective-permute-start | bytes 786440 | tf_op jit(solution)/shard_map/ppermute | solution.py:23
  80.3 10.7 %collective-permute-start.31 = (bf16[1024,128]{1,0:T(8,128)(2,1)S(1)}, bf16[1024,128]{1,0:T(8,128)(2,1)S(1)}, u32[]{:S(2)}, u32[]{:S(2)}) collective-permute-start(bf16[1024,128]{1,0:T(8,128)(2,1)S(1)} %collective-permute-done.28.refs_1_), channel_id=1, source_target_pairs={{0,8},{8,0},{1,9},{9,1},{2,10},{10,2},{3,11},{11,3},{4,12},{12,4},... | collective-permute-start | bytes 786440 | tf_op jit(solution)/shard_map/ppermute | solution.py:23
  80.3 6.4 %collective-permute-start.34 = (bf16[1024,128]{1,0:T(8,128)(2,1)S(1)}, bf16[1024,128]{1,0:T(8,128)(2,1)S(1)}, u32[]{:S(2)}, u32[]{:S(2)}) collective-permute-start(bf16[1024,128]{1,0:T(8,128)(2,1)S(1)} %collective-permute-done.28.refs_1_), channel_id=1, source_target_pairs={{0,16},{16,0},{1,17},{17,1},{2,18},{18,2},{3,19},{19,3},{4,20},{20... | collective-permute-start | bytes 786440 | tf_op jit(solution)/shard_map/ppermute | solution.py:23
  81.2 9.8 %collective-permute-start.32 = (bf16[1024,128]{1,0:T(8,128)(2,1)S(1)}, bf16[1024,128]{1,0:T(8,128)(2,1)S(1)}, u32[]{:S(2)}, u32[]{:S(2)}) collective-permute-start(bf16[1024,128]{1,0:T(8,128)(2,1)S(1)} %collective-permute-done.29.refs_2_), channel_id=1, source_target_pairs={{0,8},{8,0},{1,9},{9,1},{2,10},{10,2},{3,11},{11,3},{4,12},{12,4},... | collective-permute-start | bytes 786440 | tf_op jit(solution)/shard_map/ppermute | solution.py:23
  83.0 10.4 %collective-permute-start.21 = (bf16[1024,128]{1,0:T(8,128)(2,1)S(1)}, bf16[1024,128]{1,0:T(8,128)(2,1)S(1)}, u32[]{:S(2)}, u32[]{:S(2)}) collective-permute-start(bf16[1024,128]{1,0:T(8,128)(2,1)S(1)} %pad_maximum_fusion.refs_0_), channel_id=1, source_target_pairs={{0,16},{16,0},{1,17},{17,1},{2,18},{18,2},{3,19},{19,3},{4,20},{20... | collective-permute-start | bytes 786440 | tf_op jit(solution)/shard_map/ppermute | solution.py:23
  83.6 11.7 %collective-permute-start.37 = (bf16[1024,128]{1,0:T(8,128)(2,1)S(1)}, bf16[1024,128]{1,0:T(8,128)(2,1)S(1)}, u32[]{:S(2)}, u32[]{:S(2)}) collective-permute-start(bf16[1024,128]{1,0:T(8,128)(2,1)S(1)} %pad_maximum_fusion.refs_0_), channel_id=1, source_target_pairs={{0,1},{1,0},{2,3},{3,2},{4,5},{5,4},{6,7},{7,6},{8,9},{9,8},{10,11... | collective-permute-start | bytes 786440 | tf_op jit(solution)/shard_map/ppermute | solution.py:23
  86.7 9.1 %collective-permute-start.35 = (bf16[1024,128]{1,0:T(8,128)(2,1)S(1)}, bf16[1024,128]{1,0:T(8,128)(2,1)S(1)}, u32[]{:S(2)}, u32[]{:S(2)}) collective-permute-start(bf16[1024,128]{1,0:T(8,128)(2,1)S(1)} %collective-permute-done.34.refs_0_), channel_id=1, source_target_pairs={{0,8},{8,0},{1,9},{9,1},{2,10},{10,2},{3,11},{11,3},{4,12},{12,4},... | collective-permute-start | bytes 786440 | tf_op jit(solution)/shard_map/ppermute | solution.py:23
  93.4 6.7 %collective-permute-start.33 = (bf16[1024,128]{1,0:T(8,128)(2,1)S(1)}, bf16[1024,128]{1,0:T(8,128)(2,1)S(1)}, u32[]{:S(2)}, u32[]{:S(2)}) collective-permute-start(bf16[1024,128]{1,0:T(8,128)(2,1)S(1)} %collective-permute-done.21.refs_2_), channel_id=1, source_target_pairs={{0,1},{1,0},{2,3},{3,2},{4,5},{5,4},{6,7},{7,6},{8,9},{9,8},{10,11... | collective-permute-start | bytes 786440 | tf_op jit(solution)/shard_map/ppermute | solution.py:23
  93.9 8.3 %collective-permute-start.38 = (bf16[1024,128]{1,0:T(8,128)(2,1)S(1)}, bf16[1024,128]{1,0:T(8,128)(2,1)S(1)}, u32[]{:S(2)}, u32[]{:S(2)}) collective-permute-start(bf16[1024,128]{1,0:T(8,128)(2,1)S(1)} %pad_maximum_fusion.refs_0_), channel_id=1, source_target_pairs={{0,8},{8,0},{1,9},{9,1},{2,10},{10,2},{3,11},{11,3},{4,12},{12,4},... | collective-permute-start | bytes 786440 | tf_op jit(solution)/shard_map/ppermute | solution.py:23
  95.3 6.9 %collective-permute-start.40 = (bf16[1024,128]{1,0:T(8,128)(2,1)S(1)}, bf16[1024,128]{1,0:T(8,128)(2,1)S(1)}, u32[]{:S(2)}, u32[]{:S(2)}) collective-permute-start(bf16[1024,128]{1,0:T(8,128)(2,1)S(1)} %collective-permute-done.21.refs_2_), channel_id=1, source_target_pairs={{0,8},{8,0},{1,9},{9,1},{2,10},{10,2},{3,11},{11,3},{4,12},{12,4},... | collective-permute-start | bytes 786440 | tf_op jit(solution)/shard_map/ppermute | solution.py:23
  95.3 6.9 %collective-permute-start.39 = (bf16[1024,128]{1,0:T(8,128)(2,1)S(1)}, bf16[1024,128]{1,0:T(8,128)(2,1)S(1)}, u32[]{:S(2)}, u32[]{:S(2)}) collective-permute-start(bf16[1024,128]{1,0:T(8,128)(2,1)S(1)} %collective-permute-done.37.refs_1_), channel_id=1, source_target_pairs={{0,8},{8,0},{1,9},{9,1},{2,10},{10,2},{3,11},{11,3},{4,12},{12,4},... | collective-permute-start | bytes 786440 | tf_op jit(solution)/shard_map/ppermute | solution.py:23
  100.1 4.7 %collective-permute-start.36 = (bf16[1024,128]{1,0:T(8,128)(2,1)S(1)}, bf16[1024,128]{1,0:T(8,128)(2,1)S(1)}, u32[]{:S(2)}, u32[]{:S(2)}) collective-permute-start(bf16[1024,128]{1,0:T(8,128)(2,1)S(1)} %collective-permute-done.33.refs_6_), channel_id=1, source_target_pairs={{0,8},{8,0},{1,9},{9,1},{2,10},{10,2},{3,11},{11,3},{4,12},{12,4},... | collective-permute-start | bytes 786440 | tf_op jit(solution)/shard_map/ppermute | solution.py:23
  (10 other events, 25.9 us)

commit v7 on v6

--- a/solution.py
+++ b/solution.py
@@ -39,12 +39,11 @@
     return total
 
 
-def terms_kernel(sizes, offsets, where_ref, *refs):
-    layers, height, across, width, share, chunk, rows, decks, outs = sizes
+def slopes_kernel(sizes, offsets, where_ref, *refs):
+    layers, height, across, width, share, rows, decks, outs = sizes
     members = len(offsets)
     blocks, edges = refs[:members], refs[members : 2 * members]
-    out_refs = refs[2 * members : 2 * members + outs]
-    field, edge, source, turned, phi, own, even, odd, total = refs[2 * members + outs :]
+    turned, phi, own, field, edge, source = refs[2 * members :]
     slab = layers * height * across
     count = members * slab
     span = source.shape[2]
@@ -112,27 +111,28 @@
                     source[3, b, at, :] = value * half
         return first_layer
 
-    tall = width + share * TILE
-    row, column = (lax.broadcasted_iota(jnp.int32, (tall, width), d) for d in range(2))
-    mode = lax.div(row - width, TILE) + (
-        where_ref[3] * (share // decks) if outs > 1 else 0
+    row, column = (lax.broadcasted_iota(jnp.int32, (width, width), d) for d in range(2))
+    eye = (row == column).astype(jnp.bfloat16)
+    row, column = (
+        lax.broadcasted_iota(jnp.int32, (CHUNKS * share * TILE, width), d) for d in range(2)
     )
+    chunk = sum((row >= n * share * TILE).astype(jnp.int32) for n in range(1, CHUNKS))
+    mode = lax.shift_right_logical(row, TILE.bit_length() - 1) - chunk * share
+    mode = mode + (where_ref[3] * (share // decks) if outs > 1 else 0)
     mode = jnp.where(mode >= share, mode - share, mode)
     mode = mode + (member(where_ref, rows, (0, 0, 0)) * CHUNKS + chunk) * share
-    pick = (column == jnp.where(row < width, row, mode)).astype(jnp.bfloat16)
-    eye = pick[:width]
+    pick = (column == mode).astype(jnp.bfloat16)
 
     def one_group(group, _):
         first_layer = group * group_layers
         lax.fori_loop(first_layer, first_layer + group_layers, one_layer, first_layer)
         lanes = pl.ds(pl.multiple_of(group * span, LANES), span)
 
-        def turn_phi(b, _):
+        def pick_phi(b, _):
             value = source[0, b].astype(jnp.bfloat16)
+            phi[b, lanes, :] = value
             value = lax.dot_general(pick, value, TURNED, preferred_element_type=jnp.float32)
-            value = value.astype(jnp.bfloat16)
-            phi[b, :, lanes] = value[:width]
-            own[b, :, lanes] = value[width:]
+            own[b, :, lanes] = value.astype(jnp.bfloat16)
             return 0
 
         def turn_slope(unit, _):
@@ -142,11 +142,50 @@
             turned[a, b, :, lanes] = value.astype(jnp.bfloat16)
             return 0
 
-        lax.fori_loop(0, 3, turn_phi, 0)
+        lax.fori_loop(0, 3, pick_phi, 0)
         lax.fori_loop(0, 9, turn_slope, 0)
         return 0
 
     lax.fori_loop(0, count // span, one_group, 0)
+
+def plane_slopes(where, blocks, edges, offsets, share, rows, decks, outs):
+    layers, height, comps, across, width = blocks[0].shape
+    members = len(blocks)
+    slab = layers * height * across
+    count = members * slab
+    span = next(n * 2 * slab for n in (1, 2, 4, members // 2) if n * 2 * slab % LANES == 0)
+    sizes = (layers, height, across, width, share, rows, decks, outs)
+    vmem = pl.BlockSpec(memory_space=pltpu.VMEM)
+    results = [
+        ((3, comps, width, count), jnp.bfloat16),
+        ((3, count, width), jnp.bfloat16),
+        ((3, CHUNKS * share * TILE, count), jnp.bfloat16),
+    ]
+    scratch = [
+        ((members,) + blocks[0].shape, jnp.float32),
+        ((members,) + edges[0].shape, jnp.float32),
+        ((4, comps, span, width), jnp.float32),
+    ]
+    inputs = [(v.shape, v.dtype) for v in blocks + edges]
+    return pl.pallas_call(
+        functools.partial(slopes_kernel, sizes, offsets),
+        out_shape=[jax.ShapeDtypeStruct(*result) for result in results],
+        in_specs=[pl.BlockSpec(memory_space=pltpu.SMEM)] + [vmem] * (2 * members),
+        out_specs=[vmem] * len(results),
+        scratch_shapes=[pltpu.VMEM(*shape) for shape in scratch],
+        compiler_params=pltpu.CompilerParams(vmem_limit_bytes=grant(results + scratch + inputs)),
+        cost_estimate=pl.CostEstimate(
+            flops=2 * 12 * count * width * width, bytes_accessed=2**22, transcendentals=0
+        ),
+    )(where, *blocks, *edges)
+
+
+def terms_kernel(share, chunk, turned, phi, own, *refs):
+    *out_refs, even, odd, total = refs
+    outs = len(out_refs)
+    width, count = turned.shape[2:]
+
+    first = chunk * share
 
     def build(unit, quad):
         pair, a = lax.div(unit, 3), lax.rem(unit, 3)
@@ -154,7 +193,7 @@
             lanes = slice(start, start + LANES)
             spread = [
                 [
-                    own[b, pl.ds(pl.multiple_of((2 * pair + h) * TILE, TILE), TILE), lanes]
+                    own[b, pl.ds(pl.multiple_of((first + 2 * pair + h) * TILE, TILE), TILE), lanes]
                     for b in range(3)
                 ]
                 for h in range(2)
@@ -169,9 +208,7 @@
 
     def contract(unit, quad):
         pair, a = lax.div(unit, 3), lax.rem(unit, 3)
-        total[pair] += lax.dot_general(
-            phi[a], quad[...], TURNED, preferred_element_type=jnp.float32
-        )
+        total[pair] += jnp.dot(quad[...], phi[a], preferred_element_type=jnp.float32)
 
     units = share // 2 * 3
     total[...] = jnp.zeros_like(total)
@@ -196,44 +233,32 @@
             start = (2 * pair + h) * width
             out_ref = out_refs[start * outs // (share * width)]
             start = start % (share * width // outs)
-            out_ref[start : start + width, :] = total[pair, :, h * width : (h + 1) * width].astype(
-                out_ref.dtype
-            )
-
-
-def plane_terms(where, blocks, edges, offsets, chunk, share, rows, decks, outs):
-    layers, height, comps, across, width = blocks[0].shape
-    members = len(blocks)
-    slab = layers * height * across
-    count = members * slab
-    span = next(n * 2 * slab for n in (1, 2, 4, members // 2) if n * 2 * slab % LANES == 0)
-    sizes = (layers, height, across, width, share, chunk, rows, decks, outs)
+            value = total[pair, h * width : (h + 1) * width, :].T
+            out_ref[start : start + width, :] = value.astype(out_ref.dtype)
+
+
+def plane_terms(turned, phi, own, chunk, share, outs):
+    width, count = turned.shape[2:]
     vmem = pl.BlockSpec(memory_space=pltpu.VMEM)
     dtypes = [jnp.float32 if outs > 1 and n == 0 else jnp.bfloat16 for n in range(outs)]
     results = [((share * width // outs, width), t) for t in dtypes]
     scratch = [
-        ((members,) + blocks[0].shape, jnp.float32),
-        ((members,) + edges[0].shape, jnp.float32),
-        ((4, comps, span, width), jnp.float32),
-        ((3, comps, width, count), jnp.bfloat16),
-        ((3, width, count), jnp.bfloat16),
-        ((3, share * TILE, count), jnp.bfloat16),
         ((2 * width, count), jnp.bfloat16),
         ((2 * width, count), jnp.bfloat16),
-        ((share // 2, width, 2 * width), jnp.float32),
+        ((share // 2, 2 * width, width), jnp.float32),
     ]
-    inputs = [(v.shape, v.dtype) for v in blocks + edges]
+    inputs = [(v.shape, v.dtype) for v in (turned, phi, own)]
     return pl.pallas_call(
-        functools.partial(terms_kernel, sizes, offsets),
+        functools.partial(terms_kernel, share, chunk),
         out_shape=[jax.ShapeDtypeStruct(*result) for result in results],
-        in_specs=[pl.BlockSpec(memory_space=pltpu.SMEM)] + [vmem] * (2 * members),
+        in_specs=[vmem] * 3,
         out_specs=[vmem] * outs,
         scratch_shapes=[pltpu.VMEM(*shape) for shape in scratch],
         compiler_params=pltpu.CompilerParams(vmem_limit_bytes=grant(results + scratch + inputs)),
         cost_estimate=pl.CostEstimate(
             flops=2 * share * width * width * count * 3, bytes_accessed=2**22, transcendentals=0
         ),
-    )(where, *blocks, *edges)
+    )(turned, phi, own)
 
 
 def place_kernel(plan, pieces, given, where_ref, *refs):
@@ -347,10 +372,8 @@
     edges = spread_small(edge_piece(cells, cell_weight))
     offsets = list(blocks)
     blocks, edges = ([d[o] for o in offsets] for d in (blocks, edges))
-    terms = [
-        plane_terms(where, blocks, edges, offsets, n, share, rows, decks, outs)
-        for n in range(CHUNKS)
-    ]
+    slopes = plane_slopes(where, blocks, edges, offsets, share, rows, decks, outs)
+    terms = [plane_terms(*slopes, n, share, outs) for n in range(CHUNKS)]
 
     def put_all(result, chosen):
         return put(where, result, width * width, rows, decks, chosen)

time: 106 us -> 101 us (0.953)
  Pallas kernels: 36 us -> 30.2 us
    pallas_call x2 -> x3, Pallas kernels: 28 us -> 22.2 us  [the longest x2 13.8 us: plane_terms(): pl.pallas_call(functools.partial(terms_kernel, share, chunk), out_shape=[...]
  transfers between devices with their start and end apart: 41 -> 41, of which waited for: 10 -> 10; matrix products, arithmetic and copies ran while one was open for 1% -> 1% of each run, Pallas kernels for 19% -> 13%
where the time goes in v7:
time: 101 us; the launch traced here: 100 us
  starting transfers between devices  54.3 us (54%)
  Pallas kernels  30.2 us (30%)
  waiting for transfers between devices  12.9 us (13%)
  other arithmetic  2.02 us (2%)
    ppermute x38, starting transfers between devices, rotate(): lax.ppermute(value, axis, [(i, (i + by) % count) for i in range(count)])  53.6 us
    pallas_call x2, Pallas kernels, plane_terms(): pl.pallas_call(functools.partial(terms_kernel, share, chunk), out_shape=[...  13.8 us
    ppermute x38, waiting for transfers between devices, rotate(): lax.ppermute(value, axis, [(i, (i + by) % count) for i in range(count)])  12.9 us
    pallas_call x1, Pallas kernels, plane_slopes(): pl.pallas_call(functools.partial(slopes_kernel, sizes, offsets), out_shap...  8.37 us
    pallas_call x4, Pallas kernels, put(): pl.pallas_call(functools.partial(place_kernel, (rows, decks, line, block,...  8.02 us
  transfers between devices with their start and end apart: 41, of which 10 were waited for; matrix products, arithmetic and copies ran while one was open for 1% of the time, Pallas kernels for 13%

profile of v7, /device:TPU:1, one launch (start us, length us, event | category | flops | bytes accessed | tf_op | source)
XLA Modules:
  0.0 100.5 jit_solution(10413965990721235505)
XLA Ops:
  0.0 1.0 %broadcast_select_fusion = bf16[2,10,3,2,128]{4,3,2,1,0:T(2,128)(2,1)S(1)} fusion(pred[]{:T(512)S(6)} %eq.3, bf16[2,10,3,8,128]{4,3,2,1,0:T(8,128)(2,1)} %bitcast.7), kind=kLoop, calls=%fused_computation.6 | loop fusion | flops 15360 | bytes 92161 | tf_op jit(solution)/shard_map/jit(_where)/select_n | solution.py:322
  2.6 6.2 %collective-permute-start.9 = (bf16[2,32,384]{2,1,0:T(8,128)(2,1)S(1)}, bf16[2,32,384]{2,1,0:T(8,128)(2,1)S(1)}, u32[]{:S(2)}, u32[]{:S(2)}) collective-permute-start(bf16[2,32,384]{2,1,0:T(8,128)(2,1)S(1)} %fusion.1.refs_8_), channel_id=1, source_target_pairs={{0,1},{1,0},{2,3},{3,2},{4,5},{5,4},{6,7},{7,6},{8,9},{9,8},{10,11... | collective-permute-start | bytes 147464 | tf_op jit(solution)/shard_map/ppermute | solution.py:23
  8.7 1.2 %collective-permute-start.11 = (bf16[2,32,384]{2,1,0:T(8,128)(2,1)S(1)}, bf16[2,32,384]{2,1,0:T(8,128)(2,1)S(1)}, u32[]{:S(2)}, u32[]{:S(2)}) collective-permute-start(bf16[2,32,384]{2,1,0:T(8,128)(2,1)S(1)} %fusion.1.refs_8_), channel_id=1, source_target_pairs={{0,16},{16,0},{1,17},{17,1},{2,18},{18,2},{3,19},{19,3},{4,20},{20... | collective-permute-start | bytes 147464 | tf_op jit(solution)/shard_map/ppermute | solution.py:23
  10.0 1.4 %collective-permute-start.1 = (bf16[2,10,3,8,128]{4,3,2,1,0:T(8,128)(2,1)}, bf16[2,10,3,8,128]{4,3,2,1,0:T(8,128)(2,1)S(1)}, u32[]{:S(2)}, u32[]{:S(2)}) collective-permute-start(bf16[2,10,3,8,128]{4,3,2,1,0:T(8,128)(2,1)} %bitcast.8), channel_id=1, source_target_pairs={{0,1},{1,0},{2,3},{3,2},{4,5},{5,4},{6,7},{7,6},{8,9},{9,8},{10,11... | collective-permute-start | bytes 368648 | tf_op jit(solution)/shard_map/ppermute | solution.py:23
  11.4 1.2 %collective-permute-start.3 = (bf16[2,10,3,8,128]{4,3,2,1,0:T(8,128)(2,1)}, bf16[2,10,3,8,128]{4,3,2,1,0:T(8,128)(2,1)S(1)}, u32[]{:S(2)}, u32[]{:S(2)}) collective-permute-start(bf16[2,10,3,8,128]{4,3,2,1,0:T(8,128)(2,1)} %bitcast.9), channel_id=1, source_target_pairs={{0,16},{16,0},{1,17},{17,1},{2,18},{18,2},{3,19},{19,3},{4,20},{20... | collective-permute-start | bytes 368648 | tf_op jit(solution)/shard_map/ppermute | solution.py:23
  12.7 3.3 %collective-permute-start = (bf16[2,10,3,8,128]{4,3,2,1,0:T(8,128)(2,1)}, bf16[2,10,3,8,128]{4,3,2,1,0:T(8,128)(2,1)S(1)}, u32[]{:S(2)}, u32[]{:S(2)}) collective-permute-start(bf16[2,10,3,8,128]{4,3,2,1,0:T(8,128)(2,1)} %bitcast.11), channel_id=1, source_target_pairs={{0,8},{8,0},{1,9},{9,1},{2,10},{10,2},{3,11},{11,3},{4,12},{12,4},... | collective-permute-start | bytes 368648 | tf_op jit(solution)/shard_map/ppermute | solution.py:23
  15.9 1.9 %collective-permute-start.8 = (bf16[2,32,384]{2,1,0:T(8,128)(2,1)S(1)}, bf16[2,32,384]{2,1,0:T(8,128)(2,1)S(1)}, u32[]{:S(2)}, u32[]{:S(2)}) collective-permute-start(bf16[2,32,384]{2,1,0:T(8,128)(2,1)S(1)} %fusion.1.refs_8_), channel_id=1, source_target_pairs={{0,8},{8,0},{1,9},{9,1},{2,10},{10,2},{3,11},{11,3},{4,12},{12,4},... | collective-permute-start | bytes 147464 | tf_op jit(solution)/shard_map/ppermute | solution.py:23
  20.1 1.7 %collective-permute-start.6 = (bf16[2,10,3,8,128]{4,3,2,1,0:T(8,128)(2,1)S(1)}, bf16[2,10,3,8,128]{4,3,2,1,0:T(8,128)(2,1)S(1)}, u32[]{:S(2)}, u32[]{:S(2)}) collective-permute-start(bf16[2,10,3,8,128]{4,3,2,1,0:T(8,128)(2,1)S(1)} %collective-permute-done.5.refs_6_), channel_id=1, source_target_pairs={{0,8},{8,0},{1,9},{9,1},{2,10},{10,2},{3,11},{11,3},{4,12},{12,4},... | collective-permute-start | bytes 368648 | tf_op jit(solution)/shard_map/ppermute | solution.py:23
  24.2 8.4 %shard_map.28 = (bf16[3,3,128,1280]{3,2,1,0:T(8,128)(2,1)S(1)}, bf16[3,1280,128]{2,1,0:T(8,128)(2,1)S(1)}, bf16[3,256,1280]{2,1,0:T(8,128)(2,1)S(1)}) custom-call(s32[4]{0:T(128)S(1)} %pad_add_fusion.where_ref, bf16[2,10,3,8,128]{4,3,2,1,0:T(8,128)(2,1)S(1)} %bitcast.12, bf16[2,10,3,8,128]{4,3,2,1,0:T(8,128)(2,1)S(1)} %collective-permute-done.refs_1_, ...), custom_call_target="tpu_custom_call" | custom-call | flops 503316480 | bytes 4194304 | tf_op jit(solution)/shard_map/pallas_call | solution.py:170
  32.6 6.9 %shard_map.30 = (f32[256,128]{1,0:T(8,128)S(1)}, bf16[256,128]{1,0:T(8,128)(2,1)S(1)}, bf16[256,128]{1,0:T(8,128)(2,1)S(1)}, bf16[256,128]{1,0:T(8,128)(2,1)S(1)}) custom-call(bf16[3,3,128,1280]{3,2,1,0:T(8,128)(2,1)S(1)} %get-tuple-element.20.turned, bf16[3,1280,128]{2,1,0:T(8,128)(2,1)S(1)} %get-tuple-element.21.phi, ...), custom_call_target="tpu_custom_call" | custom-call | flops 1006632960 | bytes 4194304 | tf_op jit(solution)/shard_map/pallas_call | solution.py:251
  39.5 1.3 %collective-permute-start.22 = (bf16[256,128]{1,0:T(8,128)(2,1)S(1)}, bf16[256,128]{1,0:T(8,128)(2,1)S(1)}, u32[]{:S(2)}, u32[]{:S(2)}) collective-permute-start(bf16[256,128]{1,0:T(8,128)(2,1)S(1)} %get-tuple-element.28), channel_id=1, source_target_pairs={{0,2},{2,4},{4,6},{6,0},{1,3},{3,5},{5,7},{7,1},{8,10},{10,12},{12... | collective-permute-start | bytes 196616 | tf_op jit(solution)/shard_map/ppermute | solution.py:23
  40.8 1.1 %collective-permute-start.23 = (bf16[256,128]{1,0:T(8,128)(2,1)S(1)}, bf16[256,128]{1,0:T(8,128)(2,1)S(1)}, u32[]{:S(2)}, u32[]{:S(2)}) collective-permute-start(bf16[256,128]{1,0:T(8,128)(2,1)S(1)} %get-tuple-element.29), channel_id=1, source_target_pairs={{0,4},{2,6},{4,0},{6,2},{1,5},{3,7},{5,1},{7,3},{8,12},{10,14},{12... | collective-permute-start | bytes 196616 | tf_op jit(solution)/shard_map/ppermute | solution.py:23
  41.9 2.3 %collective-permute-start.24 = (bf16[256,128]{1,0:T(8,128)(2,1)S(1)}, bf16[256,128]{1,0:T(8,128)(2,1)S(1)}, u32[]{:S(2)}, u32[]{:S(2)}) collective-permute-start(bf16[256,128]{1,0:T(8,128)(2,1)S(1)} %get-tuple-element.30), channel_id=1, source_target_pairs={{0,6},{2,0},{4,2},{6,4},{1,7},{3,1},{5,3},{7,5},{8,14},{10,8},{12,... | collective-permute-start | bytes 196616 | tf_op jit(solution)/shard_map/ppermute | solution.py:23
  44.5 3.7 %collective-permute-done.23 = bf16[256,128]{1,0:T(8,128)(2,1)S(1)} collective-permute-done((bf16[256,128]{1,0:T(8,128)(2,1)S(1)}, bf16[256,128]{1,0:T(8,128)(2,1)S(1)}, u32[]{:S(2)}, u32[]{:S(2)}) %collective-permute-start.23) | collective-permute-done | bytes 65568 | tf_op jit(solution)/shard_map/ppermute | solution.py:23
  48.2 1.7 %collective-permute-start.25 = (bf16[256,128]{1,0:T(8,128)(2,1)S(1)}, bf16[256,128]{1,0:T(8,128)(2,1)S(1)}, u32[]{:S(2)}, u32[]{:S(2)}) collective-permute-start(bf16[256,128]{1,0:T(8,128)(2,1)S(1)} %add_convert_fusion), channel_id=1, source_target_pairs={{0,2},{2,4},{4,6},{6,0},{1,3},{3,5},{5,7},{7,1},{8,10},{10,12},{12... | collective-permute-start | bytes 196616 | tf_op jit(solution)/shard_map/ppermute | solution.py:23
  50.3 1.8 %collective-permute-start.27 = (bf16[256,128]{1,0:T(8,128)(2,1)S(1)}, bf16[256,128]{1,0:T(8,128)(2,1)S(1)}, u32[]{:S(2)}, u32[]{:S(2)}) collective-permute-start(bf16[256,128]{1,0:T(8,128)(2,1)S(1)} %add_convert_fusion), channel_id=1, source_target_pairs={{0,6},{2,0},{4,2},{6,4},{1,7},{3,1},{5,3},{7,5},{8,14},{10,8},{12,... | collective-permute-start | bytes 196616 | tf_op jit(solution)/shard_map/ppermute | solution.py:23
  52.1 6.9 %shard_map.29 = (f32[256,128]{1,0:T(8,128)S(1)}, bf16[256,128]{1,0:T(8,128)(2,1)S(1)}, bf16[256,128]{1,0:T(8,128)(2,1)S(1)}, bf16[256,128]{1,0:T(8,128)(2,1)S(1)}) custom-call(bf16[3,3,128,1280]{3,2,1,0:T(8,128)(2,1)S(1)} %get-tuple-element.20.turned, bf16[3,1280,128]{2,1,0:T(8,128)(2,1)S(1)} %get-tuple-element.21.phi, ...), custom_call_target="tpu_custom_call" | custom-call | flops 1006632960 | bytes 4194304 | tf_op jit(solution)/shard_map/pallas_call | solution.py:251
  59.0 1.7 %collective-permute-start.16 = (bf16[256,128]{1,0:T(8,128)(2,1)S(1)}, bf16[256,128]{1,0:T(8,128)(2,1)S(1)}, u32[]{:S(2)}, u32[]{:S(2)}) collective-permute-start(bf16[256,128]{1,0:T(8,128)(2,1)S(1)} %get-tuple-element.25), channel_id=1, source_target_pairs={{0,4},{2,6},{4,0},{6,2},{1,5},{3,7},{5,1},{7,3},{8,12},{10,14},{12... | collective-permute-start | bytes 196616 | tf_op jit(solution)/shard_map/ppermute | solution.py:23
  60.7 1.6 %collective-permute-start.17 = (bf16[256,128]{1,0:T(8,128)(2,1)S(1)}, bf16[256,128]{1,0:T(8,128)(2,1)S(1)}, u32[]{:S(2)}, u32[]{:S(2)}) collective-permute-start(bf16[256,128]{1,0:T(8,128)(2,1)S(1)} %get-tuple-element.26), channel_id=1, source_target_pairs={{0,6},{2,0},{4,2},{6,4},{1,7},{3,1},{5,3},{7,5},{8,14},{10,8},{12,... | collective-permute-start | bytes 196616 | tf_op jit(solution)/shard_map/ppermute | solution.py:23
  64.7 3.2 %collective-permute-start.18 = (bf16[256,128]{1,0:T(8,128)(2,1)S(1)}, bf16[256,128]{1,0:T(8,128)(2,1)S(1)}, u32[]{:S(2)}, u32[]{:S(2)}) collective-permute-start(bf16[256,128]{1,0:T(8,128)(2,1)S(1)} %add_convert_fusion.1), channel_id=1, source_target_pairs={{0,2},{2,4},{4,6},{6,0},{1,3},{3,5},{5,7},{7,1},{8,10},{10,12},{12... | collective-permute-start | bytes 196616 | tf_op jit(solution)/shard_map/ppermute | solution.py:23
  67.9 1.3 %collective-permute-start.19 = (bf16[256,128]{1,0:T(8,128)(2,1)S(1)}, bf16[256,128]{1,0:T(8,128)(2,1)S(1)}, u32[]{:S(2)}, u32[]{:S(2)}) collective-permute-start(bf16[256,128]{1,0:T(8,128)(2,1)S(1)} %add_convert_fusion.1), channel_id=1, source_target_pairs={{0,4},{2,6},{4,0},{6,2},{1,5},{3,7},{5,1},{7,3},{8,12},{10,14},{12... | collective-permute-start | bytes 196616 | tf_op jit(solution)/shard_map/ppermute | solution.py:23
  70.5 4.0 %collective-permute-start.30 = (bf16[1024,128]{1,0:T(8,128)(2,1)S(1)}, bf16[1024,128]{1,0:T(8,128)(2,1)S(1)}, u32[]{:S(2)}, u32[]{:S(2)}) collective-permute-start(bf16[1024,128]{1,0:T(8,128)(2,1)S(1)} %pad_maximum_fusion.1.refs_0_), channel_id=1, source_target_pairs={{0,8},{8,0},{1,9},{9,1},{2,10},{10,2},{3,11},{11,3},{4,12},{12,4},... | collective-permute-start | bytes 786440 | tf_op jit(solution)/shard_map/ppermute | solution.py:23
  75.4 1.7 %collective-permute-start.32 = (bf16[1024,128]{1,0:T(8,128)(2,1)S(1)}, bf16[1024,128]{1,0:T(8,128)(2,1)S(1)}, u32[]{:S(2)}, u32[]{:S(2)}) collective-permute-start(bf16[1024,128]{1,0:T(8,128)(2,1)S(1)} %collective-permute-done.29.refs_2_), channel_id=1, source_target_pairs={{0,8},{8,0},{1,9},{9,1},{2,10},{10,2},{3,11},{11,3},{4,12},{12,4},... | collective-permute-start | bytes 786440 | tf_op jit(solution)/shard_map/ppermute | solution.py:23
  78.2 2.7 %collective-permute-done.34.refs_0_ = bf16[1024,128]{1,0:T(8,128)(2,1)S(1)} collective-permute-done((bf16[1024,128]{1,0:T(8,128)(2,1)S(1)}, bf16[1024,128]{1,0:T(8,128)(2,1)S(1)}, u32[]{:S(2)}, u32[]{:S(2)}) %collective-permute-start.34) | collective-permute-done | bytes 262176 | tf_op jit(solution)/shard_map/ppermute | solution.py:23
  80.9 4.3 %collective-permute-start.35 = (bf16[1024,128]{1,0:T(8,128)(2,1)S(1)}, bf16[1024,128]{1,0:T(8,128)(2,1)S(1)}, u32[]{:S(2)}, u32[]{:S(2)}) collective-permute-start(bf16[1024,128]{1,0:T(8,128)(2,1)S(1)} %collective-permute-done.34.refs_0_), channel_id=1, source_target_pairs={{0,8},{8,0},{1,9},{9,1},{2,10},{10,2},{3,11},{11,3},{4,12},{12,4},... | collective-permute-start | bytes 786440 | tf_op jit(solution)/shard_map/ppermute | solution.py:23
  85.2 2.4 %shard_map.31.refs_2_ = f32[16384,128]{1,0:T(8,128)} custom-call(s32[4]{0:T(128)S(1)} %pad_add_fusion.where_ref, bf16[1024,128]{1,0:T(8,128)(2,1)S(1)} %pad_maximum_fusion.1.refs_0_, bf16[1024,128]{1,0:T(8,128)(2,1)S(1)} %collective-permute-done.28.refs_1_, bf16[1024,128]{1,0:T(8,128)(2,1)S(1)} %collective-permute-done.29.refs_2_, ...), custom_call_target="tpu_custom_call" | custom-call | bytes 4718592 | tf_op jit(solution)/shard_map/pallas_call | solution.py:301
  88.1 1.4 %collective-permute-start.38 = (bf16[1024,128]{1,0:T(8,128)(2,1)S(1)}, bf16[1024,128]{1,0:T(8,128)(2,1)S(1)}, u32[]{:S(2)}, u32[]{:S(2)}) collective-permute-start(bf16[1024,128]{1,0:T(8,128)(2,1)S(1)} %pad_maximum_fusion.refs_0_), channel_id=1, source_target_pairs={{0,8},{8,0},{1,9},{9,1},{2,10},{10,2},{3,11},{11,3},{4,12},{12,4},... | collective-permute-start | bytes 786440 | tf_op jit(solution)/shard_map/ppermute | solution.py:23
  90.0 1.6 %shard_map.32.refs_7_ = f32[16384,128]{1,0:T(8,128)} custom-call(s32[4]{0:T(128)S(1)} %pad_add_fusion.where_ref, bf16[1024,128]{1,0:T(8,128)(2,1)S(1)} %collective-permute-done.34.refs_0_, bf16[1024,128]{1,0:T(8,128)(2,1)S(1)} %collective-permute-done.35.refs_1_, f32[16384,128]{1,0:T(8,128)} %shard_map.31.refs_2_), custom_call_target="tpu_custom_call", output_to_operand_aliasing={{}: (3, {})} | custom-call | bytes 1572864 | tf_op jit(solution)/shard_map/pallas_call | solution.py:301
  91.6 2.7 %collective-permute-done.33.refs_6_ = bf16[1024,128]{1,0:T(8,128)(2,1)S(1)} collective-permute-done((bf16[1024,128]{1,0:T(8,128)(2,1)S(1)}, bf16[1024,128]{1,0:T(8,128)(2,1)S(1)}, u32[]{:S(2)}, u32[]{:S(2)}) %collective-permute-start.33) | collective-permute-done | bytes 262176 | tf_op jit(solution)/shard_map/ppermute | solution.py:23
  94.4 2.1 %collective-permute-start.36 = (bf16[1024,128]{1,0:T(8,128)(2,1)S(1)}, bf16[1024,128]{1,0:T(8,128)(2,1)S(1)}, u32[]{:S(2)}, u32[]{:S(2)}) collective-permute-start(bf16[1024,128]{1,0:T(8,128)(2,1)S(1)} %collective-permute-done.33.refs_6_), channel_id=1, source_target_pairs={{0,8},{8,0},{1,9},{9,1},{2,10},{10,2},{3,11},{11,3},{4,12},{12,4},... | collective-permute-start | bytes 786440 | tf_op jit(solution)/shard_map/ppermute | solution.py:23
  96.5 2.6 %shard_map.33.refs_1_ = f32[16384,128]{1,0:T(8,128)} custom-call(s32[4]{0:T(128)S(1)} %pad_add_fusion.where_ref, bf16[1024,128]{1,0:T(8,128)(2,1)S(1)} %pad_maximum_fusion.refs_0_, bf16[1024,128]{1,0:T(8,128)(2,1)S(1)} %collective-permute-done.37.refs_1_, bf16[1024,128]{1,0:T(8,128)(2,1)S(1)} %collective-permute-done.21.refs_2_, ...), custom_call_target="tpu_custom_call", output_to_operand_aliasing={{}: (8, {})} | custom-call | bytes 5505024 | tf_op jit(solution)/shard_map/pallas_call | solution.py:301
  99.1 1.4 %shard_map.34 = f32[16384,128]{1,0:T(8,128)} custom-call(s32[4]{0:T(128)S(1)} %pad_add_fusion.where_ref, bf16[1024,128]{1,0:T(8,128)(2,1)S(1)} %collective-permute-done.36.refs_0_, f32[16384,128]{1,0:T(8,128)} %shard_map.33.refs_1_), custom_call_target="tpu_custom_call", output_to_operand_aliasing={{}: (2, {})} | custom-call | bytes 786432 | tf_op jit(solution)/shard_map/pallas_call | solution.py:301
  (70 shorter events, 13.5 us)
Async XLA Ops:
  2.6 10.1 %collective-permute-start.9 = (bf16[2,32,384]{2,1,0:T(8,128)(2,1)S(1)}, bf16[2,32,384]{2,1,0:T(8,128)(2,1)S(1)}, u32[]{:S(2)}, u32[]{:S(2)}) collective-permute-start(bf16[2,32,384]{2,1,0:T(8,128)(2,1)S(1)} %fusion.1.refs_8_), channel_id=1, source_target_pairs={{0,1},{1,0},{2,3},{3,2},{4,5},{5,4},{6,7},{7,6},{8,9},{9,8},{10,11... | collective-permute-start | bytes 147464 | tf_op jit(solution)/shard_map/ppermute | solution.py:23
  10.0 6.0 %collective-permute-start.13 = (bf16[2,32,384]{2,1,0:T(8,128)(2,1)S(1)}, bf16[2,32,384]{2,1,0:T(8,128)(2,1)S(1)}, u32[]{:S(2)}, u32[]{:S(2)}) collective-permute-start(bf16[2,32,384]{2,1,0:T(8,128)(2,1)S(1)} %fusion.1.refs_8_), channel_id=1, source_target_pairs={{0,17},{1,16},{16,1},{17,0},{2,19},{3,18},{18,3},{19,2},{4,21},{5,... | collective-permute-start | bytes 147464 | tf_op jit(solution)/shard_map/ppermute | solution.py:345
  10.0 9.1 %collective-permute-start.1 = (bf16[2,10,3,8,128]{4,3,2,1,0:T(8,128)(2,1)}, bf16[2,10,3,8,128]{4,3,2,1,0:T(8,128)(2,1)S(1)}, u32[]{:S(2)}, u32[]{:S(2)}) collective-permute-start(bf16[2,10,3,8,128]{4,3,2,1,0:T(8,128)(2,1)} %bitcast.8), channel_id=1, source_target_pairs={{0,1},{1,0},{2,3},{3,2},{4,5},{5,4},{6,7},{7,6},{8,9},{9,8},{10,11... | collective-permute-start | bytes 368648 | tf_op jit(solution)/shard_map/ppermute | solution.py:23
  11.4 7.9 %collective-permute-start.3 = (bf16[2,10,3,8,128]{4,3,2,1,0:T(8,128)(2,1)}, bf16[2,10,3,8,128]{4,3,2,1,0:T(8,128)(2,1)S(1)}, u32[]{:S(2)}, u32[]{:S(2)}) collective-permute-start(bf16[2,10,3,8,128]{4,3,2,1,0:T(8,128)(2,1)} %bitcast.9), channel_id=1, source_target_pairs={{0,16},{16,0},{1,17},{17,1},{2,18},{18,2},{3,19},{19,3},{4,20},{20... | collective-permute-start | bytes 368648 | tf_op jit(solution)/shard_map/ppermute | solution.py:23
  12.6 7.5 %collective-permute-start.5 = (bf16[2,10,3,8,128]{4,3,2,1,0:T(8,128)(2,1)}, bf16[2,10,3,8,128]{4,3,2,1,0:T(8,128)(2,1)S(1)}, u32[]{:S(2)}, u32[]{:S(2)}) collective-permute-start(bf16[2,10,3,8,128]{4,3,2,1,0:T(8,128)(2,1)} %bitcast.10), channel_id=1, source_target_pairs={{0,17},{1,16},{16,1},{17,0},{2,19},{3,18},{18,3},{19,2},{4,21},{5,... | collective-permute-start | bytes 368648 | tf_op jit(solution)/shard_map/ppermute | solution.py:345
  12.7 9.2 %collective-permute-start = (bf16[2,10,3,8,128]{4,3,2,1,0:T(8,128)(2,1)}, bf16[2,10,3,8,128]{4,3,2,1,0:T(8,128)(2,1)S(1)}, u32[]{:S(2)}, u32[]{:S(2)}) collective-permute-start(bf16[2,10,3,8,128]{4,3,2,1,0:T(8,128)(2,1)} %bitcast.11), channel_id=1, source_target_pairs={{0,8},{8,0},{1,9},{9,1},{2,10},{10,2},{3,11},{11,3},{4,12},{12,4},... | collective-permute-start | bytes 368648 | tf_op jit(solution)/shard_map/ppermute | solution.py:23
  19.1 4.2 %collective-permute-start.2 = (bf16[2,10,3,8,128]{4,3,2,1,0:T(8,128)(2,1)S(1)}, bf16[2,10,3,8,128]{4,3,2,1,0:T(8,128)(2,1)S(1)}, u32[]{:S(2)}, u32[]{:S(2)}) collective-permute-start(bf16[2,10,3,8,128]{4,3,2,1,0:T(8,128)(2,1)S(1)} %collective-permute-done.1.refs_2_), channel_id=1, source_target_pairs={{0,8},{8,0},{1,9},{9,1},{2,10},{10,2},{3,11},{11,3},{4,12},{12,4},... | collective-permute-start | bytes 368648 | tf_op jit(solution)/shard_map/ppermute | solution.py:23
  39.5 5.0 %collective-permute-start.22 = (bf16[256,128]{1,0:T(8,128)(2,1)S(1)}, bf16[256,128]{1,0:T(8,128)(2,1)S(1)}, u32[]{:S(2)}, u32[]{:S(2)}) collective-permute-start(bf16[256,128]{1,0:T(8,128)(2,1)S(1)} %get-tuple-element.28), channel_id=1, source_target_pairs={{0,2},{2,4},{4,6},{6,0},{1,3},{3,5},{5,7},{7,1},{8,10},{10,12},{12... | collective-permute-start | bytes 196616 | tf_op jit(solution)/shard_map/ppermute | solution.py:23
  40.8 7.3 %collective-permute-start.23 = (bf16[256,128]{1,0:T(8,128)(2,1)S(1)}, bf16[256,128]{1,0:T(8,128)(2,1)S(1)}, u32[]{:S(2)}, u32[]{:S(2)}) collective-permute-start(bf16[256,128]{1,0:T(8,128)(2,1)S(1)} %get-tuple-element.29), channel_id=1, source_target_pairs={{0,4},{2,6},{4,0},{6,2},{1,5},{3,7},{5,1},{7,3},{8,12},{10,14},{12... | collective-permute-start | bytes 196616 | tf_op jit(solution)/shard_map/ppermute | solution.py:23
  41.9 6.2 %collective-permute-start.24 = (bf16[256,128]{1,0:T(8,128)(2,1)S(1)}, bf16[256,128]{1,0:T(8,128)(2,1)S(1)}, u32[]{:S(2)}, u32[]{:S(2)}) collective-permute-start(bf16[256,128]{1,0:T(8,128)(2,1)S(1)} %get-tuple-element.30), channel_id=1, source_target_pairs={{0,6},{2,0},{4,2},{6,4},{1,7},{3,1},{5,3},{7,5},{8,14},{10,8},{12,... | collective-permute-start | bytes 196616 | tf_op jit(solution)/shard_map/ppermute | solution.py:23
  48.2 12.5 %collective-permute-start.25 = (bf16[256,128]{1,0:T(8,128)(2,1)S(1)}, bf16[256,128]{1,0:T(8,128)(2,1)S(1)}, u32[]{:S(2)}, u32[]{:S(2)}) collective-permute-start(bf16[256,128]{1,0:T(8,128)(2,1)S(1)} %add_convert_fusion), channel_id=1, source_target_pairs={{0,2},{2,4},{4,6},{6,0},{1,3},{3,5},{5,7},{7,1},{8,10},{10,12},{12... | collective-permute-start | bytes 196616 | tf_op jit(solution)/shard_map/ppermute | solution.py:23
  49.9 12.4 %collective-permute-start.26 = (bf16[256,128]{1,0:T(8,128)(2,1)S(1)}, bf16[256,128]{1,0:T(8,128)(2,1)S(1)}, u32[]{:S(2)}, u32[]{:S(2)}) collective-permute-start(bf16[256,128]{1,0:T(8,128)(2,1)S(1)} %add_convert_fusion), channel_id=1, source_target_pairs={{0,4},{2,6},{4,0},{6,2},{1,5},{3,7},{5,1},{7,3},{8,12},{10,14},{12... | collective-permute-start | bytes 196616 | tf_op jit(solution)/shard_map/ppermute | solution.py:23
  50.3 12.0 %collective-permute-start.27 = (bf16[256,128]{1,0:T(8,128)(2,1)S(1)}, bf16[256,128]{1,0:T(8,128)(2,1)S(1)}, u32[]{:S(2)}, u32[]{:S(2)}) collective-permute-start(bf16[256,128]{1,0:T(8,128)(2,1)S(1)} %add_convert_fusion), channel_id=1, source_target_pairs={{0,6},{2,0},{4,2},{6,4},{1,7},{3,1},{5,3},{7,5},{8,14},{10,8},{12,... | collective-permute-start | bytes 196616 | tf_op jit(solution)/shard_map/ppermute | solution.py:23
  59.0 5.0 %collective-permute-start.15 = (bf16[256,128]{1,0:T(8,128)(2,1)S(1)}, bf16[256,128]{1,0:T(8,128)(2,1)S(1)}, u32[]{:S(2)}, u32[]{:S(2)}) collective-permute-start(bf16[256,128]{1,0:T(8,128)(2,1)S(1)} %get-tuple-element.24), channel_id=1, source_target_pairs={{0,2},{2,4},{4,6},{6,0},{1,3},{3,5},{5,7},{7,1},{8,10},{10,12},{12... | collective-permute-start | bytes 196616 | tf_op jit(solution)/shard_map/ppermute | solution.py:23
  59.0 4.9 %collective-permute-start.16 = (bf16[256,128]{1,0:T(8,128)(2,1)S(1)}, bf16[256,128]{1,0:T(8,128)(2,1)S(1)}, u32[]{:S(2)}, u32[]{:S(2)}) collective-permute-start(bf16[256,128]{1,0:T(8,128)(2,1)S(1)} %get-tuple-element.25), channel_id=1, source_target_pairs={{0,4},{2,6},{4,0},{6,2},{1,5},{3,7},{5,1},{7,3},{8,12},{10,14},{12... | collective-permute-start | bytes 196616 | tf_op jit(solution)/shard_map/ppermute | solution.py:23
  62.3 12.2 %collective-permute-start.28 = (bf16[1024,128]{1,0:T(8,128)(2,1)S(1)}, bf16[1024,128]{1,0:T(8,128)(2,1)S(1)}, u32[]{:S(2)}, u32[]{:S(2)}) collective-permute-start(bf16[1024,128]{1,0:T(8,128)(2,1)S(1)} %pad_maximum_fusion.1.refs_0_), channel_id=1, source_target_pairs={{0,1},{1,0},{2,3},{3,2},{4,5},{5,4},{6,7},{7,6},{8,9},{9,8},{10,11... | collective-permute-start | bytes 786440 | tf_op jit(solution)/shard_map/ppermute | solution.py:23
  62.7 12.7 %collective-permute-start.29 = (bf16[1024,128]{1,0:T(8,128)(2,1)S(1)}, bf16[1024,128]{1,0:T(8,128)(2,1)S(1)}, u32[]{:S(2)}, u32[]{:S(2)}) collective-permute-start(bf16[1024,128]{1,0:T(8,128)(2,1)S(1)} %pad_maximum_fusion.1.refs_0_), channel_id=1, source_target_pairs={{0,16},{16,0},{1,17},{17,1},{2,18},{18,2},{3,19},{19,3},{4,20},{20... | collective-permute-start | bytes 786440 | tf_op jit(solution)/shard_map/ppermute | solution.py:23
  64.7 5.8 %collective-permute-start.18 = (bf16[256,128]{1,0:T(8,128)(2,1)S(1)}, bf16[256,128]{1,0:T(8,128)(2,1)S(1)}, u32[]{:S(2)}, u32[]{:S(2)}) collective-permute-start(bf16[256,128]{1,0:T(8,128)(2,1)S(1)} %add_convert_fusion.1), channel_id=1, source_target_pairs={{0,2},{2,4},{4,6},{6,0},{1,3},{3,5},{5,7},{7,1},{8,10},{10,12},{12... | collective-permute-start | bytes 196616 | tf_op jit(solution)/shard_map/ppermute | solution.py:23
  67.9 6.6 %collective-permute-start.19 = (bf16[256,128]{1,0:T(8,128)(2,1)S(1)}, bf16[256,128]{1,0:T(8,128)(2,1)S(1)}, u32[]{:S(2)}, u32[]{:S(2)}) collective-permute-start(bf16[256,128]{1,0:T(8,128)(2,1)S(1)} %add_convert_fusion.1), channel_id=1, source_target_pairs={{0,4},{2,6},{4,0},{6,2},{1,5},{3,7},{5,1},{7,3},{8,12},{10,14},{12... | collective-permute-start | bytes 196616 | tf_op jit(solution)/shard_map/ppermute | solution.py:23
  69.1 8.0 %collective-permute-start.20 = (bf16[256,128]{1,0:T(8,128)(2,1)S(1)}, bf16[256,128]{1,0:T(8,128)(2,1)S(1)}, u32[]{:S(2)}, u32[]{:S(2)}) collective-permute-start(bf16[256,128]{1,0:T(8,128)(2,1)S(1)} %add_convert_fusion.1), channel_id=1, source_target_pairs={{0,6},{2,0},{4,2},{6,4},{1,7},{3,1},{5,3},{7,5},{8,14},{10,8},{12,... | collective-permute-start | bytes 196616 | tf_op jit(solution)/shard_map/ppermute | solution.py:23
  70.5 7.3 %collective-permute-start.30 = (bf16[1024,128]{1,0:T(8,128)(2,1)S(1)}, bf16[1024,128]{1,0:T(8,128)(2,1)S(1)}, u32[]{:S(2)}, u32[]{:S(2)}) collective-permute-start(bf16[1024,128]{1,0:T(8,128)(2,1)S(1)} %pad_maximum_fusion.1.refs_0_), channel_id=1, source_target_pairs={{0,8},{8,0},{1,9},{9,1},{2,10},{10,2},{3,11},{11,3},{4,12},{12,4},... | collective-permute-start | bytes 786440 | tf_op jit(solution)/shard_map/ppermute | solution.py:23
  74.5 10.7 %collective-permute-start.31 = (bf16[1024,128]{1,0:T(8,128)(2,1)S(1)}, bf16[1024,128]{1,0:T(8,128)(2,1)S(1)}, u32[]{:S(2)}, u32[]{:S(2)}) collective-permute-start(bf16[1024,128]{1,0:T(8,128)(2,1)S(1)} %collective-permute-done.28.refs_1_), channel_id=1, source_target_pairs={{0,8},{8,0},{1,9},{9,1},{2,10},{10,2},{3,11},{11,3},{4,12},{12,4},... | collective-permute-start | bytes 786440 | tf_op jit(solution)/shard_map/ppermute | solution.py:23
  74.5 6.4 %collective-permute-start.34 = (bf16[1024,128]{1,0:T(8,128)(2,1)S(1)}, bf16[1024,128]{1,0:T(8,128)(2,1)S(1)}, u32[]{:S(2)}, u32[]{:S(2)}) collective-permute-start(bf16[1024,128]{1,0:T(8,128)(2,1)S(1)} %collective-permute-done.28.refs_1_), channel_id=1, source_target_pairs={{0,16},{16,0},{1,17},{17,1},{2,18},{18,2},{3,19},{19,3},{4,20},{20... | collective-permute-start | bytes 786440 | tf_op jit(solution)/shard_map/ppermute | solution.py:23
  75.4 9.8 %collective-permute-start.32 = (bf16[1024,128]{1,0:T(8,128)(2,1)S(1)}, bf16[1024,128]{1,0:T(8,128)(2,1)S(1)}, u32[]{:S(2)}, u32[]{:S(2)}) collective-permute-start(bf16[1024,128]{1,0:T(8,128)(2,1)S(1)} %collective-permute-done.29.refs_2_), channel_id=1, source_target_pairs={{0,8},{8,0},{1,9},{9,1},{2,10},{10,2},{3,11},{11,3},{4,12},{12,4},... | collective-permute-start | bytes 786440 | tf_op jit(solution)/shard_map/ppermute | solution.py:23
  77.2 10.5 %collective-permute-start.21 = (bf16[1024,128]{1,0:T(8,128)(2,1)S(1)}, bf16[1024,128]{1,0:T(8,128)(2,1)S(1)}, u32[]{:S(2)}, u32[]{:S(2)}) collective-permute-start(bf16[1024,128]{1,0:T(8,128)(2,1)S(1)} %pad_maximum_fusion.refs_0_), channel_id=1, source_target_pairs={{0,16},{16,0},{1,17},{17,1},{2,18},{18,2},{3,19},{19,3},{4,20},{20... | collective-permute-start | bytes 786440 | tf_op jit(solution)/shard_map/ppermute | solution.py:23
  77.8 11.7 %collective-permute-start.37 = (bf16[1024,128]{1,0:T(8,128)(2,1)S(1)}, bf16[1024,128]{1,0:T(8,128)(2,1)S(1)}, u32[]{:S(2)}, u32[]{:S(2)}) collective-permute-start(bf16[1024,128]{1,0:T(8,128)(2,1)S(1)} %pad_maximum_fusion.refs_0_), channel_id=1, source_target_pairs={{0,1},{1,0},{2,3},{3,2},{4,5},{5,4},{6,7},{7,6},{8,9},{9,8},{10,11... | collective-permute-start | bytes 786440 | tf_op jit(solution)/shard_map/ppermute | solution.py:23
  80.9 9.1 %collective-permute-start.35 = (bf16[1024,128]{1,0:T(8,128)(2,1)S(1)}, bf16[1024,128]{1,0:T(8,128)(2,1)S(1)}, u32[]{:S(2)}, u32[]{:S(2)}) collective-permute-start(bf16[1024,128]{1,0:T(8,128)(2,1)S(1)} %collective-permute-done.34.refs_0_), channel_id=1, source_target_pairs={{0,8},{8,0},{1,9},{9,1},{2,10},{10,2},{3,11},{11,3},{4,12},{12,4},... | collective-permute-start | bytes 786440 | tf_op jit(solution)/shard_map/ppermute | solution.py:23
  87.7 6.7 %collective-permute-start.33 = (bf16[1024,128]{1,0:T(8,128)(2,1)S(1)}, bf16[1024,128]{1,0:T(8,128)(2,1)S(1)}, u32[]{:S(2)}, u32[]{:S(2)}) collective-permute-start(bf16[1024,128]{1,0:T(8,128)(2,1)S(1)} %collective-permute-done.21.refs_2_), channel_id=1, source_target_pairs={{0,1},{1,0},{2,3},{3,2},{4,5},{5,4},{6,7},{7,6},{8,9},{9,8},{10,11... | collective-permute-start | bytes 786440 | tf_op jit(solution)/shard_map/ppermute | solution.py:23
  88.1 8.4 %collective-permute-start.38 = (bf16[1024,128]{1,0:T(8,128)(2,1)S(1)}, bf16[1024,128]{1,0:T(8,128)(2,1)S(1)}, u32[]{:S(2)}, u32[]{:S(2)}) collective-permute-start(bf16[1024,128]{1,0:T(8,128)(2,1)S(1)} %pad_maximum_fusion.refs_0_), channel_id=1, source_target_pairs={{0,8},{8,0},{1,9},{9,1},{2,10},{10,2},{3,11},{11,3},{4,12},{12,4},... | collective-permute-start | bytes 786440 | tf_op jit(solution)/shard_map/ppermute | solution.py:23
  89.5 6.9 %collective-permute-start.40 = (bf16[1024,128]{1,0:T(8,128)(2,1)S(1)}, bf16[1024,128]{1,0:T(8,128)(2,1)S(1)}, u32[]{:S(2)}, u32[]{:S(2)}) collective-permute-start(bf16[1024,128]{1,0:T(8,128)(2,1)S(1)} %collective-permute-done.21.refs_2_), channel_id=1, source_target_pairs={{0,8},{8,0},{1,9},{9,1},{2,10},{10,2},{3,11},{11,3},{4,12},{12,4},... | collective-permute-start | bytes 786440 | tf_op jit(solution)/shard_map/ppermute | solution.py:23
  89.5 6.9 %collective-permute-start.39 = (bf16[1024,128]{1,0:T(8,128)(2,1)S(1)}, bf16[1024,128]{1,0:T(8,128)(2,1)S(1)}, u32[]{:S(2)}, u32[]{:S(2)}) collective-permute-start(bf16[1024,128]{1,0:T(8,128)(2,1)S(1)} %collective-permute-done.37.refs_1_), channel_id=1, source_target_pairs={{0,8},{8,0},{1,9},{9,1},{2,10},{10,2},{3,11},{11,3},{4,12},{12,4},... | collective-permute-start | bytes 786440 | tf_op jit(solution)/shard_map/ppermute | solution.py:23
  94.4 4.7 %collective-permute-start.36 = (bf16[1024,128]{1,0:T(8,128)(2,1)S(1)}, bf16[1024,128]{1,0:T(8,128)(2,1)S(1)}, u32[]{:S(2)}, u32[]{:S(2)}) collective-permute-start(bf16[1024,128]{1,0:T(8,128)(2,1)S(1)} %collective-permute-done.33.refs_6_), channel_id=1, source_target_pairs={{0,8},{8,0},{1,9},{9,1},{2,10},{10,2},{3,11},{11,3},{4,12},{12,4},... | collective-permute-start | bytes 786440 | tf_op jit(solution)/shard_map/ppermute | solution.py:23
  (10 other events, 25.9 us)

commit v8 on v7

v8 whole, which is shorter than its diff:
```python
import functools
import math

import jax
import jax.numpy as jnp
from jax import lax
from jax.experimental import pallas as pl
from jax.experimental.pallas import tpu as pltpu
from jax.sharding import Mesh, PartitionSpec as P

STREAM = ("row", "core")
SPAN = ("deck", "side")
DIAGONAL = ("row", "side")
WEIGHT_PARTS = 3
LANES = 128
TILE = 16
CHUNKS = 2
TURNED = (((1,), (1,)), ((), ()))


def rotate(value, axis, by=1):
    count = lax.axis_size(axis)
    return lax.ppermute(value, axis, [(i, (i + by) % count) for i in range(count)])


def member(where, rows, offsets):
    r, c, s = offsets
    row = lax.rem(where[0] - r + rows, rows)
    return (row * 2 + lax.rem(where[1] + c, 2)) * 2 + lax.rem(where[2] + s, 2)


def grant(shapes, slack=6 * 2**20):
    total = slack
    for shape, dtype in shapes:
        *outer, rows, columns = shape
        size = jnp.dtype(dtype).itemsize
        rows, columns = pl.cdiv(rows, TILE) * TILE, pl.cdiv(columns, LANES) * LANES
        total += math.prod(outer) * rows * columns * size
    return total


def slopes_kernel(sizes, offsets, where_ref, *refs):
    layers, height, across, width, share, rows, decks, outs = sizes
    members = len(offsets)
    blocks, edges = refs[:members], refs[members : 2 * members]
    turned, own, field, edge, *sources = refs[2 * members :]
    count = members * layers * height * across
    depth = members // 2 * layers
    piece = 4 * count // depth
    parts = count // piece

    field[:2] = jnp.zeros_like(field[:2])
    field[members + 2 :] = jnp.zeros_like(field[members + 2 :])
    for n in range(members):
        at = member(where_ref, rows, offsets[n])
        field[at + 2] = blocks[n][...].astype(jnp.float32)
        edge[at] = edges[n][...].astype(jnp.float32)

    index = lax.broadcasted_iota(jnp.int32, (across, width), 0)
    weight_row = edge.shape[2] - across
    row, column = (lax.broadcasted_iota(jnp.int32, (width, width), d) for d in range(2))
    eye = (row == column).astype(jnp.bfloat16)

    def stencil(x, b, source):
        def layer_at(step, side):
            at = x + step + layers
            return lax.div(at, layers) * 2 + side, lax.rem(at, layers)

        for side in range(2):
            here_at, layer = layer_at(0, side)
            at = here_at - 2
            tile = edge[at, layer, weight_row:, 0:width]
            weights = tile
            for part in range(1, WEIGHT_PARTS):
                weights = weights + pltpu.roll(tile, width - part * height, 1)
            beside = {step: layer_at(step, side) for step in (-2, -1, 1, 2)}
            found = []
            for z in range(height):
                weight = jnp.broadcast_to(weights[:, z : z + 1], (across, width))
                twelfth, half = weight * (1.0 / 12.0), weight * 0.5
                base = 2 * z // across * across
                here = field[here_at, layer, z, b]
                along = {step: field[m, l, z, b] for step, (m, l) in beside.items()}
                value_x = 8.0 * (along[1] - along[-1]) - (along[2] - along[-2])

                outer = edge[at, layer, base : base + across, b * width : (b + 1) * width]
                beyond = field[here_at + 1 - 2 * side, layer, z, b]
                if side == 0:
                    prev = pltpu.roll(outer, (across - 2 - (2 * z - base)) % across, 0)
                    after = beyond
                else:
                    prev = beyond
                    after = pltpu.roll(outer, (across - (2 * z - base)) % across, 0)
                near = pltpu.roll(jnp.where(index < 1, after, here), across - 1, 0)
                near = near - pltpu.roll(jnp.where(index >= across - 1, prev, here), 1, 0)
                far = pltpu.roll(jnp.where(index < 2, after, here), across - 2, 0)
                far = far - pltpu.roll(jnp.where(index >= across - 2, prev, here), 2, 0)
                value_y = 8.0 * near - far

                value_z = jnp.zeros_like(here)
                if z < height - 1:
                    value_z = field[here_at, layer, z + 1, b]
                if z > 0:
                    value_z = value_z - field[here_at, layer, z - 1, b]
                found.append((here, value_x * twelfth, value_y * twelfth, value_z * half))
                if len(found) * across == TILE:
                    start = ((at * layers + layer) * height + z + 1) * across - TILE
                    to = pl.ds(pl.multiple_of(start, TILE), TILE)
                    for q in range(4):
                        value = jnp.concatenate([f[q] for f in found], axis=0)
                        source[q, to, :] = value.astype(jnp.bfloat16)
                    found = []

    def turn(x, b, source):
        q, part = lax.div(x, parts), lax.rem(x, parts)
        at = pl.ds(pl.multiple_of(part * piece, piece), piece)
        value = lax.dot_general(eye, source[q, at, :], TURNED, preferred_element_type=jnp.float32)
        turned[q, b, :, at] = value.astype(jnp.bfloat16)

    for step in range(4):

        def one_layer(x, _):
            if step < 3:
                stencil(x, step, sources[step % 2])
            if step > 0:
                turn(x, step - 1, sources[(step - 1) % 2])
            return 0

        lax.fori_loop(0, depth, one_layer, 0)

    row, column = (
        lax.broadcasted_iota(jnp.int32, (CHUNKS * share * TILE, width), d) for d in range(2)
    )
    chunk = sum((row >= n * share * TILE).astype(jnp.int32) for n in range(1, CHUNKS))
    mode = lax.shift_right_logical(row, TILE.bit_length() - 1) - chunk * share
    mode = mode + (where_ref[3] * (share // decks) if outs > 1 else 0)
    mode = jnp.where(mode >= share, mode - share, mode)
    mode = mode + (member(where_ref, rows, (0, 0, 0)) * CHUNKS + chunk) * share
    pick = (column == mode).astype(jnp.bfloat16)
    for b in range(3):
        value = jnp.dot(pick, turned[0, b], preferred_element_type=jnp.float32)
        own[b] = value.astype(jnp.bfloat16)


def plane_slopes(where, blocks, edges, offsets, share, rows, decks, outs):
    layers, height, comps, across, width = blocks[0].shape
    members = len(blocks)
    count = members * layers * height * across
    sizes = (layers, height, across, width, share, rows, decks, outs)
    vmem = pl.BlockSpec(memory_space=pltpu.VMEM)
    results = [
        ((4, comps, width, count), jnp.bfloat16),
        ((comps, CHUNKS * share * TILE, count), jnp.bfloat16),
    ]
    scratch = [
        ((members + 4,) + blocks[0].shape, jnp.float32),
        ((members,) + edges[0].shape, jnp.float32),
        ((4, count, width), jnp.bfloat16),
        ((4, count, width), jnp.bfloat16),
    ]
    inputs = [(v.shape, v.dtype) for v in blocks + edges]
    return pl.pallas_call(
        functools.partial(slopes_kernel, sizes, offsets),
        out_shape=[jax.ShapeDtypeStruct(*result) for result in results],
        in_specs=[pl.BlockSpec(memory_space=pltpu.SMEM)] + [vmem] * (2 * members),
        out_specs=[vmem] * len(results),
        scratch_shapes=[pltpu.VMEM(*shape) for shape in scratch],
        compiler_params=pltpu.CompilerParams(vmem_limit_bytes=grant(results + scratch + inputs)),
        cost_estimate=pl.CostEstimate(
            flops=2 * 12 * count * width * width, bytes_accessed=2**22, transcendentals=0
        ),
    )(where, *blocks, *edges)


def terms_kernel(share, chunk, turned, own, *refs):
    *out_refs, even, odd = refs
    outs = len(out_refs)
    width, count = turned.shape[2:]
    first = chunk * share
    for pair in range(share // 2):
        quad = (even, odd)[pair % 2]
        for a in range(3):
            for start in range(0, count, LANES):
                lanes = slice(start, start + LANES)
                spread = [
                    [
                        own[b, (first + 2 * pair + h) * TILE : (first + 2 * pair + h + 1) * TILE, lanes]
                        for b in range(3)
                    ]
                    for h in range(2)
                ]
                for k in range(0, width, TILE):
                    slope = [turned[1 + a, b, k : k + TILE, lanes] for b in range(3)]
                    for h in range(2):
                        value = spread[h][0] * slope[0]
                        value = value + spread[h][1] * slope[1]
                        value = value + spread[h][2] * slope[2]
                        quad[a, h * width + k : h * width + k + TILE, lanes] = value
        total = sum(
            lax.dot_general(turned[0, a], quad[a], TURNED, preferred_element_type=jnp.float32)
            for a in range(3)
        )
        for h in range(2):
            start = (2 * pair + h) * width
            out_ref = out_refs[start * outs // (share * width)]
            start = start % (share * width // outs)
            out_ref[start : start + width, :] = total[:, h * width : (h + 1) * width].astype(
                out_ref.dtype
            )


def plane_terms(turned, own, chunk, share, outs):
    width, count = turned.shape[2:]
    vmem = pl.BlockSpec(memory_space=pltpu.VMEM)
    dtypes = [jnp.float32 if outs > 1 and n == 0 else jnp.bfloat16 for n in range(outs)]
    results = [((share * width // outs, width), t) for t in dtypes]
    second = 2 if share > 2 else 1
    scratch = [((3, 2 * width, count), jnp.bfloat16)] * second
    scratch += [((TILE, LANES), jnp.bfloat16)] * (2 - second)
    inputs = [(v.shape, v.dtype) for v in (turned, own)]
    return pl.pallas_call(
        functools.partial(terms_kernel, share, chunk),
        out_shape=[jax.ShapeDtypeStruct(*result) for result in results],
        in_specs=[vmem] * 2,
        out_specs=[vmem] * outs,
        scratch_shapes=[pltpu.VMEM(*shape) for shape in scratch],
        compiler_params=pltpu.CompilerParams(vmem_limit_bytes=grant(results + scratch + inputs)),
        cost_estimate=pl.CostEstimate(
            flops=2 * share * width * width * count * 3, bytes_accessed=2**22, transcendentals=0
        ),
    )(turned, own)


def place_kernel(plan, pieces, given, where_ref, *refs):
    rows, decks, line, block, runs = plan
    out_ref, wide, sems = refs[pieces + given :]
    step = math.gcd(line, LANES)
    copies = []
    for n, (piece, offsets, chunk, d) in enumerate(runs):
        done = n * line

        def widen(k, _):
            at = pl.multiple_of(k * step, step)
            wide[pl.ds(done + at, step), :] = refs[piece][pl.ds(d * line + at, step), :].astype(
                jnp.float32
            )
            return 0

        lax.fori_loop(0, line // step, widen, 0)
        start = (member(where_ref, rows, offsets) * CHUNKS + chunk) * block
        start = start + lax.rem(where_ref[3] - d + decks, decks) * line
        to = pl.ds(pl.multiple_of(start, line), line)
        copies.append(
            pltpu.make_async_copy(wide.at[done : done + line], out_ref.at[to], sems.at[n])
        )
        copies[-1].start()
    for copy in copies:
        copy.wait()


def put(where, result, total_rows, rows, decks, chosen):
    values = [value for _, _, value in chosen]
    block, width = values[0].shape
    line = block // decks
    runs = [
        (n, offsets, chunk, d) for n, (chunk, offsets, _) in enumerate(chosen) for d in range(decks)
    ]
    given = [] if result is None else [result]
    vmem, anywhere = (pl.BlockSpec(memory_space=m) for m in (pltpu.VMEM, pl.ANY))
    wide = ((len(runs) * line, width), jnp.float32)
    return pl.pallas_call(
        functools.partial(place_kernel, (rows, decks, line, block, runs), len(values), len(given)),
        out_shape=jax.ShapeDtypeStruct((total_rows, width), jnp.float32),
        in_specs=[pl.BlockSpec(memory_space=pltpu.SMEM)]
        + [vmem] * len(values)
        + [anywhere] * len(given),
        out_specs=anywhere,
        scratch_shapes=[pltpu.VMEM(*wide), pltpu.SemaphoreType.DMA((len(runs),))],
        input_output_aliases={1 + len(values): 0} if given else {},
        compiler_params=pltpu.CompilerParams(
            vmem_limit_bytes=grant([wide] + [(v.shape, v.dtype) for v in values], 2**21)
        ),
        cost_estimate=pl.CostEstimate(
            flops=0, bytes_accessed=6 * wide[0][0] * width, transcendentals=0
        ),
    )(where, *values, *given)


def outer_rows(cells):
    across = cells.shape[3]
    decks = lax.axis_size("deck")
    rows = jnp.where(lax.axis_index("side") == 1, cells[..., across - 2 :, :], cells[..., :2, :])
    joints = [(2 * d + 1, 2 * d + 2) for d in range(decks - 1)]
    return lax.ppermute(rows, SPAN, joints + [(j, i) for i, j in joints])


def edge_piece(outer, weight):
    layers, height, comps, _, width = outer.shape
    across = weight.shape[1]
    outer = outer.transpose(0, 1, 3, 2, 4).reshape(layers, 2 * height, comps * width)
    parts = []
    for _ in range(WEIGHT_PARTS):
        part = lax.reduce_precision(weight, 8, 7)
        weight = weight - part
        parts.append(part.astype(jnp.bfloat16))
    tile = jnp.concatenate(parts, axis=2)
    total = pl.cdiv(2 * height + across, TILE) * TILE
    outer = jnp.pad(outer, ((0, 0), (0, total - across - 2 * height), (0, 0)))
    tile = jnp.pad(tile, ((0, 0), (0, 0), (0, comps * width - tile.shape[2])))
    return jnp.concatenate([outer, tile], axis=1)


def spread_near(piece):
    rows = lax.axis_size("row")
    got = {(0, 0): piece, (0, 1): rotate(piece, "side")}
    for r in range(1, rows):
        got[(r, 0)] = rotate(piece, "row", r)
        pairs = [(2 * i + s, 2 * ((i + r) % rows) + 1 - s) for i in range(rows) for s in range(2)]
        got[(r, 1)] = lax.ppermute(piece, DIAGONAL, pairs)
    return got


def spread_cores(got):
    out = {}
    for (r, s), value in got.items():
        out[(r, 0, s)] = value
        out[(r, 1, s)] = rotate(value, "core")
    return out


def sum_over_decks(terms, decks):
    if len(terms) > 1:
        parts = [terms[0]] + [rotate(terms[r], "deck", r) for r in range(1, decks)]
    else:
        width = terms[0].shape[1]
        parts = list(lax.all_to_all(terms[0].reshape(decks, -1, width), "deck", 0, 0))
    return sum(part.astype(jnp.float32) for part in parts).astype(jnp.bfloat16)


def shards(velocity_modes, cell_weight):
    width = velocity_modes.shape[-1]
    rows, decks = lax.axis_size("row"), lax.axis_size("deck")
    members = rows * 4
    share = width // members // CHUNKS
    where = jnp.stack([lax.axis_index(a) for a in ("row", "core", "side", "deck")]).astype(jnp.int32)
    outs = decks if share % (2 * decks) == 0 else 1

    cells = velocity_modes.transpose(0, 2, 3, 1, 4)
    outer = outer_rows(cells)
    near = spread_near(cells)
    outer, near = lax.optimization_barrier((outer, near))
    near[(0, 0)] = cells
    blocks = spread_cores(near)
    edges = spread_cores(spread_near(edge_piece(outer, cell_weight)))
    offsets = list(blocks)
    blocks, edges = ([d[o] for o in offsets] for d in (blocks, edges))
    slopes = plane_slopes(where, blocks, edges, offsets, share, rows, decks, outs)
    terms = [plane_terms(*slopes, n, share, outs) for n in range(CHUNKS)]

    def put_all(result, chosen):
        return put(where, result, width * width, rows, decks, chosen)

    result = None
    waiting = []
    for n in range(CHUNKS):
        mine = sum_over_decks(terms[n], decks)
        piece = jnp.concatenate([mine] + [rotate(mine, "deck", r) for r in range(1, decks)], axis=0)
        across = rotate(piece, "side")
        along = [rotate(piece, "row", r) for r in range(1, rows)]
        near = [(n, (0, 0, 0), piece), (n, (0, 0, 1), across)]
        near += [(n, (r, 0, 0), v) for r, v in enumerate(along, 1)]
        if n == 0:
            diagonal = [rotate(across, "row", r) for r in range(1, rows)]
        else:
            result = put_all(result, waiting.pop(0))
            along, result = lax.optimization_barrier((along, result))
            diagonal = [rotate(v, "side") for v in along]
        near_core = [(n, (r, 1, s), rotate(v, "core")) for _, (r, _, s), v in near]
        if n == CHUNKS - 1:
            result = put_all(result, waiting.pop(0) + near)
            diagonal, result = lax.optimization_barrier((diagonal, result))
            waiting.append(near_core)
        else:
            waiting.append(near + near_core)
        far = [(n, (r, 0, 1), v) for r, v in enumerate(diagonal, 1)]
        far_core = [(n, (r, 1, 1), rotate(v, "core")) for r, v in enumerate(diagonal, 1)]
        if n == CHUNKS - 1:
            waiting[-1] += far
            waiting.append(far_core)
        else:
            waiting.append(far + far_core)
    for chosen in waiting:
        result = put_all(result, chosen)
    return result.reshape(width, width, width)


def solution(mesh):
    streams, spans = (mesh.shape[name] for name in ("stream", "span"))
    split = Mesh(mesh.devices.reshape(streams // 2, 2, spans // 2, 2), STREAM + SPAN)
    placed = (P(STREAM, SPAN, None, None, None), P(STREAM, SPAN, None))
    return jax.shard_map(shards, mesh=split, in_specs=placed, out_specs=P(), check_vma=False)
```

time: 101 us -> 96 us (0.950)
  Pallas kernels: 30.2 us -> 26.8 us
  starting transfers between devices: 54.3 us -> 52.5 us
    pallas_call x2, Pallas kernels: 13.8 us -> 10.8 us  [plane_terms(): pl.pallas_call(functools.partial(terms_kernel, share, chunk), out_shape=[...]
    ppermute x38, starting transfers between devices: 53.6 us -> 51.8 us  [rotate(): lax.ppermute(value, axis, [(i, (i + by) % count) for i in range(count)])]
    ppermute x3, waiting for transfers between devices: 0.01 us -> 1.44 us  [the longest x2 1.44 us: spread_near(): got[r, 1] = lax.ppermute(piece, DIAGONAL, pairs)]
    ppermute x38, waiting for transfers between devices: 12.9 us -> 11.8 us  [rotate(): lax.ppermute(value, axis, [(i, (i + by) % count) for i in range(count)])]
  transfers between devices with their start and end apart: 41 -> 41, of which waited for: 10 -> 10; matrix products, arithmetic and copies ran while one was open for 1% -> 2% of each run, Pallas kernels for 13% -> 13%
where the time goes in v8:
time: 96 us; the launch traced here: 95.8 us
  starting transfers between devices  52.5 us (55%)
  Pallas kernels  26.8 us (28%)
  waiting for transfers between devices  13.3 us (14%)
  other arithmetic  2.01 us (2%)
    ppermute x38, starting transfers between devices, rotate(): lax.ppermute(value, axis, [(i, (i + by) % count) for i in range(count)])  51.8 us
    ppermute x38, waiting for transfers between devices, rotate(): lax.ppermute(value, axis, [(i, (i + by) % count) for i in range(count)])  11.8 us
    pallas_call x2, Pallas kernels, plane_terms(): pl.pallas_call(functools.partial(terms_kernel, share, chunk), out_shape=[...  10.8 us
    pallas_call x4, Pallas kernels, put(): pl.pallas_call(functools.partial(place_kernel, (rows, decks, line, block,...  8.02 us
    pallas_call x1, Pallas kernels, plane_slopes(): pl.pallas_call(functools.partial(slopes_kernel, sizes, offsets), out_shap...  7.96 us
  transfers between devices with their start and end apart: 41, of which 10 were waited for; matrix products, arithmetic and copies ran while one was open for 2% of the time, Pallas kernels for 13%

profile of v8, /device:TPU:1, one launch (start us, length us, event | category | flops | bytes accessed | tf_op | source)
XLA Modules:
  0.0 95.8 jit_solution(5138152793980752792)
XLA Ops:
  0.0 2.0 %collective-permute-start.2 = (bf16[2,10,3,8,128]{4,3,2,1,0:T(8,128)(2,1)}, bf16[2,10,3,8,128]{4,3,2,1,0:T(8,128)(2,1)S(1)}, u32[]{:S(2)}, u32[]{:S(2)}) collective-permute-start(bf16[2,10,3,8,128]{4,3,2,1,0:T(8,128)(2,1)} %bitcast.7), channel_id=1, source_target_pairs={{0,1},{1,0},{2,3},{3,2},{4,5},{5,4},{6,7},{7,6},{8,9},{9,8},{10,11... | collective-permute-start | bytes 368648 | tf_op jit(solution)/shard_map/ppermute | solution.py:23
  2.0 1.2 %collective-permute-start.3 = (bf16[2,10,3,8,128]{4,3,2,1,0:T(8,128)(2,1)}, bf16[2,10,3,8,128]{4,3,2,1,0:T(8,128)(2,1)S(1)}, u32[]{:S(2)}, u32[]{:S(2)}) collective-permute-start(bf16[2,10,3,8,128]{4,3,2,1,0:T(8,128)(2,1)} %bitcast.8), channel_id=1, source_target_pairs={{0,16},{16,0},{1,17},{17,1},{2,18},{18,2},{3,19},{19,3},{4,20},{20... | collective-permute-start | bytes 368648 | tf_op jit(solution)/shard_map/ppermute | solution.py:23
  7.0 1.4 %collective-permute-done.4.refs_6_ = bf16[2,10,3,8,128]{4,3,2,1,0:T(8,128)(2,1)S(1)} collective-permute-done((bf16[2,10,3,8,128]{4,3,2,1,0:T(8,128)(2,1)}, bf16[2,10,3,8,128]{4,3,2,1,0:T(8,128)(2,1)S(1)}, u32[]{:S(2)}, u32[]{:S(2)}) %collective-permute-start.4) | collective-permute-done | bytes 122912 | tf_op jit(solution)/shard_map/ppermute | solution.py:319
  8.5 4.4 %collective-permute-start.9 = (bf16[2,32,384]{2,1,0:T(8,128)(2,1)S(1)}, bf16[2,32,384]{2,1,0:T(8,128)(2,1)S(1)}, u32[]{:S(2)}, u32[]{:S(2)}) collective-permute-start(bf16[2,32,384]{2,1,0:T(8,128)(2,1)S(1)} %fusion.1.refs_8_), channel_id=1, source_target_pairs={{0,1},{1,0},{2,3},{3,2},{4,5},{5,4},{6,7},{7,6},{8,9},{9,8},{10,11... | collective-permute-start | bytes 147464 | tf_op jit(solution)/shard_map/ppermute | solution.py:23
  12.9 1.2 %collective-permute-start.11 = (bf16[2,32,384]{2,1,0:T(8,128)(2,1)S(1)}, bf16[2,32,384]{2,1,0:T(8,128)(2,1)S(1)}, u32[]{:S(2)}, u32[]{:S(2)}) collective-permute-start(bf16[2,32,384]{2,1,0:T(8,128)(2,1)S(1)} %fusion.1.refs_8_), channel_id=1, source_target_pairs={{0,16},{16,0},{1,17},{17,1},{2,18},{18,2},{3,19},{19,3},{4,20},{20... | collective-permute-start | bytes 147464 | tf_op jit(solution)/shard_map/ppermute | solution.py:23
  14.2 1.7 %collective-permute-start.8 = (bf16[2,32,384]{2,1,0:T(8,128)(2,1)S(1)}, bf16[2,32,384]{2,1,0:T(8,128)(2,1)S(1)}, u32[]{:S(2)}, u32[]{:S(2)}) collective-permute-start(bf16[2,32,384]{2,1,0:T(8,128)(2,1)S(1)} %fusion.1.refs_8_), channel_id=1, source_target_pairs={{0,8},{8,0},{1,9},{9,1},{2,10},{10,2},{3,11},{11,3},{4,12},{12,4},... | collective-permute-start | bytes 147464 | tf_op jit(solution)/shard_map/ppermute | solution.py:23
  16.4 2.5 %collective-permute-start.6 = (bf16[2,10,3,8,128]{4,3,2,1,0:T(8,128)(2,1)S(1)}, bf16[2,10,3,8,128]{4,3,2,1,0:T(8,128)(2,1)S(1)}, u32[]{:S(2)}, u32[]{:S(2)}) collective-permute-start(bf16[2,10,3,8,128]{4,3,2,1,0:T(8,128)(2,1)S(1)} %collective-permute-done.3.refs_4_), channel_id=1, source_target_pairs={{0,8},{8,0},{1,9},{9,1},{2,10},{10,2},{3,11},{11,3},{4,12},{12,4},... | collective-permute-start | bytes 368648 | tf_op jit(solution)/shard_map/ppermute | solution.py:23
  19.0 1.9 %collective-permute-start.7 = (bf16[2,10,3,8,128]{4,3,2,1,0:T(8,128)(2,1)S(1)}, bf16[2,10,3,8,128]{4,3,2,1,0:T(8,128)(2,1)S(1)}, u32[]{:S(2)}, u32[]{:S(2)}) collective-permute-start(bf16[2,10,3,8,128]{4,3,2,1,0:T(8,128)(2,1)S(1)} %collective-permute-done.4.refs_6_), channel_id=1, source_target_pairs={{0,8},{8,0},{1,9},{9,1},{2,10},{10,2},{3,11},{11,3},{4,12},{12,4},... | collective-permute-start | bytes 368648 | tf_op jit(solution)/shard_map/ppermute | solution.py:23
  23.2 8.0 %shard_map.28 = (bf16[4,3,128,1280]{3,2,1,0:T(8,128)(2,1)S(1)}, bf16[3,256,1280]{2,1,0:T(8,128)(2,1)S(1)}) custom-call(s32[4]{0:T(128)S(1)} %pad_add_fusion.where_ref, bf16[2,10,3,8,128]{4,3,2,1,0:T(8,128)(2,1)S(1)} %bitcast.12, bf16[2,10,3,8,128]{4,3,2,1,0:T(8,128)(2,1)S(1)} %collective-permute-done.refs_1_, ...), custom_call_target="tpu_custom_call" | custom-call | flops 503316480 | bytes 4194304 | tf_op jit(solution)/shard_map/pallas_call | solution.py:162
  31.1 5.4 %shard_map.30 = (f32[256,128]{1,0:T(8,128)S(1)}, bf16[256,128]{1,0:T(8,128)(2,1)S(1)}, bf16[256,128]{1,0:T(8,128)(2,1)S(1)}, bf16[256,128]{1,0:T(8,128)(2,1)S(1)}) custom-call(bf16[4,3,128,1280]{3,2,1,0:T(8,128)(2,1)S(1)} %get-tuple-element.27.turned, bf16[3,256,1280]{2,1,0:T(8,128)(2,1)S(1)} %get-tuple-element.28.own), custom_call_target="tpu_custom_call" | custom-call | flops 1006632960 | bytes 4194304 | tf_op jit(solution)/shard_map/pallas_call | solution.py:221
  36.6 1.3 %collective-permute-start.22 = (bf16[256,128]{1,0:T(8,128)(2,1)S(1)}, bf16[256,128]{1,0:T(8,128)(2,1)S(1)}, u32[]{:S(2)}, u32[]{:S(2)}) collective-permute-start(bf16[256,128]{1,0:T(8,128)(2,1)S(1)} %get-tuple-element.34), channel_id=1, source_target_pairs={{0,2},{2,4},{4,6},{6,0},{1,3},{3,5},{5,7},{7,1},{8,10},{10,12},{12... | collective-permute-start | bytes 196616 | tf_op jit(solution)/shard_map/ppermute | solution.py:23
  39.0 2.3 %collective-permute-start.24 = (bf16[256,128]{1,0:T(8,128)(2,1)S(1)}, bf16[256,128]{1,0:T(8,128)(2,1)S(1)}, u32[]{:S(2)}, u32[]{:S(2)}) collective-permute-start(bf16[256,128]{1,0:T(8,128)(2,1)S(1)} %get-tuple-element.36), channel_id=1, source_target_pairs={{0,6},{2,0},{4,2},{6,4},{1,7},{3,1},{5,3},{7,5},{8,14},{10,8},{12,... | collective-permute-start | bytes 196616 | tf_op jit(solution)/shard_map/ppermute | solution.py:23
  41.6 3.6 %collective-permute-done.23 = bf16[256,128]{1,0:T(8,128)(2,1)S(1)} collective-permute-done((bf16[256,128]{1,0:T(8,128)(2,1)S(1)}, bf16[256,128]{1,0:T(8,128)(2,1)S(1)}, u32[]{:S(2)}, u32[]{:S(2)}) %collective-permute-start.23) | collective-permute-done | bytes 65568 | tf_op jit(solution)/shard_map/ppermute | solution.py:23
  45.3 1.7 %collective-permute-start.25 = (bf16[256,128]{1,0:T(8,128)(2,1)S(1)}, bf16[256,128]{1,0:T(8,128)(2,1)S(1)}, u32[]{:S(2)}, u32[]{:S(2)}) collective-permute-start(bf16[256,128]{1,0:T(8,128)(2,1)S(1)} %add_convert_fusion), channel_id=1, source_target_pairs={{0,2},{2,4},{4,6},{6,0},{1,3},{3,5},{5,7},{7,1},{8,10},{10,12},{12... | collective-permute-start | bytes 196616 | tf_op jit(solution)/shard_map/ppermute | solution.py:23
  47.4 1.8 %collective-permute-start.27 = (bf16[256,128]{1,0:T(8,128)(2,1)S(1)}, bf16[256,128]{1,0:T(8,128)(2,1)S(1)}, u32[]{:S(2)}, u32[]{:S(2)}) collective-permute-start(bf16[256,128]{1,0:T(8,128)(2,1)S(1)} %add_convert_fusion), channel_id=1, source_target_pairs={{0,6},{2,0},{4,2},{6,4},{1,7},{3,1},{5,3},{7,5},{8,14},{10,8},{12,... | collective-permute-start | bytes 196616 | tf_op jit(solution)/shard_map/ppermute | solution.py:23
  49.2 5.4 %shard_map.29 = (f32[256,128]{1,0:T(8,128)S(1)}, bf16[256,128]{1,0:T(8,128)(2,1)S(1)}, bf16[256,128]{1,0:T(8,128)(2,1)S(1)}, bf16[256,128]{1,0:T(8,128)(2,1)S(1)}) custom-call(bf16[4,3,128,1280]{3,2,1,0:T(8,128)(2,1)S(1)} %get-tuple-element.27.turned, bf16[3,256,1280]{2,1,0:T(8,128)(2,1)S(1)} %get-tuple-element.28.own), custom_call_target="tpu_custom_call" | custom-call | flops 1006632960 | bytes 4194304 | tf_op jit(solution)/shard_map/pallas_call | solution.py:221
  54.7 1.7 %collective-permute-start.16 = (bf16[256,128]{1,0:T(8,128)(2,1)S(1)}, bf16[256,128]{1,0:T(8,128)(2,1)S(1)}, u32[]{:S(2)}, u32[]{:S(2)}) collective-permute-start(bf16[256,128]{1,0:T(8,128)(2,1)S(1)} %get-tuple-element.31), channel_id=1, source_target_pairs={{0,4},{2,6},{4,0},{6,2},{1,5},{3,7},{5,1},{7,3},{8,12},{10,14},{12... | collective-permute-start | bytes 196616 | tf_op jit(solution)/shard_map/ppermute | solution.py:23
  56.3 1.6 %collective-permute-start.17 = (bf16[256,128]{1,0:T(8,128)(2,1)S(1)}, bf16[256,128]{1,0:T(8,128)(2,1)S(1)}, u32[]{:S(2)}, u32[]{:S(2)}) collective-permute-start(bf16[256,128]{1,0:T(8,128)(2,1)S(1)} %get-tuple-element.32), channel_id=1, source_target_pairs={{0,6},{2,0},{4,2},{6,4},{1,7},{3,1},{5,3},{7,5},{8,14},{10,8},{12,... | collective-permute-start | bytes 196616 | tf_op jit(solution)/shard_map/ppermute | solution.py:23
  60.3 3.4 %collective-permute-start.18 = (bf16[256,128]{1,0:T(8,128)(2,1)S(1)}, bf16[256,128]{1,0:T(8,128)(2,1)S(1)}, u32[]{:S(2)}, u32[]{:S(2)}) collective-permute-start(bf16[256,128]{1,0:T(8,128)(2,1)S(1)} %add_convert_fusion.1), channel_id=1, source_target_pairs={{0,2},{2,4},{4,6},{6,0},{1,3},{3,5},{5,7},{7,1},{8,10},{10,12},{12... | collective-permute-start | bytes 196616 | tf_op jit(solution)/shard_map/ppermute | solution.py:23
  63.7 1.3 %collective-permute-start.19 = (bf16[256,128]{1,0:T(8,128)(2,1)S(1)}, bf16[256,128]{1,0:T(8,128)(2,1)S(1)}, u32[]{:S(2)}, u32[]{:S(2)}) collective-permute-start(bf16[256,128]{1,0:T(8,128)(2,1)S(1)} %add_convert_fusion.1), channel_id=1, source_target_pairs={{0,4},{2,6},{4,0},{6,2},{1,5},{3,7},{5,1},{7,3},{8,12},{10,14},{12... | collective-permute-start | bytes 196616 | tf_op jit(solution)/shard_map/ppermute | solution.py:23
  66.3 4.0 %collective-permute-start.30 = (bf16[1024,128]{1,0:T(8,128)(2,1)S(1)}, bf16[1024,128]{1,0:T(8,128)(2,1)S(1)}, u32[]{:S(2)}, u32[]{:S(2)}) collective-permute-start(bf16[1024,128]{1,0:T(8,128)(2,1)S(1)} %pad_maximum_fusion.1.refs_0_), channel_id=1, source_target_pairs={{0,8},{8,0},{1,9},{9,1},{2,10},{10,2},{3,11},{11,3},{4,12},{12,4},... | collective-permute-start | bytes 786440 | tf_op jit(solution)/shard_map/ppermute | solution.py:23
  70.6 1.7 %collective-permute-start.32 = (bf16[1024,128]{1,0:T(8,128)(2,1)S(1)}, bf16[1024,128]{1,0:T(8,128)(2,1)S(1)}, u32[]{:S(2)}, u32[]{:S(2)}) collective-permute-start(bf16[1024,128]{1,0:T(8,128)(2,1)S(1)} %collective-permute-done.29.refs_2_), channel_id=1, source_target_pairs={{0,8},{8,0},{1,9},{9,1},{2,10},{10,2},{3,11},{11,3},{4,12},{12,4},... | collective-permute-start | bytes 786440 | tf_op jit(solution)/shard_map/ppermute | solution.py:23
  72.3 1.3 %collective-permute-start.21 = (bf16[1024,128]{1,0:T(8,128)(2,1)S(1)}, bf16[1024,128]{1,0:T(8,128)(2,1)S(1)}, u32[]{:S(2)}, u32[]{:S(2)}) collective-permute-start(bf16[1024,128]{1,0:T(8,128)(2,1)S(1)} %pad_maximum_fusion.refs_2_), channel_id=1, source_target_pairs={{0,16},{16,0},{1,17},{17,1},{2,18},{18,2},{3,19},{19,3},{4,20},{20... | collective-permute-start | bytes 786440 | tf_op jit(solution)/shard_map/ppermute | solution.py:23
  74.0 2.7 %collective-permute-done.34.refs_0_ = bf16[1024,128]{1,0:T(8,128)(2,1)S(1)} collective-permute-done((bf16[1024,128]{1,0:T(8,128)(2,1)S(1)}, bf16[1024,128]{1,0:T(8,128)(2,1)S(1)}, u32[]{:S(2)}, u32[]{:S(2)}) %collective-permute-start.34) | collective-permute-done | bytes 262176 | tf_op jit(solution)/shard_map/ppermute | solution.py:23
  76.7 4.3 %collective-permute-start.35 = (bf16[1024,128]{1,0:T(8,128)(2,1)S(1)}, bf16[1024,128]{1,0:T(8,128)(2,1)S(1)}, u32[]{:S(2)}, u32[]{:S(2)}) collective-permute-start(bf16[1024,128]{1,0:T(8,128)(2,1)S(1)} %collective-permute-done.34.refs_0_), channel_id=1, source_target_pairs={{0,8},{8,0},{1,9},{9,1},{2,10},{10,2},{3,11},{11,3},{4,12},{12,4},... | collective-permute-start | bytes 786440 | tf_op jit(solution)/shard_map/ppermute | solution.py:23
  81.0 2.4 %shard_map.31.refs_5_ = f32[16384,128]{1,0:T(8,128)} custom-call(s32[4]{0:T(128)S(1)} %pad_add_fusion.where_ref, bf16[1024,128]{1,0:T(8,128)(2,1)S(1)} %pad_maximum_fusion.1.refs_0_, bf16[1024,128]{1,0:T(8,128)(2,1)S(1)} %collective-permute-done.28.refs_1_, bf16[1024,128]{1,0:T(8,128)(2,1)S(1)} %collective-permute-done.29.refs_2_, ...), custom_call_target="tpu_custom_call" | custom-call | bytes 4718592 | tf_op jit(solution)/shard_map/pallas_call | solution.py:271
  83.9 1.4 %collective-permute-start.38 = (bf16[1024,128]{1,0:T(8,128)(2,1)S(1)}, bf16[1024,128]{1,0:T(8,128)(2,1)S(1)}, u32[]{:S(2)}, u32[]{:S(2)}) collective-permute-start(bf16[1024,128]{1,0:T(8,128)(2,1)S(1)} %pad_maximum_fusion.refs_2_), channel_id=1, source_target_pairs={{0,8},{8,0},{1,9},{9,1},{2,10},{10,2},{3,11},{11,3},{4,12},{12,4},... | collective-permute-start | bytes 786440 | tf_op jit(solution)/shard_map/ppermute | solution.py:23
  85.8 2.2 %shard_map.32.refs_4_ = f32[16384,128]{1,0:T(8,128)} custom-call(s32[4]{0:T(128)S(1)} %pad_add_fusion.where_ref, bf16[1024,128]{1,0:T(8,128)(2,1)S(1)} %collective-permute-done.34.refs_0_, bf16[1024,128]{1,0:T(8,128)(2,1)S(1)} %collective-permute-done.35.refs_1_, bf16[1024,128]{1,0:T(8,128)(2,1)S(1)} %pad_maximum_fusion.refs_2_, ...), custom_call_target="tpu_custom_call", output_to_operand_aliasing={{}: (6, {})} | custom-call | bytes 3932160 | tf_op jit(solution)/shard_map/pallas_call | solution.py:271
  88.1 2.1 %collective-permute-done.33.refs_3_ = bf16[1024,128]{1,0:T(8,128)(2,1)S(1)} collective-permute-done((bf16[1024,128]{1,0:T(8,128)(2,1)S(1)}, bf16[1024,128]{1,0:T(8,128)(2,1)S(1)}, u32[]{:S(2)}, u32[]{:S(2)}) %collective-permute-start.33) | collective-permute-done | bytes 262176 | tf_op jit(solution)/shard_map/ppermute | solution.py:23
  90.1 2.1 %collective-permute-start.37 = (bf16[1024,128]{1,0:T(8,128)(2,1)S(1)}, bf16[1024,128]{1,0:T(8,128)(2,1)S(1)}, u32[]{:S(2)}, u32[]{:S(2)}) collective-permute-start(bf16[1024,128]{1,0:T(8,128)(2,1)S(1)} %collective-permute-done.33.refs_3_), channel_id=1, source_target_pairs={{0,8},{8,0},{1,9},{9,1},{2,10},{10,2},{3,11},{11,3},{4,12},{12,4},... | collective-permute-start | bytes 786440 | tf_op jit(solution)/shard_map/ppermute | solution.py:23
  92.3 2.0 %shard_map.33.refs_1_ = f32[16384,128]{1,0:T(8,128)} custom-call(s32[4]{0:T(128)S(1)} %pad_add_fusion.where_ref, bf16[1024,128]{1,0:T(8,128)(2,1)S(1)} %collective-permute-done.38.refs_0_, bf16[1024,128]{1,0:T(8,128)(2,1)S(1)} %collective-permute-done.39.refs_1_, ...), custom_call_target="tpu_custom_call", output_to_operand_aliasing={{}: (5, {})} | custom-call | bytes 3145728 | tf_op jit(solution)/shard_map/pallas_call | solution.py:271
  94.3 1.4 %shard_map.34 = f32[16384,128]{1,0:T(8,128)} custom-call(s32[4]{0:T(128)S(1)} %pad_add_fusion.where_ref, bf16[1024,128]{1,0:T(8,128)(2,1)S(1)} %collective-permute-done.37.refs_0_, f32[16384,128]{1,0:T(8,128)} %shard_map.33.refs_1_), custom_call_target="tpu_custom_call", output_to_operand_aliasing={{}: (2, {})} | custom-call | bytes 786432 | tf_op jit(solution)/shard_map/pallas_call | solution.py:271
  (70 shorter events, 13.9 us)
Async XLA Ops:
  0.0 7.0 %collective-permute-start.2 = (bf16[2,10,3,8,128]{4,3,2,1,0:T(8,128)(2,1)}, bf16[2,10,3,8,128]{4,3,2,1,0:T(8,128)(2,1)S(1)}, u32[]{:S(2)}, u32[]{:S(2)}) collective-permute-start(bf16[2,10,3,8,128]{4,3,2,1,0:T(8,128)(2,1)} %bitcast.7), channel_id=1, source_target_pairs={{0,1},{1,0},{2,3},{3,2},{4,5},{5,4},{6,7},{7,6},{8,9},{9,8},{10,11... | collective-permute-start | bytes 368648 | tf_op jit(solution)/shard_map/ppermute | solution.py:23
  2.0 5.0 %collective-permute-start.3 = (bf16[2,10,3,8,128]{4,3,2,1,0:T(8,128)(2,1)}, bf16[2,10,3,8,128]{4,3,2,1,0:T(8,128)(2,1)S(1)}, u32[]{:S(2)}, u32[]{:S(2)}) collective-permute-start(bf16[2,10,3,8,128]{4,3,2,1,0:T(8,128)(2,1)} %bitcast.8), channel_id=1, source_target_pairs={{0,16},{16,0},{1,17},{17,1},{2,18},{18,2},{3,19},{19,3},{4,20},{20... | collective-permute-start | bytes 368648 | tf_op jit(solution)/shard_map/ppermute | solution.py:23
  3.3 5.2 %collective-permute-start.4 = (bf16[2,10,3,8,128]{4,3,2,1,0:T(8,128)(2,1)}, bf16[2,10,3,8,128]{4,3,2,1,0:T(8,128)(2,1)S(1)}, u32[]{:S(2)}, u32[]{:S(2)}) collective-permute-start(bf16[2,10,3,8,128]{4,3,2,1,0:T(8,128)(2,1)} %bitcast.9), channel_id=1, source_target_pairs={{0,17},{1,16},{16,1},{17,0},{2,19},{3,18},{18,3},{19,2},{4,21},{5,... | collective-permute-start | bytes 368648 | tf_op jit(solution)/shard_map/ppermute | solution.py:319
  3.3 13.1 %collective-permute-start = (bf16[2,10,3,8,128]{4,3,2,1,0:T(8,128)(2,1)}, bf16[2,10,3,8,128]{4,3,2,1,0:T(8,128)(2,1)S(1)}, u32[]{:S(2)}, u32[]{:S(2)}) collective-permute-start(bf16[2,10,3,8,128]{4,3,2,1,0:T(8,128)(2,1)} %bitcast.10), channel_id=1, source_target_pairs={{0,8},{8,0},{1,9},{9,1},{2,10},{10,2},{3,11},{11,3},{4,12},{12,4},... | collective-permute-start | bytes 368648 | tf_op jit(solution)/shard_map/ppermute | solution.py:23
  8.5 7.4 %collective-permute-start.9 = (bf16[2,32,384]{2,1,0:T(8,128)(2,1)S(1)}, bf16[2,32,384]{2,1,0:T(8,128)(2,1)S(1)}, u32[]{:S(2)}, u32[]{:S(2)}) collective-permute-start(bf16[2,32,384]{2,1,0:T(8,128)(2,1)S(1)} %fusion.1.refs_8_), channel_id=1, source_target_pairs={{0,1},{1,0},{2,3},{3,2},{4,5},{5,4},{6,7},{7,6},{8,9},{9,8},{10,11... | collective-permute-start | bytes 147464 | tf_op jit(solution)/shard_map/ppermute | solution.py:23
  14.2 6.7 %collective-permute-start.8 = (bf16[2,32,384]{2,1,0:T(8,128)(2,1)S(1)}, bf16[2,32,384]{2,1,0:T(8,128)(2,1)S(1)}, u32[]{:S(2)}, u32[]{:S(2)}) collective-permute-start(bf16[2,32,384]{2,1,0:T(8,128)(2,1)S(1)} %fusion.1.refs_8_), channel_id=1, source_target_pairs={{0,8},{8,0},{1,9},{9,1},{2,10},{10,2},{3,11},{11,3},{4,12},{12,4},... | collective-permute-start | bytes 147464 | tf_op jit(solution)/shard_map/ppermute | solution.py:23
  15.9 5.0 %collective-permute-start.10 = (bf16[2,32,384]{2,1,0:T(8,128)(2,1)S(1)}, bf16[2,32,384]{2,1,0:T(8,128)(2,1)S(1)}, u32[]{:S(2)}, u32[]{:S(2)}) collective-permute-start(bf16[2,32,384]{2,1,0:T(8,128)(2,1)S(1)} %collective-permute-done.9.refs_10_), channel_id=1, source_target_pairs={{0,8},{8,0},{1,9},{9,1},{2,10},{10,2},{3,11},{11,3},{4,12},{12,4},... | collective-permute-start | bytes 147464 | tf_op jit(solution)/shard_map/ppermute | solution.py:23
  16.4 5.8 %collective-permute-start.5 = (bf16[2,10,3,8,128]{4,3,2,1,0:T(8,128)(2,1)S(1)}, bf16[2,10,3,8,128]{4,3,2,1,0:T(8,128)(2,1)S(1)}, u32[]{:S(2)}, u32[]{:S(2)}) collective-permute-start(bf16[2,10,3,8,128]{4,3,2,1,0:T(8,128)(2,1)S(1)} %collective-permute-done.2.refs_2_), channel_id=1, source_target_pairs={{0,8},{8,0},{1,9},{9,1},{2,10},{10,2},{3,11},{11,3},{4,12},{12,4},... | collective-permute-start | bytes 368648 | tf_op jit(solution)/shard_map/ppermute | solution.py:23
  16.4 5.8 %collective-permute-start.6 = (bf16[2,10,3,8,128]{4,3,2,1,0:T(8,128)(2,1)S(1)}, bf16[2,10,3,8,128]{4,3,2,1,0:T(8,128)(2,1)S(1)}, u32[]{:S(2)}, u32[]{:S(2)}) collective-permute-start(bf16[2,10,3,8,128]{4,3,2,1,0:T(8,128)(2,1)S(1)} %collective-permute-done.3.refs_4_), channel_id=1, source_target_pairs={{0,8},{8,0},{1,9},{9,1},{2,10},{10,2},{3,11},{11,3},{4,12},{12,4},... | collective-permute-start | bytes 368648 | tf_op jit(solution)/shard_map/ppermute | solution.py:23
  36.6 5.0 %collective-permute-start.22 = (bf16[256,128]{1,0:T(8,128)(2,1)S(1)}, bf16[256,128]{1,0:T(8,128)(2,1)S(1)}, u32[]{:S(2)}, u32[]{:S(2)}) collective-permute-start(bf16[256,128]{1,0:T(8,128)(2,1)S(1)} %get-tuple-element.34), channel_id=1, source_target_pairs={{0,2},{2,4},{4,6},{6,0},{1,3},{3,5},{5,7},{7,1},{8,10},{10,12},{12... | collective-permute-start | bytes 196616 | tf_op jit(solution)/shard_map/ppermute | solution.py:23
  37.9 7.3 %collective-permute-start.23 = (bf16[256,128]{1,0:T(8,128)(2,1)S(1)}, bf16[256,128]{1,0:T(8,128)(2,1)S(1)}, u32[]{:S(2)}, u32[]{:S(2)}) collective-permute-start(bf16[256,128]{1,0:T(8,128)(2,1)S(1)} %get-tuple-element.35), channel_id=1, source_target_pairs={{0,4},{2,6},{4,0},{6,2},{1,5},{3,7},{5,1},{7,3},{8,12},{10,14},{12... | collective-permute-start | bytes 196616 | tf_op jit(solution)/shard_map/ppermute | solution.py:23
  39.0 6.2 %collective-permute-start.24 = (bf16[256,128]{1,0:T(8,128)(2,1)S(1)}, bf16[256,128]{1,0:T(8,128)(2,1)S(1)}, u32[]{:S(2)}, u32[]{:S(2)}) collective-permute-start(bf16[256,128]{1,0:T(8,128)(2,1)S(1)} %get-tuple-element.36), channel_id=1, source_target_pairs={{0,6},{2,0},{4,2},{6,4},{1,7},{3,1},{5,3},{7,5},{8,14},{10,8},{12,... | collective-permute-start | bytes 196616 | tf_op jit(solution)/shard_map/ppermute | solution.py:23
  45.3 11.0 %collective-permute-start.25 = (bf16[256,128]{1,0:T(8,128)(2,1)S(1)}, bf16[256,128]{1,0:T(8,128)(2,1)S(1)}, u32[]{:S(2)}, u32[]{:S(2)}) collective-permute-start(bf16[256,128]{1,0:T(8,128)(2,1)S(1)} %add_convert_fusion), channel_id=1, source_target_pairs={{0,2},{2,4},{4,6},{6,0},{1,3},{3,5},{5,7},{7,1},{8,10},{10,12},{12... | collective-permute-start | bytes 196616 | tf_op jit(solution)/shard_map/ppermute | solution.py:23
  47.0 10.9 %collective-permute-start.26 = (bf16[256,128]{1,0:T(8,128)(2,1)S(1)}, bf16[256,128]{1,0:T(8,128)(2,1)S(1)}, u32[]{:S(2)}, u32[]{:S(2)}) collective-permute-start(bf16[256,128]{1,0:T(8,128)(2,1)S(1)} %add_convert_fusion), channel_id=1, source_target_pairs={{0,4},{2,6},{4,0},{6,2},{1,5},{3,7},{5,1},{7,3},{8,12},{10,14},{12... | collective-permute-start | bytes 196616 | tf_op jit(solution)/shard_map/ppermute | solution.py:23
  47.4 10.5 %collective-permute-start.27 = (bf16[256,128]{1,0:T(8,128)(2,1)S(1)}, bf16[256,128]{1,0:T(8,128)(2,1)S(1)}, u32[]{:S(2)}, u32[]{:S(2)}) collective-permute-start(bf16[256,128]{1,0:T(8,128)(2,1)S(1)} %add_convert_fusion), channel_id=1, source_target_pairs={{0,6},{2,0},{4,2},{6,4},{1,7},{3,1},{5,3},{7,5},{8,14},{10,8},{12,... | collective-permute-start | bytes 196616 | tf_op jit(solution)/shard_map/ppermute | solution.py:23
  54.6 5.0 %collective-permute-start.15 = (bf16[256,128]{1,0:T(8,128)(2,1)S(1)}, bf16[256,128]{1,0:T(8,128)(2,1)S(1)}, u32[]{:S(2)}, u32[]{:S(2)}) collective-permute-start(bf16[256,128]{1,0:T(8,128)(2,1)S(1)} %get-tuple-element.30), channel_id=1, source_target_pairs={{0,2},{2,4},{4,6},{6,0},{1,3},{3,5},{5,7},{7,1},{8,10},{10,12},{12... | collective-permute-start | bytes 196616 | tf_op jit(solution)/shard_map/ppermute | solution.py:23
  57.9 12.3 %collective-permute-start.28 = (bf16[1024,128]{1,0:T(8,128)(2,1)S(1)}, bf16[1024,128]{1,0:T(8,128)(2,1)S(1)}, u32[]{:S(2)}, u32[]{:S(2)}) collective-permute-start(bf16[1024,128]{1,0:T(8,128)(2,1)S(1)} %pad_maximum_fusion.1.refs_0_), channel_id=1, source_target_pairs={{0,1},{1,0},{2,3},{3,2},{4,5},{5,4},{6,7},{7,6},{8,9},{9,8},{10,11... | collective-permute-start | bytes 786440 | tf_op jit(solution)/shard_map/ppermute | solution.py:23
  58.3 12.2 %collective-permute-start.29 = (bf16[1024,128]{1,0:T(8,128)(2,1)S(1)}, bf16[1024,128]{1,0:T(8,128)(2,1)S(1)}, u32[]{:S(2)}, u32[]{:S(2)}) collective-permute-start(bf16[1024,128]{1,0:T(8,128)(2,1)S(1)} %pad_maximum_fusion.1.refs_0_), channel_id=1, source_target_pairs={{0,16},{16,0},{1,17},{17,1},{2,18},{18,2},{3,19},{19,3},{4,20},{20... | collective-permute-start | bytes 786440 | tf_op jit(solution)/shard_map/ppermute | solution.py:23
  60.3 6.0 %collective-permute-start.18 = (bf16[256,128]{1,0:T(8,128)(2,1)S(1)}, bf16[256,128]{1,0:T(8,128)(2,1)S(1)}, u32[]{:S(2)}, u32[]{:S(2)}) collective-permute-start(bf16[256,128]{1,0:T(8,128)(2,1)S(1)} %add_convert_fusion.1), channel_id=1, source_target_pairs={{0,2},{2,4},{4,6},{6,0},{1,3},{3,5},{5,7},{7,1},{8,10},{10,12},{12... | collective-permute-start | bytes 196616 | tf_op jit(solution)/shard_map/ppermute | solution.py:23
  63.7 6.6 %collective-permute-start.19 = (bf16[256,128]{1,0:T(8,128)(2,1)S(1)}, bf16[256,128]{1,0:T(8,128)(2,1)S(1)}, u32[]{:S(2)}, u32[]{:S(2)}) collective-permute-start(bf16[256,128]{1,0:T(8,128)(2,1)S(1)} %add_convert_fusion.1), channel_id=1, source_target_pairs={{0,4},{2,6},{4,0},{6,2},{1,5},{3,7},{5,1},{7,3},{8,12},{10,14},{12... | collective-permute-start | bytes 196616 | tf_op jit(solution)/shard_map/ppermute | solution.py:23
  64.9 7.3 %collective-permute-start.20 = (bf16[256,128]{1,0:T(8,128)(2,1)S(1)}, bf16[256,128]{1,0:T(8,128)(2,1)S(1)}, u32[]{:S(2)}, u32[]{:S(2)}) collective-permute-start(bf16[256,128]{1,0:T(8,128)(2,1)S(1)} %add_convert_fusion.1), channel_id=1, source_target_pairs={{0,6},{2,0},{4,2},{6,4},{1,7},{3,1},{5,3},{7,5},{8,14},{10,8},{12,... | collective-permute-start | bytes 196616 | tf_op jit(solution)/shard_map/ppermute | solution.py:23
  66.3 7.3 %collective-permute-start.30 = (bf16[1024,128]{1,0:T(8,128)(2,1)S(1)}, bf16[1024,128]{1,0:T(8,128)(2,1)S(1)}, u32[]{:S(2)}, u32[]{:S(2)}) collective-permute-start(bf16[1024,128]{1,0:T(8,128)(2,1)S(1)} %pad_maximum_fusion.1.refs_0_), channel_id=1, source_target_pairs={{0,8},{8,0},{1,9},{9,1},{2,10},{10,2},{3,11},{11,3},{4,12},{12,4},... | collective-permute-start | bytes 786440 | tf_op jit(solution)/shard_map/ppermute | solution.py:23
  70.3 10.7 %collective-permute-start.31 = (bf16[1024,128]{1,0:T(8,128)(2,1)S(1)}, bf16[1024,128]{1,0:T(8,128)(2,1)S(1)}, u32[]{:S(2)}, u32[]{:S(2)}) collective-permute-start(bf16[1024,128]{1,0:T(8,128)(2,1)S(1)} %collective-permute-done.28.refs_1_), channel_id=1, source_target_pairs={{0,8},{8,0},{1,9},{9,1},{2,10},{10,2},{3,11},{11,3},{4,12},{12,4},... | collective-permute-start | bytes 786440 | tf_op jit(solution)/shard_map/ppermute | solution.py:23
  70.3 6.4 %collective-permute-start.34 = (bf16[1024,128]{1,0:T(8,128)(2,1)S(1)}, bf16[1024,128]{1,0:T(8,128)(2,1)S(1)}, u32[]{:S(2)}, u32[]{:S(2)}) collective-permute-start(bf16[1024,128]{1,0:T(8,128)(2,1)S(1)} %collective-permute-done.28.refs_1_), channel_id=1, source_target_pairs={{0,16},{16,0},{1,17},{17,1},{2,18},{18,2},{3,19},{19,3},{4,20},{20... | collective-permute-start | bytes 786440 | tf_op jit(solution)/shard_map/ppermute | solution.py:23
  70.6 10.4 %collective-permute-start.32 = (bf16[1024,128]{1,0:T(8,128)(2,1)S(1)}, bf16[1024,128]{1,0:T(8,128)(2,1)S(1)}, u32[]{:S(2)}, u32[]{:S(2)}) collective-permute-start(bf16[1024,128]{1,0:T(8,128)(2,1)S(1)} %collective-permute-done.29.refs_2_), channel_id=1, source_target_pairs={{0,8},{8,0},{1,9},{9,1},{2,10},{10,2},{3,11},{11,3},{4,12},{12,4},... | collective-permute-start | bytes 786440 | tf_op jit(solution)/shard_map/ppermute | solution.py:23
  72.3 11.2 %collective-permute-start.21 = (bf16[1024,128]{1,0:T(8,128)(2,1)S(1)}, bf16[1024,128]{1,0:T(8,128)(2,1)S(1)}, u32[]{:S(2)}, u32[]{:S(2)}) collective-permute-start(bf16[1024,128]{1,0:T(8,128)(2,1)S(1)} %pad_maximum_fusion.refs_2_), channel_id=1, source_target_pairs={{0,16},{16,0},{1,17},{17,1},{2,18},{18,2},{3,19},{19,3},{4,20},{20... | collective-permute-start | bytes 786440 | tf_op jit(solution)/shard_map/ppermute | solution.py:23
  73.6 11.7 %collective-permute-start.36 = (bf16[1024,128]{1,0:T(8,128)(2,1)S(1)}, bf16[1024,128]{1,0:T(8,128)(2,1)S(1)}, u32[]{:S(2)}, u32[]{:S(2)}) collective-permute-start(bf16[1024,128]{1,0:T(8,128)(2,1)S(1)} %pad_maximum_fusion.refs_2_), channel_id=1, source_target_pairs={{0,1},{1,0},{2,3},{3,2},{4,5},{5,4},{6,7},{7,6},{8,9},{9,8},{10,11... | collective-permute-start | bytes 786440 | tf_op jit(solution)/shard_map/ppermute | solution.py:23
  76.7 9.1 %collective-permute-start.35 = (bf16[1024,128]{1,0:T(8,128)(2,1)S(1)}, bf16[1024,128]{1,0:T(8,128)(2,1)S(1)}, u32[]{:S(2)}, u32[]{:S(2)}) collective-permute-start(bf16[1024,128]{1,0:T(8,128)(2,1)S(1)} %collective-permute-done.34.refs_0_), channel_id=1, source_target_pairs={{0,8},{8,0},{1,9},{9,1},{2,10},{10,2},{3,11},{11,3},{4,12},{12,4},... | collective-permute-start | bytes 786440 | tf_op jit(solution)/shard_map/ppermute | solution.py:23
  83.5 6.7 %collective-permute-start.33 = (bf16[1024,128]{1,0:T(8,128)(2,1)S(1)}, bf16[1024,128]{1,0:T(8,128)(2,1)S(1)}, u32[]{:S(2)}, u32[]{:S(2)}) collective-permute-start(bf16[1024,128]{1,0:T(8,128)(2,1)S(1)} %collective-permute-done.21.refs_4_), channel_id=1, source_target_pairs={{0,1},{1,0},{2,3},{3,2},{4,5},{5,4},{6,7},{7,6},{8,9},{9,8},{10,11... | collective-permute-start | bytes 786440 | tf_op jit(solution)/shard_map/ppermute | solution.py:23
  83.9 8.3 %collective-permute-start.38 = (bf16[1024,128]{1,0:T(8,128)(2,1)S(1)}, bf16[1024,128]{1,0:T(8,128)(2,1)S(1)}, u32[]{:S(2)}, u32[]{:S(2)}) collective-permute-start(bf16[1024,128]{1,0:T(8,128)(2,1)S(1)} %pad_maximum_fusion.refs_2_), channel_id=1, source_target_pairs={{0,8},{8,0},{1,9},{9,1},{2,10},{10,2},{3,11},{11,3},{4,12},{12,4},... | collective-permute-start | bytes 786440 | tf_op jit(solution)/shard_map/ppermute | solution.py:23
  85.3 6.9 %collective-permute-start.40 = (bf16[1024,128]{1,0:T(8,128)(2,1)S(1)}, bf16[1024,128]{1,0:T(8,128)(2,1)S(1)}, u32[]{:S(2)}, u32[]{:S(2)}) collective-permute-start(bf16[1024,128]{1,0:T(8,128)(2,1)S(1)} %collective-permute-done.21.refs_4_), channel_id=1, source_target_pairs={{0,8},{8,0},{1,9},{9,1},{2,10},{10,2},{3,11},{11,3},{4,12},{12,4},... | collective-permute-start | bytes 786440 | tf_op jit(solution)/shard_map/ppermute | solution.py:23
  85.3 6.9 %collective-permute-start.39 = (bf16[1024,128]{1,0:T(8,128)(2,1)S(1)}, bf16[1024,128]{1,0:T(8,128)(2,1)S(1)}, u32[]{:S(2)}, u32[]{:S(2)}) collective-permute-start(bf16[1024,128]{1,0:T(8,128)(2,1)S(1)} %collective-permute-done.36.refs_3_), channel_id=1, source_target_pairs={{0,8},{8,0},{1,9},{9,1},{2,10},{10,2},{3,11},{11,3},{4,12},{12,4},... | collective-permute-start | bytes 786440 | tf_op jit(solution)/shard_map/ppermute | solution.py:23
  (10 other events, 29.6 us)

commit v9 on v8

--- a/solution.py
+++ b/solution.py
@@ -40,25 +40,30 @@
 
 
 def slopes_kernel(sizes, offsets, where_ref, *refs):
-    layers, height, across, width, share, rows, decks, outs = sizes
+    layers, height, across, width, rows = sizes
     members = len(offsets)
     blocks, edges = refs[:members], refs[members : 2 * members]
-    turned, own, field, edge, *sources = refs[2 * members :]
+    turned, phi, field, edge, mine, sem, *sources = refs[2 * members :]
     count = members * layers * height * across
     depth = members // 2 * layers
     piece = 4 * count // depth
     parts = count // piece
 
+    fetch = pltpu.make_async_copy(blocks[0], mine, sem)
+    fetch.start()
     field[:2] = jnp.zeros_like(field[:2])
     field[members + 2 :] = jnp.zeros_like(field[members + 2 :])
     for n in range(members):
         at = member(where_ref, rows, offsets[n])
-        field[at + 2] = blocks[n][...].astype(jnp.float32)
         edge[at] = edges[n][...].astype(jnp.float32)
+        if n > 0:
+            field[at + 2] = blocks[n][...].astype(jnp.float32)
+    fetch.wait()
+    field[member(where_ref, rows, offsets[0]) + 2] = mine[...].astype(jnp.float32)
 
     index = lax.broadcasted_iota(jnp.int32, (across, width), 0)
     weight_row = edge.shape[2] - across
-    row, column = (lax.broadcasted_iota(jnp.int32, (width, width), d) for d in range(2))
+    row, column = (lax.broadcasted_iota(jnp.int32, (2 * width, 2 * width), d) for d in range(2))
     eye = (row == column).astype(jnp.bfloat16)
 
     def stencil(x, b, source):
@@ -108,63 +113,59 @@
                     to = pl.ds(pl.multiple_of(start, TILE), TILE)
                     for q in range(4):
                         value = jnp.concatenate([f[q] for f in found], axis=0)
-                        source[q, to, :] = value.astype(jnp.bfloat16)
+                        columns = slice(q % 2 * width, (q % 2 + 1) * width)
+                        source[q // 2, to, columns] = value.astype(jnp.bfloat16)
                     found = []
 
     def turn(x, b, source):
-        q, part = lax.div(x, parts), lax.rem(x, parts)
+        both, part = lax.div(x, parts), lax.rem(x, parts)
         at = pl.ds(pl.multiple_of(part * piece, piece), piece)
-        value = lax.dot_general(eye, source[q, at, :], TURNED, preferred_element_type=jnp.float32)
-        turned[q, b, :, at] = value.astype(jnp.bfloat16)
+        value = lax.dot_general(eye, source[both, at, :], TURNED, preferred_element_type=jnp.float32)
+        for n in range(2):
+            turned[2 * both + n, b, :, at] = value[n * width : (n + 1) * width].astype(jnp.bfloat16)
+
+        @pl.when(both == 0)
+        def _():
+            phi[b, :, at] = value[:width]
 
     for step in range(4):
 
-        def one_layer(x, _):
+        def two_layers(x, _):
             if step < 3:
-                stencil(x, step, sources[step % 2])
+                stencil(2 * x, step, sources[step % 2])
+                stencil(2 * x + 1, step, sources[step % 2])
             if step > 0:
                 turn(x, step - 1, sources[(step - 1) % 2])
             return 0
 
-        lax.fori_loop(0, depth, one_layer, 0)
-
-    row, column = (
-        lax.broadcasted_iota(jnp.int32, (CHUNKS * share * TILE, width), d) for d in range(2)
-    )
-    chunk = sum((row >= n * share * TILE).astype(jnp.int32) for n in range(1, CHUNKS))
-    mode = lax.shift_right_logical(row, TILE.bit_length() - 1) - chunk * share
-    mode = mode + (where_ref[3] * (share // decks) if outs > 1 else 0)
-    mode = jnp.where(mode >= share, mode - share, mode)
-    mode = mode + (member(where_ref, rows, (0, 0, 0)) * CHUNKS + chunk) * share
-    pick = (column == mode).astype(jnp.bfloat16)
-    for b in range(3):
-        value = jnp.dot(pick, turned[0, b], preferred_element_type=jnp.float32)
-        own[b] = value.astype(jnp.bfloat16)
-
-
-def plane_slopes(where, blocks, edges, offsets, share, rows, decks, outs):
+        lax.fori_loop(0, depth // 2, two_layers, 0)
+
+
+def plane_slopes(where, blocks, edges, offsets, rows):
     layers, height, comps, across, width = blocks[0].shape
     members = len(blocks)
     count = members * layers * height * across
-    sizes = (layers, height, across, width, share, rows, decks, outs)
-    vmem = pl.BlockSpec(memory_space=pltpu.VMEM)
+    sizes = (layers, height, across, width, rows)
+    vmem, anywhere = (pl.BlockSpec(memory_space=m) for m in (pltpu.VMEM, pl.ANY))
     results = [
         ((4, comps, width, count), jnp.bfloat16),
-        ((comps, CHUNKS * share * TILE, count), jnp.bfloat16),
+        ((comps, width, count), jnp.float32),
     ]
     scratch = [
         ((members + 4,) + blocks[0].shape, jnp.float32),
         ((members,) + edges[0].shape, jnp.float32),
-        ((4, count, width), jnp.bfloat16),
-        ((4, count, width), jnp.bfloat16),
+        (blocks[0].shape, blocks[0].dtype),
+        ((2, count, 2 * width), jnp.bfloat16),
+        ((2, count, 2 * width), jnp.bfloat16),
     ]
     inputs = [(v.shape, v.dtype) for v in blocks + edges]
+    buffers = [pltpu.VMEM(*shape) for shape in scratch]
     return pl.pallas_call(
         functools.partial(slopes_kernel, sizes, offsets),
         out_shape=[jax.ShapeDtypeStruct(*result) for result in results],
-        in_specs=[pl.BlockSpec(memory_space=pltpu.SMEM)] + [vmem] * (2 * members),
+        in_specs=[pl.BlockSpec(memory_space=pltpu.SMEM), anywhere] + [vmem] * (2 * members - 1),
         out_specs=[vmem] * len(results),
-        scratch_shapes=[pltpu.VMEM(*shape) for shape in scratch],
+        scratch_shapes=buffers[:3] + [pltpu.SemaphoreType.DMA] + buffers[3:],
         compiler_params=pltpu.CompilerParams(vmem_limit_bytes=grant(results + scratch + inputs)),
         cost_estimate=pl.CostEstimate(
             flops=2 * 12 * count * width * width, bytes_accessed=2**22, transcendentals=0
@@ -172,63 +173,68 @@
     )(where, *blocks, *edges)
 
 
-def terms_kernel(share, chunk, turned, own, *refs):
-    *out_refs, even, odd = refs
+def terms_kernel(share, chunk, rows, decks, where_ref, turned, phi, *refs):
+    out_refs = [ref for ref in refs if len(ref.shape) == 2]
+    own, *quads = refs[len(out_refs) :]
     outs = len(out_refs)
     width, count = turned.shape[2:]
-    first = chunk * share
-    for pair in range(share // 2):
-        quad = (even, odd)[pair % 2]
+    base = (member(where_ref, rows, (0, 0, 0)) * CHUNKS + chunk) * share
+    first = where_ref[3] * (share // decks) if outs > 1 else 0
+    together = min(2, share // 2)
+    for i in range(share):
+        mode = base + lax.rem(i + first, share)
+        for b in range(3):
+            own[b, i] = jnp.broadcast_to(phi[b, pl.ds(mode, 1), :], (TILE, count))
+    for group in range(share // 2 // together):
+        modes = range(group * 2 * together, (group + 1) * 2 * together)
+        held = [quads[(group * together + p) % len(quads)] for p in range(together)]
         for a in range(3):
             for start in range(0, count, LANES):
                 lanes = slice(start, start + LANES)
-                spread = [
-                    [
-                        own[b, (first + 2 * pair + h) * TILE : (first + 2 * pair + h + 1) * TILE, lanes]
-                        for b in range(3)
+                spread = [[own[b, mode, :, lanes] for b in range(3)] for mode in modes]
+                for k in range(0, width, TILE):
+                    slope = [
+                        turned[1 + a, b, k : k + TILE, lanes].astype(jnp.float32) for b in range(3)
                     ]
-                    for h in range(2)
-                ]
-                for k in range(0, width, TILE):
-                    slope = [turned[1 + a, b, k : k + TILE, lanes] for b in range(3)]
-                    for h in range(2):
-                        value = spread[h][0] * slope[0]
-                        value = value + spread[h][1] * slope[1]
-                        value = value + spread[h][2] * slope[2]
-                        quad[a, h * width + k : h * width + k + TILE, lanes] = value
-        total = sum(
-            lax.dot_general(turned[0, a], quad[a], TURNED, preferred_element_type=jnp.float32)
-            for a in range(3)
-        )
-        for h in range(2):
-            start = (2 * pair + h) * width
-            out_ref = out_refs[start * outs // (share * width)]
-            start = start % (share * width // outs)
-            out_ref[start : start + width, :] = total[:, h * width : (h + 1) * width].astype(
-                out_ref.dtype
+                    for i, row in enumerate(spread):
+                        value = row[0] * slope[0] + row[1] * slope[1] + row[2] * slope[2]
+                        at = i % 2 * width + k
+                        held[i // 2][a, at : at + TILE, lanes] = value.astype(jnp.bfloat16)
+        for p in range(together):
+            total = sum(
+                lax.dot_general(
+                    turned[0, a], held[p][a], TURNED, preferred_element_type=jnp.float32
+                )
+                for a in range(3)
             )
-
-
-def plane_terms(turned, own, chunk, share, outs):
+            for h in range(2):
+                start = (2 * (group * together + p) + h) * width
+                out_ref = out_refs[start * outs // (share * width)]
+                start = start % (share * width // outs)
+                out_ref[start : start + width, :] = total[:, h * width : (h + 1) * width].astype(
+                    out_ref.dtype
+                )
+
+
+def plane_terms(where, turned, phi, chunk, share, rows, decks, outs):
     width, count = turned.shape[2:]
     vmem = pl.BlockSpec(memory_space=pltpu.VMEM)
     dtypes = [jnp.float32 if outs > 1 and n == 0 else jnp.bfloat16 for n in range(outs)]
     results = [((share * width // outs, width), t) for t in dtypes]
-    second = 2 if share > 2 else 1
-    scratch = [((3, 2 * width, count), jnp.bfloat16)] * second
-    scratch += [((TILE, LANES), jnp.bfloat16)] * (2 - second)
-    inputs = [(v.shape, v.dtype) for v in (turned, own)]
+    scratch = [((3, share, TILE, count), jnp.float32)]
+    scratch += [((3, 2 * width, count), jnp.bfloat16)] * min(4, share // 2)
+    inputs = [(v.shape, v.dtype) for v in (turned, phi)]
     return pl.pallas_call(
-        functools.partial(terms_kernel, share, chunk),
+        functools.partial(terms_kernel, share, chunk, rows, decks),
         out_shape=[jax.ShapeDtypeStruct(*result) for result in results],
-        in_specs=[vmem] * 2,
+        in_specs=[pl.BlockSpec(memory_space=pltpu.SMEM)] + [vmem] * 2,
         out_specs=[vmem] * outs,
         scratch_shapes=[pltpu.VMEM(*shape) for shape in scratch],
         compiler_params=pltpu.CompilerParams(vmem_limit_bytes=grant(results + scratch + inputs)),
         cost_estimate=pl.CostEstimate(
             flops=2 * share * width * width * count * 3, bytes_accessed=2**22, transcendentals=0
         ),
-    )(turned, own)
+    )(where, turned, phi)
 
 
 def place_kernel(plan, pieces, given, where_ref, *refs):
@@ -354,8 +360,8 @@
     edges = spread_cores(spread_near(edge_piece(outer, cell_weight)))
     offsets = list(blocks)
     blocks, edges = ([d[o] for o in offsets] for d in (blocks, edges))
-    slopes = plane_slopes(where, blocks, edges, offsets, share, rows, decks, outs)
-    terms = [plane_terms(*slopes, n, share, outs) for n in range(CHUNKS)]
+    slopes = plane_slopes(where, blocks, edges, offsets, rows)
+    terms = [plane_terms(where, *slopes, n, share, rows, decks, outs) for n in range(CHUNKS)]
 
     def put_all(result, chosen):
         return put(where, result, width * width, rows, decks, chosen)
@@ -365,32 +371,16 @@
     for n in range(CHUNKS):
         mine = sum_over_decks(terms[n], decks)
         piece = jnp.concatenate([mine] + [rotate(mine, "deck", r) for r in range(1, decks)], axis=0)
-        across = rotate(piece, "side")
-        along = [rotate(piece, "row", r) for r in range(1, rows)]
-        near = [(n, (0, 0, 0), piece), (n, (0, 0, 1), across)]
-        near += [(n, (r, 0, 0), v) for r, v in enumerate(along, 1)]
-        if n == 0:
-            diagonal = [rotate(across, "row", r) for r in range(1, rows)]
-        else:
+        got = spread_near(piece)
+        near = [(n, (r, 0, s), v) for (r, s), v in got.items()]
+        if n > 0:
             result = put_all(result, waiting.pop(0))
-            along, result = lax.optimization_barrier((along, result))
-            diagonal = [rotate(v, "side") for v in along]
-        near_core = [(n, (r, 1, s), rotate(v, "core")) for _, (r, _, s), v in near]
-        if n == CHUNKS - 1:
-            result = put_all(result, waiting.pop(0) + near)
-            diagonal, result = lax.optimization_barrier((diagonal, result))
-            waiting.append(near_core)
-        else:
-            waiting.append(near + near_core)
-        far = [(n, (r, 0, 1), v) for r, v in enumerate(diagonal, 1)]
-        far_core = [(n, (r, 1, 1), rotate(v, "core")) for r, v in enumerate(diagonal, 1)]
-        if n == CHUNKS - 1:
-            waiting[-1] += far
-            waiting.append(far_core)
-        else:
-            waiting.append(far + far_core)
-    for chosen in waiting:
-        result = put_all(result, chosen)
+            near, result = lax.optimization_barrier(([v for _, _, v in near], result))
+            near = [(n, (r, 0, s), v) for (r, s), v in zip(got, near)]
+        waiting.append(near + [(n, (r, 1, s), rotate(v, "core")) for _, (r, _, s), v in near])
+    *chosen, last = waiting.pop(0)
+    result = put_all(result, chosen)
+    result = put_all(result, [last])
     return result.reshape(width, width, width)
 
 

time: 96 us -> 99.8 us (1.040)
  waiting for transfers between devices: 13.3 us -> 21.8 us
  Pallas kernels: 26.8 us -> 24 us
  starting transfers between devices: 52.5 us -> 50.1 us
    ppermute x38 -> x36, waiting for transfers between devices: 11.8 us -> 20.3 us  [rotate(): lax.ppermute(value, axis, [(i, (i + by) % count) for i in range(count)])]
    ppermute x38 -> x36, starting transfers between devices: 51.8 us -> 45.8 us  [rotate(): lax.ppermute(value, axis, [(i, (i + by) % count) for i in range(count)])]
    ppermute x2 -> x4, starting transfers between devices: 0.02 us -> 3.68 us  [spread_near(): got[r, 1] = lax.ppermute(piece, DIAGONAL, pairs)]
    pallas_call x1, Pallas kernels: 7.96 us -> 5.78 us  [plane_slopes(): pl.pallas_call(functools.partial(slopes_kernel, sizes, offsets), out_shap...]
    pallas_call x4 -> x3, Pallas kernels: 8.02 us -> 6.84 us  [put(): pl.pallas_call(functools.partial(place_kernel, (rows, decks, line, block,...]
  transfers between devices with their start and end apart: 41 -> 41, of which waited for: 10 -> 13; matrix products, arithmetic and copies ran while one was open for 2% -> 2% of each run, Pallas kernels for 13% -> 11%
where the time goes in v9:
time: 99.8 us; the launch traced here: 99.2 us
  starting transfers between devices  50.1 us (50%)
  Pallas kernels  24 us (24%)
  waiting for transfers between devices  21.8 us (22%)
  other arithmetic  2.01 us (2%)
    ppermute x36, starting transfers between devices, rotate(): lax.ppermute(value, axis, [(i, (i + by) % count) for i in range(count)])  45.8 us
    ppermute x36, waiting for transfers between devices, rotate(): lax.ppermute(value, axis, [(i, (i + by) % count) for i in range(count)])  20.3 us
    pallas_call x2, Pallas kernels, plane_terms(): pl.pallas_call(functools.partial(terms_kernel, share, chunk, rows, decks)...  11.4 us
    pallas_call x3, Pallas kernels, put(): pl.pallas_call(functools.partial(place_kernel, (rows, decks, line, block,...  6.84 us
    pallas_call x1, Pallas kernels, plane_slopes(): pl.pallas_call(functools.partial(slopes_kernel, sizes, offsets), out_shap...  5.78 us
    ppermute x4, starting transfers between devices, spread_near(): got[r, 1] = lax.ppermute(piece, DIAGONAL, pairs)  3.68 us
  transfers between devices with their start and end apart: 41, of which 13 were waited for; matrix products, arithmetic and copies ran while one was open for 2% of the time, Pallas kernels for 11%

profile of v9, /device:TPU:1, one launch (start us, length us, event | category | flops | bytes accessed | tf_op | source)
XLA Modules:
  0.0 99.2 jit_solution(8686560196629846860)
XLA Ops:
  0.0 2.0 %collective-permute-start.2 = (bf16[2,10,3,8,128]{4,3,2,1,0:T(8,128)(2,1)}, bf16[2,10,3,8,128]{4,3,2,1,0:T(8,128)(2,1)S(1)}, u32[]{:S(2)}, u32[]{:S(2)}) collective-permute-start(bf16[2,10,3,8,128]{4,3,2,1,0:T(8,128)(2,1)} %bitcast.7), channel_id=1, source_target_pairs={{0,1},{1,0},{2,3},{3,2},{4,5},{5,4},{6,7},{7,6},{8,9},{9,8},{10,11... | collective-permute-start | bytes 368648 | tf_op jit(solution)/shard_map/ppermute | solution.py:23
  7.0 1.4 %collective-permute-done.4.refs_6_ = bf16[2,10,3,8,128]{4,3,2,1,0:T(8,128)(2,1)S(1)} collective-permute-done((bf16[2,10,3,8,128]{4,3,2,1,0:T(8,128)(2,1)}, bf16[2,10,3,8,128]{4,3,2,1,0:T(8,128)(2,1)S(1)}, u32[]{:S(2)}, u32[]{:S(2)}) %collective-permute-start.4) | collective-permute-done | bytes 122912 | tf_op jit(solution)/shard_map/ppermute | solution.py:325
  8.5 4.4 %collective-permute-start.9 = (bf16[2,32,384]{2,1,0:T(8,128)(2,1)S(1)}, bf16[2,32,384]{2,1,0:T(8,128)(2,1)S(1)}, u32[]{:S(2)}, u32[]{:S(2)}) collective-permute-start(bf16[2,32,384]{2,1,0:T(8,128)(2,1)S(1)} %fusion.1.refs_8_), channel_id=1, source_target_pairs={{0,1},{1,0},{2,3},{3,2},{4,5},{5,4},{6,7},{7,6},{8,9},{9,8},{10,11... | collective-permute-start | bytes 147464 | tf_op jit(solution)/shard_map/ppermute | solution.py:23
  14.2 1.7 %collective-permute-start.8 = (bf16[2,32,384]{2,1,0:T(8,128)(2,1)S(1)}, bf16[2,32,384]{2,1,0:T(8,128)(2,1)S(1)}, u32[]{:S(2)}, u32[]{:S(2)}) collective-permute-start(bf16[2,32,384]{2,1,0:T(8,128)(2,1)S(1)} %fusion.1.refs_8_), channel_id=1, source_target_pairs={{0,8},{8,0},{1,9},{9,1},{2,10},{10,2},{3,11},{11,3},{4,12},{12,4},... | collective-permute-start | bytes 147464 | tf_op jit(solution)/shard_map/ppermute | solution.py:23
  16.4 2.5 %collective-permute-start.6 = (bf16[2,10,3,8,128]{4,3,2,1,0:T(8,128)(2,1)S(1)}, bf16[2,10,3,8,128]{4,3,2,1,0:T(8,128)(2,1)S(1)}, u32[]{:S(2)}, u32[]{:S(2)}) collective-permute-start(bf16[2,10,3,8,128]{4,3,2,1,0:T(8,128)(2,1)S(1)} %collective-permute-done.3.refs_4_), channel_id=1, source_target_pairs={{0,8},{8,0},{1,9},{9,1},{2,10},{10,2},{3,11},{11,3},{4,12},{12,4},... | collective-permute-start | bytes 368648 | tf_op jit(solution)/shard_map/ppermute | solution.py:23
  19.0 1.9 %collective-permute-start.7 = (bf16[2,10,3,8,128]{4,3,2,1,0:T(8,128)(2,1)S(1)}, bf16[2,10,3,8,128]{4,3,2,1,0:T(8,128)(2,1)S(1)}, u32[]{:S(2)}, u32[]{:S(2)}) collective-permute-start(bf16[2,10,3,8,128]{4,3,2,1,0:T(8,128)(2,1)S(1)} %collective-permute-done.4.refs_6_), channel_id=1, source_target_pairs={{0,8},{8,0},{1,9},{9,1},{2,10},{10,2},{3,11},{11,3},{4,12},{12,4},... | collective-permute-start | bytes 368648 | tf_op jit(solution)/shard_map/ppermute | solution.py:23
  23.2 5.8 %shard_map.28 = (bf16[4,3,128,1280]{3,2,1,0:T(8,128)(2,1)S(1)}, f32[3,128,1280]{2,1,0:T(8,128)S(1)}) custom-call(s32[4]{0:T(128)S(1)} %pad_add_fusion.where_ref, bf16[2,10,3,8,128]{4,3,2,1,0:T(8,128)(2,1)S(1)} %bitcast.12, bf16[2,10,3,8,128]{4,3,2,1,0:T(8,128)(2,1)S(1)} %collective-permute-done.refs_1_, ...), custom_call_target="tpu_custom_call" | custom-call | flops 503316480 | bytes 4194304 | tf_op jit(solution)/shard_map/pallas_call | solution.py:163
  29.0 5.7 %shard_map.30 = (f32[256,128]{1,0:T(8,128)S(1)}, bf16[256,128]{1,0:T(8,128)(2,1)S(1)}, bf16[256,128]{1,0:T(8,128)(2,1)S(1)}, bf16[256,128]{1,0:T(8,128)(2,1)S(1)}) custom-call(s32[4]{0:T(128)S(1)} %pad_add_fusion.where_ref, bf16[4,3,128,1280]{3,2,1,0:T(8,128)(2,1)S(1)} %get-tuple-element.28.turned, f32[3,128,1280]{2,1,0:T(8,128)S(1)} %get-tuple-element.29.phi), custom_call_target="tpu_custom_call" | custom-call | flops 1006632960 | bytes 4194304 | tf_op jit(solution)/shard_map/pallas_call | solution.py:227
  34.7 1.3 %collective-permute-start.24 = (bf16[256,128]{1,0:T(8,128)(2,1)S(1)}, bf16[256,128]{1,0:T(8,128)(2,1)S(1)}, u32[]{:S(2)}, u32[]{:S(2)}) collective-permute-start(bf16[256,128]{1,0:T(8,128)(2,1)S(1)} %get-tuple-element.35), channel_id=1, source_target_pairs={{0,2},{2,4},{4,6},{6,0},{1,3},{3,5},{5,7},{7,1},{8,10},{10,12},{12... | collective-permute-start | bytes 196616 | tf_op jit(solution)/shard_map/ppermute | solution.py:23
  37.1 2.3 %collective-permute-start.26 = (bf16[256,128]{1,0:T(8,128)(2,1)S(1)}, bf16[256,128]{1,0:T(8,128)(2,1)S(1)}, u32[]{:S(2)}, u32[]{:S(2)}) collective-permute-start(bf16[256,128]{1,0:T(8,128)(2,1)S(1)} %get-tuple-element.37), channel_id=1, source_target_pairs={{0,6},{2,0},{4,2},{6,4},{1,7},{3,1},{5,3},{7,5},{8,14},{10,8},{12,... | collective-permute-start | bytes 196616 | tf_op jit(solution)/shard_map/ppermute | solution.py:23
  39.7 3.7 %collective-permute-done.25 = bf16[256,128]{1,0:T(8,128)(2,1)S(1)} collective-permute-done((bf16[256,128]{1,0:T(8,128)(2,1)S(1)}, bf16[256,128]{1,0:T(8,128)(2,1)S(1)}, u32[]{:S(2)}, u32[]{:S(2)}) %collective-permute-start.25) | collective-permute-done | bytes 65568 | tf_op jit(solution)/shard_map/ppermute | solution.py:23
  43.4 1.7 %collective-permute-start.27 = (bf16[256,128]{1,0:T(8,128)(2,1)S(1)}, bf16[256,128]{1,0:T(8,128)(2,1)S(1)}, u32[]{:S(2)}, u32[]{:S(2)}) collective-permute-start(bf16[256,128]{1,0:T(8,128)(2,1)S(1)} %add_convert_fusion), channel_id=1, source_target_pairs={{0,2},{2,4},{4,6},{6,0},{1,3},{3,5},{5,7},{7,1},{8,10},{10,12},{12... | collective-permute-start | bytes 196616 | tf_op jit(solution)/shard_map/ppermute | solution.py:23
  45.5 1.8 %collective-permute-start.29 = (bf16[256,128]{1,0:T(8,128)(2,1)S(1)}, bf16[256,128]{1,0:T(8,128)(2,1)S(1)}, u32[]{:S(2)}, u32[]{:S(2)}) collective-permute-start(bf16[256,128]{1,0:T(8,128)(2,1)S(1)} %add_convert_fusion), channel_id=1, source_target_pairs={{0,6},{2,0},{4,2},{6,4},{1,7},{3,1},{5,3},{7,5},{8,14},{10,8},{12,... | collective-permute-start | bytes 196616 | tf_op jit(solution)/shard_map/ppermute | solution.py:23
  47.3 5.7 %shard_map.29 = (f32[256,128]{1,0:T(8,128)S(1)}, bf16[256,128]{1,0:T(8,128)(2,1)S(1)}, bf16[256,128]{1,0:T(8,128)(2,1)S(1)}, bf16[256,128]{1,0:T(8,128)(2,1)S(1)}) custom-call(s32[4]{0:T(128)S(1)} %pad_add_fusion.where_ref, bf16[4,3,128,1280]{3,2,1,0:T(8,128)(2,1)S(1)} %get-tuple-element.28.turned, f32[3,128,1280]{2,1,0:T(8,128)S(1)} %get-tuple-element.29.phi), custom_call_target="tpu_custom_call" | custom-call | flops 1006632960 | bytes 4194304 | tf_op jit(solution)/shard_map/pallas_call | solution.py:227
  53.1 1.7 %collective-permute-start.16 = (bf16[256,128]{1,0:T(8,128)(2,1)S(1)}, bf16[256,128]{1,0:T(8,128)(2,1)S(1)}, u32[]{:S(2)}, u32[]{:S(2)}) collective-permute-start(bf16[256,128]{1,0:T(8,128)(2,1)S(1)} %get-tuple-element.32), channel_id=1, source_target_pairs={{0,4},{2,6},{4,0},{6,2},{1,5},{3,7},{5,1},{7,3},{8,12},{10,14},{12... | collective-permute-start | bytes 196616 | tf_op jit(solution)/shard_map/ppermute | solution.py:23
  54.7 1.6 %collective-permute-start.17 = (bf16[256,128]{1,0:T(8,128)(2,1)S(1)}, bf16[256,128]{1,0:T(8,128)(2,1)S(1)}, u32[]{:S(2)}, u32[]{:S(2)}) collective-permute-start(bf16[256,128]{1,0:T(8,128)(2,1)S(1)} %get-tuple-element.33), channel_id=1, source_target_pairs={{0,6},{2,0},{4,2},{6,4},{1,7},{3,1},{5,3},{7,5},{8,14},{10,8},{12,... | collective-permute-start | bytes 196616 | tf_op jit(solution)/shard_map/ppermute | solution.py:23
  56.8 1.2 %collective-permute-done.15 = bf16[256,128]{1,0:T(8,128)(2,1)S(1)} collective-permute-done((bf16[256,128]{1,0:T(8,128)(2,1)S(1)}, bf16[256,128]{1,0:T(8,128)(2,1)S(1)}, u32[]{:S(2)}, u32[]{:S(2)}) %collective-permute-start.15) | collective-permute-done | bytes 65568 | tf_op jit(solution)/shard_map/ppermute | solution.py:23
  58.7 3.3 %collective-permute-start.18 = (bf16[256,128]{1,0:T(8,128)(2,1)S(1)}, bf16[256,128]{1,0:T(8,128)(2,1)S(1)}, u32[]{:S(2)}, u32[]{:S(2)}) collective-permute-start(bf16[256,128]{1,0:T(8,128)(2,1)S(1)} %add_convert_fusion.1), channel_id=1, source_target_pairs={{0,2},{2,4},{4,6},{6,0},{1,3},{3,5},{5,7},{7,1},{8,10},{10,12},{12... | collective-permute-start | bytes 196616 | tf_op jit(solution)/shard_map/ppermute | solution.py:23
  62.3 1.3 %collective-permute-start.32 = (bf16[1024,128]{1,0:T(8,128)(2,1)S(1)}, bf16[1024,128]{1,0:T(8,128)(2,1)S(1)}, u32[]{:S(2)}, u32[]{:S(2)}) collective-permute-start(bf16[1024,128]{1,0:T(8,128)(2,1)S(1)} %pad_maximum_fusion.1.refs_0_), channel_id=1, source_target_pairs={{0,17},{1,16},{16,1},{17,0},{2,19},{3,18},{18,3},{19,2},{4,21},{5,... | collective-permute-start | bytes 786440 | tf_op jit(solution)/shard_map/ppermute | solution.py:325
  63.6 2.2 %collective-permute-start.33 = (bf16[1024,128]{1,0:T(8,128)(2,1)S(1)}, bf16[1024,128]{1,0:T(8,128)(2,1)S(1)}, u32[]{:S(2)}, u32[]{:S(2)}) collective-permute-start(bf16[1024,128]{1,0:T(8,128)(2,1)S(1)} %pad_maximum_fusion.1.refs_0_), channel_id=1, source_target_pairs={{0,8},{8,0},{1,9},{9,1},{2,10},{10,2},{3,11},{11,3},{4,12},{12,4},... | collective-permute-start | bytes 786440 | tf_op jit(solution)/shard_map/ppermute | solution.py:23
  65.9 1.7 %collective-permute-start.19 = (bf16[256,128]{1,0:T(8,128)(2,1)S(1)}, bf16[256,128]{1,0:T(8,128)(2,1)S(1)}, u32[]{:S(2)}, u32[]{:S(2)}) collective-permute-start(bf16[256,128]{1,0:T(8,128)(2,1)S(1)} %add_convert_fusion.1), channel_id=1, source_target_pairs={{0,4},{2,6},{4,0},{6,2},{1,5},{3,7},{5,1},{7,3},{8,12},{10,14},{12... | collective-permute-start | bytes 196616 | tf_op jit(solution)/shard_map/ppermute | solution.py:23
  67.6 3.3 %collective-permute-done.19 = bf16[256,128]{1,0:T(8,128)(2,1)S(1)} collective-permute-done((bf16[256,128]{1,0:T(8,128)(2,1)S(1)}, bf16[256,128]{1,0:T(8,128)(2,1)S(1)}, u32[]{:S(2)}, u32[]{:S(2)}) %collective-permute-start.19) | collective-permute-done | bytes 65568 | tf_op jit(solution)/shard_map/ppermute | solution.py:23
  70.9 2.4 %collective-permute-start.20 = (bf16[256,128]{1,0:T(8,128)(2,1)S(1)}, bf16[256,128]{1,0:T(8,128)(2,1)S(1)}, u32[]{:S(2)}, u32[]{:S(2)}) collective-permute-start(bf16[256,128]{1,0:T(8,128)(2,1)S(1)} %add_convert_fusion.1), channel_id=1, source_target_pairs={{0,6},{2,0},{4,2},{6,4},{1,7},{3,1},{5,3},{7,5},{8,14},{10,8},{12,... | collective-permute-start | bytes 196616 | tf_op jit(solution)/shard_map/ppermute | solution.py:23
  73.3 1.3 %collective-permute-done.20 = bf16[256,128]{1,0:T(8,128)(2,1)S(1)} collective-permute-done((bf16[256,128]{1,0:T(8,128)(2,1)S(1)}, bf16[256,128]{1,0:T(8,128)(2,1)S(1)}, u32[]{:S(2)}, u32[]{:S(2)}) %collective-permute-start.20) | collective-permute-done | bytes 65568 | tf_op jit(solution)/shard_map/ppermute | solution.py:23
  74.6 2.2 %collective-permute-start.21 = (bf16[1024,128]{1,0:T(8,128)(2,1)S(1)}, bf16[1024,128]{1,0:T(8,128)(2,1)S(1)}, u32[]{:S(2)}, u32[]{:S(2)}) collective-permute-start(bf16[1024,128]{1,0:T(8,128)(2,1)S(1)} %pad_maximum_fusion.refs_0_), channel_id=1, source_target_pairs={{0,1},{1,0},{2,3},{3,2},{4,5},{5,4},{6,7},{7,6},{8,9},{9,8},{10,11... | collective-permute-start | bytes 786440 | tf_op jit(solution)/shard_map/ppermute | solution.py:23
  76.8 1.9 %collective-permute-start.35 = (bf16[1024,128]{1,0:T(8,128)(2,1)S(1)}, bf16[1024,128]{1,0:T(8,128)(2,1)S(1)}, u32[]{:S(2)}, u32[]{:S(2)}) collective-permute-start(bf16[1024,128]{1,0:T(8,128)(2,1)S(1)} %collective-permute-done.31.refs_2_), channel_id=1, source_target_pairs={{0,8},{8,0},{1,9},{9,1},{2,10},{10,2},{3,11},{11,3},{4,12},{12,4},... | collective-permute-start | bytes 786440 | tf_op jit(solution)/shard_map/ppermute | solution.py:23
  79.0 2.3 %collective-permute-start.23 = (bf16[1024,128]{1,0:T(8,128)(2,1)S(1)}, bf16[1024,128]{1,0:T(8,128)(2,1)S(1)}, u32[]{:S(2)}, u32[]{:S(2)}) collective-permute-start(bf16[1024,128]{1,0:T(8,128)(2,1)S(1)} %pad_maximum_fusion.refs_0_), channel_id=1, source_target_pairs={{0,17},{1,16},{16,1},{17,0},{2,19},{3,18},{18,3},{19,2},{4,21},{5,... | collective-permute-start | bytes 786440 | tf_op jit(solution)/shard_map/ppermute | solution.py:325
  81.4 2.8 %shard_map.31.refs_7_ = f32[16384,128]{1,0:T(8,128)} custom-call(s32[4]{0:T(128)S(1)} %pad_add_fusion.where_ref, bf16[1024,128]{1,0:T(8,128)(2,1)S(1)} %pad_maximum_fusion.1.refs_0_, bf16[1024,128]{1,0:T(8,128)(2,1)S(1)} %collective-permute-done.30.refs_1_, bf16[1024,128]{1,0:T(8,128)(2,1)S(1)} %collective-permute-done.31.refs_2_, ...), custom_call_target="tpu_custom_call" | custom-call | bytes 6291456 | tf_op jit(solution)/shard_map/pallas_call | solution.py:277
  84.2 7.6 %collective-permute-done.22.refs_2_ = bf16[1024,128]{1,0:T(8,128)(2,1)S(1)} collective-permute-done((bf16[1024,128]{1,0:T(8,128)(2,1)S(1)}, bf16[1024,128]{1,0:T(8,128)(2,1)S(1)}, u32[]{:S(2)}, u32[]{:S(2)}) %collective-permute-start.22) | collective-permute-done | bytes 262176 | tf_op jit(solution)/shard_map/ppermute | solution.py:23
  91.8 1.3 %collective-permute-start.38 = (bf16[1024,128]{1,0:T(8,128)(2,1)S(1)}, bf16[1024,128]{1,0:T(8,128)(2,1)S(1)}, u32[]{:S(2)}, u32[]{:S(2)}) collective-permute-start(bf16[1024,128]{1,0:T(8,128)(2,1)S(1)} %pad_maximum_fusion.refs_0_), channel_id=1, source_target_pairs={{0,8},{8,0},{1,9},{9,1},{2,10},{10,2},{3,11},{11,3},{4,12},{12,4},... | collective-permute-start | bytes 786440 | tf_op jit(solution)/shard_map/ppermute | solution.py:23
  95.0 2.6 %shard_map.32.refs_1_ = f32[16384,128]{1,0:T(8,128)} custom-call(s32[4]{0:T(128)S(1)} %pad_add_fusion.where_ref, bf16[1024,128]{1,0:T(8,128)(2,1)S(1)} %pad_maximum_fusion.refs_0_, bf16[1024,128]{1,0:T(8,128)(2,1)S(1)} %collective-permute-done.21.refs_1_, bf16[1024,128]{1,0:T(8,128)(2,1)S(1)} %collective-permute-done.22.refs_2_, ...), custom_call_target="tpu_custom_call", output_to_operand_aliasing={{}: (8, {})} | custom-call | bytes 5505024 | tf_op jit(solution)/shard_map/pallas_call | solution.py:277
  97.7 1.4 %shard_map.33 = f32[16384,128]{1,0:T(8,128)} custom-call(s32[4]{0:T(128)S(1)} %pad_add_fusion.where_ref, bf16[1024,128]{1,0:T(8,128)(2,1)S(1)} %collective-permute-done.37.refs_0_, f32[16384,128]{1,0:T(8,128)} %shard_map.32.refs_1_), custom_call_target="tpu_custom_call", output_to_operand_aliasing={{}: (2, {})} | custom-call | bytes 786432 | tf_op jit(solution)/shard_map/pallas_call | solution.py:277
  (69 shorter events, 14.6 us)
Async XLA Ops:
  0.0 7.0 %collective-permute-start.2 = (bf16[2,10,3,8,128]{4,3,2,1,0:T(8,128)(2,1)}, bf16[2,10,3,8,128]{4,3,2,1,0:T(8,128)(2,1)S(1)}, u32[]{:S(2)}, u32[]{:S(2)}) collective-permute-start(bf16[2,10,3,8,128]{4,3,2,1,0:T(8,128)(2,1)} %bitcast.7), channel_id=1, source_target_pairs={{0,1},{1,0},{2,3},{3,2},{4,5},{5,4},{6,7},{7,6},{8,9},{9,8},{10,11... | collective-permute-start | bytes 368648 | tf_op jit(solution)/shard_map/ppermute | solution.py:23
  2.0 5.0 %collective-permute-start.3 = (bf16[2,10,3,8,128]{4,3,2,1,0:T(8,128)(2,1)}, bf16[2,10,3,8,128]{4,3,2,1,0:T(8,128)(2,1)S(1)}, u32[]{:S(2)}, u32[]{:S(2)}) collective-permute-start(bf16[2,10,3,8,128]{4,3,2,1,0:T(8,128)(2,1)} %bitcast.8), channel_id=1, source_target_pairs={{0,16},{16,0},{1,17},{17,1},{2,18},{18,2},{3,19},{19,3},{4,20},{20... | collective-permute-start | bytes 368648 | tf_op jit(solution)/shard_map/ppermute | solution.py:23
  3.3 5.2 %collective-permute-start.4 = (bf16[2,10,3,8,128]{4,3,2,1,0:T(8,128)(2,1)}, bf16[2,10,3,8,128]{4,3,2,1,0:T(8,128)(2,1)S(1)}, u32[]{:S(2)}, u32[]{:S(2)}) collective-permute-start(bf16[2,10,3,8,128]{4,3,2,1,0:T(8,128)(2,1)} %bitcast.9), channel_id=1, source_target_pairs={{0,17},{1,16},{16,1},{17,0},{2,19},{3,18},{18,3},{19,2},{4,21},{5,... | collective-permute-start | bytes 368648 | tf_op jit(solution)/shard_map/ppermute | solution.py:325
  3.3 13.1 %collective-permute-start = (bf16[2,10,3,8,128]{4,3,2,1,0:T(8,128)(2,1)}, bf16[2,10,3,8,128]{4,3,2,1,0:T(8,128)(2,1)S(1)}, u32[]{:S(2)}, u32[]{:S(2)}) collective-permute-start(bf16[2,10,3,8,128]{4,3,2,1,0:T(8,128)(2,1)} %bitcast.10), channel_id=1, source_target_pairs={{0,8},{8,0},{1,9},{9,1},{2,10},{10,2},{3,11},{11,3},{4,12},{12,4},... | collective-permute-start | bytes 368648 | tf_op jit(solution)/shard_map/ppermute | solution.py:23
  8.5 7.4 %collective-permute-start.9 = (bf16[2,32,384]{2,1,0:T(8,128)(2,1)S(1)}, bf16[2,32,384]{2,1,0:T(8,128)(2,1)S(1)}, u32[]{:S(2)}, u32[]{:S(2)}) collective-permute-start(bf16[2,32,384]{2,1,0:T(8,128)(2,1)S(1)} %fusion.1.refs_8_), channel_id=1, source_target_pairs={{0,1},{1,0},{2,3},{3,2},{4,5},{5,4},{6,7},{7,6},{8,9},{9,8},{10,11... | collective-permute-start | bytes 147464 | tf_op jit(solution)/shard_map/ppermute | solution.py:23
  14.2 4.8 %collective-permute-start.13 = (bf16[2,32,384]{2,1,0:T(8,128)(2,1)S(1)}, bf16[2,32,384]{2,1,0:T(8,128)(2,1)S(1)}, u32[]{:S(2)}, u32[]{:S(2)}) collective-permute-start(bf16[2,32,384]{2,1,0:T(8,128)(2,1)S(1)} %fusion.1.refs_8_), channel_id=1, source_target_pairs={{0,17},{1,16},{16,1},{17,0},{2,19},{3,18},{18,3},{19,2},{4,21},{5,... | collective-permute-start | bytes 147464 | tf_op jit(solution)/shard_map/ppermute | solution.py:325
  14.2 6.7 %collective-permute-start.8 = (bf16[2,32,384]{2,1,0:T(8,128)(2,1)S(1)}, bf16[2,32,384]{2,1,0:T(8,128)(2,1)S(1)}, u32[]{:S(2)}, u32[]{:S(2)}) collective-permute-start(bf16[2,32,384]{2,1,0:T(8,128)(2,1)S(1)} %fusion.1.refs_8_), channel_id=1, source_target_pairs={{0,8},{8,0},{1,9},{9,1},{2,10},{10,2},{3,11},{11,3},{4,12},{12,4},... | collective-permute-start | bytes 147464 | tf_op jit(solution)/shard_map/ppermute | solution.py:23
  15.9 5.0 %collective-permute-start.10 = (bf16[2,32,384]{2,1,0:T(8,128)(2,1)S(1)}, bf16[2,32,384]{2,1,0:T(8,128)(2,1)S(1)}, u32[]{:S(2)}, u32[]{:S(2)}) collective-permute-start(bf16[2,32,384]{2,1,0:T(8,128)(2,1)S(1)} %collective-permute-done.9.refs_10_), channel_id=1, source_target_pairs={{0,8},{8,0},{1,9},{9,1},{2,10},{10,2},{3,11},{11,3},{4,12},{12,4},... | collective-permute-start | bytes 147464 | tf_op jit(solution)/shard_map/ppermute | solution.py:23
  16.4 5.8 %collective-permute-start.5 = (bf16[2,10,3,8,128]{4,3,2,1,0:T(8,128)(2,1)S(1)}, bf16[2,10,3,8,128]{4,3,2,1,0:T(8,128)(2,1)S(1)}, u32[]{:S(2)}, u32[]{:S(2)}) collective-permute-start(bf16[2,10,3,8,128]{4,3,2,1,0:T(8,128)(2,1)S(1)} %collective-permute-done.2.refs_2_), channel_id=1, source_target_pairs={{0,8},{8,0},{1,9},{9,1},{2,10},{10,2},{3,11},{11,3},{4,12},{12,4},... | collective-permute-start | bytes 368648 | tf_op jit(solution)/shard_map/ppermute | solution.py:23
  16.4 5.8 %collective-permute-start.6 = (bf16[2,10,3,8,128]{4,3,2,1,0:T(8,128)(2,1)S(1)}, bf16[2,10,3,8,128]{4,3,2,1,0:T(8,128)(2,1)S(1)}, u32[]{:S(2)}, u32[]{:S(2)}) collective-permute-start(bf16[2,10,3,8,128]{4,3,2,1,0:T(8,128)(2,1)S(1)} %collective-permute-done.3.refs_4_), channel_id=1, source_target_pairs={{0,8},{8,0},{1,9},{9,1},{2,10},{10,2},{3,11},{11,3},{4,12},{12,4},... | collective-permute-start | bytes 368648 | tf_op jit(solution)/shard_map/ppermute | solution.py:23
  34.7 5.0 %collective-permute-start.24 = (bf16[256,128]{1,0:T(8,128)(2,1)S(1)}, bf16[256,128]{1,0:T(8,128)(2,1)S(1)}, u32[]{:S(2)}, u32[]{:S(2)}) collective-permute-start(bf16[256,128]{1,0:T(8,128)(2,1)S(1)} %get-tuple-element.35), channel_id=1, source_target_pairs={{0,2},{2,4},{4,6},{6,0},{1,3},{3,5},{5,7},{7,1},{8,10},{10,12},{12... | collective-permute-start | bytes 196616 | tf_op jit(solution)/shard_map/ppermute | solution.py:23
  36.0 7.3 %collective-permute-start.25 = (bf16[256,128]{1,0:T(8,128)(2,1)S(1)}, bf16[256,128]{1,0:T(8,128)(2,1)S(1)}, u32[]{:S(2)}, u32[]{:S(2)}) collective-permute-start(bf16[256,128]{1,0:T(8,128)(2,1)S(1)} %get-tuple-element.36), channel_id=1, source_target_pairs={{0,4},{2,6},{4,0},{6,2},{1,5},{3,7},{5,1},{7,3},{8,12},{10,14},{12... | collective-permute-start | bytes 196616 | tf_op jit(solution)/shard_map/ppermute | solution.py:23
  37.1 6.2 %collective-permute-start.26 = (bf16[256,128]{1,0:T(8,128)(2,1)S(1)}, bf16[256,128]{1,0:T(8,128)(2,1)S(1)}, u32[]{:S(2)}, u32[]{:S(2)}) collective-permute-start(bf16[256,128]{1,0:T(8,128)(2,1)S(1)} %get-tuple-element.37), channel_id=1, source_target_pairs={{0,6},{2,0},{4,2},{6,4},{1,7},{3,1},{5,3},{7,5},{8,14},{10,8},{12,... | collective-permute-start | bytes 196616 | tf_op jit(solution)/shard_map/ppermute | solution.py:23
  43.4 11.3 %collective-permute-start.27 = (bf16[256,128]{1,0:T(8,128)(2,1)S(1)}, bf16[256,128]{1,0:T(8,128)(2,1)S(1)}, u32[]{:S(2)}, u32[]{:S(2)}) collective-permute-start(bf16[256,128]{1,0:T(8,128)(2,1)S(1)} %add_convert_fusion), channel_id=1, source_target_pairs={{0,2},{2,4},{4,6},{6,0},{1,3},{3,5},{5,7},{7,1},{8,10},{10,12},{12... | collective-permute-start | bytes 196616 | tf_op jit(solution)/shard_map/ppermute | solution.py:23
  45.1 11.2 %collective-permute-start.28 = (bf16[256,128]{1,0:T(8,128)(2,1)S(1)}, bf16[256,128]{1,0:T(8,128)(2,1)S(1)}, u32[]{:S(2)}, u32[]{:S(2)}) collective-permute-start(bf16[256,128]{1,0:T(8,128)(2,1)S(1)} %add_convert_fusion), channel_id=1, source_target_pairs={{0,4},{2,6},{4,0},{6,2},{1,5},{3,7},{5,1},{7,3},{8,12},{10,14},{12... | collective-permute-start | bytes 196616 | tf_op jit(solution)/shard_map/ppermute | solution.py:23
  45.5 10.8 %collective-permute-start.29 = (bf16[256,128]{1,0:T(8,128)(2,1)S(1)}, bf16[256,128]{1,0:T(8,128)(2,1)S(1)}, u32[]{:S(2)}, u32[]{:S(2)}) collective-permute-start(bf16[256,128]{1,0:T(8,128)(2,1)S(1)} %add_convert_fusion), channel_id=1, source_target_pairs={{0,6},{2,0},{4,2},{6,4},{1,7},{3,1},{5,3},{7,5},{8,14},{10,8},{12,... | collective-permute-start | bytes 196616 | tf_op jit(solution)/shard_map/ppermute | solution.py:23
  53.0 5.0 %collective-permute-start.15 = (bf16[256,128]{1,0:T(8,128)(2,1)S(1)}, bf16[256,128]{1,0:T(8,128)(2,1)S(1)}, u32[]{:S(2)}, u32[]{:S(2)}) collective-permute-start(bf16[256,128]{1,0:T(8,128)(2,1)S(1)} %get-tuple-element.31), channel_id=1, source_target_pairs={{0,2},{2,4},{4,6},{6,0},{1,3},{3,5},{5,7},{7,1},{8,10},{10,12},{12... | collective-permute-start | bytes 196616 | tf_op jit(solution)/shard_map/ppermute | solution.py:23
  53.1 4.9 %collective-permute-start.16 = (bf16[256,128]{1,0:T(8,128)(2,1)S(1)}, bf16[256,128]{1,0:T(8,128)(2,1)S(1)}, u32[]{:S(2)}, u32[]{:S(2)}) collective-permute-start(bf16[256,128]{1,0:T(8,128)(2,1)S(1)} %get-tuple-element.32), channel_id=1, source_target_pairs={{0,4},{2,6},{4,0},{6,2},{1,5},{3,7},{5,1},{7,3},{8,12},{10,14},{12... | collective-permute-start | bytes 196616 | tf_op jit(solution)/shard_map/ppermute | solution.py:23
  54.7 3.9 %collective-permute-start.17 = (bf16[256,128]{1,0:T(8,128)(2,1)S(1)}, bf16[256,128]{1,0:T(8,128)(2,1)S(1)}, u32[]{:S(2)}, u32[]{:S(2)}) collective-permute-start(bf16[256,128]{1,0:T(8,128)(2,1)S(1)} %get-tuple-element.33), channel_id=1, source_target_pairs={{0,6},{2,0},{4,2},{6,4},{1,7},{3,1},{5,3},{7,5},{8,14},{10,8},{12,... | collective-permute-start | bytes 196616 | tf_op jit(solution)/shard_map/ppermute | solution.py:23
  56.3 9.5 %collective-permute-start.30 = (bf16[1024,128]{1,0:T(8,128)(2,1)S(1)}, bf16[1024,128]{1,0:T(8,128)(2,1)S(1)}, u32[]{:S(2)}, u32[]{:S(2)}) collective-permute-start(bf16[1024,128]{1,0:T(8,128)(2,1)S(1)} %pad_maximum_fusion.1.refs_0_), channel_id=1, source_target_pairs={{0,1},{1,0},{2,3},{3,2},{4,5},{5,4},{6,7},{7,6},{8,9},{9,8},{10,11... | collective-permute-start | bytes 786440 | tf_op jit(solution)/shard_map/ppermute | solution.py:23
  58.7 7.2 %collective-permute-start.18 = (bf16[256,128]{1,0:T(8,128)(2,1)S(1)}, bf16[256,128]{1,0:T(8,128)(2,1)S(1)}, u32[]{:S(2)}, u32[]{:S(2)}) collective-permute-start(bf16[256,128]{1,0:T(8,128)(2,1)S(1)} %add_convert_fusion.1), channel_id=1, source_target_pairs={{0,2},{2,4},{4,6},{6,0},{1,3},{3,5},{5,7},{7,1},{8,10},{10,12},{12... | collective-permute-start | bytes 196616 | tf_op jit(solution)/shard_map/ppermute | solution.py:23
  62.0 14.8 %collective-permute-start.31 = (bf16[1024,128]{1,0:T(8,128)(2,1)S(1)}, bf16[1024,128]{1,0:T(8,128)(2,1)S(1)}, u32[]{:S(2)}, u32[]{:S(2)}) collective-permute-start(bf16[1024,128]{1,0:T(8,128)(2,1)S(1)} %pad_maximum_fusion.1.refs_0_), channel_id=1, source_target_pairs={{0,16},{16,0},{1,17},{17,1},{2,18},{18,2},{3,19},{19,3},{4,20},{20... | collective-permute-start | bytes 786440 | tf_op jit(solution)/shard_map/ppermute | solution.py:23
  62.3 16.4 %collective-permute-start.32 = (bf16[1024,128]{1,0:T(8,128)(2,1)S(1)}, bf16[1024,128]{1,0:T(8,128)(2,1)S(1)}, u32[]{:S(2)}, u32[]{:S(2)}) collective-permute-start(bf16[1024,128]{1,0:T(8,128)(2,1)S(1)} %pad_maximum_fusion.1.refs_0_), channel_id=1, source_target_pairs={{0,17},{1,16},{16,1},{17,0},{2,19},{3,18},{18,3},{19,2},{4,21},{5,... | collective-permute-start | bytes 786440 | tf_op jit(solution)/shard_map/ppermute | solution.py:325
  63.6 15.2 %collective-permute-start.33 = (bf16[1024,128]{1,0:T(8,128)(2,1)S(1)}, bf16[1024,128]{1,0:T(8,128)(2,1)S(1)}, u32[]{:S(2)}, u32[]{:S(2)}) collective-permute-start(bf16[1024,128]{1,0:T(8,128)(2,1)S(1)} %pad_maximum_fusion.1.refs_0_), channel_id=1, source_target_pairs={{0,8},{8,0},{1,9},{9,1},{2,10},{10,2},{3,11},{11,3},{4,12},{12,4},... | collective-permute-start | bytes 786440 | tf_op jit(solution)/shard_map/ppermute | solution.py:23
  65.9 13.2 %collective-permute-start.34 = (bf16[1024,128]{1,0:T(8,128)(2,1)S(1)}, bf16[1024,128]{1,0:T(8,128)(2,1)S(1)}, u32[]{:S(2)}, u32[]{:S(2)}) collective-permute-start(bf16[1024,128]{1,0:T(8,128)(2,1)S(1)} %collective-permute-done.30.refs_1_), channel_id=1, source_target_pairs={{0,8},{8,0},{1,9},{9,1},{2,10},{10,2},{3,11},{11,3},{4,12},{12,4},... | collective-permute-start | bytes 786440 | tf_op jit(solution)/shard_map/ppermute | solution.py:23
  65.9 5.0 %collective-permute-start.19 = (bf16[256,128]{1,0:T(8,128)(2,1)S(1)}, bf16[256,128]{1,0:T(8,128)(2,1)S(1)}, u32[]{:S(2)}, u32[]{:S(2)}) collective-permute-start(bf16[256,128]{1,0:T(8,128)(2,1)S(1)} %add_convert_fusion.1), channel_id=1, source_target_pairs={{0,4},{2,6},{4,0},{6,2},{1,5},{3,7},{5,1},{7,3},{8,12},{10,14},{12... | collective-permute-start | bytes 196616 | tf_op jit(solution)/shard_map/ppermute | solution.py:23
  70.9 3.7 %collective-permute-start.20 = (bf16[256,128]{1,0:T(8,128)(2,1)S(1)}, bf16[256,128]{1,0:T(8,128)(2,1)S(1)}, u32[]{:S(2)}, u32[]{:S(2)}) collective-permute-start(bf16[256,128]{1,0:T(8,128)(2,1)S(1)} %add_convert_fusion.1), channel_id=1, source_target_pairs={{0,6},{2,0},{4,2},{6,4},{1,7},{3,1},{5,3},{7,5},{8,14},{10,8},{12,... | collective-permute-start | bytes 196616 | tf_op jit(solution)/shard_map/ppermute | solution.py:23
  74.6 9.6 %collective-permute-start.21 = (bf16[1024,128]{1,0:T(8,128)(2,1)S(1)}, bf16[1024,128]{1,0:T(8,128)(2,1)S(1)}, u32[]{:S(2)}, u32[]{:S(2)}) collective-permute-start(bf16[1024,128]{1,0:T(8,128)(2,1)S(1)} %pad_maximum_fusion.refs_0_), channel_id=1, source_target_pairs={{0,1},{1,0},{2,3},{3,2},{4,5},{5,4},{6,7},{7,6},{8,9},{9,8},{10,11... | collective-permute-start | bytes 786440 | tf_op jit(solution)/shard_map/ppermute | solution.py:23
  76.8 4.5 %collective-permute-start.35 = (bf16[1024,128]{1,0:T(8,128)(2,1)S(1)}, bf16[1024,128]{1,0:T(8,128)(2,1)S(1)}, u32[]{:S(2)}, u32[]{:S(2)}) collective-permute-start(bf16[1024,128]{1,0:T(8,128)(2,1)S(1)} %collective-permute-done.31.refs_2_), channel_id=1, source_target_pairs={{0,8},{8,0},{1,9},{9,1},{2,10},{10,2},{3,11},{11,3},{4,12},{12,4},... | collective-permute-start | bytes 786440 | tf_op jit(solution)/shard_map/ppermute | solution.py:23
  78.8 13.1 %collective-permute-start.22 = (bf16[1024,128]{1,0:T(8,128)(2,1)S(1)}, bf16[1024,128]{1,0:T(8,128)(2,1)S(1)}, u32[]{:S(2)}, u32[]{:S(2)}) collective-permute-start(bf16[1024,128]{1,0:T(8,128)(2,1)S(1)} %pad_maximum_fusion.refs_0_), channel_id=1, source_target_pairs={{0,16},{16,0},{1,17},{17,1},{2,18},{18,2},{3,19},{19,3},{4,20},{20... | collective-permute-start | bytes 786440 | tf_op jit(solution)/shard_map/ppermute | solution.py:23
  79.0 12.8 %collective-permute-start.23 = (bf16[1024,128]{1,0:T(8,128)(2,1)S(1)}, bf16[1024,128]{1,0:T(8,128)(2,1)S(1)}, u32[]{:S(2)}, u32[]{:S(2)}) collective-permute-start(bf16[1024,128]{1,0:T(8,128)(2,1)S(1)} %pad_maximum_fusion.refs_0_), channel_id=1, source_target_pairs={{0,17},{1,16},{16,1},{17,0},{2,19},{3,18},{18,3},{19,2},{4,21},{5,... | collective-permute-start | bytes 786440 | tf_op jit(solution)/shard_map/ppermute | solution.py:325
  93.6 4.0 %collective-permute-start.37 = (bf16[1024,128]{1,0:T(8,128)(2,1)S(1)}, bf16[1024,128]{1,0:T(8,128)(2,1)S(1)}, u32[]{:S(2)}, u32[]{:S(2)}) collective-permute-start(bf16[1024,128]{1,0:T(8,128)(2,1)S(1)} %collective-permute-done.23.refs_3_), channel_id=1, source_target_pairs={{0,8},{8,0},{1,9},{9,1},{2,10},{10,2},{3,11},{11,3},{4,12},{12,4},... | collective-permute-start | bytes 786440 | tf_op jit(solution)/shard_map/ppermute | solution.py:23
  (10 other events, 20.3 us)

commit v10 on v9

--- a/solution.py
+++ b/solution.py
@@ -42,27 +42,25 @@
 def slopes_kernel(sizes, offsets, where_ref, *refs):
     layers, height, across, width, rows = sizes
     members = len(offsets)
-    blocks, edges = refs[:members], refs[members : 2 * members]
-    turned, phi, field, edge, mine, sem, *sources = refs[2 * members :]
+    blocks, edges = refs[:members], refs[members : members + 2]
+    turned, phi, field, edge, *sources = refs[members + 2 :]
     count = members * layers * height * across
     depth = members // 2 * layers
     piece = 4 * count // depth
     parts = count // piece
 
-    fetch = pltpu.make_async_copy(blocks[0], mine, sem)
-    fetch.start()
     field[:2] = jnp.zeros_like(field[:2])
     field[members + 2 :] = jnp.zeros_like(field[members + 2 :])
     for n in range(members):
-        at = member(where_ref, rows, offsets[n])
-        edge[at] = edges[n][...].astype(jnp.float32)
-        if n > 0:
-            field[at + 2] = blocks[n][...].astype(jnp.float32)
-    fetch.wait()
-    field[member(where_ref, rows, offsets[0]) + 2] = mine[...].astype(jnp.float32)
+        field[member(where_ref, rows, offsets[n]) + 2] = blocks[n][...].astype(jnp.float32)
+    for c in range(2):
+        for r in range(rows):
+            stream = lax.div(member(where_ref, rows, (r, c, 0)), 2)
+            for h in range(2):
+                upper = lax.rem(where_ref[2] + h, 2)
+                edge[stream, upper] = edges[c][2 * r + h].astype(jnp.float32)
 
     index = lax.broadcasted_iota(jnp.int32, (across, width), 0)
-    weight_row = edge.shape[2] - across
     row, column = (lax.broadcasted_iota(jnp.int32, (2 * width, 2 * width), d) for d in range(2))
     eye = (row == column).astype(jnp.bfloat16)
 
@@ -74,7 +72,8 @@
         for side in range(2):
             here_at, layer = layer_at(0, side)
             at = here_at - 2
-            tile = edge[at, layer, weight_row:, 0:width]
+            stream = lax.div(at, 2)
+            tile = field[here_at, layer, 3 * height]
             weights = tile
             for part in range(1, WEIGHT_PARTS):
                 weights = weights + pltpu.roll(tile, width - part * height, 1)
@@ -84,12 +83,13 @@
                 weight = jnp.broadcast_to(weights[:, z : z + 1], (across, width))
                 twelfth, half = weight * (1.0 / 12.0), weight * 0.5
                 base = 2 * z // across * across
-                here = field[here_at, layer, z, b]
-                along = {step: field[m, l, z, b] for step, (m, l) in beside.items()}
+                here = field[here_at, layer, 3 * z + b]
+                along = {step: field[m, l, 3 * z + b] for step, (m, l) in beside.items()}
                 value_x = 8.0 * (along[1] - along[-1]) - (along[2] - along[-2])
 
-                outer = edge[at, layer, base : base + across, b * width : (b + 1) * width]
-                beyond = field[here_at + 1 - 2 * side, layer, z, b]
+                columns = slice(b * width, (b + 1) * width)
+                outer = edge[stream, side, layer, base : base + across, columns]
+                beyond = field[here_at + 1 - 2 * side, layer, 3 * z + b]
                 if side == 0:
                     prev = pltpu.roll(outer, (across - 2 - (2 * z - base)) % across, 0)
                     after = beyond
@@ -104,9 +104,9 @@
 
                 value_z = jnp.zeros_like(here)
                 if z < height - 1:
-                    value_z = field[here_at, layer, z + 1, b]
+                    value_z = field[here_at, layer, 3 * (z + 1) + b]
                 if z > 0:
-                    value_z = value_z - field[here_at, layer, z - 1, b]
+                    value_z = value_z - field[here_at, layer, 3 * (z - 1) + b]
                 found.append((here, value_x * twelfth, value_y * twelfth, value_z * half))
                 if len(found) * across == TILE:
                     start = ((at * layers + layer) * height + z + 1) * across - TILE
@@ -141,31 +141,30 @@
         lax.fori_loop(0, depth // 2, two_layers, 0)
 
 
-def plane_slopes(where, blocks, edges, offsets, rows):
-    layers, height, comps, across, width = blocks[0].shape
+def plane_slopes(where, blocks, edges, offsets, rows, comps):
+    layers, planes, across, width = blocks[0].shape
+    height = planes // comps
     members = len(blocks)
     count = members * layers * height * across
     sizes = (layers, height, across, width, rows)
-    vmem, anywhere = (pl.BlockSpec(memory_space=m) for m in (pltpu.VMEM, pl.ANY))
+    vmem = pl.BlockSpec(memory_space=pltpu.VMEM)
     results = [
         ((4, comps, width, count), jnp.bfloat16),
         ((comps, width, count), jnp.float32),
     ]
     scratch = [
         ((members + 4,) + blocks[0].shape, jnp.float32),
-        ((members,) + edges[0].shape, jnp.float32),
-        (blocks[0].shape, blocks[0].dtype),
+        ((members // 2, 2) + edges[0].shape[1:], jnp.float32),
         ((2, count, 2 * width), jnp.bfloat16),
         ((2, count, 2 * width), jnp.bfloat16),
     ]
     inputs = [(v.shape, v.dtype) for v in blocks + edges]
-    buffers = [pltpu.VMEM(*shape) for shape in scratch]
     return pl.pallas_call(
         functools.partial(slopes_kernel, sizes, offsets),
         out_shape=[jax.ShapeDtypeStruct(*result) for result in results],
-        in_specs=[pl.BlockSpec(memory_space=pltpu.SMEM), anywhere] + [vmem] * (2 * members - 1),
+        in_specs=[pl.BlockSpec(memory_space=pltpu.SMEM)] + [vmem] * (members + 2),
         out_specs=[vmem] * len(results),
-        scratch_shapes=buffers[:3] + [pltpu.SemaphoreType.DMA] + buffers[3:],
+        scratch_shapes=[pltpu.VMEM(*shape) for shape in scratch],
         compiler_params=pltpu.CompilerParams(vmem_limit_bytes=grant(results + scratch + inputs)),
         cost_estimate=pl.CostEstimate(
             flops=2 * 12 * count * width * width, bytes_accessed=2**22, transcendentals=0
@@ -180,14 +179,14 @@
     width, count = turned.shape[2:]
     base = (member(where_ref, rows, (0, 0, 0)) * CHUNKS + chunk) * share
     first = where_ref[3] * (share // decks) if outs > 1 else 0
-    together = min(2, share // 2)
+    together = min(4, share)
     for i in range(share):
         mode = base + lax.rem(i + first, share)
         for b in range(3):
             own[b, i] = jnp.broadcast_to(phi[b, pl.ds(mode, 1), :], (TILE, count))
-    for group in range(share // 2 // together):
-        modes = range(group * 2 * together, (group + 1) * 2 * together)
-        held = [quads[(group * together + p) % len(quads)] for p in range(together)]
+    for group in range(share // together):
+        modes = range(group * together, (group + 1) * together)
+        quad = quads[group % len(quads)]
         for a in range(3):
             for start in range(0, count, LANES):
                 lanes = slice(start, start + LANES)
@@ -198,22 +197,19 @@
                     ]
                     for i, row in enumerate(spread):
                         value = row[0] * slope[0] + row[1] * slope[1] + row[2] * slope[2]
-                        at = i % 2 * width + k
-                        held[i // 2][a, at : at + TILE, lanes] = value.astype(jnp.bfloat16)
-        for p in range(together):
-            total = sum(
-                lax.dot_general(
-                    turned[0, a], held[p][a], TURNED, preferred_element_type=jnp.float32
-                )
-                for a in range(3)
+                        at = i * width + k
+                        quad[a, at : at + TILE, lanes] = value.astype(jnp.bfloat16)
+        total = sum(
+            lax.dot_general(turned[0, a], quad[a], TURNED, preferred_element_type=jnp.float32)
+            for a in range(3)
+        )
+        for i, mode in enumerate(modes):
+            start = mode * width
+            out_ref = out_refs[start * outs // (share * width)]
+            start = start % (share * width // outs)
+            out_ref[start : start + width, :] = total[:, i * width : (i + 1) * width].astype(
+                out_ref.dtype
             )
-            for h in range(2):
-                start = (2 * (group * together + p) + h) * width
-                out_ref = out_refs[start * outs // (share * width)]
-                start = start % (share * width // outs)
-                out_ref[start : start + width, :] = total[:, h * width : (h + 1) * width].astype(
-                    out_ref.dtype
-                )
 
 
 def plane_terms(where, turned, phi, chunk, share, rows, decks, outs):
@@ -222,7 +218,8 @@
     dtypes = [jnp.float32 if outs > 1 and n == 0 else jnp.bfloat16 for n in range(outs)]
     results = [((share * width // outs, width), t) for t in dtypes]
     scratch = [((3, share, TILE, count), jnp.float32)]
-    scratch += [((3, 2 * width, count), jnp.bfloat16)] * min(4, share // 2)
+    together = min(4, share)
+    scratch += [((3, together * width, count), jnp.bfloat16)] * min(2, share // together)
     inputs = [(v.shape, v.dtype) for v in (turned, phi)]
     return pl.pallas_call(
         functools.partial(terms_kernel, share, chunk, rows, decks),
@@ -292,28 +289,38 @@
     )(where, *values, *given)
 
 
-def outer_rows(cells):
-    across = cells.shape[3]
-    decks = lax.axis_size("deck")
-    rows = jnp.where(lax.axis_index("side") == 1, cells[..., across - 2 :, :], cells[..., :2, :])
-    joints = [(2 * d + 1, 2 * d + 2) for d in range(decks - 1)]
-    return lax.ppermute(rows, SPAN, joints + [(j, i) for i, j in joints])
-
-
-def edge_piece(outer, weight):
-    layers, height, comps, _, width = outer.shape
-    across = weight.shape[1]
-    outer = outer.transpose(0, 1, 3, 2, 4).reshape(layers, 2 * height, comps * width)
+def raw_piece(cells, weight):
+    layers, height, comps, across, width = cells.shape
     parts = []
     for _ in range(WEIGHT_PARTS):
         part = lax.reduce_precision(weight, 8, 7)
         weight = weight - part
         parts.append(part.astype(jnp.bfloat16))
     tile = jnp.concatenate(parts, axis=2)
-    total = pl.cdiv(2 * height + across, TILE) * TILE
-    outer = jnp.pad(outer, ((0, 0), (0, total - across - 2 * height), (0, 0)))
-    tile = jnp.pad(tile, ((0, 0), (0, 0), (0, comps * width - tile.shape[2])))
-    return jnp.concatenate([outer, tile], axis=1)
+    tile = jnp.pad(tile, ((0, 0), (0, 0), (0, width - tile.shape[2])))
+    cells = cells.reshape(layers, height * comps, across, width)
+    return jnp.concatenate([cells, tile[:, None]], axis=1)
+
+
+def outer_rows(cells):
+    layers, height, comps, across, width = cells.shape
+    rows, decks = lax.axis_size("row"), lax.axis_size("deck")
+    ends = jnp.where(lax.axis_index("side") == 1, cells[..., across - 2 :, :], cells[..., :2, :])
+    ends = ends.transpose(0, 1, 3, 2, 4).reshape(layers, 2 * height, comps * width)
+    total = pl.cdiv(2 * height, TILE) * TILE
+    ends = jnp.pad(ends, ((0, 0), (0, total - 2 * height), (0, 0)))
+    found = []
+    for r in range(rows):
+        for other in range(2):
+            pairs = []
+            for i in range(rows):
+                to = (i + r) % rows
+                for d in range(decks - 1):
+                    low, high = 2 * (i * decks + d) + 1, 2 * (i * decks + d + 1)
+                    pairs.append((low, 2 * (to * decks + d + 1) + other))
+                    pairs.append((high, 2 * (to * decks + d) + 1 - other))
+            found.append(lax.ppermute(ends, ("row",) + SPAN, pairs))
+    return jnp.stack(found)
 
 
 def spread_near(piece):
@@ -334,13 +341,11 @@
     return out
 
 
-def sum_over_decks(terms, decks):
+def parts_over_decks(terms, decks):
     if len(terms) > 1:
-        parts = [terms[0]] + [rotate(terms[r], "deck", r) for r in range(1, decks)]
-    else:
-        width = terms[0].shape[1]
-        parts = list(lax.all_to_all(terms[0].reshape(decks, -1, width), "deck", 0, 0))
-    return sum(part.astype(jnp.float32) for part in parts).astype(jnp.bfloat16)
+        return [terms[0]] + [rotate(terms[r], "deck", r) for r in range(1, decks)]
+    width = terms[0].shape[1]
+    return list(lax.all_to_all(terms[0].reshape(decks, -1, width), "deck", 0, 0))
 
 
 def shards(velocity_modes, cell_weight):
@@ -352,35 +357,57 @@
     outs = decks if share % (2 * decks) == 0 else 1
 
     cells = velocity_modes.transpose(0, 2, 3, 1, 4)
+    blocks = spread_cores(spread_near(raw_piece(cells, cell_weight)))
+    offsets = list(blocks)
     outer = outer_rows(cells)
-    near = spread_near(cells)
-    outer, near = lax.optimization_barrier((outer, near))
-    near[(0, 0)] = cells
-    blocks = spread_cores(near)
-    edges = spread_cores(spread_near(edge_piece(outer, cell_weight)))
-    offsets = list(blocks)
-    blocks, edges = ([d[o] for o in offsets] for d in (blocks, edges))
-    slopes = plane_slopes(where, blocks, edges, offsets, rows)
+    edges = [outer, rotate(outer, "core")]
+    slopes = plane_slopes(where, list(blocks.values()), edges, offsets, rows, cells.shape[2])
     terms = [plane_terms(where, *slopes, n, share, rows, decks, outs) for n in range(CHUNKS)]
 
     def put_all(result, chosen):
         return put(where, result, width * width, rows, decks, chosen)
 
+    parts = [parts_over_decks(t, decks) for t in terms]
+    parts[0], parts[1][0] = lax.optimization_barrier((parts[0], parts[1][0]))
+    pieces = []
+    for n in range(CHUNKS):
+        mine = sum(part.astype(jnp.float32) for part in parts[n]).astype(jnp.bfloat16)
+        pieces.append(
+            jnp.concatenate([mine] + [rotate(mine, "deck", r) for r in range(1, decks)], axis=0)
+        )
+
+    def to_core(chosen):
+        return [(n, (r, 1, s), rotate(v, "core")) for n, (r, _, s), v in chosen]
+
     result = None
-    waiting = []
+    near, far = [], []
+    for n, piece in enumerate(pieces):
+        across = rotate(piece, "side")
+        along = [rotate(piece, "row", r) for r in range(1, rows)]
+        near.append([piece, across] + along)
     for n in range(CHUNKS):
-        mine = sum_over_decks(terms[n], decks)
-        piece = jnp.concatenate([mine] + [rotate(mine, "deck", r) for r in range(1, decks)], axis=0)
-        got = spread_near(piece)
-        near = [(n, (r, 0, s), v) for (r, s), v in got.items()]
         if n > 0:
-            result = put_all(result, waiting.pop(0))
-            near, result = lax.optimization_barrier(([v for _, _, v in near], result))
-            near = [(n, (r, 0, s), v) for (r, s), v in zip(got, near)]
-        waiting.append(near + [(n, (r, 1, s), rotate(v, "core")) for _, (r, _, s), v in near])
-    *chosen, last = waiting.pop(0)
-    result = put_all(result, chosen)
-    result = put_all(result, [last])
+            near[n], result = lax.optimization_barrier((near[n], result))
+        piece, across, *along = near[n]
+        if n % 2 == 0:
+            diagonal = [rotate(across, "row", r) for r in range(1, rows)]
+        else:
+            diagonal = [rotate(v, "side") for v in along]
+        if n < CHUNKS - 1:
+            near[n], near[n + 1][0] = lax.optimization_barrier((near[n], near[n + 1][0]))
+        chosen = [(n, (0, 0, 0), near[n][0]), (n, (0, 0, 1), near[n][1])]
+        chosen += [(n, (r, 0, 0), v) for r, v in enumerate(near[n][2:], 1)]
+        cores = to_core(chosen)
+        if n < CHUNKS - 1:
+            result = put_all(result, chosen + cores)
+            far = [(n, (r, 0, 1), v) for r, v in enumerate(diagonal, 1)]
+            far += to_core(far)
+        else:
+            result = put_all(result, far + chosen)
+            diagonal, result = lax.optimization_barrier((diagonal, result))
+            far = [(n, (r, 0, 1), v) for r, v in enumerate(diagonal, 1)]
+            result = put_all(result, cores + far)
+            result = put_all(result, to_core(far))
     return result.reshape(width, width, width)
 
 

time: 99.8 us -> 98.4 us (0.986)
  waiting for transfers between devices: 21.8 us -> 19.6 us
  Pallas kernels: 24 us -> 25 us
    ppermute x36 -> x33, starting transfers between devices: 45.8 us -> 34.8 us  [rotate(): lax.ppermute(value, axis, [(i, (i + by) % count) for i in range(count)])]
    ppermute x4 -> x1, starting transfers between devices: 3.68 us -> 11.4 us  [spread_near(): got[r, 1] = lax.ppermute(piece, DIAGONAL, pairs)]
    ppermute x1 -> x4, starting transfers between devices: 0.66 us -> 3.91 us  [outer_rows(): found.append(lax.ppermute(ends, ('row',) + SPAN, pairs))]
    ppermute x4 -> x1, waiting for transfers between devices: 1.45 us -> 0.01 us  [spread_near(): got[r, 1] = lax.ppermute(piece, DIAGONAL, pairs)]
    pallas_call x3 -> x4, Pallas kernels: 6.84 us -> 8.02 us  [put(): pl.pallas_call(functools.partial(place_kernel, (rows, decks, line, block,...]
    select_n x1 -> x0, other arithmetic: 1.03 us -> none  [outer_rows(): jnp.where(lax.axis_index('side') == 1, cells[..., across - 2:, :], cells[...]
    transpose x0 -> x1, other arithmetic: none -> 1.03 us  [outer_rows(): ends.transpose(0, 1, 3, 2, 4).reshape(layers, 2 * height, comps * width)]
    ppermute x36 -> x33, waiting for transfers between devices: 20.3 us -> 19.6 us  [rotate(): lax.ppermute(value, axis, [(i, (i + by) % count) for i in range(count)])]
  transfers between devices with their start and end apart: 41 -> 38, of which waited for: 13 -> 10; matrix products, arithmetic and copies ran while one was open for 2% -> 2% of each run, Pallas kernels for 11% -> 13%
where the time goes in v10:
time: 98.4 us; the launch traced here: 98.1 us
  starting transfers between devices  50.1 us (51%)
  Pallas kernels  25 us (25%)
  waiting for transfers between devices  19.6 us (20%)
  other arithmetic  2.95 us (3%)
    ppermute x33, starting transfers between devices, rotate(): lax.ppermute(value, axis, [(i, (i + by) % count) for i in range(count)])  34.8 us
    ppermute x33, waiting for transfers between devices, rotate(): lax.ppermute(value, axis, [(i, (i + by) % count) for i in range(count)])  19.6 us
    pallas_call x2, Pallas kernels, plane_terms(): pl.pallas_call(functools.partial(terms_kernel, share, chunk, rows, decks)...  11.5 us
    ppermute x1, starting transfers between devices, spread_near(): got[r, 1] = lax.ppermute(piece, DIAGONAL, pairs)  11.4 us
    pallas_call x4, Pallas kernels, put(): pl.pallas_call(functools.partial(place_kernel, (rows, decks, line, block,...  8.02 us
    pallas_call x1, Pallas kernels, plane_slopes(): pl.pallas_call(functools.partial(slopes_kernel, sizes, offsets), out_shap...  5.57 us
    ppermute x4, starting transfers between devices, outer_rows(): found.append(lax.ppermute(ends, ('row',) + SPAN, pairs))  3.91 us
  transfers between devices with their start and end apart: 38, of which 10 were waited for; matrix products, arithmetic and copies ran while one was open for 2% of the time, Pallas kernels for 13%

profile of v10, /device:TPU:1, one launch (start us, length us, event | category | flops | bytes accessed | tf_op | source)
XLA Modules:
  0.0 98.1 jit_solution(10046284201334074130)
XLA Ops:
  1.1 1.3 %collective-permute-start.10 = (bf16[2,32,384]{2,1,0:T(8,128)(2,1)S(1)}, bf16[2,32,384]{2,1,0:T(8,128)(2,1)S(1)}, u32[]{:S(2)}, u32[]{:S(2)}) collective-permute-start(bf16[2,32,384]{2,1,0:T(8,128)(2,1)S(1)} %pad.9), channel_id=1, source_target_pairs={{1,19},{2,16},{3,21},{4,18},{5,23},{6,20},{17,3},{18,0},{19,5},{20... | collective-permute-start | bytes 147464 | tf_op jit(solution)/shard_map/ppermute | solution.py:322
  3.1 1.3 %collective-permute-start.8 = (bf16[2,32,384]{2,1,0:T(8,128)(2,1)S(1)}, bf16[2,32,384]{2,1,0:T(8,128)(2,1)S(1)}, u32[]{:S(2)}, u32[]{:S(2)}) collective-permute-start(bf16[2,32,384]{2,1,0:T(8,128)(2,1)S(1)} %pad.9), channel_id=1, source_target_pairs={{1,3},{2,0},{3,5},{4,2},{5,7},{6,4},{17,19},{18,16},{19,21},{20,18... | collective-permute-start | bytes 147464 | tf_op jit(solution)/shard_map/ppermute | solution.py:322
  6.8 11.4 %collective-permute-start.5 = (bf16[2,31,8,128]{3,2,1,0:T(8,128)(2,1)S(1)}, bf16[2,31,8,128]{3,2,1,0:T(8,128)(2,1)S(1)}, u32[]{:S(2)}, u32[]{:S(2)}) collective-permute-start(bf16[2,31,8,128]{3,2,1,0:T(8,128)(2,1)S(1)} %pad_maximum_fusion.3.refs_0_), channel_id=1, source_target_pairs={{0,17},{1,16},{16,1},{17,0},{2,19},{3,18},{18,3},{19,2},{4,21},{5,... | collective-permute-start | bytes 380936 | tf_op jit(solution)/shard_map/ppermute | solution.py:332
  18.5 2.1 %collective-permute-start.11 = (bf16[4,2,32,384]{3,2,1,0:T(8,128)(2,1)S(1)}, bf16[4,2,32,384]{3,2,1,0:T(8,128)(2,1)S(1)}, u32[]{:S(2)}, u32[]{:S(2)}) collective-permute-start(bf16[4,2,32,384]{3,2,1,0:T(8,128)(2,1)S(1)} %pad_maximum_fusion.2.refs_8_), channel_id=1, source_target_pairs={{0,8},{8,0},{1,9},{9,1},{2,10},{10,2},{3,11},{11,3},{4,12},{12,4},... | collective-permute-start | bytes 589832 | tf_op jit(solution)/shard_map/ppermute | solution.py:23
  20.8 2.5 %collective-permute-start.6 = (bf16[2,31,8,128]{3,2,1,0:T(8,128)(2,1)S(1)}, bf16[2,31,8,128]{3,2,1,0:T(8,128)(2,1)S(1)}, u32[]{:S(2)}, u32[]{:S(2)}) collective-permute-start(bf16[2,31,8,128]{3,2,1,0:T(8,128)(2,1)S(1)} %collective-permute-done.5.refs_6_), channel_id=1, source_target_pairs={{0,8},{8,0},{1,9},{9,1},{2,10},{10,2},{3,11},{11,3},{4,12},{12,4},... | collective-permute-start | bytes 380936 | tf_op jit(solution)/shard_map/ppermute | solution.py:23
  23.9 1.4 %collective-permute-start.4 = (bf16[2,31,8,128]{3,2,1,0:T(8,128)(2,1)S(1)}, bf16[2,31,8,128]{3,2,1,0:T(8,128)(2,1)S(1)}, u32[]{:S(2)}, u32[]{:S(2)}) collective-permute-start(bf16[2,31,8,128]{3,2,1,0:T(8,128)(2,1)S(1)} %collective-permute-done.3.refs_4_), channel_id=1, source_target_pairs={{0,8},{8,0},{1,9},{9,1},{2,10},{10,2},{3,11},{11,3},{4,12},{12,4},... | collective-permute-start | bytes 380936 | tf_op jit(solution)/shard_map/ppermute | solution.py:23
  26.6 5.6 %shard_map.28 = (bf16[4,3,128,1280]{3,2,1,0:T(8,128)(2,1)S(1)}, f32[3,128,1280]{2,1,0:T(8,128)S(1)}) custom-call(s32[4]{0:T(128)S(1)} %pad_add_fusion.where_ref, bf16[2,31,8,128]{3,2,1,0:T(8,128)(2,1)S(1)} %pad_maximum_fusion.3.refs_0_, bf16[2,31,8,128]{3,2,1,0:T(8,128)(2,1)S(1)} %collective-permute-done.refs_1_, ...), custom_call_target="tpu_custom_call" | custom-call | flops 503316480 | bytes 4194304 | tf_op jit(solution)/shard_map/pallas_call | solution.py:162
  32.2 5.7 %shard_map.29 = (f32[256,128]{1,0:T(8,128)S(1)}, bf16[256,128]{1,0:T(8,128)(2,1)S(1)}, bf16[256,128]{1,0:T(8,128)(2,1)S(1)}, bf16[256,128]{1,0:T(8,128)(2,1)S(1)}) custom-call(s32[4]{0:T(128)S(1)} %pad_add_fusion.where_ref, bf16[4,3,128,1280]{3,2,1,0:T(8,128)(2,1)S(1)} %get-tuple-element.30.turned, f32[3,128,1280]{2,1,0:T(8,128)S(1)} %get-tuple-element.31.phi), custom_call_target="tpu_custom_call" | custom-call | flops 1006632960 | bytes 4194304 | tf_op jit(solution)/shard_map/pallas_call | solution.py:224
  38.0 1.8 %collective-permute-start.12 = (bf16[256,128]{1,0:T(8,128)(2,1)S(1)}, bf16[256,128]{1,0:T(8,128)(2,1)S(1)}, u32[]{:S(2)}, u32[]{:S(2)}) collective-permute-start(bf16[256,128]{1,0:T(8,128)(2,1)S(1)} %get-tuple-element.33), channel_id=1, source_target_pairs={{0,2},{2,4},{4,6},{6,0},{1,3},{3,5},{5,7},{7,1},{8,10},{10,12},{12... | collective-permute-start | bytes 196616 | tf_op jit(solution)/shard_map/ppermute | solution.py:23
  39.8 1.3 %collective-permute-start.13 = (bf16[256,128]{1,0:T(8,128)(2,1)S(1)}, bf16[256,128]{1,0:T(8,128)(2,1)S(1)}, u32[]{:S(2)}, u32[]{:S(2)}) collective-permute-start(bf16[256,128]{1,0:T(8,128)(2,1)S(1)} %get-tuple-element.34), channel_id=1, source_target_pairs={{0,4},{2,6},{4,0},{6,2},{1,5},{3,7},{5,1},{7,3},{8,12},{10,14},{12... | collective-permute-start | bytes 196616 | tf_op jit(solution)/shard_map/ppermute | solution.py:23
  41.0 2.3 %collective-permute-start.14 = (bf16[256,128]{1,0:T(8,128)(2,1)S(1)}, bf16[256,128]{1,0:T(8,128)(2,1)S(1)}, u32[]{:S(2)}, u32[]{:S(2)}) collective-permute-start(bf16[256,128]{1,0:T(8,128)(2,1)S(1)} %get-tuple-element.35), channel_id=1, source_target_pairs={{0,6},{2,0},{4,2},{6,4},{1,7},{3,1},{5,3},{7,5},{8,14},{10,8},{12,... | collective-permute-start | bytes 196616 | tf_op jit(solution)/shard_map/ppermute | solution.py:23
  43.3 5.7 %shard_map.30 = (f32[256,128]{1,0:T(8,128)S(1)}, bf16[256,128]{1,0:T(8,128)(2,1)S(1)}, bf16[256,128]{1,0:T(8,128)(2,1)S(1)}, bf16[256,128]{1,0:T(8,128)(2,1)S(1)}) custom-call(s32[4]{0:T(128)S(1)} %pad_add_fusion.where_ref, bf16[4,3,128,1280]{3,2,1,0:T(8,128)(2,1)S(1)} %get-tuple-element.30.turned, f32[3,128,1280]{2,1,0:T(8,128)S(1)} %get-tuple-element.31.phi), custom_call_target="tpu_custom_call" | custom-call | flops 1006632960 | bytes 4194304 | tf_op jit(solution)/shard_map/pallas_call | solution.py:224
  50.7 1.3 %collective-permute-start.20 = (bf16[256,128]{1,0:T(8,128)(2,1)S(1)}, bf16[256,128]{1,0:T(8,128)(2,1)S(1)}, u32[]{:S(2)}, u32[]{:S(2)}) collective-permute-start(bf16[256,128]{1,0:T(8,128)(2,1)S(1)} %get-tuple-element.42), channel_id=1, source_target_pairs={{0,2},{2,4},{4,6},{6,0},{1,3},{3,5},{5,7},{7,1},{8,10},{10,12},{12... | collective-permute-start | bytes 196616 | tf_op jit(solution)/shard_map/ppermute | solution.py:23
  51.9 1.2 %collective-permute-start.21 = (bf16[256,128]{1,0:T(8,128)(2,1)S(1)}, bf16[256,128]{1,0:T(8,128)(2,1)S(1)}, u32[]{:S(2)}, u32[]{:S(2)}) collective-permute-start(bf16[256,128]{1,0:T(8,128)(2,1)S(1)} %get-tuple-element.43), channel_id=1, source_target_pairs={{0,4},{2,6},{4,0},{6,2},{1,5},{3,7},{5,1},{7,3},{8,12},{10,14},{12... | collective-permute-start | bytes 196616 | tf_op jit(solution)/shard_map/ppermute | solution.py:23
  53.1 2.3 %collective-permute-start.22 = (bf16[256,128]{1,0:T(8,128)(2,1)S(1)}, bf16[256,128]{1,0:T(8,128)(2,1)S(1)}, u32[]{:S(2)}, u32[]{:S(2)}) collective-permute-start(bf16[256,128]{1,0:T(8,128)(2,1)S(1)} %get-tuple-element.44), channel_id=1, source_target_pairs={{0,6},{2,0},{4,2},{6,4},{1,7},{3,1},{5,3},{7,5},{8,14},{10,8},{12,... | collective-permute-start | bytes 196616 | tf_op jit(solution)/shard_map/ppermute | solution.py:23
  56.9 4.2 %collective-permute-done.21 = bf16[256,128]{1,0:T(8,128)(2,1)S(1)} collective-permute-done((bf16[256,128]{1,0:T(8,128)(2,1)S(1)}, bf16[256,128]{1,0:T(8,128)(2,1)S(1)}, u32[]{:S(2)}, u32[]{:S(2)}) %collective-permute-start.21) | collective-permute-done | bytes 65568 | tf_op jit(solution)/shard_map/ppermute | solution.py:23
  61.1 3.5 %collective-permute-start.25 = (bf16[256,128]{1,0:T(8,128)(2,1)S(1)}, bf16[256,128]{1,0:T(8,128)(2,1)S(1)}, u32[]{:S(2)}, u32[]{:S(2)}) collective-permute-start(bf16[256,128]{1,0:T(8,128)(2,1)S(1)} %add_convert_fusion), channel_id=1, source_target_pairs={{0,6},{2,0},{4,2},{6,4},{1,7},{3,1},{5,3},{7,5},{8,14},{10,8},{12,... | collective-permute-start | bytes 196616 | tf_op jit(solution)/shard_map/ppermute | solution.py:23
  66.0 2.7 %collective-permute-done.24 = bf16[256,128]{1,0:T(8,128)(2,1)S(1)} collective-permute-done((bf16[256,128]{1,0:T(8,128)(2,1)S(1)}, bf16[256,128]{1,0:T(8,128)(2,1)S(1)}, u32[]{:S(2)}, u32[]{:S(2)}) %collective-permute-start.24) | collective-permute-done | bytes 65568 | tf_op jit(solution)/shard_map/ppermute | solution.py:23
  68.6 1.5 %collective-permute-done.23 = bf16[256,128]{1,0:T(8,128)(2,1)S(1)} collective-permute-done((bf16[256,128]{1,0:T(8,128)(2,1)S(1)}, bf16[256,128]{1,0:T(8,128)(2,1)S(1)}, u32[]{:S(2)}, u32[]{:S(2)}) %collective-permute-start.23) | collective-permute-done | bytes 65568 | tf_op jit(solution)/shard_map/ppermute | solution.py:23
  70.2 2.1 %collective-permute-start.28 = (bf16[1024,128]{1,0:T(8,128)(2,1)S(1)}, bf16[1024,128]{1,0:T(8,128)(2,1)S(1)}, u32[]{:S(2)}, u32[]{:S(2)}) collective-permute-start(bf16[1024,128]{1,0:T(8,128)(2,1)S(1)} %pad_maximum_fusion.refs_0_), channel_id=1, source_target_pairs={{0,8},{8,0},{1,9},{9,1},{2,10},{10,2},{3,11},{11,3},{4,12},{12,4},... | collective-permute-start | bytes 786440 | tf_op jit(solution)/shard_map/ppermute | solution.py:23
  74.3 1.3 %collective-permute-start.26 = (bf16[1024,128]{1,0:T(8,128)(2,1)S(1)}, bf16[1024,128]{1,0:T(8,128)(2,1)S(1)}, u32[]{:S(2)}, u32[]{:S(2)}) collective-permute-start(bf16[1024,128]{1,0:T(8,128)(2,1)S(1)} %pad_maximum_fusion.1.refs_2_), channel_id=1, source_target_pairs={{0,1},{1,0},{2,3},{3,2},{4,5},{5,4},{6,7},{7,6},{8,9},{9,8},{10,11... | collective-permute-start | bytes 786440 | tf_op jit(solution)/shard_map/ppermute | solution.py:23
  75.6 4.6 %collective-permute-done.32.refs_0_ = bf16[1024,128]{1,0:T(8,128)(2,1)S(1)} collective-permute-done((bf16[1024,128]{1,0:T(8,128)(2,1)S(1)}, bf16[1024,128]{1,0:T(8,128)(2,1)S(1)}, u32[]{:S(2)}, u32[]{:S(2)}) %collective-permute-start.32) | collective-permute-done | bytes 262176 | tf_op jit(solution)/shard_map/ppermute | solution.py:23
  80.2 1.3 %collective-permute-start.33 = (bf16[1024,128]{1,0:T(8,128)(2,1)S(1)}, bf16[1024,128]{1,0:T(8,128)(2,1)S(1)}, u32[]{:S(2)}, u32[]{:S(2)}) collective-permute-start(bf16[1024,128]{1,0:T(8,128)(2,1)S(1)} %collective-permute-done.32.refs_0_), channel_id=1, source_target_pairs={{0,8},{8,0},{1,9},{9,1},{2,10},{10,2},{3,11},{11,3},{4,12},{12,4},... | collective-permute-start | bytes 786440 | tf_op jit(solution)/shard_map/ppermute | solution.py:23
  81.5 2.4 %shard_map.31.refs_5_ = f32[16384,128]{1,0:T(8,128)} custom-call(s32[4]{0:T(128)S(1)} %pad_add_fusion.where_ref, bf16[1024,128]{1,0:T(8,128)(2,1)S(1)} %pad_maximum_fusion.refs_0_, bf16[1024,128]{1,0:T(8,128)(2,1)S(1)} %collective-permute-done.18.refs_1_, bf16[1024,128]{1,0:T(8,128)(2,1)S(1)} %collective-permute-done.19.refs_2_, ...), custom_call_target="tpu_custom_call" | custom-call | bytes 4718592 | tf_op jit(solution)/shard_map/pallas_call | solution.py:274
  83.9 1.9 %collective-permute-done.27.refs_4_ = bf16[1024,128]{1,0:T(8,128)(2,1)S(1)} collective-permute-done((bf16[1024,128]{1,0:T(8,128)(2,1)S(1)}, bf16[1024,128]{1,0:T(8,128)(2,1)S(1)}, u32[]{:S(2)}, u32[]{:S(2)}) %collective-permute-start.27) | collective-permute-done | bytes 262176 | tf_op jit(solution)/shard_map/ppermute | solution.py:23
  85.8 1.3 %collective-permute-start.31 = (bf16[1024,128]{1,0:T(8,128)(2,1)S(1)}, bf16[1024,128]{1,0:T(8,128)(2,1)S(1)}, u32[]{:S(2)}, u32[]{:S(2)}) collective-permute-start(bf16[1024,128]{1,0:T(8,128)(2,1)S(1)} %collective-permute-done.27.refs_4_), channel_id=1, source_target_pairs={{0,1},{1,0},{2,3},{3,2},{4,5},{5,4},{6,7},{7,6},{8,9},{9,8},{10,11... | collective-permute-start | bytes 786440 | tf_op jit(solution)/shard_map/ppermute | solution.py:23
  87.2 1.1 %collective-permute-start.37 = (bf16[1024,128]{1,0:T(8,128)(2,1)S(1)}, bf16[1024,128]{1,0:T(8,128)(2,1)S(1)}, u32[]{:S(2)}, u32[]{:S(2)}) collective-permute-start(bf16[1024,128]{1,0:T(8,128)(2,1)S(1)} %collective-permute-done.27.refs_4_), channel_id=1, source_target_pairs={{0,8},{8,0},{1,9},{9,1},{2,10},{10,2},{3,11},{11,3},{4,12},{12,4},... | collective-permute-start | bytes 786440 | tf_op jit(solution)/shard_map/ppermute | solution.py:23
  88.8 2.2 %shard_map.32.refs_4_ = f32[16384,128]{1,0:T(8,128)} custom-call(s32[4]{0:T(128)S(1)} %pad_add_fusion.where_ref, bf16[1024,128]{1,0:T(8,128)(2,1)S(1)} %collective-permute-done.32.refs_0_, bf16[1024,128]{1,0:T(8,128)(2,1)S(1)} %collective-permute-done.33.refs_1_, bf16[1024,128]{1,0:T(8,128)(2,1)S(1)} %pad_maximum_fusion.1.refs_2_, ...), custom_call_target="tpu_custom_call", output_to_operand_aliasing={{}: (6, {})} | custom-call | bytes 3932160 | tf_op jit(solution)/shard_map/pallas_call | solution.py:274
  91.0 1.8 %collective-permute-done.31.refs_3_ = bf16[1024,128]{1,0:T(8,128)(2,1)S(1)} collective-permute-done((bf16[1024,128]{1,0:T(8,128)(2,1)S(1)}, bf16[1024,128]{1,0:T(8,128)(2,1)S(1)}, u32[]{:S(2)}, u32[]{:S(2)}) %collective-permute-start.31) | collective-permute-done | bytes 262176 | tf_op jit(solution)/shard_map/ppermute | solution.py:23
  92.8 1.7 %collective-permute-start.34 = (bf16[1024,128]{1,0:T(8,128)(2,1)S(1)}, bf16[1024,128]{1,0:T(8,128)(2,1)S(1)}, u32[]{:S(2)}, u32[]{:S(2)}) collective-permute-start(bf16[1024,128]{1,0:T(8,128)(2,1)S(1)} %collective-permute-done.31.refs_3_), channel_id=1, source_target_pairs={{0,8},{8,0},{1,9},{9,1},{2,10},{10,2},{3,11},{11,3},{4,12},{12,4},... | collective-permute-start | bytes 786440 | tf_op jit(solution)/shard_map/ppermute | solution.py:23
  94.6 2.0 %shard_map.33.refs_1_ = f32[16384,128]{1,0:T(8,128)} custom-call(s32[4]{0:T(128)S(1)} %pad_add_fusion.where_ref, bf16[1024,128]{1,0:T(8,128)(2,1)S(1)} %collective-permute-done.35.refs_0_, bf16[1024,128]{1,0:T(8,128)(2,1)S(1)} %collective-permute-done.36.refs_1_, ...), custom_call_target="tpu_custom_call", output_to_operand_aliasing={{}: (5, {})} | custom-call | bytes 3145728 | tf_op jit(solution)/shard_map/pallas_call | solution.py:274
  96.6 1.4 %shard_map.34 = f32[16384,128]{1,0:T(8,128)} custom-call(s32[4]{0:T(128)S(1)} %pad_add_fusion.where_ref, bf16[1024,128]{1,0:T(8,128)(2,1)S(1)} %collective-permute-done.34.refs_0_, f32[16384,128]{1,0:T(8,128)} %shard_map.33.refs_1_), custom_call_target="tpu_custom_call", output_to_operand_aliasing={{}: (2, {})} | custom-call | bytes 786432 | tf_op jit(solution)/shard_map/pallas_call | solution.py:274
  (64 shorter events, 13.6 us)
Async XLA Ops:
  1.1 17.0 %collective-permute-start.10 = (bf16[2,32,384]{2,1,0:T(8,128)(2,1)S(1)}, bf16[2,32,384]{2,1,0:T(8,128)(2,1)S(1)}, u32[]{:S(2)}, u32[]{:S(2)}) collective-permute-start(bf16[2,32,384]{2,1,0:T(8,128)(2,1)S(1)} %pad.9), channel_id=1, source_target_pairs={{1,19},{2,16},{3,21},{4,18},{5,23},{6,20},{17,3},{18,0},{19,5},{20... | collective-permute-start | bytes 147464 | tf_op jit(solution)/shard_map/ppermute | solution.py:322
  2.4 15.9 %collective-permute-start.9 = (bf16[2,32,384]{2,1,0:T(8,128)(2,1)S(1)}, bf16[2,32,384]{2,1,0:T(8,128)(2,1)S(1)}, u32[]{:S(2)}, u32[]{:S(2)}) collective-permute-start(bf16[2,32,384]{2,1,0:T(8,128)(2,1)S(1)} %pad.9), channel_id=1, source_target_pairs={{1,18},{2,17},{3,20},{4,19},{5,22},{6,21},{17,2},{18,1},{19,4},{20... | collective-permute-start | bytes 147464 | tf_op jit(solution)/shard_map/ppermute | solution.py:322
  3.1 15.4 %collective-permute-start.8 = (bf16[2,32,384]{2,1,0:T(8,128)(2,1)S(1)}, bf16[2,32,384]{2,1,0:T(8,128)(2,1)S(1)}, u32[]{:S(2)}, u32[]{:S(2)}) collective-permute-start(bf16[2,32,384]{2,1,0:T(8,128)(2,1)S(1)} %pad.9), channel_id=1, source_target_pairs={{1,3},{2,0},{3,5},{4,2},{5,7},{6,4},{17,19},{18,16},{19,21},{20,18... | collective-permute-start | bytes 147464 | tf_op jit(solution)/shard_map/ppermute | solution.py:322
  4.4 14.1 %collective-permute-start.7 = (bf16[2,32,384]{2,1,0:T(8,128)(2,1)S(1)}, bf16[2,32,384]{2,1,0:T(8,128)(2,1)S(1)}, u32[]{:S(2)}, u32[]{:S(2)}) collective-permute-start(bf16[2,32,384]{2,1,0:T(8,128)(2,1)S(1)} %pad.9), channel_id=1, source_target_pairs={{1,2},{2,1},{3,4},{4,3},{5,6},{6,5},{17,18},{18,17},{19,20},{20,19... | collective-permute-start | bytes 147464 | tf_op jit(solution)/shard_map/ppermute | solution.py:322
  6.8 14.0 %collective-permute-start.5 = (bf16[2,31,8,128]{3,2,1,0:T(8,128)(2,1)S(1)}, bf16[2,31,8,128]{3,2,1,0:T(8,128)(2,1)S(1)}, u32[]{:S(2)}, u32[]{:S(2)}) collective-permute-start(bf16[2,31,8,128]{3,2,1,0:T(8,128)(2,1)S(1)} %pad_maximum_fusion.3.refs_0_), channel_id=1, source_target_pairs={{0,17},{1,16},{16,1},{17,0},{2,19},{3,18},{18,3},{19,2},{4,21},{5,... | collective-permute-start | bytes 380936 | tf_op jit(solution)/shard_map/ppermute | solution.py:332
  18.1 5.8 %collective-permute-start.3 = (bf16[2,31,8,128]{3,2,1,0:T(8,128)(2,1)S(1)}, bf16[2,31,8,128]{3,2,1,0:T(8,128)(2,1)S(1)}, u32[]{:S(2)}, u32[]{:S(2)}) collective-permute-start(bf16[2,31,8,128]{3,2,1,0:T(8,128)(2,1)S(1)} %pad_maximum_fusion.3.refs_0_), channel_id=1, source_target_pairs={{0,16},{16,0},{1,17},{17,1},{2,18},{18,2},{3,19},{19,3},{4,20},{20... | collective-permute-start | bytes 380936 | tf_op jit(solution)/shard_map/ppermute | solution.py:23
  18.3 7.0 %collective-permute-start.1 = (bf16[2,31,8,128]{3,2,1,0:T(8,128)(2,1)S(1)}, bf16[2,31,8,128]{3,2,1,0:T(8,128)(2,1)S(1)}, u32[]{:S(2)}, u32[]{:S(2)}) collective-permute-start(bf16[2,31,8,128]{3,2,1,0:T(8,128)(2,1)S(1)} %pad_maximum_fusion.3.refs_0_), channel_id=1, source_target_pairs={{0,1},{1,0},{2,3},{3,2},{4,5},{5,4},{6,7},{7,6},{8,9},{9,8},{10,11... | collective-permute-start | bytes 380936 | tf_op jit(solution)/shard_map/ppermute | solution.py:23
  18.5 6.9 %collective-permute-start.11 = (bf16[4,2,32,384]{3,2,1,0:T(8,128)(2,1)S(1)}, bf16[4,2,32,384]{3,2,1,0:T(8,128)(2,1)S(1)}, u32[]{:S(2)}, u32[]{:S(2)}) collective-permute-start(bf16[4,2,32,384]{3,2,1,0:T(8,128)(2,1)S(1)} %pad_maximum_fusion.2.refs_8_), channel_id=1, source_target_pairs={{0,8},{8,0},{1,9},{9,1},{2,10},{10,2},{3,11},{11,3},{4,12},{12,4},... | collective-permute-start | bytes 589832 | tf_op jit(solution)/shard_map/ppermute | solution.py:23
  20.7 4.8 %collective-permute-start = (bf16[2,31,8,128]{3,2,1,0:T(8,128)(2,1)S(1)}, bf16[2,31,8,128]{3,2,1,0:T(8,128)(2,1)S(1)}, u32[]{:S(2)}, u32[]{:S(2)}) collective-permute-start(bf16[2,31,8,128]{3,2,1,0:T(8,128)(2,1)S(1)} %pad_maximum_fusion.3.refs_0_), channel_id=1, source_target_pairs={{0,8},{8,0},{1,9},{9,1},{2,10},{10,2},{3,11},{11,3},{4,12},{12,4},... | collective-permute-start | bytes 380936 | tf_op jit(solution)/shard_map/ppermute | solution.py:23
  20.8 4.7 %collective-permute-start.6 = (bf16[2,31,8,128]{3,2,1,0:T(8,128)(2,1)S(1)}, bf16[2,31,8,128]{3,2,1,0:T(8,128)(2,1)S(1)}, u32[]{:S(2)}, u32[]{:S(2)}) collective-permute-start(bf16[2,31,8,128]{3,2,1,0:T(8,128)(2,1)S(1)} %collective-permute-done.5.refs_6_), channel_id=1, source_target_pairs={{0,8},{8,0},{1,9},{9,1},{2,10},{10,2},{3,11},{11,3},{4,12},{12,4},... | collective-permute-start | bytes 380936 | tf_op jit(solution)/shard_map/ppermute | solution.py:23
  38.0 11.1 %collective-permute-start.12 = (bf16[256,128]{1,0:T(8,128)(2,1)S(1)}, bf16[256,128]{1,0:T(8,128)(2,1)S(1)}, u32[]{:S(2)}, u32[]{:S(2)}) collective-permute-start(bf16[256,128]{1,0:T(8,128)(2,1)S(1)} %get-tuple-element.33), channel_id=1, source_target_pairs={{0,2},{2,4},{4,6},{6,0},{1,3},{3,5},{5,7},{7,1},{8,10},{10,12},{12... | collective-permute-start | bytes 196616 | tf_op jit(solution)/shard_map/ppermute | solution.py:23
  39.8 9.3 %collective-permute-start.13 = (bf16[256,128]{1,0:T(8,128)(2,1)S(1)}, bf16[256,128]{1,0:T(8,128)(2,1)S(1)}, u32[]{:S(2)}, u32[]{:S(2)}) collective-permute-start(bf16[256,128]{1,0:T(8,128)(2,1)S(1)} %get-tuple-element.34), channel_id=1, source_target_pairs={{0,4},{2,6},{4,0},{6,2},{1,5},{3,7},{5,1},{7,3},{8,12},{10,14},{12... | collective-permute-start | bytes 196616 | tf_op jit(solution)/shard_map/ppermute | solution.py:23
  41.0 8.0 %collective-permute-start.14 = (bf16[256,128]{1,0:T(8,128)(2,1)S(1)}, bf16[256,128]{1,0:T(8,128)(2,1)S(1)}, u32[]{:S(2)}, u32[]{:S(2)}) collective-permute-start(bf16[256,128]{1,0:T(8,128)(2,1)S(1)} %get-tuple-element.35), channel_id=1, source_target_pairs={{0,6},{2,0},{4,2},{6,4},{1,7},{3,1},{5,3},{7,5},{8,14},{10,8},{12,... | collective-permute-start | bytes 196616 | tf_op jit(solution)/shard_map/ppermute | solution.py:23
  49.2 6.2 %collective-permute-start.16 = (bf16[256,128]{1,0:T(8,128)(2,1)S(1)}, bf16[256,128]{1,0:T(8,128)(2,1)S(1)}, u32[]{:S(2)}, u32[]{:S(2)}) collective-permute-start(bf16[256,128]{1,0:T(8,128)(2,1)S(1)} %add_convert_fusion.1), channel_id=1, source_target_pairs={{0,4},{2,6},{4,0},{6,2},{1,5},{3,7},{5,1},{7,3},{8,12},{10,14},{12... | collective-permute-start | bytes 196616 | tf_op jit(solution)/shard_map/ppermute | solution.py:23
  49.6 5.8 %collective-permute-start.15 = (bf16[256,128]{1,0:T(8,128)(2,1)S(1)}, bf16[256,128]{1,0:T(8,128)(2,1)S(1)}, u32[]{:S(2)}, u32[]{:S(2)}) collective-permute-start(bf16[256,128]{1,0:T(8,128)(2,1)S(1)} %add_convert_fusion.1), channel_id=1, source_target_pairs={{0,2},{2,4},{4,6},{6,0},{1,3},{3,5},{5,7},{7,1},{8,10},{10,12},{12... | collective-permute-start | bytes 196616 | tf_op jit(solution)/shard_map/ppermute | solution.py:23
  50.7 6.2 %collective-permute-start.20 = (bf16[256,128]{1,0:T(8,128)(2,1)S(1)}, bf16[256,128]{1,0:T(8,128)(2,1)S(1)}, u32[]{:S(2)}, u32[]{:S(2)}) collective-permute-start(bf16[256,128]{1,0:T(8,128)(2,1)S(1)} %get-tuple-element.42), channel_id=1, source_target_pairs={{0,2},{2,4},{4,6},{6,0},{1,3},{3,5},{5,7},{7,1},{8,10},{10,12},{12... | collective-permute-start | bytes 196616 | tf_op jit(solution)/shard_map/ppermute | solution.py:23
  51.9 9.1 %collective-permute-start.21 = (bf16[256,128]{1,0:T(8,128)(2,1)S(1)}, bf16[256,128]{1,0:T(8,128)(2,1)S(1)}, u32[]{:S(2)}, u32[]{:S(2)}) collective-permute-start(bf16[256,128]{1,0:T(8,128)(2,1)S(1)} %get-tuple-element.43), channel_id=1, source_target_pairs={{0,4},{2,6},{4,0},{6,2},{1,5},{3,7},{5,1},{7,3},{8,12},{10,14},{12... | collective-permute-start | bytes 196616 | tf_op jit(solution)/shard_map/ppermute | solution.py:23
  53.1 7.9 %collective-permute-start.22 = (bf16[256,128]{1,0:T(8,128)(2,1)S(1)}, bf16[256,128]{1,0:T(8,128)(2,1)S(1)}, u32[]{:S(2)}, u32[]{:S(2)}) collective-permute-start(bf16[256,128]{1,0:T(8,128)(2,1)S(1)} %get-tuple-element.44), channel_id=1, source_target_pairs={{0,6},{2,0},{4,2},{6,4},{1,7},{3,1},{5,3},{7,5},{8,14},{10,8},{12,... | collective-permute-start | bytes 196616 | tf_op jit(solution)/shard_map/ppermute | solution.py:23
  55.4 14.8 %collective-permute-start.19 = (bf16[1024,128]{1,0:T(8,128)(2,1)S(1)}, bf16[1024,128]{1,0:T(8,128)(2,1)S(1)}, u32[]{:S(2)}, u32[]{:S(2)}) collective-permute-start(bf16[1024,128]{1,0:T(8,128)(2,1)S(1)} %pad_maximum_fusion.refs_0_), channel_id=1, source_target_pairs={{0,16},{16,0},{1,17},{17,1},{2,18},{18,2},{3,19},{19,3},{4,20},{20... | collective-permute-start | bytes 786440 | tf_op jit(solution)/shard_map/ppermute | solution.py:23
  56.3 13.9 %collective-permute-start.18 = (bf16[1024,128]{1,0:T(8,128)(2,1)S(1)}, bf16[1024,128]{1,0:T(8,128)(2,1)S(1)}, u32[]{:S(2)}, u32[]{:S(2)}) collective-permute-start(bf16[1024,128]{1,0:T(8,128)(2,1)S(1)} %pad_maximum_fusion.refs_0_), channel_id=1, source_target_pairs={{0,1},{1,0},{2,3},{3,2},{4,5},{5,4},{6,7},{7,6},{8,9},{9,8},{10,11... | collective-permute-start | bytes 786440 | tf_op jit(solution)/shard_map/ppermute | solution.py:23
  61.1 4.9 %collective-permute-start.25 = (bf16[256,128]{1,0:T(8,128)(2,1)S(1)}, bf16[256,128]{1,0:T(8,128)(2,1)S(1)}, u32[]{:S(2)}, u32[]{:S(2)}) collective-permute-start(bf16[256,128]{1,0:T(8,128)(2,1)S(1)} %add_convert_fusion), channel_id=1, source_target_pairs={{0,6},{2,0},{4,2},{6,4},{1,7},{3,1},{5,3},{7,5},{8,14},{10,8},{12,... | collective-permute-start | bytes 196616 | tf_op jit(solution)/shard_map/ppermute | solution.py:23
  64.6 5.6 %collective-permute-start.23 = (bf16[256,128]{1,0:T(8,128)(2,1)S(1)}, bf16[256,128]{1,0:T(8,128)(2,1)S(1)}, u32[]{:S(2)}, u32[]{:S(2)}) collective-permute-start(bf16[256,128]{1,0:T(8,128)(2,1)S(1)} %add_convert_fusion), channel_id=1, source_target_pairs={{0,2},{2,4},{4,6},{6,0},{1,3},{3,5},{5,7},{7,1},{8,10},{10,12},{12... | collective-permute-start | bytes 196616 | tf_op jit(solution)/shard_map/ppermute | solution.py:23
  72.3 7.9 %collective-permute-start.32 = (bf16[1024,128]{1,0:T(8,128)(2,1)S(1)}, bf16[1024,128]{1,0:T(8,128)(2,1)S(1)}, u32[]{:S(2)}, u32[]{:S(2)}) collective-permute-start(bf16[1024,128]{1,0:T(8,128)(2,1)S(1)} %collective-permute-done.18.refs_1_), channel_id=1, source_target_pairs={{0,16},{16,0},{1,17},{17,1},{2,18},{18,2},{3,19},{19,3},{4,20},{20... | collective-permute-start | bytes 786440 | tf_op jit(solution)/shard_map/ppermute | solution.py:23
  73.4 8.1 %collective-permute-start.29 = (bf16[1024,128]{1,0:T(8,128)(2,1)S(1)}, bf16[1024,128]{1,0:T(8,128)(2,1)S(1)}, u32[]{:S(2)}, u32[]{:S(2)}) collective-permute-start(bf16[1024,128]{1,0:T(8,128)(2,1)S(1)} %collective-permute-done.18.refs_1_), channel_id=1, source_target_pairs={{0,8},{8,0},{1,9},{9,1},{2,10},{10,2},{3,11},{11,3},{4,12},{12,4},... | collective-permute-start | bytes 786440 | tf_op jit(solution)/shard_map/ppermute | solution.py:23
  73.8 7.7 %collective-permute-start.30 = (bf16[1024,128]{1,0:T(8,128)(2,1)S(1)}, bf16[1024,128]{1,0:T(8,128)(2,1)S(1)}, u32[]{:S(2)}, u32[]{:S(2)}) collective-permute-start(bf16[1024,128]{1,0:T(8,128)(2,1)S(1)} %collective-permute-done.19.refs_2_), channel_id=1, source_target_pairs={{0,8},{8,0},{1,9},{9,1},{2,10},{10,2},{3,11},{11,3},{4,12},{12,4},... | collective-permute-start | bytes 786440 | tf_op jit(solution)/shard_map/ppermute | solution.py:23
  74.0 11.9 %collective-permute-start.27 = (bf16[1024,128]{1,0:T(8,128)(2,1)S(1)}, bf16[1024,128]{1,0:T(8,128)(2,1)S(1)}, u32[]{:S(2)}, u32[]{:S(2)}) collective-permute-start(bf16[1024,128]{1,0:T(8,128)(2,1)S(1)} %pad_maximum_fusion.1.refs_2_), channel_id=1, source_target_pairs={{0,16},{16,0},{1,17},{17,1},{2,18},{18,2},{3,19},{19,3},{4,20},{20... | collective-permute-start | bytes 786440 | tf_op jit(solution)/shard_map/ppermute | solution.py:23
  74.3 11.5 %collective-permute-start.26 = (bf16[1024,128]{1,0:T(8,128)(2,1)S(1)}, bf16[1024,128]{1,0:T(8,128)(2,1)S(1)}, u32[]{:S(2)}, u32[]{:S(2)}) collective-permute-start(bf16[1024,128]{1,0:T(8,128)(2,1)S(1)} %pad_maximum_fusion.1.refs_2_), channel_id=1, source_target_pairs={{0,1},{1,0},{2,3},{3,2},{4,5},{5,4},{6,7},{7,6},{8,9},{9,8},{10,11... | collective-permute-start | bytes 786440 | tf_op jit(solution)/shard_map/ppermute | solution.py:23
  80.2 8.6 %collective-permute-start.33 = (bf16[1024,128]{1,0:T(8,128)(2,1)S(1)}, bf16[1024,128]{1,0:T(8,128)(2,1)S(1)}, u32[]{:S(2)}, u32[]{:S(2)}) collective-permute-start(bf16[1024,128]{1,0:T(8,128)(2,1)S(1)} %collective-permute-done.32.refs_0_), channel_id=1, source_target_pairs={{0,8},{8,0},{1,9},{9,1},{2,10},{10,2},{3,11},{11,3},{4,12},{12,4},... | collective-permute-start | bytes 786440 | tf_op jit(solution)/shard_map/ppermute | solution.py:23
  85.8 7.0 %collective-permute-start.31 = (bf16[1024,128]{1,0:T(8,128)(2,1)S(1)}, bf16[1024,128]{1,0:T(8,128)(2,1)S(1)}, u32[]{:S(2)}, u32[]{:S(2)}) collective-permute-start(bf16[1024,128]{1,0:T(8,128)(2,1)S(1)} %collective-permute-done.27.refs_4_), channel_id=1, source_target_pairs={{0,1},{1,0},{2,3},{3,2},{4,5},{5,4},{6,7},{7,6},{8,9},{9,8},{10,11... | collective-permute-start | bytes 786440 | tf_op jit(solution)/shard_map/ppermute | solution.py:23
  87.2 7.4 %collective-permute-start.37 = (bf16[1024,128]{1,0:T(8,128)(2,1)S(1)}, bf16[1024,128]{1,0:T(8,128)(2,1)S(1)}, u32[]{:S(2)}, u32[]{:S(2)}) collective-permute-start(bf16[1024,128]{1,0:T(8,128)(2,1)S(1)} %collective-permute-done.27.refs_4_), channel_id=1, source_target_pairs={{0,8},{8,0},{1,9},{9,1},{2,10},{10,2},{3,11},{11,3},{4,12},{12,4},... | collective-permute-start | bytes 786440 | tf_op jit(solution)/shard_map/ppermute | solution.py:23
  88.3 6.3 %collective-permute-start.35 = (bf16[1024,128]{1,0:T(8,128)(2,1)S(1)}, bf16[1024,128]{1,0:T(8,128)(2,1)S(1)}, u32[]{:S(2)}, u32[]{:S(2)}) collective-permute-start(bf16[1024,128]{1,0:T(8,128)(2,1)S(1)} %pad_maximum_fusion.1.refs_2_), channel_id=1, source_target_pairs={{0,8},{8,0},{1,9},{9,1},{2,10},{10,2},{3,11},{11,3},{4,12},{12,4},... | collective-permute-start | bytes 786440 | tf_op jit(solution)/shard_map/ppermute | solution.py:23
  88.3 6.3 %collective-permute-start.36 = (bf16[1024,128]{1,0:T(8,128)(2,1)S(1)}, bf16[1024,128]{1,0:T(8,128)(2,1)S(1)}, u32[]{:S(2)}, u32[]{:S(2)}) collective-permute-start(bf16[1024,128]{1,0:T(8,128)(2,1)S(1)} %collective-permute-done.26.refs_3_), channel_id=1, source_target_pairs={{0,8},{8,0},{1,9},{9,1},{2,10},{10,2},{3,11},{11,3},{4,12},{12,4},... | collective-permute-start | bytes 786440 | tf_op jit(solution)/shard_map/ppermute | solution.py:23
  (6 other events, 19.5 us)

commit v11 on v10

--- a/solution.py
+++ b/solution.py
@@ -42,8 +42,8 @@
 def slopes_kernel(sizes, offsets, where_ref, *refs):
     layers, height, across, width, rows = sizes
     members = len(offsets)
-    blocks, edges = refs[:members], refs[members : members + 2]
-    turned, phi, field, edge, *sources = refs[members + 2 :]
+    blocks = refs[:members]
+    turned, phi, field, *sources = refs[members:]
     count = members * layers * height * across
     depth = members // 2 * layers
     piece = 4 * count // depth
@@ -53,13 +53,6 @@
     field[members + 2 :] = jnp.zeros_like(field[members + 2 :])
     for n in range(members):
         field[member(where_ref, rows, offsets[n]) + 2] = blocks[n][...].astype(jnp.float32)
-    for c in range(2):
-        for r in range(rows):
-            stream = lax.div(member(where_ref, rows, (r, c, 0)), 2)
-            for h in range(2):
-                upper = lax.rem(where_ref[2] + h, 2)
-                edge[stream, upper] = edges[c][2 * r + h].astype(jnp.float32)
-
     index = lax.broadcasted_iota(jnp.int32, (across, width), 0)
     row, column = (lax.broadcasted_iota(jnp.int32, (2 * width, 2 * width), d) for d in range(2))
     eye = (row == column).astype(jnp.bfloat16)
@@ -72,7 +65,6 @@
         for side in range(2):
             here_at, layer = layer_at(0, side)
             at = here_at - 2
-            stream = lax.div(at, 2)
             tile = field[here_at, layer, 3 * height]
             weights = tile
             for part in range(1, WEIGHT_PARTS):
@@ -87,8 +79,7 @@
                 along = {step: field[m, l, 3 * z + b] for step, (m, l) in beside.items()}
                 value_x = 8.0 * (along[1] - along[-1]) - (along[2] - along[-2])
 
-                columns = slice(b * width, (b + 1) * width)
-                outer = edge[stream, side, layer, base : base + across, columns]
+                outer = field[here_at, layer, 3 * height + 1 + base // across * 3 + b]
                 beyond = field[here_at + 1 - 2 * side, layer, 3 * z + b]
                 if side == 0:
                     prev = pltpu.roll(outer, (across - 2 - (2 * z - base)) % across, 0)
@@ -141,9 +132,8 @@
         lax.fori_loop(0, depth // 2, two_layers, 0)
 
 
-def plane_slopes(where, blocks, edges, offsets, rows, comps):
-    layers, planes, across, width = blocks[0].shape
-    height = planes // comps
+def plane_slopes(where, blocks, offsets, rows, height, comps):
+    layers, _, across, width = blocks[0].shape
     members = len(blocks)
     count = members * layers * height * across
     sizes = (layers, height, across, width, rows)
@@ -154,22 +144,21 @@
     ]
     scratch = [
         ((members + 4,) + blocks[0].shape, jnp.float32),
-        ((members // 2, 2) + edges[0].shape[1:], jnp.float32),
         ((2, count, 2 * width), jnp.bfloat16),
         ((2, count, 2 * width), jnp.bfloat16),
     ]
-    inputs = [(v.shape, v.dtype) for v in blocks + edges]
+    inputs = [(v.shape, v.dtype) for v in blocks]
     return pl.pallas_call(
         functools.partial(slopes_kernel, sizes, offsets),
         out_shape=[jax.ShapeDtypeStruct(*result) for result in results],
-        in_specs=[pl.BlockSpec(memory_space=pltpu.SMEM)] + [vmem] * (members + 2),
+        in_specs=[pl.BlockSpec(memory_space=pltpu.SMEM)] + [vmem] * members,
         out_specs=[vmem] * len(results),
         scratch_shapes=[pltpu.VMEM(*shape) for shape in scratch],
         compiler_params=pltpu.CompilerParams(vmem_limit_bytes=grant(results + scratch + inputs)),
         cost_estimate=pl.CostEstimate(
             flops=2 * 12 * count * width * width, bytes_accessed=2**22, transcendentals=0
         ),
-    )(where, *blocks, *edges)
+    )(where, *blocks)
 
 
 def terms_kernel(share, chunk, rows, decks, where_ref, turned, phi, *refs):
@@ -235,22 +224,22 @@
 
 
 def place_kernel(plan, pieces, given, where_ref, *refs):
-    rows, decks, line, block, runs = plan
+    rows, decks, line, runs = plan
     out_ref, wide, sems = refs[pieces + given :]
     step = math.gcd(line, LANES)
     copies = []
-    for n, (piece, offsets, chunk, d) in enumerate(runs):
+    for n, (piece, offsets, chunk, d, first) in enumerate(runs):
         done = n * line
 
         def widen(k, _):
             at = pl.multiple_of(k * step, step)
-            wide[pl.ds(done + at, step), :] = refs[piece][pl.ds(d * line + at, step), :].astype(
+            wide[pl.ds(done + at, step), :] = refs[piece][pl.ds(first * line + at, step), :].astype(
                 jnp.float32
             )
             return 0
 
         lax.fori_loop(0, line // step, widen, 0)
-        start = (member(where_ref, rows, offsets) * CHUNKS + chunk) * block
+        start = (member(where_ref, rows, offsets) * CHUNKS + chunk) * decks * line
         start = start + lax.rem(where_ref[3] - d + decks, decks) * line
         to = pl.ds(pl.multiple_of(start, line), line)
         copies.append(
@@ -261,18 +250,19 @@
         copy.wait()
 
 
-def put(where, result, total_rows, rows, decks, chosen):
+def put(where, result, total_rows, rows, decks, chosen, line):
     values = [value for _, _, value in chosen]
-    block, width = values[0].shape
-    line = block // decks
+    width = values[0].shape[1]
     runs = [
-        (n, offsets, chunk, d) for n, (chunk, offsets, _) in enumerate(chosen) for d in range(decks)
+        (n, offsets, chunk, d, at)
+        for n, (chunk, parts, _) in enumerate(chosen)
+        for at, (offsets, d) in enumerate((o, d) for o, ds in parts for d in ds)
     ]
     given = [] if result is None else [result]
     vmem, anywhere = (pl.BlockSpec(memory_space=m) for m in (pltpu.VMEM, pl.ANY))
     wide = ((len(runs) * line, width), jnp.float32)
     return pl.pallas_call(
-        functools.partial(place_kernel, (rows, decks, line, block, runs), len(values), len(given)),
+        functools.partial(place_kernel, (rows, decks, line, runs), len(values), len(given)),
         out_shape=jax.ShapeDtypeStruct((total_rows, width), jnp.float32),
         in_specs=[pl.BlockSpec(memory_space=pltpu.SMEM)]
         + [vmem] * len(values)
@@ -289,7 +279,15 @@
     )(where, *values, *given)
 
 
-def raw_piece(cells, weight):
+def outer_rows(cells):
+    across = cells.shape[3]
+    decks = lax.axis_size("deck")
+    ends = jnp.where(lax.axis_index("side") == 1, cells[..., across - 2 :, :], cells[..., :2, :])
+    joints = [(2 * d + 1, 2 * d + 2) for d in range(decks - 1)]
+    return lax.ppermute(ends, SPAN, joints + [(j, i) for i, j in joints])
+
+
+def whole_piece(cells, outer, weight):
     layers, height, comps, across, width = cells.shape
     parts = []
     for _ in range(WEIGHT_PARTS):
@@ -299,28 +297,12 @@
     tile = jnp.concatenate(parts, axis=2)
     tile = jnp.pad(tile, ((0, 0), (0, 0), (0, width - tile.shape[2])))
     cells = cells.reshape(layers, height * comps, across, width)
-    return jnp.concatenate([cells, tile[:, None]], axis=1)
-
-
-def outer_rows(cells):
-    layers, height, comps, across, width = cells.shape
-    rows, decks = lax.axis_size("row"), lax.axis_size("deck")
-    ends = jnp.where(lax.axis_index("side") == 1, cells[..., across - 2 :, :], cells[..., :2, :])
-    ends = ends.transpose(0, 1, 3, 2, 4).reshape(layers, 2 * height, comps * width)
-    total = pl.cdiv(2 * height, TILE) * TILE
-    ends = jnp.pad(ends, ((0, 0), (0, total - 2 * height), (0, 0)))
-    found = []
-    for r in range(rows):
-        for other in range(2):
-            pairs = []
-            for i in range(rows):
-                to = (i + r) % rows
-                for d in range(decks - 1):
-                    low, high = 2 * (i * decks + d) + 1, 2 * (i * decks + d + 1)
-                    pairs.append((low, 2 * (to * decks + d + 1) + other))
-                    pairs.append((high, 2 * (to * decks + d) + 1 - other))
-            found.append(lax.ppermute(ends, ("row",) + SPAN, pairs))
-    return jnp.stack(found)
+    outer = outer.transpose(0, 1, 3, 2, 4).reshape(layers, 2 * height, comps, width)
+    groups = pl.cdiv(2 * height, across)
+    outer = jnp.pad(outer, ((0, 0), (0, groups * across - 2 * height), (0, 0), (0, 0)))
+    outer = outer.reshape(layers, groups, across, comps, width).transpose(0, 1, 3, 2, 4)
+    outer = outer.reshape(layers, groups * comps, across, width)
+    return jnp.concatenate([cells, tile[:, None], outer], axis=1)
 
 
 def spread_near(piece):
@@ -357,18 +339,20 @@
     outs = decks if share % (2 * decks) == 0 else 1
 
     cells = velocity_modes.transpose(0, 2, 3, 1, 4)
-    blocks = spread_cores(spread_near(raw_piece(cells, cell_weight)))
+    blocks = spread_cores(spread_near(whole_piece(cells, outer_rows(cells), cell_weight)))
     offsets = list(blocks)
-    outer = outer_rows(cells)
-    edges = [outer, rotate(outer, "core")]
-    slopes = plane_slopes(where, list(blocks.values()), edges, offsets, rows, cells.shape[2])
+    height, comps = cells.shape[1:3]
+    slopes = plane_slopes(where, list(blocks.values()), offsets, rows, height, comps)
     terms = [plane_terms(where, *slopes, n, share, rows, decks, outs) for n in range(CHUNKS)]
 
+    line = share * width // decks
+    every = range(decks)
+    half = decks // 2
+
     def put_all(result, chosen):
-        return put(where, result, width * width, rows, decks, chosen)
+        return put(where, result, width * width, rows, decks, chosen, line)
 
     parts = [parts_over_decks(t, decks) for t in terms]
-    parts[0], parts[1][0] = lax.optimization_barrier((parts[0], parts[1][0]))
     pieces = []
     for n in range(CHUNKS):
         mine = sum(part.astype(jnp.float32) for part in parts[n]).astype(jnp.bfloat16)
@@ -377,36 +361,35 @@
         )
 
     def to_core(chosen):
-        return [(n, (r, 1, s), rotate(v, "core")) for n, (r, _, s), v in chosen]
+        joined = rotate(jnp.concatenate([v for _, _, v in chosen], axis=0), "core")
+        parts = [((r, 1, s), ds) for _, ps, _ in chosen for (r, _, s), ds in ps]
+        return [(chosen[0][0], parts, joined)]
 
     result = None
-    near, far = [], []
+    waiting = []
     for n, piece in enumerate(pieces):
         across = rotate(piece, "side")
         along = [rotate(piece, "row", r) for r in range(1, rows)]
-        near.append([piece, across] + along)
-    for n in range(CHUNKS):
-        if n > 0:
-            near[n], result = lax.optimization_barrier((near[n], result))
-        piece, across, *along = near[n]
-        if n % 2 == 0:
-            diagonal = [rotate(across, "row", r) for r in range(1, rows)]
+        near = [(n, [((0, 0, 0), every)], piece), (n, [((0, 0, 1), every)], across)]
+        near += [(n, [((r, 0, 0), every)], v) for r, v in enumerate(along, 1)]
+        halves = [across[: half * line]] + [v[half * line :] for v in along]
+        if waiting:
+            result = put_all(result, waiting.pop(0))
+            halves, result = lax.optimization_barrier((halves, result))
+        far = [
+            (n, [((r, 0, 1), every[:half])], rotate(halves[0], "row", r)) for r in range(1, rows)
+        ]
+        far += [
+            (n, [((r, 0, 1), every[half:])], rotate(halves[r], "side")) for r in range(1, rows)
+        ]
+        if n < CHUNKS - 1:
+            waiting += [near, far + to_core(near + far)]
         else:
-            diagonal = [rotate(v, "side") for v in along]
-        if n < CHUNKS - 1:
-            near[n], near[n + 1][0] = lax.optimization_barrier((near[n], near[n + 1][0]))
-        chosen = [(n, (0, 0, 0), near[n][0]), (n, (0, 0, 1), near[n][1])]
-        chosen += [(n, (r, 0, 0), v) for r, v in enumerate(near[n][2:], 1)]
-        cores = to_core(chosen)
-        if n < CHUNKS - 1:
-            result = put_all(result, chosen + cores)
-            far = [(n, (r, 0, 1), v) for r, v in enumerate(diagonal, 1)]
-            far += to_core(far)
-        else:
-            result = put_all(result, far + chosen)
-            diagonal, result = lax.optimization_barrier((diagonal, result))
-            far = [(n, (r, 0, 1), v) for r, v in enumerate(diagonal, 1)]
-            result = put_all(result, cores + far)
+            core = to_core(near)
+            result = put_all(result, sum(waiting, []) + near)
+            last, result = lax.optimization_barrier(([v for _, _, v in far], result))
+            far = [(n, ps, v) for (_, ps, _), v in zip(far, last)]
+            result = put_all(result, core + far)
             result = put_all(result, to_core(far))
     return result.reshape(width, width, width)
 

time: 98.4 us -> 97.5 us (level)
  waiting for transfers between devices: 19.6 us -> 17.9 us
    ppermute x33 -> x29, starting transfers between devices: 34.8 us -> 42.9 us  [rotate(): lax.ppermute(value, axis, [(i, (i + by) % count) for i in range(count)])]
    ppermute x1, starting transfers between devices: 11.4 us -> 7.13 us  [spread_near(): got[r, 1] = lax.ppermute(piece, DIAGONAL, pairs)]
    ppermute x4 -> x1, starting transfers between devices: 3.91 us -> 0.66 us  [outer_rows(): return lax.ppermute(ends, SPAN, joints + [(j, i) for i, j in joints])]
    ppermute x33 -> x29, waiting for transfers between devices: 19.6 us -> 17.9 us  [rotate(): lax.ppermute(value, axis, [(i, (i + by) % count) for i in range(count)])]
    select_n x0 -> x1, other arithmetic: none -> 1.03 us  [outer_rows(): jnp.where(lax.axis_index('side') == 1, cells[..., across - 2:, :], cells[...]
    transpose x1 -> x0, other arithmetic: 1.03 us -> none  [outer_rows(): ends.transpose(0, 1, 3, 2, 4).reshape(layers, 2 * height, comps * width)]
  transfers between devices with their start and end apart: 38 -> 31, of which waited for: 10 -> 9; matrix products, arithmetic and copies ran while one was open for 2% -> 1% of each run, Pallas kernels for 13% -> 13%
where the time goes in v11:
time: 97.5 us; the launch traced here: 97.3 us
  starting transfers between devices  50.7 us (52%)
  Pallas kernels  25 us (26%)
  waiting for transfers between devices  17.9 us (18%)
  other arithmetic  2.94 us (3%)
    ppermute x29, starting transfers between devices, rotate(): lax.ppermute(value, axis, [(i, (i + by) % count) for i in range(count)])  42.9 us
    ppermute x29, waiting for transfers between devices, rotate(): lax.ppermute(value, axis, [(i, (i + by) % count) for i in range(count)])  17.9 us
    pallas_call x2, Pallas kernels, plane_terms(): pl.pallas_call(functools.partial(terms_kernel, share, chunk, rows, decks)...  11.5 us
    pallas_call x4, Pallas kernels, put(): pl.pallas_call(functools.partial(place_kernel, (rows, decks, line, runs),...  8.01 us
    ppermute x1, starting transfers between devices, spread_near(): got[r, 1] = lax.ppermute(piece, DIAGONAL, pairs)  7.13 us
    pallas_call x1, Pallas kernels, plane_slopes(): pl.pallas_call(functools.partial(slopes_kernel, sizes, offsets), out_shap...  5.49 us
  transfers between devices with their start and end apart: 31, of which 9 were waited for; matrix products, arithmetic and copies ran while one was open for 1% of the time, Pallas kernels for 13%

profile of v11, /device:TPU:1, one launch (start us, length us, event | category | flops | bytes accessed | tf_op | source)
XLA Modules:
  0.0 97.3 jit_solution(12391062338886093906)
XLA Ops:
  0.0 1.0 %broadcast_select_fusion = bf16[2,10,3,2,128]{4,3,2,1,0:T(2,128)(2,1)S(1)} fusion(pred[]{:T(512)S(6)} %eq.3, bf16[2,10,3,8,128]{4,3,2,1,0:T(8,128)(2,1)} %bitcast.17), kind=kLoop, calls=%fused_computation.6 | loop fusion | flops 15360 | bytes 92161 | tf_op jit(solution)/shard_map/jit(_where)/select_n | solution.py:285
  2.6 0.9 pad_maximum_fusion.3.refs_0_
  3.5 7.1 %collective-permute-start.6 = (bf16[2,40,8,128]{3,2,1,0:T(8,128)(2,1)S(1)}, bf16[2,40,8,128]{3,2,1,0:T(8,128)(2,1)S(1)}, u32[]{:S(2)}, u32[]{:S(2)}) collective-permute-start(bf16[2,40,8,128]{3,2,1,0:T(8,128)(2,1)S(1)} %pad_maximum_fusion.3.refs_0_), channel_id=1, source_target_pairs={{0,17},{1,16},{16,1},{17,0},{2,19},{3,18},{18,3},{19,2},{4,21},{5,... | collective-permute-start | bytes 491528 | tf_op jit(solution)/shard_map/ppermute | solution.py:314
  11.0 2.4 %collective-permute-start.1 = (bf16[2,40,8,128]{3,2,1,0:T(8,128)(2,1)S(1)}, bf16[2,40,8,128]{3,2,1,0:T(8,128)(2,1)S(1)}, u32[]{:S(2)}, u32[]{:S(2)}) collective-permute-start(bf16[2,40,8,128]{3,2,1,0:T(8,128)(2,1)S(1)} %pad_maximum_fusion.3.refs_0_), channel_id=1, source_target_pairs={{0,8},{8,0},{1,9},{9,1},{2,10},{10,2},{3,11},{11,3},{4,12},{12,4},... | collective-permute-start | bytes 491528 | tf_op jit(solution)/shard_map/ppermute | solution.py:23
  13.4 3.8 %collective-permute-start.7 = (bf16[2,40,8,128]{3,2,1,0:T(8,128)(2,1)S(1)}, bf16[2,40,8,128]{3,2,1,0:T(8,128)(2,1)S(1)}, u32[]{:S(2)}, u32[]{:S(2)}) collective-permute-start(bf16[2,40,8,128]{3,2,1,0:T(8,128)(2,1)S(1)} %collective-permute-done.6.refs_6_), channel_id=1, source_target_pairs={{0,8},{8,0},{1,9},{9,1},{2,10},{10,2},{3,11},{11,3},{4,12},{12,4},... | collective-permute-start | bytes 491528 | tf_op jit(solution)/shard_map/ppermute | solution.py:23
  17.9 1.4 %collective-permute-start.5 = (bf16[2,40,8,128]{3,2,1,0:T(8,128)(2,1)S(1)}, bf16[2,40,8,128]{3,2,1,0:T(8,128)(2,1)S(1)}, u32[]{:S(2)}, u32[]{:S(2)}) collective-permute-start(bf16[2,40,8,128]{3,2,1,0:T(8,128)(2,1)S(1)} %collective-permute-done.4.refs_4_), channel_id=1, source_target_pairs={{0,8},{8,0},{1,9},{9,1},{2,10},{10,2},{3,11},{11,3},{4,12},{12,4},... | collective-permute-start | bytes 491528 | tf_op jit(solution)/shard_map/ppermute | solution.py:23
  19.4 0.9 collective-permute-done.5.refs_5_
  20.7 5.5 %shard_map.28 = (bf16[4,3,128,1280]{3,2,1,0:T(8,128)(2,1)S(1)}, f32[3,128,1280]{2,1,0:T(8,128)S(1)}) custom-call(s32[4]{0:T(128)S(1)} %pad_add_fusion.where_ref, bf16[2,40,8,128]{3,2,1,0:T(8,128)(2,1)S(1)} %pad_maximum_fusion.3.refs_0_, bf16[2,40,8,128]{3,2,1,0:T(8,128)(2,1)S(1)} %collective-permute-done.1.refs_1_, ...), custom_call_target="tpu_custom_call" | custom-call | flops 503316480 | bytes 4194304 | tf_op jit(solution)/shard_map/pallas_call | solution.py:151
  26.2 5.7 %shard_map.30 = (f32[256,128]{1,0:T(8,128)S(1)}, bf16[256,128]{1,0:T(8,128)(2,1)S(1)}, bf16[256,128]{1,0:T(8,128)(2,1)S(1)}, bf16[256,128]{1,0:T(8,128)(2,1)S(1)}) custom-call(s32[4]{0:T(128)S(1)} %pad_add_fusion.where_ref, bf16[4,3,128,1280]{3,2,1,0:T(8,128)(2,1)S(1)} %get-tuple-element.21.turned, f32[3,128,1280]{2,1,0:T(8,128)S(1)} %get-tuple-element.22.phi), custom_call_target="tpu_custom_call" | custom-call | flops 1006632960 | bytes 4194304 | tf_op jit(solution)/shard_map/pallas_call | solution.py:213
  31.9 1.5 %collective-permute-start.16 = (bf16[256,128]{1,0:T(8,128)(2,1)S(1)}, bf16[256,128]{1,0:T(8,128)(2,1)S(1)}, u32[]{:S(2)}, u32[]{:S(2)}) collective-permute-start(bf16[256,128]{1,0:T(8,128)(2,1)S(1)} %get-tuple-element.28), channel_id=1, source_target_pairs={{0,2},{2,4},{4,6},{6,0},{1,3},{3,5},{5,7},{7,1},{8,10},{10,12},{12... | collective-permute-start | bytes 196616 | tf_op jit(solution)/shard_map/ppermute | solution.py:23
  33.5 2.0 %collective-permute-start.17 = (bf16[256,128]{1,0:T(8,128)(2,1)S(1)}, bf16[256,128]{1,0:T(8,128)(2,1)S(1)}, u32[]{:S(2)}, u32[]{:S(2)}) collective-permute-start(bf16[256,128]{1,0:T(8,128)(2,1)S(1)} %get-tuple-element.29), channel_id=1, source_target_pairs={{0,4},{2,6},{4,0},{6,2},{1,5},{3,7},{5,1},{7,3},{8,12},{10,14},{12... | collective-permute-start | bytes 196616 | tf_op jit(solution)/shard_map/ppermute | solution.py:23
  35.5 1.3 %collective-permute-start.18 = (bf16[256,128]{1,0:T(8,128)(2,1)S(1)}, bf16[256,128]{1,0:T(8,128)(2,1)S(1)}, u32[]{:S(2)}, u32[]{:S(2)}) collective-permute-start(bf16[256,128]{1,0:T(8,128)(2,1)S(1)} %get-tuple-element.30), channel_id=1, source_target_pairs={{0,6},{2,0},{4,2},{6,4},{1,7},{3,1},{5,3},{7,5},{8,14},{10,8},{12,... | collective-permute-start | bytes 196616 | tf_op jit(solution)/shard_map/ppermute | solution.py:23
  36.9 5.7 %shard_map.29 = (f32[256,128]{1,0:T(8,128)S(1)}, bf16[256,128]{1,0:T(8,128)(2,1)S(1)}, bf16[256,128]{1,0:T(8,128)(2,1)S(1)}, bf16[256,128]{1,0:T(8,128)(2,1)S(1)}) custom-call(s32[4]{0:T(128)S(1)} %pad_add_fusion.where_ref, bf16[4,3,128,1280]{3,2,1,0:T(8,128)(2,1)S(1)} %get-tuple-element.21.turned, f32[3,128,1280]{2,1,0:T(8,128)S(1)} %get-tuple-element.22.phi), custom_call_target="tpu_custom_call" | custom-call | flops 1006632960 | bytes 4194304 | tf_op jit(solution)/shard_map/pallas_call | solution.py:213
  43.1 2.8 %collective-permute-start.10 = (bf16[256,128]{1,0:T(8,128)(2,1)S(1)}, bf16[256,128]{1,0:T(8,128)(2,1)S(1)}, u32[]{:S(2)}, u32[]{:S(2)}) collective-permute-start(bf16[256,128]{1,0:T(8,128)(2,1)S(1)} %get-tuple-element.26), channel_id=1, source_target_pairs={{0,6},{2,0},{4,2},{6,4},{1,7},{3,1},{5,3},{7,5},{8,14},{10,8},{12,... | collective-permute-start | bytes 196616 | tf_op jit(solution)/shard_map/ppermute | solution.py:23
  46.4 1.1 %collective-permute-start.20 = (bf16[256,128]{1,0:T(8,128)(2,1)S(1)}, bf16[256,128]{1,0:T(8,128)(2,1)S(1)}, u32[]{:S(2)}, u32[]{:S(2)}) collective-permute-start(bf16[256,128]{1,0:T(8,128)(2,1)S(1)} %get-tuple-element.40), channel_id=1, source_target_pairs={{0,4},{2,6},{4,0},{6,2},{1,5},{3,7},{5,1},{7,3},{8,12},{10,14},{12... | collective-permute-start | bytes 196616 | tf_op jit(solution)/shard_map/ppermute | solution.py:23
  47.6 1.3 %collective-permute-start.19 = (bf16[256,128]{1,0:T(8,128)(2,1)S(1)}, bf16[256,128]{1,0:T(8,128)(2,1)S(1)}, u32[]{:S(2)}, u32[]{:S(2)}) collective-permute-start(bf16[256,128]{1,0:T(8,128)(2,1)S(1)} %get-tuple-element.40), channel_id=1, source_target_pairs={{0,2},{2,4},{4,6},{6,0},{1,3},{3,5},{5,7},{7,1},{8,10},{10,12},{12... | collective-permute-start | bytes 196616 | tf_op jit(solution)/shard_map/ppermute | solution.py:23
  49.0 6.7 %collective-permute-start.13 = (bf16[256,128]{1,0:T(8,128)(2,1)S(1)}, bf16[256,128]{1,0:T(8,128)(2,1)S(1)}, u32[]{:S(2)}, u32[]{:S(2)}) collective-permute-start(bf16[256,128]{1,0:T(8,128)(2,1)S(1)} %get-tuple-element.38), channel_id=1, source_target_pairs={{0,6},{2,0},{4,2},{6,4},{1,7},{3,1},{5,3},{7,5},{8,14},{10,8},{12,... | collective-permute-start | bytes 196616 | tf_op jit(solution)/shard_map/ppermute | solution.py:23
  56.1 0.9 collective-permute-done.20
  57.1 2.0 %collective-permute-start.23 = (bf16[1024,128]{1,0:T(8,128)(2,1)S(1)}, bf16[1024,128]{1,0:T(8,128)(2,1)S(1)}, u32[]{:S(2)}, u32[]{:S(2)}) collective-permute-start(bf16[1024,128]{1,0:T(8,128)(2,1)S(1)} %pad_maximum_fusion.1.refs_0_), channel_id=1, source_target_pairs={{0,16},{16,0},{1,17},{17,1},{2,18},{18,2},{3,19},{19,3},{4,20},{20... | collective-permute-start | bytes 786440 | tf_op jit(solution)/shard_map/ppermute | solution.py:23
  59.7 3.5 %collective-permute-done.23.refs_2_ = bf16[1024,128]{1,0:T(8,128)(2,1)S(1)} collective-permute-done((bf16[1024,128]{1,0:T(8,128)(2,1)S(1)}, bf16[1024,128]{1,0:T(8,128)(2,1)S(1)}, u32[]{:S(2)}, u32[]{:S(2)}) %collective-permute-start.23) | collective-permute-done | bytes 262176 | tf_op jit(solution)/shard_map/ppermute | solution.py:23
  63.2 1.4 %collective-permute-start.27 = (bf16[512,128]{1,0:T(8,128)(2,1)S(1)}, bf16[512,128]{1,0:T(8,128)(2,1)S(1)}, u32[]{:S(2)}, u32[]{:S(2)}) collective-permute-start(bf16[512,128]{1,0:T(8,128)(2,1)S(1)} %slice.29), channel_id=1, source_target_pairs={{0,1},{1,0},{2,3},{3,2},{4,5},{5,4},{6,7},{7,6},{8,9},{9,8},{10,11... | collective-permute-start | bytes 393224 | tf_op jit(solution)/shard_map/ppermute | solution.py:23
  65.3 3.5 %collective-permute-done.26.refs_0_ = bf16[512,128]{1,0:T(8,128)(2,1)S(1)} collective-permute-done((bf16[512,128]{1,0:T(8,128)(2,1)S(1)}, bf16[512,128]{1,0:T(8,128)(2,1)S(1)}, u32[]{:S(2)}, u32[]{:S(2)}) %collective-permute-start.26) | collective-permute-done | bytes 131104 | tf_op jit(solution)/shard_map/ppermute | solution.py:23
  68.9 6.5 %collective-permute-start.28 = (bf16[4096,128]{1,0:T(8,128)(2,1)S(1)}, bf16[4096,128]{1,0:T(8,128)(2,1)S(1)}, u32[]{:S(2)}, u32[]{:S(2)}) collective-permute-start(bf16[4096,128]{1,0:T(8,128)(2,1)S(1)} %constant_dynamic-update-slice_fusion), channel_id=1, source_target_pairs={{0,8},{8,0},{1,9},{9,1},{2,10},{10,2},{3,11},{11,3},{4,12},{12,4},... | collective-permute-start | bytes 3145736 | tf_op jit(solution)/shard_map/ppermute | solution.py:23
  75.5 1.4 %collective-permute-start.14 = (bf16[1024,128]{1,0:T(8,128)(2,1)S(1)}, bf16[1024,128]{1,0:T(8,128)(2,1)S(1)}, u32[]{:S(2)}, u32[]{:S(2)}) collective-permute-start(bf16[1024,128]{1,0:T(8,128)(2,1)S(1)} %pad_maximum_fusion.refs_3_), channel_id=1, source_target_pairs={{0,1},{1,0},{2,3},{3,2},{4,5},{5,4},{6,7},{7,6},{8,9},{9,8},{10,11... | collective-permute-start | bytes 786440 | tf_op jit(solution)/shard_map/ppermute | solution.py:23
  77.0 6.5 %collective-permute-done.14.refs_4_ = bf16[1024,128]{1,0:T(8,128)(2,1)S(1)} collective-permute-done((bf16[1024,128]{1,0:T(8,128)(2,1)S(1)}, bf16[1024,128]{1,0:T(8,128)(2,1)S(1)}, u32[]{:S(2)}, u32[]{:S(2)}) %collective-permute-start.14) | collective-permute-done | bytes 262176 | tf_op jit(solution)/shard_map/ppermute | solution.py:23
  84.5 1.8 %shard_map.31.refs_6_ = f32[16384,128]{1,0:T(8,128)} custom-call(s32[4]{0:T(128)S(1)} %pad_add_fusion.where_ref, bf16[1024,128]{1,0:T(8,128)(2,1)S(1)} %pad_maximum_fusion.1.refs_0_, bf16[1024,128]{1,0:T(8,128)(2,1)S(1)} %collective-permute-done.22.refs_1_, bf16[1024,128]{1,0:T(8,128)(2,1)S(1)} %collective-permute-done.23.refs_2_), custom_call_target="tpu_custom_call" | custom-call | bytes 2359296 | tf_op jit(solution)/shard_map/pallas_call | solution.py:264
  86.3 1.5 %collective-permute-start.24 = (bf16[512,128]{1,0:T(8,128)(2,1)S(1)}, bf16[512,128]{1,0:T(8,128)(2,1)S(1)}, u32[]{:S(2)}, u32[]{:S(2)}) collective-permute-start(bf16[512,128]{1,0:T(8,128)(2,1)S(1)} %slice.26), channel_id=1, source_target_pairs={{0,16},{16,0},{1,17},{17,1},{2,18},{18,2},{3,19},{19,3},{4,20},{20... | collective-permute-start | bytes 393224 | tf_op jit(solution)/shard_map/ppermute | solution.py:23
  88.3 2.8 %shard_map.32.refs_3_ = f32[16384,128]{1,0:T(8,128)} custom-call(s32[4]{0:T(128)S(1)} %pad_add_fusion.where_ref, bf16[512,128]{1,0:T(8,128)(2,1)S(1)} %collective-permute-done.26.refs_0_, bf16[512,128]{1,0:T(8,128)(2,1)S(1)} %collective-permute-done.27.refs_1_, ...), custom_call_target="tpu_custom_call", output_to_operand_aliasing={{}: (7, {})} | custom-call | bytes 6291456 | tf_op jit(solution)/shard_map/pallas_call | solution.py:264
  91.5 1.1 %collective-permute-done.25.refs_2_ = bf16[512,128]{1,0:T(8,128)(2,1)S(1)} collective-permute-done((bf16[512,128]{1,0:T(8,128)(2,1)S(1)}, bf16[512,128]{1,0:T(8,128)(2,1)S(1)}, u32[]{:S(2)}, u32[]{:S(2)}) %collective-permute-start.25) | collective-permute-done | bytes 131104 | tf_op jit(solution)/shard_map/ppermute | solution.py:23
  92.6 1.2 %collective-permute-start.29 = (bf16[1024,128]{1,0:T(8,128)(2,1)S(1)}, bf16[1024,128]{1,0:T(8,128)(2,1)S(1)}, u32[]{:S(2)}, u32[]{:S(2)}) collective-permute-start(bf16[1024,128]{1,0:T(8,128)(2,1)S(1)} %pad_maximum_fusion.2), channel_id=1, source_target_pairs={{0,8},{8,0},{1,9},{9,1},{2,10},{10,2},{3,11},{11,3},{4,12},{12,4},... | collective-permute-start | bytes 786440 | tf_op jit(solution)/shard_map/ppermute | solution.py:23
  93.7 2.0 %shard_map.33.refs_1_ = f32[16384,128]{1,0:T(8,128)} custom-call(s32[4]{0:T(128)S(1)} %pad_add_fusion.where_ref, bf16[3072,128]{1,0:T(8,128)(2,1)S(1)} %collective-permute-done.30.refs_0_, bf16[512,128]{1,0:T(8,128)(2,1)S(1)} %collective-permute-done.24.refs_1_, ...), custom_call_target="tpu_custom_call", output_to_operand_aliasing={{}: (4, {})} | custom-call | bytes 3145728 | tf_op jit(solution)/shard_map/pallas_call | solution.py:264
  95.8 1.4 %shard_map.34 = f32[16384,128]{1,0:T(8,128)} custom-call(s32[4]{0:T(128)S(1)} %pad_add_fusion.where_ref, bf16[1024,128]{1,0:T(8,128)(2,1)S(1)} %collective-permute-done.29.refs_0_, f32[16384,128]{1,0:T(8,128)} %shard_map.33.refs_1_), custom_call_target="tpu_custom_call", output_to_operand_aliasing={{}: (2, {})} | custom-call | bytes 786432 | tf_op jit(solution)/shard_map/pallas_call | solution.py:264
  (67 shorter events, 7.8 us)
Async XLA Ops:
  1.0 1.5 %collective-permute-start = (bf16[2,10,3,2,128]{4,3,2,1,0:T(2,128)(2,1)S(1)}, bf16[2,10,3,2,128]{4,3,2,1,0:T(2,128)(2,1)S(1)}, u32[]{:S(2)}, u32[]{:S(2)}) collective-permute-start(bf16[2,10,3,2,128]{4,3,2,1,0:T(2,128)(2,1)S(1)} %broadcast_select_fusion), channel_id=1, source_target_pairs={{1,2},{3,4},{5,6},{2,1},{4,3},{6,5},{9,10},{11,12},{13,14},{10,9},... | collective-permute-start | bytes 92168 | tf_op jit(solution)/shard_map/ppermute | solution.py:287
  3.5 9.9 %collective-permute-start.6 = (bf16[2,40,8,128]{3,2,1,0:T(8,128)(2,1)S(1)}, bf16[2,40,8,128]{3,2,1,0:T(8,128)(2,1)S(1)}, u32[]{:S(2)}, u32[]{:S(2)}) collective-permute-start(bf16[2,40,8,128]{3,2,1,0:T(8,128)(2,1)S(1)} %pad_maximum_fusion.3.refs_0_), channel_id=1, source_target_pairs={{0,17},{1,16},{16,1},{17,0},{2,19},{3,18},{18,3},{19,2},{4,21},{5,... | collective-permute-start | bytes 491528 | tf_op jit(solution)/shard_map/ppermute | solution.py:314
  10.6 7.2 %collective-permute-start.4 = (bf16[2,40,8,128]{3,2,1,0:T(8,128)(2,1)S(1)}, bf16[2,40,8,128]{3,2,1,0:T(8,128)(2,1)S(1)}, u32[]{:S(2)}, u32[]{:S(2)}) collective-permute-start(bf16[2,40,8,128]{3,2,1,0:T(8,128)(2,1)S(1)} %pad_maximum_fusion.3.refs_0_), channel_id=1, source_target_pairs={{0,16},{16,0},{1,17},{17,1},{2,18},{18,2},{3,19},{19,3},{4,20},{20... | collective-permute-start | bytes 491528 | tf_op jit(solution)/shard_map/ppermute | solution.py:23
  10.9 8.4 %collective-permute-start.2 = (bf16[2,40,8,128]{3,2,1,0:T(8,128)(2,1)S(1)}, bf16[2,40,8,128]{3,2,1,0:T(8,128)(2,1)S(1)}, u32[]{:S(2)}, u32[]{:S(2)}) collective-permute-start(bf16[2,40,8,128]{3,2,1,0:T(8,128)(2,1)S(1)} %pad_maximum_fusion.3.refs_0_), channel_id=1, source_target_pairs={{0,1},{1,0},{2,3},{3,2},{4,5},{5,4},{6,7},{7,6},{8,9},{9,8},{10,11... | collective-permute-start | bytes 491528 | tf_op jit(solution)/shard_map/ppermute | solution.py:23
  11.0 8.4 %collective-permute-start.1 = (bf16[2,40,8,128]{3,2,1,0:T(8,128)(2,1)S(1)}, bf16[2,40,8,128]{3,2,1,0:T(8,128)(2,1)S(1)}, u32[]{:S(2)}, u32[]{:S(2)}) collective-permute-start(bf16[2,40,8,128]{3,2,1,0:T(8,128)(2,1)S(1)} %pad_maximum_fusion.3.refs_0_), channel_id=1, source_target_pairs={{0,8},{8,0},{1,9},{9,1},{2,10},{10,2},{3,11},{11,3},{4,12},{12,4},... | collective-permute-start | bytes 491528 | tf_op jit(solution)/shard_map/ppermute | solution.py:23
  13.4 6.0 %collective-permute-start.7 = (bf16[2,40,8,128]{3,2,1,0:T(8,128)(2,1)S(1)}, bf16[2,40,8,128]{3,2,1,0:T(8,128)(2,1)S(1)}, u32[]{:S(2)}, u32[]{:S(2)}) collective-permute-start(bf16[2,40,8,128]{3,2,1,0:T(8,128)(2,1)S(1)} %collective-permute-done.6.refs_6_), channel_id=1, source_target_pairs={{0,8},{8,0},{1,9},{9,1},{2,10},{10,2},{3,11},{11,3},{4,12},{12,4},... | collective-permute-start | bytes 491528 | tf_op jit(solution)/shard_map/ppermute | solution.py:23
  17.9 2.5 %collective-permute-start.5 = (bf16[2,40,8,128]{3,2,1,0:T(8,128)(2,1)S(1)}, bf16[2,40,8,128]{3,2,1,0:T(8,128)(2,1)S(1)}, u32[]{:S(2)}, u32[]{:S(2)}) collective-permute-start(bf16[2,40,8,128]{3,2,1,0:T(8,128)(2,1)S(1)} %collective-permute-done.4.refs_4_), channel_id=1, source_target_pairs={{0,8},{8,0},{1,9},{9,1},{2,10},{10,2},{3,11},{11,3},{4,12},{12,4},... | collective-permute-start | bytes 491528 | tf_op jit(solution)/shard_map/ppermute | solution.py:23
  19.3 1.4 %collective-permute-start.3 = (bf16[2,40,8,128]{3,2,1,0:T(8,128)(2,1)S(1)}, bf16[2,40,8,128]{3,2,1,0:T(8,128)(2,1)S(1)}, u32[]{:S(2)}, u32[]{:S(2)}) collective-permute-start(bf16[2,40,8,128]{3,2,1,0:T(8,128)(2,1)S(1)} %collective-permute-done.2.refs_2_), channel_id=1, source_target_pairs={{0,8},{8,0},{1,9},{9,1},{2,10},{10,2},{3,11},{11,3},{4,12},{12,4},... | collective-permute-start | bytes 491528 | tf_op jit(solution)/shard_map/ppermute | solution.py:23
  31.9 11.2 %collective-permute-start.16 = (bf16[256,128]{1,0:T(8,128)(2,1)S(1)}, bf16[256,128]{1,0:T(8,128)(2,1)S(1)}, u32[]{:S(2)}, u32[]{:S(2)}) collective-permute-start(bf16[256,128]{1,0:T(8,128)(2,1)S(1)} %get-tuple-element.28), channel_id=1, source_target_pairs={{0,2},{2,4},{4,6},{6,0},{1,3},{3,5},{5,7},{7,1},{8,10},{10,12},{12... | collective-permute-start | bytes 196616 | tf_op jit(solution)/shard_map/ppermute | solution.py:23
  33.5 12.4 %collective-permute-start.17 = (bf16[256,128]{1,0:T(8,128)(2,1)S(1)}, bf16[256,128]{1,0:T(8,128)(2,1)S(1)}, u32[]{:S(2)}, u32[]{:S(2)}) collective-permute-start(bf16[256,128]{1,0:T(8,128)(2,1)S(1)} %get-tuple-element.29), channel_id=1, source_target_pairs={{0,4},{2,6},{4,0},{6,2},{1,5},{3,7},{5,1},{7,3},{8,12},{10,14},{12... | collective-permute-start | bytes 196616 | tf_op jit(solution)/shard_map/ppermute | solution.py:23
  35.5 10.4 %collective-permute-start.18 = (bf16[256,128]{1,0:T(8,128)(2,1)S(1)}, bf16[256,128]{1,0:T(8,128)(2,1)S(1)}, u32[]{:S(2)}, u32[]{:S(2)}) collective-permute-start(bf16[256,128]{1,0:T(8,128)(2,1)S(1)} %get-tuple-element.30), channel_id=1, source_target_pairs={{0,6},{2,0},{4,2},{6,4},{1,7},{3,1},{5,3},{7,5},{8,14},{10,8},{12,... | collective-permute-start | bytes 196616 | tf_op jit(solution)/shard_map/ppermute | solution.py:23
  42.6 5.0 %collective-permute-start.8 = (bf16[256,128]{1,0:T(8,128)(2,1)S(1)}, bf16[256,128]{1,0:T(8,128)(2,1)S(1)}, u32[]{:S(2)}, u32[]{:S(2)}) collective-permute-start(bf16[256,128]{1,0:T(8,128)(2,1)S(1)} %get-tuple-element.24), channel_id=1, source_target_pairs={{0,2},{2,4},{4,6},{6,0},{1,3},{3,5},{5,7},{7,1},{8,10},{10,12},{12... | collective-permute-start | bytes 196616 | tf_op jit(solution)/shard_map/ppermute | solution.py:23
  42.8 6.2 %collective-permute-start.9 = (bf16[256,128]{1,0:T(8,128)(2,1)S(1)}, bf16[256,128]{1,0:T(8,128)(2,1)S(1)}, u32[]{:S(2)}, u32[]{:S(2)}) collective-permute-start(bf16[256,128]{1,0:T(8,128)(2,1)S(1)} %get-tuple-element.25), channel_id=1, source_target_pairs={{0,4},{2,6},{4,0},{6,2},{1,5},{3,7},{5,1},{7,3},{8,12},{10,14},{12... | collective-permute-start | bytes 196616 | tf_op jit(solution)/shard_map/ppermute | solution.py:23
  43.1 5.9 %collective-permute-start.10 = (bf16[256,128]{1,0:T(8,128)(2,1)S(1)}, bf16[256,128]{1,0:T(8,128)(2,1)S(1)}, u32[]{:S(2)}, u32[]{:S(2)}) collective-permute-start(bf16[256,128]{1,0:T(8,128)(2,1)S(1)} %get-tuple-element.26), channel_id=1, source_target_pairs={{0,6},{2,0},{4,2},{6,4},{1,7},{3,1},{5,3},{7,5},{8,14},{10,8},{12,... | collective-permute-start | bytes 196616 | tf_op jit(solution)/shard_map/ppermute | solution.py:23
  46.0 9.8 %collective-permute-start.21 = (bf16[256,128]{1,0:T(8,128)(2,1)S(1)}, bf16[256,128]{1,0:T(8,128)(2,1)S(1)}, u32[]{:S(2)}, u32[]{:S(2)}) collective-permute-start(bf16[256,128]{1,0:T(8,128)(2,1)S(1)} %get-tuple-element.40), channel_id=1, source_target_pairs={{0,6},{2,0},{4,2},{6,4},{1,7},{3,1},{5,3},{7,5},{8,14},{10,8},{12,... | collective-permute-start | bytes 196616 | tf_op jit(solution)/shard_map/ppermute | solution.py:23
  46.4 10.6 %collective-permute-start.20 = (bf16[256,128]{1,0:T(8,128)(2,1)S(1)}, bf16[256,128]{1,0:T(8,128)(2,1)S(1)}, u32[]{:S(2)}, u32[]{:S(2)}) collective-permute-start(bf16[256,128]{1,0:T(8,128)(2,1)S(1)} %get-tuple-element.40), channel_id=1, source_target_pairs={{0,4},{2,6},{4,0},{6,2},{1,5},{3,7},{5,1},{7,3},{8,12},{10,14},{12... | collective-permute-start | bytes 196616 | tf_op jit(solution)/shard_map/ppermute | solution.py:23
  47.6 9.4 %collective-permute-start.19 = (bf16[256,128]{1,0:T(8,128)(2,1)S(1)}, bf16[256,128]{1,0:T(8,128)(2,1)S(1)}, u32[]{:S(2)}, u32[]{:S(2)}) collective-permute-start(bf16[256,128]{1,0:T(8,128)(2,1)S(1)} %get-tuple-element.40), channel_id=1, source_target_pairs={{0,2},{2,4},{4,6},{6,0},{1,3},{3,5},{5,7},{7,1},{8,10},{10,12},{12... | collective-permute-start | bytes 196616 | tf_op jit(solution)/shard_map/ppermute | solution.py:23
  49.0 26.4 %collective-permute-start.13 = (bf16[256,128]{1,0:T(8,128)(2,1)S(1)}, bf16[256,128]{1,0:T(8,128)(2,1)S(1)}, u32[]{:S(2)}, u32[]{:S(2)}) collective-permute-start(bf16[256,128]{1,0:T(8,128)(2,1)S(1)} %get-tuple-element.38), channel_id=1, source_target_pairs={{0,6},{2,0},{4,2},{6,4},{1,7},{3,1},{5,3},{7,5},{8,14},{10,8},{12,... | collective-permute-start | bytes 196616 | tf_op jit(solution)/shard_map/ppermute | solution.py:23
  55.8 19.6 %collective-permute-start.12 = (bf16[256,128]{1,0:T(8,128)(2,1)S(1)}, bf16[256,128]{1,0:T(8,128)(2,1)S(1)}, u32[]{:S(2)}, u32[]{:S(2)}) collective-permute-start(bf16[256,128]{1,0:T(8,128)(2,1)S(1)} %get-tuple-element.38), channel_id=1, source_target_pairs={{0,4},{2,6},{4,0},{6,2},{1,5},{3,7},{5,1},{7,3},{8,12},{10,14},{12... | collective-permute-start | bytes 196616 | tf_op jit(solution)/shard_map/ppermute | solution.py:23
  55.8 19.6 %collective-permute-start.11 = (bf16[256,128]{1,0:T(8,128)(2,1)S(1)}, bf16[256,128]{1,0:T(8,128)(2,1)S(1)}, u32[]{:S(2)}, u32[]{:S(2)}) collective-permute-start(bf16[256,128]{1,0:T(8,128)(2,1)S(1)} %get-tuple-element.38), channel_id=1, source_target_pairs={{0,2},{2,4},{4,6},{6,0},{1,3},{3,5},{5,7},{7,1},{8,10},{10,12},{12... | collective-permute-start | bytes 196616 | tf_op jit(solution)/shard_map/ppermute | solution.py:23
  57.1 6.1 %collective-permute-start.23 = (bf16[1024,128]{1,0:T(8,128)(2,1)S(1)}, bf16[1024,128]{1,0:T(8,128)(2,1)S(1)}, u32[]{:S(2)}, u32[]{:S(2)}) collective-permute-start(bf16[1024,128]{1,0:T(8,128)(2,1)S(1)} %pad_maximum_fusion.1.refs_0_), channel_id=1, source_target_pairs={{0,16},{16,0},{1,17},{17,1},{2,18},{18,2},{3,19},{19,3},{4,20},{20... | collective-permute-start | bytes 786440 | tf_op jit(solution)/shard_map/ppermute | solution.py:23
  59.1 5.5 %collective-permute-start.22 = (bf16[1024,128]{1,0:T(8,128)(2,1)S(1)}, bf16[1024,128]{1,0:T(8,128)(2,1)S(1)}, u32[]{:S(2)}, u32[]{:S(2)}) collective-permute-start(bf16[1024,128]{1,0:T(8,128)(2,1)S(1)} %pad_maximum_fusion.1.refs_0_), channel_id=1, source_target_pairs={{0,1},{1,0},{2,3},{3,2},{4,5},{5,4},{6,7},{7,6},{8,9},{9,8},{10,11... | collective-permute-start | bytes 786440 | tf_op jit(solution)/shard_map/ppermute | solution.py:23
  63.2 5.7 %collective-permute-start.27 = (bf16[512,128]{1,0:T(8,128)(2,1)S(1)}, bf16[512,128]{1,0:T(8,128)(2,1)S(1)}, u32[]{:S(2)}, u32[]{:S(2)}) collective-permute-start(bf16[512,128]{1,0:T(8,128)(2,1)S(1)} %slice.29), channel_id=1, source_target_pairs={{0,1},{1,0},{2,3},{3,2},{4,5},{5,4},{6,7},{7,6},{8,9},{9,8},{10,11... | collective-permute-start | bytes 393224 | tf_op jit(solution)/shard_map/ppermute | solution.py:23
  64.6 4.2 %collective-permute-start.26 = (bf16[512,128]{1,0:T(8,128)(2,1)S(1)}, bf16[512,128]{1,0:T(8,128)(2,1)S(1)}, u32[]{:S(2)}, u32[]{:S(2)}) collective-permute-start(bf16[512,128]{1,0:T(8,128)(2,1)S(1)} %slice.28), channel_id=1, source_target_pairs={{0,16},{16,0},{1,17},{17,1},{2,18},{18,2},{3,19},{19,3},{4,20},{20... | collective-permute-start | bytes 393224 | tf_op jit(solution)/shard_map/ppermute | solution.py:23
  68.9 19.4 %collective-permute-start.28 = (bf16[4096,128]{1,0:T(8,128)(2,1)S(1)}, bf16[4096,128]{1,0:T(8,128)(2,1)S(1)}, u32[]{:S(2)}, u32[]{:S(2)}) collective-permute-start(bf16[4096,128]{1,0:T(8,128)(2,1)S(1)} %constant_dynamic-update-slice_fusion), channel_id=1, source_target_pairs={{0,8},{8,0},{1,9},{9,1},{2,10},{10,2},{3,11},{11,3},{4,12},{12,4},... | collective-permute-start | bytes 3145736 | tf_op jit(solution)/shard_map/ppermute | solution.py:23
  75.4 8.1 %collective-permute-start.15 = (bf16[1024,128]{1,0:T(8,128)(2,1)S(1)}, bf16[1024,128]{1,0:T(8,128)(2,1)S(1)}, u32[]{:S(2)}, u32[]{:S(2)}) collective-permute-start(bf16[1024,128]{1,0:T(8,128)(2,1)S(1)} %pad_maximum_fusion.refs_3_), channel_id=1, source_target_pairs={{0,16},{16,0},{1,17},{17,1},{2,18},{18,2},{3,19},{19,3},{4,20},{20... | collective-permute-start | bytes 786440 | tf_op jit(solution)/shard_map/ppermute | solution.py:23
  75.5 8.0 %collective-permute-start.14 = (bf16[1024,128]{1,0:T(8,128)(2,1)S(1)}, bf16[1024,128]{1,0:T(8,128)(2,1)S(1)}, u32[]{:S(2)}, u32[]{:S(2)}) collective-permute-start(bf16[1024,128]{1,0:T(8,128)(2,1)S(1)} %pad_maximum_fusion.refs_3_), channel_id=1, source_target_pairs={{0,1},{1,0},{2,3},{3,2},{4,5},{5,4},{6,7},{7,6},{8,9},{9,8},{10,11... | collective-permute-start | bytes 786440 | tf_op jit(solution)/shard_map/ppermute | solution.py:23
  83.6 10.2 %collective-permute-start.30 = (bf16[3072,128]{1,0:T(8,128)(2,1)S(1)}, bf16[3072,128]{1,0:T(8,128)(2,1)S(1)}, u32[]{:S(2)}, u32[]{:S(2)}) collective-permute-start(bf16[3072,128]{1,0:T(8,128)(2,1)S(1)} %constant_dynamic-update-slice_fusion.8), channel_id=1, source_target_pairs={{0,8},{8,0},{1,9},{9,1},{2,10},{10,2},{3,11},{11,3},{4,12},{12,4},... | collective-permute-start | bytes 2359304 | tf_op jit(solution)/shard_map/ppermute | solution.py:23
  86.3 5.2 %collective-permute-start.24 = (bf16[512,128]{1,0:T(8,128)(2,1)S(1)}, bf16[512,128]{1,0:T(8,128)(2,1)S(1)}, u32[]{:S(2)}, u32[]{:S(2)}) collective-permute-start(bf16[512,128]{1,0:T(8,128)(2,1)S(1)} %slice.26), channel_id=1, source_target_pairs={{0,16},{16,0},{1,17},{17,1},{2,18},{18,2},{3,19},{19,3},{4,20},{20... | collective-permute-start | bytes 393224 | tf_op jit(solution)/shard_map/ppermute | solution.py:23
  87.7 4.8 %collective-permute-start.25 = (bf16[512,128]{1,0:T(8,128)(2,1)S(1)}, bf16[512,128]{1,0:T(8,128)(2,1)S(1)}, u32[]{:S(2)}, u32[]{:S(2)}) collective-permute-start(bf16[512,128]{1,0:T(8,128)(2,1)S(1)} %slice.27), channel_id=1, source_target_pairs={{0,1},{1,0},{2,3},{3,2},{4,5},{5,4},{6,7},{7,6},{8,9},{9,8},{10,11... | collective-permute-start | bytes 393224 | tf_op jit(solution)/shard_map/ppermute | solution.py:23
  92.6 3.2 %collective-permute-start.29 = (bf16[1024,128]{1,0:T(8,128)(2,1)S(1)}, bf16[1024,128]{1,0:T(8,128)(2,1)S(1)}, u32[]{:S(2)}, u32[]{:S(2)}) collective-permute-start(bf16[1024,128]{1,0:T(8,128)(2,1)S(1)} %pad_maximum_fusion.2), channel_id=1, source_target_pairs={{0,8},{8,0},{1,9},{9,1},{2,10},{10,2},{3,11},{11,3},{4,12},{12,4},... | collective-permute-start | bytes 786440 | tf_op jit(solution)/shard_map/ppermute | solution.py:23

commit v12 on v11

--- a/solution.py
+++ b/solution.py
@@ -162,8 +162,8 @@
 
 
 def terms_kernel(share, chunk, rows, decks, where_ref, turned, phi, *refs):
-    out_refs = [ref for ref in refs if len(ref.shape) == 2]
-    own, *quads = refs[len(out_refs) :]
+    *out_refs, own, even, odd = refs
+    quads = (even, odd)
     outs = len(out_refs)
     width, count = turned.shape[2:]
     base = (member(where_ref, rows, (0, 0, 0)) * CHUNKS + chunk) * share
@@ -173,13 +173,18 @@
         mode = base + lax.rem(i + first, share)
         for b in range(3):
             own[b, i] = jnp.broadcast_to(phi[b, pl.ds(mode, 1), :], (TILE, count))
-    for group in range(share // together):
-        modes = range(group * together, (group + 1) * together)
-        quad = quads[group % len(quads)]
-        for a in range(3):
+    units = [(group, a) for group in range(share // together) for a in range(3)]
+    totals = {}
+    for turn in range(len(units) + 1):
+        if turn < len(units):
+            group, a = units[turn]
+            quad = quads[turn % 2]
             for start in range(0, count, LANES):
                 lanes = slice(start, start + LANES)
-                spread = [[own[b, mode, :, lanes] for b in range(3)] for mode in modes]
+                spread = [
+                    [own[b, group * together + i, :, lanes] for b in range(3)]
+                    for i in range(together)
+                ]
                 for k in range(0, width, TILE):
                     slope = [
                         turned[1 + a, b, k : k + TILE, lanes].astype(jnp.float32) for b in range(3)
@@ -187,13 +192,16 @@
                     for i, row in enumerate(spread):
                         value = row[0] * slope[0] + row[1] * slope[1] + row[2] * slope[2]
                         at = i * width + k
-                        quad[a, at : at + TILE, lanes] = value.astype(jnp.bfloat16)
-        total = sum(
-            lax.dot_general(turned[0, a], quad[a], TURNED, preferred_element_type=jnp.float32)
-            for a in range(3)
-        )
-        for i, mode in enumerate(modes):
-            start = mode * width
+                        quad[at : at + TILE, lanes] = value.astype(jnp.bfloat16)
+        if turn > 0:
+            group, a = units[turn - 1]
+            value = lax.dot_general(
+                turned[0, a], quads[(turn - 1) % 2][...], TURNED, preferred_element_type=jnp.float32
+            )
+            totals[group] = totals[group] + value if a else value
+    for group, total in totals.items():
+        for i in range(together):
+            start = (group * together + i) * width
             out_ref = out_refs[start * outs // (share * width)]
             start = start % (share * width // outs)
             out_ref[start : start + width, :] = total[:, i * width : (i + 1) * width].astype(
@@ -208,7 +216,7 @@
     results = [((share * width // outs, width), t) for t in dtypes]
     scratch = [((3, share, TILE, count), jnp.float32)]
     together = min(4, share)
-    scratch += [((3, together * width, count), jnp.bfloat16)] * min(2, share // together)
+    scratch += [((together * width, count), jnp.bfloat16)] * 2
     inputs = [(v.shape, v.dtype) for v in (turned, phi)]
     return pl.pallas_call(
         functools.partial(terms_kernel, share, chunk, rows, decks),
@@ -343,7 +351,9 @@
     offsets = list(blocks)
     height, comps = cells.shape[1:3]
     slopes = plane_slopes(where, list(blocks.values()), offsets, rows, height, comps)
-    terms = [plane_terms(where, *slopes, n, share, rows, decks, outs) for n in range(CHUNKS)]
+    terms = [
+        list(plane_terms(where, *slopes, n, share, rows, decks, outs)) for n in range(CHUNKS)
+    ]
 
     line = share * width // decks
     every = range(decks)
@@ -352,18 +362,26 @@
     def put_all(result, chosen):
         return put(where, result, width * width, rows, decks, chosen, line)
 
-    parts = [parts_over_decks(t, decks) for t in terms]
     pieces = []
     for n in range(CHUNKS):
-        mine = sum(part.astype(jnp.float32) for part in parts[n]).astype(jnp.bfloat16)
+        parts = parts_over_decks(terms[n], decks)
+        if n < CHUNKS - 1:
+            parts, terms[n + 1][0] = lax.optimization_barrier((parts, terms[n + 1][0]))
+        mine = sum(part.astype(jnp.float32) for part in parts).astype(jnp.bfloat16)
+        if n < CHUNKS - 1:
+            mine, later = lax.optimization_barrier((mine, terms[n + 1]))
+            terms[n + 1] = list(later)
         pieces.append(
             jnp.concatenate([mine] + [rotate(mine, "deck", r) for r in range(1, decks)], axis=0)
         )
 
-    def to_core(chosen):
-        joined = rotate(jnp.concatenate([v for _, _, v in chosen], axis=0), "core")
-        parts = [((r, 1, s), ds) for _, ps, _ in chosen for (r, _, s), ds in ps]
-        return [(chosen[0][0], parts, joined)]
+    def join(chosen):
+        return chosen[0][0], sum((ps for _, ps, _ in chosen), []), jnp.concatenate(
+            [v for _, _, v in chosen], axis=0
+        )
+
+    def to_core(n, parts, value):
+        return n, [((r, 1, s), ds) for (r, _, s), ds in parts], rotate(value, "core")
 
     result = None
     waiting = []
@@ -373,8 +391,8 @@
         near = [(n, [((0, 0, 0), every)], piece), (n, [((0, 0, 1), every)], across)]
         near += [(n, [((r, 0, 0), every)], v) for r, v in enumerate(along, 1)]
         halves = [across[: half * line]] + [v[half * line :] for v in along]
-        if waiting:
-            result = put_all(result, waiting.pop(0))
+        if n > 0:
+            result = put_all(result, waiting)
             halves, result = lax.optimization_barrier((halves, result))
         far = [
             (n, [((r, 0, 1), every[:half])], rotate(halves[0], "row", r)) for r in range(1, rows)
@@ -383,14 +401,19 @@
             (n, [((r, 0, 1), every[half:])], rotate(halves[r], "side")) for r in range(1, rows)
         ]
         if n < CHUNKS - 1:
-            waiting += [near, far + to_core(near + far)]
+            waiting = near
+            held = [(far, join(near + far))]
         else:
-            core = to_core(near)
-            result = put_all(result, sum(waiting, []) + near)
+            first, second = join(near), []
+            for values, (m, parts, joined) in held:
+                joined, halves = lax.optimization_barrier((joined, halves))
+                second += values + [to_core(m, parts, joined)]
+            core = to_core(*first)
+            result = put_all(result, second + near)
             last, result = lax.optimization_barrier(([v for _, _, v in far], result))
             far = [(n, ps, v) for (_, ps, _), v in zip(far, last)]
-            result = put_all(result, core + far)
-            result = put_all(result, to_core(far))
+            result = put_all(result, [core] + far)
+            result = put_all(result, [to_core(*join(far))])
     return result.reshape(width, width, width)
 
 

time: 97.5 us -> 87.3 us (0.90)
  starting transfers between devices: 50.7 us -> 42.7 us
  waiting for transfers between devices: 17.9 us -> 14.8 us
    ppermute x29, starting transfers between devices: 42.9 us -> 34.9 us  [rotate(): lax.ppermute(value, axis, [(i, (i + by) % count) for i in range(count)])]
    ppermute x29, waiting for transfers between devices: 17.9 us -> 14.8 us  [rotate(): lax.ppermute(value, axis, [(i, (i + by) % count) for i in range(count)])]
  transfers between devices with their start and end apart: 31 -> 31, of which waited for: 9 -> 13; matrix products, arithmetic and copies ran while one was open for 1% -> 1% of each run, Pallas kernels for 13% -> 15%
where the time goes in v12:
time: 87.3 us; the launch traced here: 87.1 us
  starting transfers between devices  42.7 us (49%)
  Pallas kernels  25.9 us (30%)
  waiting for transfers between devices  14.8 us (17%)
  other arithmetic  2.93 us (3%)
    ppermute x29, starting transfers between devices, rotate(): lax.ppermute(value, axis, [(i, (i + by) % count) for i in range(count)])  34.9 us
    ppermute x29, waiting for transfers between devices, rotate(): lax.ppermute(value, axis, [(i, (i + by) % count) for i in range(count)])  14.8 us
    pallas_call x2, Pallas kernels, plane_terms(): pl.pallas_call(functools.partial(terms_kernel, share, chunk, rows, decks)...  12.4 us
    pallas_call x4, Pallas kernels, put(): pl.pallas_call(functools.partial(place_kernel, (rows, decks, line, runs),...  8.01 us
    ppermute x1, starting transfers between devices, spread_near(): got[r, 1] = lax.ppermute(piece, DIAGONAL, pairs)  7.13 us
    pallas_call x1, Pallas kernels, plane_slopes(): pl.pallas_call(functools.partial(slopes_kernel, sizes, offsets), out_shap...  5.49 us
  transfers between devices with their start and end apart: 31, of which 13 were waited for; matrix products, arithmetic and copies ran while one was open for 1% of the time, Pallas kernels for 15%

profile of v12, /device:TPU:1, one launch (start us, length us, event | category | flops | bytes accessed | tf_op | source)
XLA Modules:
  0.0 87.1 jit_solution(3573296754706419753)
XLA Ops:
  0.0 1.0 %broadcast_select_fusion = bf16[2,10,3,2,128]{4,3,2,1,0:T(2,128)(2,1)S(1)} fusion(pred[]{:T(512)S(6)} %eq.3, bf16[2,10,3,8,128]{4,3,2,1,0:T(8,128)(2,1)} %bitcast.17), kind=kLoop, calls=%fused_computation.5 | loop fusion | flops 15360 | bytes 92161 | tf_op jit(solution)/shard_map/jit(_where)/select_n | solution.py:293
  3.5 7.1 %collective-permute-start.6 = (bf16[2,40,8,128]{3,2,1,0:T(8,128)(2,1)S(1)}, bf16[2,40,8,128]{3,2,1,0:T(8,128)(2,1)S(1)}, u32[]{:S(2)}, u32[]{:S(2)}) collective-permute-start(bf16[2,40,8,128]{3,2,1,0:T(8,128)(2,1)S(1)} %pad_maximum_fusion.2.refs_0_), channel_id=1, source_target_pairs={{0,17},{1,16},{16,1},{17,0},{2,19},{3,18},{18,3},{19,2},{4,21},{5,... | collective-permute-start | bytes 491528 | tf_op jit(solution)/shard_map/ppermute | solution.py:322
  11.0 2.4 %collective-permute-start.1 = (bf16[2,40,8,128]{3,2,1,0:T(8,128)(2,1)S(1)}, bf16[2,40,8,128]{3,2,1,0:T(8,128)(2,1)S(1)}, u32[]{:S(2)}, u32[]{:S(2)}) collective-permute-start(bf16[2,40,8,128]{3,2,1,0:T(8,128)(2,1)S(1)} %pad_maximum_fusion.2.refs_0_), channel_id=1, source_target_pairs={{0,8},{8,0},{1,9},{9,1},{2,10},{10,2},{3,11},{11,3},{4,12},{12,4},... | collective-permute-start | bytes 491528 | tf_op jit(solution)/shard_map/ppermute | solution.py:23
  13.4 3.8 %collective-permute-start.7 = (bf16[2,40,8,128]{3,2,1,0:T(8,128)(2,1)S(1)}, bf16[2,40,8,128]{3,2,1,0:T(8,128)(2,1)S(1)}, u32[]{:S(2)}, u32[]{:S(2)}) collective-permute-start(bf16[2,40,8,128]{3,2,1,0:T(8,128)(2,1)S(1)} %collective-permute-done.6.refs_6_), channel_id=1, source_target_pairs={{0,8},{8,0},{1,9},{9,1},{2,10},{10,2},{3,11},{11,3},{4,12},{12,4},... | collective-permute-start | bytes 491528 | tf_op jit(solution)/shard_map/ppermute | solution.py:23
  17.9 1.4 %collective-permute-start.5 = (bf16[2,40,8,128]{3,2,1,0:T(8,128)(2,1)S(1)}, bf16[2,40,8,128]{3,2,1,0:T(8,128)(2,1)S(1)}, u32[]{:S(2)}, u32[]{:S(2)}) collective-permute-start(bf16[2,40,8,128]{3,2,1,0:T(8,128)(2,1)S(1)} %collective-permute-done.4.refs_4_), channel_id=1, source_target_pairs={{0,8},{8,0},{1,9},{9,1},{2,10},{10,2},{3,11},{11,3},{4,12},{12,4},... | collective-permute-start | bytes 491528 | tf_op jit(solution)/shard_map/ppermute | solution.py:23
  20.7 5.5 %shard_map.28 = (bf16[4,3,128,1280]{3,2,1,0:T(8,128)(2,1)S(1)}, f32[3,128,1280]{2,1,0:T(8,128)S(1)}) custom-call(s32[4]{0:T(128)S(1)} %pad_add_fusion.where_ref, bf16[2,40,8,128]{3,2,1,0:T(8,128)(2,1)S(1)} %pad_maximum_fusion.2.refs_0_, bf16[2,40,8,128]{3,2,1,0:T(8,128)(2,1)S(1)} %collective-permute-done.1.refs_1_, ...), custom_call_target="tpu_custom_call" | custom-call | flops 503316480 | bytes 4194304 | tf_op jit(solution)/shard_map/pallas_call | solution.py:151
  26.2 6.2 %shard_map.29 = (f32[256,128]{1,0:T(8,128)S(1)}, bf16[256,128]{1,0:T(8,128)(2,1)S(1)}, bf16[256,128]{1,0:T(8,128)(2,1)S(1)}, bf16[256,128]{1,0:T(8,128)(2,1)S(1)}) custom-call(s32[4]{0:T(128)S(1)} %pad_add_fusion.where_ref, bf16[4,3,128,1280]{3,2,1,0:T(8,128)(2,1)S(1)} %get-tuple-element.32.turned, f32[3,128,1280]{2,1,0:T(8,128)S(1)} %get-tuple-element.33.phi), custom_call_target="tpu_custom_call" | custom-call | flops 1006632960 | bytes 4194304 | tf_op jit(solution)/shard_map/pallas_call | solution.py:221
  32.4 1.5 %collective-permute-start.8 = (bf16[256,128]{1,0:T(8,128)(2,1)S(1)}, bf16[256,128]{1,0:T(8,128)(2,1)S(1)}, u32[]{:S(2)}, u32[]{:S(2)}) collective-permute-start(bf16[256,128]{1,0:T(8,128)(2,1)S(1)} %get-tuple-element.35), channel_id=1, source_target_pairs={{0,2},{2,4},{4,6},{6,0},{1,3},{3,5},{5,7},{7,1},{8,10},{10,12},{12... | collective-permute-start | bytes 196616 | tf_op jit(solution)/shard_map/ppermute | solution.py:23
  33.9 2.0 %collective-permute-start.9 = (bf16[256,128]{1,0:T(8,128)(2,1)S(1)}, bf16[256,128]{1,0:T(8,128)(2,1)S(1)}, u32[]{:S(2)}, u32[]{:S(2)}) collective-permute-start(bf16[256,128]{1,0:T(8,128)(2,1)S(1)} %get-tuple-element.36), channel_id=1, source_target_pairs={{0,4},{2,6},{4,0},{6,2},{1,5},{3,7},{5,1},{7,3},{8,12},{10,14},{12... | collective-permute-start | bytes 196616 | tf_op jit(solution)/shard_map/ppermute | solution.py:23
  36.0 1.3 %collective-permute-start.10 = (bf16[256,128]{1,0:T(8,128)(2,1)S(1)}, bf16[256,128]{1,0:T(8,128)(2,1)S(1)}, u32[]{:S(2)}, u32[]{:S(2)}) collective-permute-start(bf16[256,128]{1,0:T(8,128)(2,1)S(1)} %get-tuple-element.37), channel_id=1, source_target_pairs={{0,6},{2,0},{4,2},{6,4},{1,7},{3,1},{5,3},{7,5},{8,14},{10,8},{12,... | collective-permute-start | bytes 196616 | tf_op jit(solution)/shard_map/ppermute | solution.py:23
  37.3 6.2 %shard_map.30 = (f32[256,128]{1,0:T(8,128)S(1)}, bf16[256,128]{1,0:T(8,128)(2,1)S(1)}, bf16[256,128]{1,0:T(8,128)(2,1)S(1)}, bf16[256,128]{1,0:T(8,128)(2,1)S(1)}) custom-call(s32[4]{0:T(128)S(1)} %pad_add_fusion.where_ref, bf16[4,3,128,1280]{3,2,1,0:T(8,128)(2,1)S(1)} %get-tuple-element.32.turned, f32[3,128,1280]{2,1,0:T(8,128)S(1)} %get-tuple-element.33.phi), custom_call_target="tpu_custom_call" | custom-call | flops 1006632960 | bytes 4194304 | tf_op jit(solution)/shard_map/pallas_call | solution.py:221
  43.8 1.1 %collective-permute-start.20 = (bf16[256,128]{1,0:T(8,128)(2,1)S(1)}, bf16[256,128]{1,0:T(8,128)(2,1)S(1)}, u32[]{:S(2)}, u32[]{:S(2)}) collective-permute-start(bf16[256,128]{1,0:T(8,128)(2,1)S(1)} %add_convert_fusion.1), channel_id=1, source_target_pairs={{0,4},{2,6},{4,0},{6,2},{1,5},{3,7},{5,1},{7,3},{8,12},{10,14},{12... | collective-permute-start | bytes 196616 | tf_op jit(solution)/shard_map/ppermute | solution.py:23
  45.1 1.3 %collective-permute-start.11 = (bf16[256,128]{1,0:T(8,128)(2,1)S(1)}, bf16[256,128]{1,0:T(8,128)(2,1)S(1)}, u32[]{:S(2)}, u32[]{:S(2)}) collective-permute-start(bf16[256,128]{1,0:T(8,128)(2,1)S(1)} %get-tuple-element.48), channel_id=1, source_target_pairs={{0,2},{2,4},{4,6},{6,0},{1,3},{3,5},{5,7},{7,1},{8,10},{10,12},{12... | collective-permute-start | bytes 196616 | tf_op jit(solution)/shard_map/ppermute | solution.py:23
  46.4 2.0 %collective-permute-start.12 = (bf16[256,128]{1,0:T(8,128)(2,1)S(1)}, bf16[256,128]{1,0:T(8,128)(2,1)S(1)}, u32[]{:S(2)}, u32[]{:S(2)}) collective-permute-start(bf16[256,128]{1,0:T(8,128)(2,1)S(1)} %get-tuple-element.49), channel_id=1, source_target_pairs={{0,4},{2,6},{4,0},{6,2},{1,5},{3,7},{5,1},{7,3},{8,12},{10,14},{12... | collective-permute-start | bytes 196616 | tf_op jit(solution)/shard_map/ppermute | solution.py:23
  48.5 1.4 %collective-permute-done.19 = bf16[256,128]{1,0:T(8,128)(2,1)S(1)} collective-permute-done((bf16[256,128]{1,0:T(8,128)(2,1)S(1)}, bf16[256,128]{1,0:T(8,128)(2,1)S(1)}, u32[]{:S(2)}, u32[]{:S(2)}) %collective-permute-start.19) | collective-permute-done | bytes 65568 | tf_op jit(solution)/shard_map/ppermute | solution.py:23
  49.9 2.0 %collective-permute-start.13 = (bf16[256,128]{1,0:T(8,128)(2,1)S(1)}, bf16[256,128]{1,0:T(8,128)(2,1)S(1)}, u32[]{:S(2)}, u32[]{:S(2)}) collective-permute-start(bf16[256,128]{1,0:T(8,128)(2,1)S(1)} %get-tuple-element.50), channel_id=1, source_target_pairs={{0,6},{2,0},{4,2},{6,4},{1,7},{3,1},{5,3},{7,5},{8,14},{10,8},{12,... | collective-permute-start | bytes 196616 | tf_op jit(solution)/shard_map/ppermute | solution.py:23
  52.0 2.8 %collective-permute-start.23 = (bf16[1024,128]{1,0:T(8,128)(2,1)S(1)}, bf16[1024,128]{1,0:T(8,128)(2,1)S(1)}, u32[]{:S(2)}, u32[]{:S(2)}) collective-permute-start(bf16[1024,128]{1,0:T(8,128)(2,1)S(1)} %get-tuple-element.62.refs_0_), channel_id=1, source_target_pairs={{0,16},{16,0},{1,17},{17,1},{2,18},{18,2},{3,19},{19,3},{4,20},{20... | collective-permute-start | bytes 786440 | tf_op jit(solution)/shard_map/ppermute | solution.py:23
  54.8 1.1 %collective-permute-done.12 = bf16[256,128]{1,0:T(8,128)(2,1)S(1)} collective-permute-done((bf16[256,128]{1,0:T(8,128)(2,1)S(1)}, bf16[256,128]{1,0:T(8,128)(2,1)S(1)}, u32[]{:S(2)}, u32[]{:S(2)}) %collective-permute-start.12) | collective-permute-done | bytes 65568 | tf_op jit(solution)/shard_map/ppermute | solution.py:23
  55.9 2.5 %collective-permute-start.16 = (bf16[256,128]{1,0:T(8,128)(2,1)S(1)}, bf16[256,128]{1,0:T(8,128)(2,1)S(1)}, u32[]{:S(2)}, u32[]{:S(2)}) collective-permute-start(bf16[256,128]{1,0:T(8,128)(2,1)S(1)} %get-tuple-element.60), channel_id=1, source_target_pairs={{0,6},{2,0},{4,2},{6,4},{1,7},{3,1},{5,3},{7,5},{8,14},{10,8},{12,... | collective-permute-start | bytes 196616 | tf_op jit(solution)/shard_map/ppermute | solution.py:23
  59.7 3.1 %collective-permute-done.15 = bf16[256,128]{1,0:T(8,128)(2,1)S(1)} collective-permute-done((bf16[256,128]{1,0:T(8,128)(2,1)S(1)}, bf16[256,128]{1,0:T(8,128)(2,1)S(1)}, u32[]{:S(2)}, u32[]{:S(2)}) %collective-permute-start.15) | collective-permute-done | bytes 65568 | tf_op jit(solution)/shard_map/ppermute | solution.py:23
  62.9 1.2 %collective-permute-done.14 = bf16[256,128]{1,0:T(8,128)(2,1)S(1)} collective-permute-done((bf16[256,128]{1,0:T(8,128)(2,1)S(1)}, bf16[256,128]{1,0:T(8,128)(2,1)S(1)}, u32[]{:S(2)}, u32[]{:S(2)}) %collective-permute-start.14) | collective-permute-done | bytes 65568 | tf_op jit(solution)/shard_map/ppermute | solution.py:23
  64.1 1.3 %collective-permute-start.18 = (bf16[1024,128]{1,0:T(8,128)(2,1)S(1)}, bf16[1024,128]{1,0:T(8,128)(2,1)S(1)}, u32[]{:S(2)}, u32[]{:S(2)}) collective-permute-start(bf16[1024,128]{1,0:T(8,128)(2,1)S(1)} %pad_maximum_fusion.refs_3_), channel_id=1, source_target_pairs={{0,16},{16,0},{1,17},{17,1},{2,18},{18,2},{3,19},{19,3},{4,20},{20... | collective-permute-start | bytes 786440 | tf_op jit(solution)/shard_map/ppermute | solution.py:23
  65.6 1.3 %collective-permute-start.27 = (bf16[512,128]{1,0:T(8,128)(2,1)S(1)}, bf16[512,128]{1,0:T(8,128)(2,1)S(1)}, u32[]{:S(2)}, u32[]{:S(2)}) collective-permute-start(bf16[512,128]{1,0:T(8,128)(2,1)S(1)} %slice.29), channel_id=1, source_target_pairs={{0,1},{1,0},{2,3},{3,2},{4,5},{5,4},{6,7},{7,6},{8,9},{9,8},{10,11... | collective-permute-start | bytes 393224 | tf_op jit(solution)/shard_map/ppermute | solution.py:23
  67.3 1.8 %shard_map.31.refs_6_ = f32[16384,128]{1,0:T(8,128)} custom-call(s32[4]{0:T(128)S(1)} %pad_add_fusion.where_ref, bf16[1024,128]{1,0:T(8,128)(2,1)S(1)} %get-tuple-element.62.refs_0_, bf16[1024,128]{1,0:T(8,128)(2,1)S(1)} %collective-permute-done.22.refs_1_, bf16[1024,128]{1,0:T(8,128)(2,1)S(1)} %collective-permute-done.23.refs_2_), custom_call_target="tpu_custom_call" | custom-call | bytes 2359296 | tf_op jit(solution)/shard_map/pallas_call | solution.py:272
  69.4 1.5 %collective-permute-done.17.refs_4_ = bf16[1024,128]{1,0:T(8,128)(2,1)S(1)} collective-permute-done((bf16[1024,128]{1,0:T(8,128)(2,1)S(1)}, bf16[1024,128]{1,0:T(8,128)(2,1)S(1)}, u32[]{:S(2)}, u32[]{:S(2)}) %collective-permute-start.17) | collective-permute-done | bytes 262176 | tf_op jit(solution)/shard_map/ppermute | solution.py:23
  70.9 1.5 %collective-permute-done.26.refs_0_ = bf16[512,128]{1,0:T(8,128)(2,1)S(1)} collective-permute-done((bf16[512,128]{1,0:T(8,128)(2,1)S(1)}, bf16[512,128]{1,0:T(8,128)(2,1)S(1)}, u32[]{:S(2)}, u32[]{:S(2)}) %collective-permute-start.26) | collective-permute-done | bytes 131104 | tf_op jit(solution)/shard_map/ppermute | solution.py:23
  73.2 3.8 %collective-permute-start.28 = (bf16[4096,128]{1,0:T(8,128)(2,1)S(1)}, bf16[4096,128]{1,0:T(8,128)(2,1)S(1)}, u32[]{:S(2)}, u32[]{:S(2)}) collective-permute-start(bf16[4096,128]{1,0:T(8,128)(2,1)S(1)} %constant_dynamic-update-slice_fusion.4), channel_id=1, source_target_pairs={{0,8},{8,0},{1,9},{9,1},{2,10},{10,2},{3,11},{11,3},{4,12},{12,4},... | collective-permute-start | bytes 3145736 | tf_op jit(solution)/shard_map/ppermute | solution.py:23
  78.2 1.1 %collective-permute-done.28.refs_2_ = bf16[4096,128]{1,0:T(8,128)(2,1)S(1)} collective-permute-done((bf16[4096,128]{1,0:T(8,128)(2,1)S(1)}, bf16[4096,128]{1,0:T(8,128)(2,1)S(1)}, u32[]{:S(2)}, u32[]{:S(2)}) %collective-permute-start.28) | collective-permute-done | bytes 1048608 | tf_op jit(solution)/shard_map/ppermute | solution.py:23
  79.3 2.8 %shard_map.32.refs_3_ = f32[16384,128]{1,0:T(8,128)} custom-call(s32[4]{0:T(128)S(1)} %pad_add_fusion.where_ref, bf16[512,128]{1,0:T(8,128)(2,1)S(1)} %collective-permute-done.26.refs_0_, bf16[512,128]{1,0:T(8,128)(2,1)S(1)} %collective-permute-done.27.refs_1_, ...), custom_call_target="tpu_custom_call", output_to_operand_aliasing={{}: (7, {})} | custom-call | bytes 6291456 | tf_op jit(solution)/shard_map/pallas_call | solution.py:272
  82.1 1.4 %collective-permute-start.29 = (bf16[1024,128]{1,0:T(8,128)(2,1)S(1)}, bf16[1024,128]{1,0:T(8,128)(2,1)S(1)}, u32[]{:S(2)}, u32[]{:S(2)}) collective-permute-start(bf16[1024,128]{1,0:T(8,128)(2,1)S(1)} %pad_maximum_fusion.1), channel_id=1, source_target_pairs={{0,8},{8,0},{1,9},{9,1},{2,10},{10,2},{3,11},{11,3},{4,12},{12,4},... | collective-permute-start | bytes 786440 | tf_op jit(solution)/shard_map/ppermute | solution.py:23
  83.5 2.0 %shard_map.33.refs_1_ = f32[16384,128]{1,0:T(8,128)} custom-call(s32[4]{0:T(128)S(1)} %pad_add_fusion.where_ref, bf16[3072,128]{1,0:T(8,128)(2,1)S(1)} %collective-permute-done.30.refs_0_, bf16[512,128]{1,0:T(8,128)(2,1)S(1)} %collective-permute-done.24.refs_1_, ...), custom_call_target="tpu_custom_call", output_to_operand_aliasing={{}: (4, {})} | custom-call | bytes 3145728 | tf_op jit(solution)/shard_map/pallas_call | solution.py:272
  85.5 1.4 %shard_map.34 = f32[16384,128]{1,0:T(8,128)} custom-call(s32[4]{0:T(128)S(1)} %pad_add_fusion.where_ref, bf16[1024,128]{1,0:T(8,128)(2,1)S(1)} %collective-permute-done.29.refs_0_, f32[16384,128]{1,0:T(8,128)} %shard_map.33.refs_1_), custom_call_target="tpu_custom_call", output_to_operand_aliasing={{}: (2, {})} | custom-call | bytes 786432 | tf_op jit(solution)/shard_map/pallas_call | solution.py:272
  (67 shorter events, 9.6 us)
Async XLA Ops:
  1.0 1.5 %collective-permute-start = (bf16[2,10,3,2,128]{4,3,2,1,0:T(2,128)(2,1)S(1)}, bf16[2,10,3,2,128]{4,3,2,1,0:T(2,128)(2,1)S(1)}, u32[]{:S(2)}, u32[]{:S(2)}) collective-permute-start(bf16[2,10,3,2,128]{4,3,2,1,0:T(2,128)(2,1)S(1)} %broadcast_select_fusion), channel_id=1, source_target_pairs={{1,2},{3,4},{5,6},{2,1},{4,3},{6,5},{9,10},{11,12},{13,14},{10,9},... | collective-permute-start | bytes 92168 | tf_op jit(solution)/shard_map/ppermute | solution.py:295
  3.5 9.9 %collective-permute-start.6 = (bf16[2,40,8,128]{3,2,1,0:T(8,128)(2,1)S(1)}, bf16[2,40,8,128]{3,2,1,0:T(8,128)(2,1)S(1)}, u32[]{:S(2)}, u32[]{:S(2)}) collective-permute-start(bf16[2,40,8,128]{3,2,1,0:T(8,128)(2,1)S(1)} %pad_maximum_fusion.2.refs_0_), channel_id=1, source_target_pairs={{0,17},{1,16},{16,1},{17,0},{2,19},{3,18},{18,3},{19,2},{4,21},{5,... | collective-permute-start | bytes 491528 | tf_op jit(solution)/shard_map/ppermute | solution.py:322
  10.6 7.2 %collective-permute-start.4 = (bf16[2,40,8,128]{3,2,1,0:T(8,128)(2,1)S(1)}, bf16[2,40,8,128]{3,2,1,0:T(8,128)(2,1)S(1)}, u32[]{:S(2)}, u32[]{:S(2)}) collective-permute-start(bf16[2,40,8,128]{3,2,1,0:T(8,128)(2,1)S(1)} %pad_maximum_fusion.2.refs_0_), channel_id=1, source_target_pairs={{0,16},{16,0},{1,17},{17,1},{2,18},{18,2},{3,19},{19,3},{4,20},{20... | collective-permute-start | bytes 491528 | tf_op jit(solution)/shard_map/ppermute | solution.py:23
  10.9 8.4 %collective-permute-start.2 = (bf16[2,40,8,128]{3,2,1,0:T(8,128)(2,1)S(1)}, bf16[2,40,8,128]{3,2,1,0:T(8,128)(2,1)S(1)}, u32[]{:S(2)}, u32[]{:S(2)}) collective-permute-start(bf16[2,40,8,128]{3,2,1,0:T(8,128)(2,1)S(1)} %pad_maximum_fusion.2.refs_0_), channel_id=1, source_target_pairs={{0,1},{1,0},{2,3},{3,2},{4,5},{5,4},{6,7},{7,6},{8,9},{9,8},{10,11... | collective-permute-start | bytes 491528 | tf_op jit(solution)/shard_map/ppermute | solution.py:23
  11.0 8.4 %collective-permute-start.1 = (bf16[2,40,8,128]{3,2,1,0:T(8,128)(2,1)S(1)}, bf16[2,40,8,128]{3,2,1,0:T(8,128)(2,1)S(1)}, u32[]{:S(2)}, u32[]{:S(2)}) collective-permute-start(bf16[2,40,8,128]{3,2,1,0:T(8,128)(2,1)S(1)} %pad_maximum_fusion.2.refs_0_), channel_id=1, source_target_pairs={{0,8},{8,0},{1,9},{9,1},{2,10},{10,2},{3,11},{11,3},{4,12},{12,4},... | collective-permute-start | bytes 491528 | tf_op jit(solution)/shard_map/ppermute | solution.py:23
  13.4 6.0 %collective-permute-start.7 = (bf16[2,40,8,128]{3,2,1,0:T(8,128)(2,1)S(1)}, bf16[2,40,8,128]{3,2,1,0:T(8,128)(2,1)S(1)}, u32[]{:S(2)}, u32[]{:S(2)}) collective-permute-start(bf16[2,40,8,128]{3,2,1,0:T(8,128)(2,1)S(1)} %collective-permute-done.6.refs_6_), channel_id=1, source_target_pairs={{0,8},{8,0},{1,9},{9,1},{2,10},{10,2},{3,11},{11,3},{4,12},{12,4},... | collective-permute-start | bytes 491528 | tf_op jit(solution)/shard_map/ppermute | solution.py:23
  17.9 2.5 %collective-permute-start.5 = (bf16[2,40,8,128]{3,2,1,0:T(8,128)(2,1)S(1)}, bf16[2,40,8,128]{3,2,1,0:T(8,128)(2,1)S(1)}, u32[]{:S(2)}, u32[]{:S(2)}) collective-permute-start(bf16[2,40,8,128]{3,2,1,0:T(8,128)(2,1)S(1)} %collective-permute-done.4.refs_4_), channel_id=1, source_target_pairs={{0,8},{8,0},{1,9},{9,1},{2,10},{10,2},{3,11},{11,3},{4,12},{12,4},... | collective-permute-start | bytes 491528 | tf_op jit(solution)/shard_map/ppermute | solution.py:23
  19.3 1.4 %collective-permute-start.3 = (bf16[2,40,8,128]{3,2,1,0:T(8,128)(2,1)S(1)}, bf16[2,40,8,128]{3,2,1,0:T(8,128)(2,1)S(1)}, u32[]{:S(2)}, u32[]{:S(2)}) collective-permute-start(bf16[2,40,8,128]{3,2,1,0:T(8,128)(2,1)S(1)} %collective-permute-done.2.refs_2_), channel_id=1, source_target_pairs={{0,8},{8,0},{1,9},{9,1},{2,10},{10,2},{3,11},{11,3},{4,12},{12,4},... | collective-permute-start | bytes 491528 | tf_op jit(solution)/shard_map/ppermute | solution.py:23
  32.4 11.1 %collective-permute-start.8 = (bf16[256,128]{1,0:T(8,128)(2,1)S(1)}, bf16[256,128]{1,0:T(8,128)(2,1)S(1)}, u32[]{:S(2)}, u32[]{:S(2)}) collective-permute-start(bf16[256,128]{1,0:T(8,128)(2,1)S(1)} %get-tuple-element.35), channel_id=1, source_target_pairs={{0,2},{2,4},{4,6},{6,0},{1,3},{3,5},{5,7},{7,1},{8,10},{10,12},{12... | collective-permute-start | bytes 196616 | tf_op jit(solution)/shard_map/ppermute | solution.py:23
  33.9 9.6 %collective-permute-start.9 = (bf16[256,128]{1,0:T(8,128)(2,1)S(1)}, bf16[256,128]{1,0:T(8,128)(2,1)S(1)}, u32[]{:S(2)}, u32[]{:S(2)}) collective-permute-start(bf16[256,128]{1,0:T(8,128)(2,1)S(1)} %get-tuple-element.36), channel_id=1, source_target_pairs={{0,4},{2,6},{4,0},{6,2},{1,5},{3,7},{5,1},{7,3},{8,12},{10,14},{12... | collective-permute-start | bytes 196616 | tf_op jit(solution)/shard_map/ppermute | solution.py:23
  36.0 7.5 %collective-permute-start.10 = (bf16[256,128]{1,0:T(8,128)(2,1)S(1)}, bf16[256,128]{1,0:T(8,128)(2,1)S(1)}, u32[]{:S(2)}, u32[]{:S(2)}) collective-permute-start(bf16[256,128]{1,0:T(8,128)(2,1)S(1)} %get-tuple-element.37), channel_id=1, source_target_pairs={{0,6},{2,0},{4,2},{6,4},{1,7},{3,1},{5,3},{7,5},{8,14},{10,8},{12,... | collective-permute-start | bytes 196616 | tf_op jit(solution)/shard_map/ppermute | solution.py:23
  43.6 8.4 %collective-permute-start.21 = (bf16[256,128]{1,0:T(8,128)(2,1)S(1)}, bf16[256,128]{1,0:T(8,128)(2,1)S(1)}, u32[]{:S(2)}, u32[]{:S(2)}) collective-permute-start(bf16[256,128]{1,0:T(8,128)(2,1)S(1)} %add_convert_fusion.1), channel_id=1, source_target_pairs={{0,6},{2,0},{4,2},{6,4},{1,7},{3,1},{5,3},{7,5},{8,14},{10,8},{12,... | collective-permute-start | bytes 196616 | tf_op jit(solution)/shard_map/ppermute | solution.py:23
  43.8 8.1 %collective-permute-start.20 = (bf16[256,128]{1,0:T(8,128)(2,1)S(1)}, bf16[256,128]{1,0:T(8,128)(2,1)S(1)}, u32[]{:S(2)}, u32[]{:S(2)}) collective-permute-start(bf16[256,128]{1,0:T(8,128)(2,1)S(1)} %add_convert_fusion.1), channel_id=1, source_target_pairs={{0,4},{2,6},{4,0},{6,2},{1,5},{3,7},{5,1},{7,3},{8,12},{10,14},{12... | collective-permute-start | bytes 196616 | tf_op jit(solution)/shard_map/ppermute | solution.py:23
  44.9 5.0 %collective-permute-start.19 = (bf16[256,128]{1,0:T(8,128)(2,1)S(1)}, bf16[256,128]{1,0:T(8,128)(2,1)S(1)}, u32[]{:S(2)}, u32[]{:S(2)}) collective-permute-start(bf16[256,128]{1,0:T(8,128)(2,1)S(1)} %add_convert_fusion.1), channel_id=1, source_target_pairs={{0,2},{2,4},{4,6},{6,0},{1,3},{3,5},{5,7},{7,1},{8,10},{10,12},{12... | collective-permute-start | bytes 196616 | tf_op jit(solution)/shard_map/ppermute | solution.py:23
  45.1 9.7 %collective-permute-start.11 = (bf16[256,128]{1,0:T(8,128)(2,1)S(1)}, bf16[256,128]{1,0:T(8,128)(2,1)S(1)}, u32[]{:S(2)}, u32[]{:S(2)}) collective-permute-start(bf16[256,128]{1,0:T(8,128)(2,1)S(1)} %get-tuple-element.48), channel_id=1, source_target_pairs={{0,2},{2,4},{4,6},{6,0},{1,3},{3,5},{5,7},{7,1},{8,10},{10,12},{12... | collective-permute-start | bytes 196616 | tf_op jit(solution)/shard_map/ppermute | solution.py:23
  46.4 9.4 %collective-permute-start.12 = (bf16[256,128]{1,0:T(8,128)(2,1)S(1)}, bf16[256,128]{1,0:T(8,128)(2,1)S(1)}, u32[]{:S(2)}, u32[]{:S(2)}) collective-permute-start(bf16[256,128]{1,0:T(8,128)(2,1)S(1)} %get-tuple-element.49), channel_id=1, source_target_pairs={{0,4},{2,6},{4,0},{6,2},{1,5},{3,7},{5,1},{7,3},{8,12},{10,14},{12... | collective-permute-start | bytes 196616 | tf_op jit(solution)/shard_map/ppermute | solution.py:23
  49.9 6.0 %collective-permute-start.13 = (bf16[256,128]{1,0:T(8,128)(2,1)S(1)}, bf16[256,128]{1,0:T(8,128)(2,1)S(1)}, u32[]{:S(2)}, u32[]{:S(2)}) collective-permute-start(bf16[256,128]{1,0:T(8,128)(2,1)S(1)} %get-tuple-element.50), channel_id=1, source_target_pairs={{0,6},{2,0},{4,2},{6,4},{1,7},{3,1},{5,3},{7,5},{8,14},{10,8},{12,... | collective-permute-start | bytes 196616 | tf_op jit(solution)/shard_map/ppermute | solution.py:23
  52.0 13.6 %collective-permute-start.23 = (bf16[1024,128]{1,0:T(8,128)(2,1)S(1)}, bf16[1024,128]{1,0:T(8,128)(2,1)S(1)}, u32[]{:S(2)}, u32[]{:S(2)}) collective-permute-start(bf16[1024,128]{1,0:T(8,128)(2,1)S(1)} %get-tuple-element.62.refs_0_), channel_id=1, source_target_pairs={{0,16},{16,0},{1,17},{17,1},{2,18},{18,2},{3,19},{19,3},{4,20},{20... | collective-permute-start | bytes 786440 | tf_op jit(solution)/shard_map/ppermute | solution.py:23
  54.7 12.2 %collective-permute-start.22 = (bf16[1024,128]{1,0:T(8,128)(2,1)S(1)}, bf16[1024,128]{1,0:T(8,128)(2,1)S(1)}, u32[]{:S(2)}, u32[]{:S(2)}) collective-permute-start(bf16[1024,128]{1,0:T(8,128)(2,1)S(1)} %get-tuple-element.62.refs_0_), channel_id=1, source_target_pairs={{0,1},{1,0},{2,3},{3,2},{4,5},{5,4},{6,7},{7,6},{8,9},{9,8},{10,11... | collective-permute-start | bytes 786440 | tf_op jit(solution)/shard_map/ppermute | solution.py:23
  55.9 3.8 %collective-permute-start.16 = (bf16[256,128]{1,0:T(8,128)(2,1)S(1)}, bf16[256,128]{1,0:T(8,128)(2,1)S(1)}, u32[]{:S(2)}, u32[]{:S(2)}) collective-permute-start(bf16[256,128]{1,0:T(8,128)(2,1)S(1)} %get-tuple-element.60), channel_id=1, source_target_pairs={{0,6},{2,0},{4,2},{6,4},{1,7},{3,1},{5,3},{7,5},{8,14},{10,8},{12,... | collective-permute-start | bytes 196616 | tf_op jit(solution)/shard_map/ppermute | solution.py:23
  58.4 4.5 %collective-permute-start.15 = (bf16[256,128]{1,0:T(8,128)(2,1)S(1)}, bf16[256,128]{1,0:T(8,128)(2,1)S(1)}, u32[]{:S(2)}, u32[]{:S(2)}) collective-permute-start(bf16[256,128]{1,0:T(8,128)(2,1)S(1)} %get-tuple-element.60), channel_id=1, source_target_pairs={{0,4},{2,6},{4,0},{6,2},{1,5},{3,7},{5,1},{7,3},{8,12},{10,14},{12... | collective-permute-start | bytes 196616 | tf_op jit(solution)/shard_map/ppermute | solution.py:23
  58.8 5.2 %collective-permute-start.14 = (bf16[256,128]{1,0:T(8,128)(2,1)S(1)}, bf16[256,128]{1,0:T(8,128)(2,1)S(1)}, u32[]{:S(2)}, u32[]{:S(2)}) collective-permute-start(bf16[256,128]{1,0:T(8,128)(2,1)S(1)} %get-tuple-element.60), channel_id=1, source_target_pairs={{0,2},{2,4},{4,6},{6,0},{1,3},{3,5},{5,7},{7,1},{8,10},{10,12},{12... | collective-permute-start | bytes 196616 | tf_op jit(solution)/shard_map/ppermute | solution.py:23
  64.1 5.3 %collective-permute-start.18 = (bf16[1024,128]{1,0:T(8,128)(2,1)S(1)}, bf16[1024,128]{1,0:T(8,128)(2,1)S(1)}, u32[]{:S(2)}, u32[]{:S(2)}) collective-permute-start(bf16[1024,128]{1,0:T(8,128)(2,1)S(1)} %pad_maximum_fusion.refs_3_), channel_id=1, source_target_pairs={{0,16},{16,0},{1,17},{17,1},{2,18},{18,2},{3,19},{19,3},{4,20},{20... | collective-permute-start | bytes 786440 | tf_op jit(solution)/shard_map/ppermute | solution.py:23
  65.3 5.5 %collective-permute-start.17 = (bf16[1024,128]{1,0:T(8,128)(2,1)S(1)}, bf16[1024,128]{1,0:T(8,128)(2,1)S(1)}, u32[]{:S(2)}, u32[]{:S(2)}) collective-permute-start(bf16[1024,128]{1,0:T(8,128)(2,1)S(1)} %pad_maximum_fusion.refs_3_), channel_id=1, source_target_pairs={{0,1},{1,0},{2,3},{3,2},{4,5},{5,4},{6,7},{7,6},{8,9},{9,8},{10,11... | collective-permute-start | bytes 786440 | tf_op jit(solution)/shard_map/ppermute | solution.py:23
  65.6 7.6 %collective-permute-start.27 = (bf16[512,128]{1,0:T(8,128)(2,1)S(1)}, bf16[512,128]{1,0:T(8,128)(2,1)S(1)}, u32[]{:S(2)}, u32[]{:S(2)}) collective-permute-start(bf16[512,128]{1,0:T(8,128)(2,1)S(1)} %slice.29), channel_id=1, source_target_pairs={{0,1},{1,0},{2,3},{3,2},{4,5},{5,4},{6,7},{7,6},{8,9},{9,8},{10,11... | collective-permute-start | bytes 393224 | tf_op jit(solution)/shard_map/ppermute | solution.py:23
  66.9 5.5 %collective-permute-start.26 = (bf16[512,128]{1,0:T(8,128)(2,1)S(1)}, bf16[512,128]{1,0:T(8,128)(2,1)S(1)}, u32[]{:S(2)}, u32[]{:S(2)}) collective-permute-start(bf16[512,128]{1,0:T(8,128)(2,1)S(1)} %slice.28), channel_id=1, source_target_pairs={{0,16},{16,0},{1,17},{17,1},{2,18},{18,2},{3,19},{19,3},{4,20},{20... | collective-permute-start | bytes 393224 | tf_op jit(solution)/shard_map/ppermute | solution.py:23
  73.2 6.1 %collective-permute-start.28 = (bf16[4096,128]{1,0:T(8,128)(2,1)S(1)}, bf16[4096,128]{1,0:T(8,128)(2,1)S(1)}, u32[]{:S(2)}, u32[]{:S(2)}) collective-permute-start(bf16[4096,128]{1,0:T(8,128)(2,1)S(1)} %constant_dynamic-update-slice_fusion.4), channel_id=1, source_target_pairs={{0,8},{8,0},{1,9},{9,1},{2,10},{10,2},{3,11},{11,3},{4,12},{12,4},... | collective-permute-start | bytes 3145736 | tf_op jit(solution)/shard_map/ppermute | solution.py:23
  77.1 6.4 %collective-permute-start.30 = (bf16[3072,128]{1,0:T(8,128)(2,1)S(1)}, bf16[3072,128]{1,0:T(8,128)(2,1)S(1)}, u32[]{:S(2)}, u32[]{:S(2)}) collective-permute-start(bf16[3072,128]{1,0:T(8,128)(2,1)S(1)} %constant_dynamic-update-slice_fusion.12), channel_id=1, source_target_pairs={{0,8},{8,0},{1,9},{9,1},{2,10},{10,2},{3,11},{11,3},{4,12},{12,4},... | collective-permute-start | bytes 2359304 | tf_op jit(solution)/shard_map/ppermute | solution.py:23
  77.2 4.9 %collective-permute-start.24 = (bf16[512,128]{1,0:T(8,128)(2,1)S(1)}, bf16[512,128]{1,0:T(8,128)(2,1)S(1)}, u32[]{:S(2)}, u32[]{:S(2)}) collective-permute-start(bf16[512,128]{1,0:T(8,128)(2,1)S(1)} %slice.26), channel_id=1, source_target_pairs={{0,16},{16,0},{1,17},{17,1},{2,18},{18,2},{3,19},{19,3},{4,20},{20... | collective-permute-start | bytes 393224 | tf_op jit(solution)/shard_map/ppermute | solution.py:23
  77.5 4.6 %collective-permute-start.25 = (bf16[512,128]{1,0:T(8,128)(2,1)S(1)}, bf16[512,128]{1,0:T(8,128)(2,1)S(1)}, u32[]{:S(2)}, u32[]{:S(2)}) collective-permute-start(bf16[512,128]{1,0:T(8,128)(2,1)S(1)} %slice.27), channel_id=1, source_target_pairs={{0,1},{1,0},{2,3},{3,2},{4,5},{5,4},{6,7},{7,6},{8,9},{9,8},{10,11... | collective-permute-start | bytes 393224 | tf_op jit(solution)/shard_map/ppermute | solution.py:23
  82.1 3.4 %collective-permute-start.29 = (bf16[1024,128]{1,0:T(8,128)(2,1)S(1)}, bf16[1024,128]{1,0:T(8,128)(2,1)S(1)}, u32[]{:S(2)}, u32[]{:S(2)}) collective-permute-start(bf16[1024,128]{1,0:T(8,128)(2,1)S(1)} %pad_maximum_fusion.1), channel_id=1, source_target_pairs={{0,8},{8,0},{1,9},{9,1},{2,10},{10,2},{3,11},{11,3},{4,12},{12,4},... | collective-permute-start | bytes 786440 | tf_op jit(solution)/shard_map/ppermute | solution.py:23

commit v13 on v11

--- a/solution.py
+++ b/solution.py
@@ -251,12 +251,12 @@
 
 
 def put(where, result, total_rows, rows, decks, chosen, line):
-    values = [value for _, _, value in chosen]
+    values = [value for _, value in chosen]
     width = values[0].shape[1]
     runs = [
         (n, offsets, chunk, d, at)
-        for n, (chunk, parts, _) in enumerate(chosen)
-        for at, (offsets, d) in enumerate((o, d) for o, ds in parts for d in ds)
+        for n, (parts, _) in enumerate(chosen)
+        for at, (chunk, offsets, d) in enumerate((c, o, d) for c, o, ds in parts for d in ds)
     ]
     given = [] if result is None else [result]
     vmem, anywhere = (pl.BlockSpec(memory_space=m) for m in (pltpu.VMEM, pl.ANY))
@@ -343,7 +343,9 @@
     offsets = list(blocks)
     height, comps = cells.shape[1:3]
     slopes = plane_slopes(where, list(blocks.values()), offsets, rows, height, comps)
-    terms = [plane_terms(where, *slopes, n, share, rows, decks, outs) for n in range(CHUNKS)]
+    terms = [
+        list(plane_terms(where, *slopes, n, share, rows, decks, outs)) for n in range(CHUNKS)
+    ]
 
     line = share * width // decks
     every = range(decks)
@@ -352,30 +354,38 @@
     def put_all(result, chosen):
         return put(where, result, width * width, rows, decks, chosen, line)
 
-    parts = [parts_over_decks(t, decks) for t in terms]
     pieces = []
     for n in range(CHUNKS):
-        mine = sum(part.astype(jnp.float32) for part in parts[n]).astype(jnp.bfloat16)
+        parts = parts_over_decks(terms[n], decks)
+        if n < CHUNKS - 1:
+            parts, terms[n + 1][0] = lax.optimization_barrier((parts, terms[n + 1][0]))
+        mine = sum(part.astype(jnp.float32) for part in parts).astype(jnp.bfloat16)
+        if n < CHUNKS - 1:
+            mine, later = lax.optimization_barrier((mine, terms[n + 1]))
+            terms[n + 1] = list(later)
         pieces.append(
             jnp.concatenate([mine] + [rotate(mine, "deck", r) for r in range(1, decks)], axis=0)
         )
 
-    def to_core(chosen):
+    def to_core(groups):
+        chosen = sum(groups, [])
         joined = rotate(jnp.concatenate([v for _, _, v in chosen], axis=0), "core")
-        parts = [((r, 1, s), ds) for _, ps, _ in chosen for (r, _, s), ds in ps]
-        return [(chosen[0][0], parts, joined)]
+        runs = [(n, (r, 1, s), ds) for n, ps, _ in chosen for (r, _, s), ds in ps]
+        return [(runs, joined)]
+
+    def flat(*groups):
+        return [([(n, o, ds) for o, ds in ps], v) for g in groups for n, ps, v in g]
 
     result = None
-    waiting = []
+    held, core = [], []
     for n, piece in enumerate(pieces):
         across = rotate(piece, "side")
         along = [rotate(piece, "row", r) for r in range(1, rows)]
         near = [(n, [((0, 0, 0), every)], piece), (n, [((0, 0, 1), every)], across)]
         near += [(n, [((r, 0, 0), every)], v) for r, v in enumerate(along, 1)]
         halves = [across[: half * line]] + [v[half * line :] for v in along]
-        if waiting:
-            result = put_all(result, waiting.pop(0))
-            halves, result = lax.optimization_barrier((halves, result))
+        if n > 0:
+            result = put_all(result, flat(held[0]) + core)
         far = [
             (n, [((r, 0, 1), every[:half])], rotate(halves[0], "row", r)) for r in range(1, rows)
         ]
@@ -383,14 +393,16 @@
             (n, [((r, 0, 1), every[half:])], rotate(halves[r], "side")) for r in range(1, rows)
         ]
         if n < CHUNKS - 1:
-            waiting += [near, far + to_core(near + far)]
+            core = to_core([near])
+            held = [near, far]
         else:
-            core = to_core(near)
-            result = put_all(result, sum(waiting, []) + near)
-            last, result = lax.optimization_barrier(([v for _, _, v in far], result))
-            far = [(n, ps, v) for (_, ps, _), v in zip(far, last)]
-            result = put_all(result, core + far)
-            result = put_all(result, to_core(far))
+            core = to_core([held[1], near])
+            result = put_all(result, flat(held[1], near))
+            values, result = lax.optimization_barrier(([v for _, _, v in far], result))
+            far = [(n, ps, v) for (_, ps, _), v in zip(far, values)]
+            last = to_core([far])
+            result = put_all(result, core + flat(far))
+            result = put_all(result, last)
     return result.reshape(width, width, width)
 
 

time: 97.5 us -> 96.4 us (0.989)
    ppermute x1, starting transfers between devices: 7.13 us -> 0.02 us  [spread_near(): got[r, 1] = lax.ppermute(piece, DIAGONAL, pairs)]
    ppermute x29, starting transfers between devices: 42.9 us -> 49.6 us  [rotate(): lax.ppermute(value, axis, [(i, (i + by) % count) for i in range(count)])]
where the time goes in v13:
time: 96.4 us; the launch traced here: 96.2 us
  starting transfers between devices  50.3 us (52%)
  Pallas kernels  25 us (26%)
  waiting for transfers between devices  17.3 us (18%)
  other arithmetic  2.95 us (3%)
    ppermute x29, starting transfers between devices, rotate(): lax.ppermute(value, axis, [(i, (i + by) % count) for i in range(count)])  49.6 us
    ppermute x29, waiting for transfers between devices, rotate(): lax.ppermute(value, axis, [(i, (i + by) % count) for i in range(count)])  17.3 us
    pallas_call x2, Pallas kernels, plane_terms(): pl.pallas_call(functools.partial(terms_kernel, share, chunk, rows, decks)...  11.5 us
    pallas_call x4, Pallas kernels, put(): pl.pallas_call(functools.partial(place_kernel, (rows, decks, line, runs),...  8.02 us
    pallas_call x1, Pallas kernels, plane_slopes(): pl.pallas_call(functools.partial(slopes_kernel, sizes, offsets), out_shap...  5.49 us
  transfers between devices with their start and end apart: 31, of which 9 were waited for; matrix products, arithmetic and copies ran while one was open for 1% of the time, Pallas kernels for 13%

profile of v13, /device:TPU:1, one launch (start us, length us, event | category | flops | bytes accessed | tf_op | source)
XLA Modules:
  0.0 96.2 jit_solution(8542065295016356341)
XLA Ops:
  0.0 1.0 %broadcast_select_fusion = bf16[2,10,3,2,128]{4,3,2,1,0:T(2,128)(2,1)S(1)} fusion(pred[]{:T(512)S(6)} %eq.3, bf16[2,10,3,8,128]{4,3,2,1,0:T(8,128)(2,1)} %bitcast.17), kind=kLoop, calls=%fused_computation.5 | loop fusion | flops 15360 | bytes 92161 | tf_op jit(solution)/shard_map/jit(_where)/select_n | solution.py:285
  3.5 6.2 %collective-permute-start.2 = (bf16[2,40,8,128]{3,2,1,0:T(8,128)(2,1)S(1)}, bf16[2,40,8,128]{3,2,1,0:T(8,128)(2,1)S(1)}, u32[]{:S(2)}, u32[]{:S(2)}) collective-permute-start(bf16[2,40,8,128]{3,2,1,0:T(8,128)(2,1)S(1)} %pad_maximum_fusion.2.refs_0_), channel_id=1, source_target_pairs={{0,1},{1,0},{2,3},{3,2},{4,5},{5,4},{6,7},{7,6},{8,9},{9,8},{10,11... | collective-permute-start | bytes 491528 | tf_op jit(solution)/shard_map/ppermute | solution.py:23
  9.7 1.2 %collective-permute-start.4 = (bf16[2,40,8,128]{3,2,1,0:T(8,128)(2,1)S(1)}, bf16[2,40,8,128]{3,2,1,0:T(8,128)(2,1)S(1)}, u32[]{:S(2)}, u32[]{:S(2)}) collective-permute-start(bf16[2,40,8,128]{3,2,1,0:T(8,128)(2,1)S(1)} %pad_maximum_fusion.2.refs_0_), channel_id=1, source_target_pairs={{0,16},{16,0},{1,17},{17,1},{2,18},{18,2},{3,19},{19,3},{4,20},{20... | collective-permute-start | bytes 491528 | tf_op jit(solution)/shard_map/ppermute | solution.py:23
  10.9 2.4 %collective-permute-start.1 = (bf16[2,40,8,128]{3,2,1,0:T(8,128)(2,1)S(1)}, bf16[2,40,8,128]{3,2,1,0:T(8,128)(2,1)S(1)}, u32[]{:S(2)}, u32[]{:S(2)}) collective-permute-start(bf16[2,40,8,128]{3,2,1,0:T(8,128)(2,1)S(1)} %pad_maximum_fusion.2.refs_0_), channel_id=1, source_target_pairs={{0,8},{8,0},{1,9},{9,1},{2,10},{10,2},{3,11},{11,3},{4,12},{12,4},... | collective-permute-start | bytes 491528 | tf_op jit(solution)/shard_map/ppermute | solution.py:23
  13.3 2.9 %collective-permute-start.3 = (bf16[2,40,8,128]{3,2,1,0:T(8,128)(2,1)S(1)}, bf16[2,40,8,128]{3,2,1,0:T(8,128)(2,1)S(1)}, u32[]{:S(2)}, u32[]{:S(2)}) collective-permute-start(bf16[2,40,8,128]{3,2,1,0:T(8,128)(2,1)S(1)} %collective-permute-done.2.refs_2_), channel_id=1, source_target_pairs={{0,8},{8,0},{1,9},{9,1},{2,10},{10,2},{3,11},{11,3},{4,12},{12,4},... | collective-permute-start | bytes 491528 | tf_op jit(solution)/shard_map/ppermute | solution.py:23
  16.3 4.1 %collective-permute-start.5 = (bf16[2,40,8,128]{3,2,1,0:T(8,128)(2,1)S(1)}, bf16[2,40,8,128]{3,2,1,0:T(8,128)(2,1)S(1)}, u32[]{:S(2)}, u32[]{:S(2)}) collective-permute-start(bf16[2,40,8,128]{3,2,1,0:T(8,128)(2,1)S(1)} %collective-permute-done.4.refs_4_), channel_id=1, source_target_pairs={{0,8},{8,0},{1,9},{9,1},{2,10},{10,2},{3,11},{11,3},{4,12},{12,4},... | collective-permute-start | bytes 491528 | tf_op jit(solution)/shard_map/ppermute | solution.py:23
  21.8 5.5 %shard_map.28 = (bf16[4,3,128,1280]{3,2,1,0:T(8,128)(2,1)S(1)}, f32[3,128,1280]{2,1,0:T(8,128)S(1)}) custom-call(s32[4]{0:T(128)S(1)} %pad_add_fusion.where_ref, bf16[2,40,8,128]{3,2,1,0:T(8,128)(2,1)S(1)} %pad_maximum_fusion.2.refs_0_, bf16[2,40,8,128]{3,2,1,0:T(8,128)(2,1)S(1)} %collective-permute-done.1.refs_1_, ...), custom_call_target="tpu_custom_call" | custom-call | flops 503316480 | bytes 4194304 | tf_op jit(solution)/shard_map/pallas_call | solution.py:151
  27.3 5.7 %shard_map.29 = (f32[256,128]{1,0:T(8,128)S(1)}, bf16[256,128]{1,0:T(8,128)(2,1)S(1)}, bf16[256,128]{1,0:T(8,128)(2,1)S(1)}, bf16[256,128]{1,0:T(8,128)(2,1)S(1)}) custom-call(s32[4]{0:T(128)S(1)} %pad_add_fusion.where_ref, bf16[4,3,128,1280]{3,2,1,0:T(8,128)(2,1)S(1)} %get-tuple-element.28.turned, f32[3,128,1280]{2,1,0:T(8,128)S(1)} %get-tuple-element.29.phi), custom_call_target="tpu_custom_call" | custom-call | flops 1006632960 | bytes 4194304 | tf_op jit(solution)/shard_map/pallas_call | solution.py:213
  33.0 2.2 %collective-permute-start.10 = (bf16[256,128]{1,0:T(8,128)(2,1)S(1)}, bf16[256,128]{1,0:T(8,128)(2,1)S(1)}, u32[]{:S(2)}, u32[]{:S(2)}) collective-permute-start(bf16[256,128]{1,0:T(8,128)(2,1)S(1)} %get-tuple-element.33), channel_id=1, source_target_pairs={{0,6},{2,0},{4,2},{6,4},{1,7},{3,1},{5,3},{7,5},{8,14},{10,8},{12,... | collective-permute-start | bytes 196616 | tf_op jit(solution)/shard_map/ppermute | solution.py:23
  35.2 1.7 %collective-permute-start.9 = (bf16[256,128]{1,0:T(8,128)(2,1)S(1)}, bf16[256,128]{1,0:T(8,128)(2,1)S(1)}, u32[]{:S(2)}, u32[]{:S(2)}) collective-permute-start(bf16[256,128]{1,0:T(8,128)(2,1)S(1)} %get-tuple-element.32), channel_id=1, source_target_pairs={{0,4},{2,6},{4,0},{6,2},{1,5},{3,7},{5,1},{7,3},{8,12},{10,14},{12... | collective-permute-start | bytes 196616 | tf_op jit(solution)/shard_map/ppermute | solution.py:23
  36.9 5.7 %shard_map.30 = (f32[256,128]{1,0:T(8,128)S(1)}, bf16[256,128]{1,0:T(8,128)(2,1)S(1)}, bf16[256,128]{1,0:T(8,128)(2,1)S(1)}, bf16[256,128]{1,0:T(8,128)(2,1)S(1)}) custom-call(s32[4]{0:T(128)S(1)} %pad_add_fusion.where_ref, bf16[4,3,128,1280]{3,2,1,0:T(8,128)(2,1)S(1)} %get-tuple-element.28.turned, f32[3,128,1280]{2,1,0:T(8,128)S(1)} %get-tuple-element.29.phi), custom_call_target="tpu_custom_call" | custom-call | flops 1006632960 | bytes 4194304 | tf_op jit(solution)/shard_map/pallas_call | solution.py:213
  42.7 1.9 %collective-permute-start.21 = (bf16[256,128]{1,0:T(8,128)(2,1)S(1)}, bf16[256,128]{1,0:T(8,128)(2,1)S(1)}, u32[]{:S(2)}, u32[]{:S(2)}) collective-permute-start(bf16[256,128]{1,0:T(8,128)(2,1)S(1)} %add_convert_fusion.1), channel_id=1, source_target_pairs={{0,2},{2,4},{4,6},{6,0},{1,3},{3,5},{5,7},{7,1},{8,10},{10,12},{12... | collective-permute-start | bytes 196616 | tf_op jit(solution)/shard_map/ppermute | solution.py:23
  44.6 2.2 %collective-permute-start.23 = (bf16[256,128]{1,0:T(8,128)(2,1)S(1)}, bf16[256,128]{1,0:T(8,128)(2,1)S(1)}, u32[]{:S(2)}, u32[]{:S(2)}) collective-permute-start(bf16[256,128]{1,0:T(8,128)(2,1)S(1)} %add_convert_fusion.1), channel_id=1, source_target_pairs={{0,6},{2,0},{4,2},{6,4},{1,7},{3,1},{5,3},{7,5},{8,14},{10,8},{12,... | collective-permute-start | bytes 196616 | tf_op jit(solution)/shard_map/ppermute | solution.py:23
  47.7 3.2 %collective-permute-done.22 = bf16[256,128]{1,0:T(8,128)(2,1)S(1)} collective-permute-done((bf16[256,128]{1,0:T(8,128)(2,1)S(1)}, bf16[256,128]{1,0:T(8,128)(2,1)S(1)}, u32[]{:S(2)}, u32[]{:S(2)}) %collective-permute-start.22) | collective-permute-done | bytes 65568 | tf_op jit(solution)/shard_map/ppermute | solution.py:23
  51.0 1.7 %collective-permute-start.24 = (bf16[1024,128]{1,0:T(8,128)(2,1)S(1)}, bf16[1024,128]{1,0:T(8,128)(2,1)S(1)}, u32[]{:S(2)}, u32[]{:S(2)}) collective-permute-start(bf16[1024,128]{1,0:T(8,128)(2,1)S(1)} %get-tuple-element.54.refs_0_), channel_id=1, source_target_pairs={{0,1},{1,0},{2,3},{3,2},{4,5},{5,4},{6,7},{7,6},{8,9},{9,8},{10,11... | collective-permute-start | bytes 786440 | tf_op jit(solution)/shard_map/ppermute | solution.py:23
  53.4 4.2 %collective-permute-done.24.refs_1_ = bf16[1024,128]{1,0:T(8,128)(2,1)S(1)} collective-permute-done((bf16[1024,128]{1,0:T(8,128)(2,1)S(1)}, bf16[1024,128]{1,0:T(8,128)(2,1)S(1)}, u32[]{:S(2)}, u32[]{:S(2)}) %collective-permute-start.24) | collective-permute-done | bytes 262176 | tf_op jit(solution)/shard_map/ppermute | solution.py:23
  58.5 2.1 %collective-permute-start.11 = (bf16[256,128]{1,0:T(8,128)(2,1)S(1)}, bf16[256,128]{1,0:T(8,128)(2,1)S(1)}, u32[]{:S(2)}, u32[]{:S(2)}) collective-permute-start(bf16[256,128]{1,0:T(8,128)(2,1)S(1)} %get-tuple-element.44), channel_id=1, source_target_pairs={{0,2},{2,4},{4,6},{6,0},{1,3},{3,5},{5,7},{7,1},{8,10},{10,12},{12... | collective-permute-start | bytes 196616 | tf_op jit(solution)/shard_map/ppermute | solution.py:23
  60.7 2.1 %collective-permute-start.13 = (bf16[256,128]{1,0:T(8,128)(2,1)S(1)}, bf16[256,128]{1,0:T(8,128)(2,1)S(1)}, u32[]{:S(2)}, u32[]{:S(2)}) collective-permute-start(bf16[256,128]{1,0:T(8,128)(2,1)S(1)} %get-tuple-element.46), channel_id=1, source_target_pairs={{0,6},{2,0},{4,2},{6,4},{1,7},{3,1},{5,3},{7,5},{8,14},{10,8},{12,... | collective-permute-start | bytes 196616 | tf_op jit(solution)/shard_map/ppermute | solution.py:23
  62.8 1.5 %collective-permute-start.27 = (bf16[512,128]{1,0:T(8,128)(2,1)S(1)}, bf16[512,128]{1,0:T(8,128)(2,1)S(1)}, u32[]{:S(2)}, u32[]{:S(2)}) collective-permute-start(bf16[512,128]{1,0:T(8,128)(2,1)S(1)} %slice.29), channel_id=1, source_target_pairs={{0,1},{1,0},{2,3},{3,2},{4,5},{5,4},{6,7},{7,6},{8,9},{9,8},{10,11... | collective-permute-start | bytes 393224 | tf_op jit(solution)/shard_map/ppermute | solution.py:23
  64.4 2.6 %collective-permute-done.27.refs_1_ = bf16[512,128]{1,0:T(8,128)(2,1)S(1)} collective-permute-done((bf16[512,128]{1,0:T(8,128)(2,1)S(1)}, bf16[512,128]{1,0:T(8,128)(2,1)S(1)}, u32[]{:S(2)}, u32[]{:S(2)}) %collective-permute-start.27) | collective-permute-done | bytes 131104 | tf_op jit(solution)/shard_map/ppermute | solution.py:23
  67.1 1.4 %collective-permute-start.15 = (bf16[256,128]{1,0:T(8,128)(2,1)S(1)}, bf16[256,128]{1,0:T(8,128)(2,1)S(1)}, u32[]{:S(2)}, u32[]{:S(2)}) collective-permute-start(bf16[256,128]{1,0:T(8,128)(2,1)S(1)} %get-tuple-element.52), channel_id=1, source_target_pairs={{0,4},{2,6},{4,0},{6,2},{1,5},{3,7},{5,1},{7,3},{8,12},{10,14},{12... | collective-permute-start | bytes 196616 | tf_op jit(solution)/shard_map/ppermute | solution.py:23
  68.6 1.8 %collective-permute-start.16 = (bf16[256,128]{1,0:T(8,128)(2,1)S(1)}, bf16[256,128]{1,0:T(8,128)(2,1)S(1)}, u32[]{:S(2)}, u32[]{:S(2)}) collective-permute-start(bf16[256,128]{1,0:T(8,128)(2,1)S(1)} %get-tuple-element.52), channel_id=1, source_target_pairs={{0,6},{2,0},{4,2},{6,4},{1,7},{3,1},{5,3},{7,5},{8,14},{10,8},{12,... | collective-permute-start | bytes 196616 | tf_op jit(solution)/shard_map/ppermute | solution.py:23
  70.4 4.7 %collective-permute-start.28 = (bf16[3072,128]{1,0:T(8,128)(2,1)S(1)}, bf16[3072,128]{1,0:T(8,128)(2,1)S(1)}, u32[]{:S(2)}, u32[]{:S(2)}) collective-permute-start(bf16[3072,128]{1,0:T(8,128)(2,1)S(1)} %constant_dynamic-update-slice_fusion.4), channel_id=1, source_target_pairs={{0,8},{8,0},{1,9},{9,1},{2,10},{10,2},{3,11},{11,3},{4,12},{12,4},... | collective-permute-start | bytes 2359304 | tf_op jit(solution)/shard_map/ppermute | solution.py:23
  75.2 1.5 %collective-permute-start.17 = (bf16[1024,128]{1,0:T(8,128)(2,1)S(1)}, bf16[1024,128]{1,0:T(8,128)(2,1)S(1)}, u32[]{:S(2)}, u32[]{:S(2)}) collective-permute-start(bf16[1024,128]{1,0:T(8,128)(2,1)S(1)} %pad_maximum_fusion.refs_2_), channel_id=1, source_target_pairs={{0,1},{1,0},{2,3},{3,2},{4,5},{5,4},{6,7},{7,6},{8,9},{9,8},{10,11... | collective-permute-start | bytes 786440 | tf_op jit(solution)/shard_map/ppermute | solution.py:23
  77.5 3.3 %collective-permute-done.17.refs_3_ = bf16[1024,128]{1,0:T(8,128)(2,1)S(1)} collective-permute-done((bf16[1024,128]{1,0:T(8,128)(2,1)S(1)}, bf16[1024,128]{1,0:T(8,128)(2,1)S(1)}, u32[]{:S(2)}, u32[]{:S(2)}) %collective-permute-start.17) | collective-permute-done | bytes 262176 | tf_op jit(solution)/shard_map/ppermute | solution.py:23
  80.8 1.4 %collective-permute-done.19.refs_4_ = bf16[1024,128]{1,0:T(8,128)(2,1)S(1)} collective-permute-done((bf16[1024,128]{1,0:T(8,128)(2,1)S(1)}, bf16[1024,128]{1,0:T(8,128)(2,1)S(1)}, u32[]{:S(2)}, u32[]{:S(2)}) %collective-permute-start.19) | collective-permute-done | bytes 262176 | tf_op jit(solution)/shard_map/ppermute | solution.py:23
  82.2 3.4 %collective-permute-start.30 = (bf16[4096,128]{1,0:T(8,128)(2,1)S(1)}, bf16[4096,128]{1,0:T(8,128)(2,1)S(1)}, u32[]{:S(2)}, u32[]{:S(2)}) collective-permute-start(bf16[4096,128]{1,0:T(8,128)(2,1)S(1)} %constant_dynamic-update-slice_fusion.10), channel_id=1, source_target_pairs={{0,8},{8,0},{1,9},{9,1},{2,10},{10,2},{3,11},{11,3},{4,12},{12,4},... | collective-permute-start | bytes 3145736 | tf_op jit(solution)/shard_map/ppermute | solution.py:23
  86.6 2.4 %shard_map.31.refs_5_ = f32[16384,128]{1,0:T(8,128)} custom-call(s32[4]{0:T(128)S(1)} %pad_add_fusion.where_ref, bf16[1024,128]{1,0:T(8,128)(2,1)S(1)} %get-tuple-element.54.refs_0_, bf16[1024,128]{1,0:T(8,128)(2,1)S(1)} %collective-permute-done.24.refs_1_, bf16[1024,128]{1,0:T(8,128)(2,1)S(1)} %collective-permute-done.26.refs_2_, ...), custom_call_target="tpu_custom_call" | custom-call | bytes 4718592 | tf_op jit(solution)/shard_map/pallas_call | solution.py:264
  89.0 2.0 %shard_map.32.refs_3_ = f32[16384,128]{1,0:T(8,128)} custom-call(s32[4]{0:T(128)S(1)} %pad_add_fusion.where_ref, bf16[512,128]{1,0:T(8,128)(2,1)S(1)} %collective-permute-done.25.refs_0_, bf16[512,128]{1,0:T(8,128)(2,1)S(1)} %collective-permute-done.27.refs_1_, bf16[1024,128]{1,0:T(8,128)(2,1)S(1)} %pad_maximum_fusion.refs_2_, ...), custom_call_target="tpu_custom_call", output_to_operand_aliasing={{}: (6, {})} | custom-call | bytes 3145728 | tf_op jit(solution)/shard_map/pallas_call | solution.py:264
  91.4 1.2 %collective-permute-start.29 = (bf16[1024,128]{1,0:T(8,128)(2,1)S(1)}, bf16[1024,128]{1,0:T(8,128)(2,1)S(1)}, u32[]{:S(2)}, u32[]{:S(2)}) collective-permute-start(bf16[1024,128]{1,0:T(8,128)(2,1)S(1)} %pad_maximum_fusion.1), channel_id=1, source_target_pairs={{0,8},{8,0},{1,9},{9,1},{2,10},{10,2},{3,11},{11,3},{4,12},{12,4},... | collective-permute-start | bytes 786440 | tf_op jit(solution)/shard_map/ppermute | solution.py:23
  92.6 2.2 %shard_map.33.refs_1_ = f32[16384,128]{1,0:T(8,128)} custom-call(s32[4]{0:T(128)S(1)} %pad_add_fusion.where_ref, bf16[4096,128]{1,0:T(8,128)(2,1)S(1)} %collective-permute-done.30.refs_0_, bf16[512,128]{1,0:T(8,128)(2,1)S(1)} %collective-permute-done.18.refs_1_, ...), custom_call_target="tpu_custom_call", output_to_operand_aliasing={{}: (4, {})} | custom-call | bytes 3932160 | tf_op jit(solution)/shard_map/pallas_call | solution.py:264
  94.8 1.4 %shard_map.34 = f32[16384,128]{1,0:T(8,128)} custom-call(s32[4]{0:T(128)S(1)} %pad_add_fusion.where_ref, bf16[1024,128]{1,0:T(8,128)(2,1)S(1)} %collective-permute-done.29.refs_0_, f32[16384,128]{1,0:T(8,128)} %shard_map.33.refs_1_), custom_call_target="tpu_custom_call", output_to_operand_aliasing={{}: (2, {})} | custom-call | bytes 786432 | tf_op jit(solution)/shard_map/pallas_call | solution.py:264
  (67 shorter events, 8.9 us)
Async XLA Ops:
  1.0 1.5 %collective-permute-start = (bf16[2,10,3,2,128]{4,3,2,1,0:T(2,128)(2,1)S(1)}, bf16[2,10,3,2,128]{4,3,2,1,0:T(2,128)(2,1)S(1)}, u32[]{:S(2)}, u32[]{:S(2)}) collective-permute-start(bf16[2,10,3,2,128]{4,3,2,1,0:T(2,128)(2,1)S(1)} %broadcast_select_fusion), channel_id=1, source_target_pairs={{1,2},{3,4},{5,6},{2,1},{4,3},{6,5},{9,10},{11,12},{13,14},{10,9},... | collective-permute-start | bytes 92168 | tf_op jit(solution)/shard_map/ppermute | solution.py:287
  3.5 9.8 %collective-permute-start.2 = (bf16[2,40,8,128]{3,2,1,0:T(8,128)(2,1)S(1)}, bf16[2,40,8,128]{3,2,1,0:T(8,128)(2,1)S(1)}, u32[]{:S(2)}, u32[]{:S(2)}) collective-permute-start(bf16[2,40,8,128]{3,2,1,0:T(8,128)(2,1)S(1)} %pad_maximum_fusion.2.refs_0_), channel_id=1, source_target_pairs={{0,1},{1,0},{2,3},{3,2},{4,5},{5,4},{6,7},{7,6},{8,9},{9,8},{10,11... | collective-permute-start | bytes 491528 | tf_op jit(solution)/shard_map/ppermute | solution.py:23
  9.7 6.6 %collective-permute-start.4 = (bf16[2,40,8,128]{3,2,1,0:T(8,128)(2,1)S(1)}, bf16[2,40,8,128]{3,2,1,0:T(8,128)(2,1)S(1)}, u32[]{:S(2)}, u32[]{:S(2)}) collective-permute-start(bf16[2,40,8,128]{3,2,1,0:T(8,128)(2,1)S(1)} %pad_maximum_fusion.2.refs_0_), channel_id=1, source_target_pairs={{0,16},{16,0},{1,17},{17,1},{2,18},{18,2},{3,19},{19,3},{4,20},{20... | collective-permute-start | bytes 491528 | tf_op jit(solution)/shard_map/ppermute | solution.py:23
  10.9 9.5 %collective-permute-start.6 = (bf16[2,40,8,128]{3,2,1,0:T(8,128)(2,1)S(1)}, bf16[2,40,8,128]{3,2,1,0:T(8,128)(2,1)S(1)}, u32[]{:S(2)}, u32[]{:S(2)}) collective-permute-start(bf16[2,40,8,128]{3,2,1,0:T(8,128)(2,1)S(1)} %pad_maximum_fusion.2.refs_0_), channel_id=1, source_target_pairs={{0,17},{1,16},{16,1},{17,0},{2,19},{3,18},{18,3},{19,2},{4,21},{5,... | collective-permute-start | bytes 491528 | tf_op jit(solution)/shard_map/ppermute | solution.py:314
  10.9 9.5 %collective-permute-start.1 = (bf16[2,40,8,128]{3,2,1,0:T(8,128)(2,1)S(1)}, bf16[2,40,8,128]{3,2,1,0:T(8,128)(2,1)S(1)}, u32[]{:S(2)}, u32[]{:S(2)}) collective-permute-start(bf16[2,40,8,128]{3,2,1,0:T(8,128)(2,1)S(1)} %pad_maximum_fusion.2.refs_0_), channel_id=1, source_target_pairs={{0,8},{8,0},{1,9},{9,1},{2,10},{10,2},{3,11},{11,3},{4,12},{12,4},... | collective-permute-start | bytes 491528 | tf_op jit(solution)/shard_map/ppermute | solution.py:23
  13.3 7.1 %collective-permute-start.3 = (bf16[2,40,8,128]{3,2,1,0:T(8,128)(2,1)S(1)}, bf16[2,40,8,128]{3,2,1,0:T(8,128)(2,1)S(1)}, u32[]{:S(2)}, u32[]{:S(2)}) collective-permute-start(bf16[2,40,8,128]{3,2,1,0:T(8,128)(2,1)S(1)} %collective-permute-done.2.refs_2_), channel_id=1, source_target_pairs={{0,8},{8,0},{1,9},{9,1},{2,10},{10,2},{3,11},{11,3},{4,12},{12,4},... | collective-permute-start | bytes 491528 | tf_op jit(solution)/shard_map/ppermute | solution.py:23
  16.3 5.1 %collective-permute-start.5 = (bf16[2,40,8,128]{3,2,1,0:T(8,128)(2,1)S(1)}, bf16[2,40,8,128]{3,2,1,0:T(8,128)(2,1)S(1)}, u32[]{:S(2)}, u32[]{:S(2)}) collective-permute-start(bf16[2,40,8,128]{3,2,1,0:T(8,128)(2,1)S(1)} %collective-permute-done.4.refs_4_), channel_id=1, source_target_pairs={{0,8},{8,0},{1,9},{9,1},{2,10},{10,2},{3,11},{11,3},{4,12},{12,4},... | collective-permute-start | bytes 491528 | tf_op jit(solution)/shard_map/ppermute | solution.py:23
  20.4 1.4 %collective-permute-start.7 = (bf16[2,40,8,128]{3,2,1,0:T(8,128)(2,1)S(1)}, bf16[2,40,8,128]{3,2,1,0:T(8,128)(2,1)S(1)}, u32[]{:S(2)}, u32[]{:S(2)}) collective-permute-start(bf16[2,40,8,128]{3,2,1,0:T(8,128)(2,1)S(1)} %collective-permute-done.6.refs_6_), channel_id=1, source_target_pairs={{0,8},{8,0},{1,9},{9,1},{2,10},{10,2},{3,11},{11,3},{4,12},{12,4},... | collective-permute-start | bytes 491528 | tf_op jit(solution)/shard_map/ppermute | solution.py:23
  33.0 9.6 %collective-permute-start.10 = (bf16[256,128]{1,0:T(8,128)(2,1)S(1)}, bf16[256,128]{1,0:T(8,128)(2,1)S(1)}, u32[]{:S(2)}, u32[]{:S(2)}) collective-permute-start(bf16[256,128]{1,0:T(8,128)(2,1)S(1)} %get-tuple-element.33), channel_id=1, source_target_pairs={{0,6},{2,0},{4,2},{6,4},{1,7},{3,1},{5,3},{7,5},{8,14},{10,8},{12,... | collective-permute-start | bytes 196616 | tf_op jit(solution)/shard_map/ppermute | solution.py:23
  35.2 7.4 %collective-permute-start.8 = (bf16[256,128]{1,0:T(8,128)(2,1)S(1)}, bf16[256,128]{1,0:T(8,128)(2,1)S(1)}, u32[]{:S(2)}, u32[]{:S(2)}) collective-permute-start(bf16[256,128]{1,0:T(8,128)(2,1)S(1)} %get-tuple-element.31), channel_id=1, source_target_pairs={{0,2},{2,4},{4,6},{6,0},{1,3},{3,5},{5,7},{7,1},{8,10},{10,12},{12... | collective-permute-start | bytes 196616 | tf_op jit(solution)/shard_map/ppermute | solution.py:23
  35.2 7.4 %collective-permute-start.9 = (bf16[256,128]{1,0:T(8,128)(2,1)S(1)}, bf16[256,128]{1,0:T(8,128)(2,1)S(1)}, u32[]{:S(2)}, u32[]{:S(2)}) collective-permute-start(bf16[256,128]{1,0:T(8,128)(2,1)S(1)} %get-tuple-element.32), channel_id=1, source_target_pairs={{0,4},{2,6},{4,0},{6,2},{1,5},{3,7},{5,1},{7,3},{8,12},{10,14},{12... | collective-permute-start | bytes 196616 | tf_op jit(solution)/shard_map/ppermute | solution.py:23
  42.7 5.0 %collective-permute-start.21 = (bf16[256,128]{1,0:T(8,128)(2,1)S(1)}, bf16[256,128]{1,0:T(8,128)(2,1)S(1)}, u32[]{:S(2)}, u32[]{:S(2)}) collective-permute-start(bf16[256,128]{1,0:T(8,128)(2,1)S(1)} %add_convert_fusion.1), channel_id=1, source_target_pairs={{0,2},{2,4},{4,6},{6,0},{1,3},{3,5},{5,7},{7,1},{8,10},{10,12},{12... | collective-permute-start | bytes 196616 | tf_op jit(solution)/shard_map/ppermute | solution.py:23
  44.6 6.3 %collective-permute-start.22 = (bf16[256,128]{1,0:T(8,128)(2,1)S(1)}, bf16[256,128]{1,0:T(8,128)(2,1)S(1)}, u32[]{:S(2)}, u32[]{:S(2)}) collective-permute-start(bf16[256,128]{1,0:T(8,128)(2,1)S(1)} %add_convert_fusion.1), channel_id=1, source_target_pairs={{0,4},{2,6},{4,0},{6,2},{1,5},{3,7},{5,1},{7,3},{8,12},{10,14},{12... | collective-permute-start | bytes 196616 | tf_op jit(solution)/shard_map/ppermute | solution.py:23
  44.6 6.4 %collective-permute-start.23 = (bf16[256,128]{1,0:T(8,128)(2,1)S(1)}, bf16[256,128]{1,0:T(8,128)(2,1)S(1)}, u32[]{:S(2)}, u32[]{:S(2)}) collective-permute-start(bf16[256,128]{1,0:T(8,128)(2,1)S(1)} %add_convert_fusion.1), channel_id=1, source_target_pairs={{0,6},{2,0},{4,2},{6,4},{1,7},{3,1},{5,3},{7,5},{8,14},{10,8},{12,... | collective-permute-start | bytes 196616 | tf_op jit(solution)/shard_map/ppermute | solution.py:23
  51.0 6.6 %collective-permute-start.24 = (bf16[1024,128]{1,0:T(8,128)(2,1)S(1)}, bf16[1024,128]{1,0:T(8,128)(2,1)S(1)}, u32[]{:S(2)}, u32[]{:S(2)}) collective-permute-start(bf16[1024,128]{1,0:T(8,128)(2,1)S(1)} %get-tuple-element.54.refs_0_), channel_id=1, source_target_pairs={{0,1},{1,0},{2,3},{3,2},{4,5},{5,4},{6,7},{7,6},{8,9},{9,8},{10,11... | collective-permute-start | bytes 786440 | tf_op jit(solution)/shard_map/ppermute | solution.py:23
  52.7 10.1 %collective-permute-start.26 = (bf16[1024,128]{1,0:T(8,128)(2,1)S(1)}, bf16[1024,128]{1,0:T(8,128)(2,1)S(1)}, u32[]{:S(2)}, u32[]{:S(2)}) collective-permute-start(bf16[1024,128]{1,0:T(8,128)(2,1)S(1)} %get-tuple-element.54.refs_0_), channel_id=1, source_target_pairs={{0,16},{16,0},{1,17},{17,1},{2,18},{18,2},{3,19},{19,3},{4,20},{20... | collective-permute-start | bytes 786440 | tf_op jit(solution)/shard_map/ppermute | solution.py:23
  57.6 6.7 %collective-permute-start.25 = (bf16[512,128]{1,0:T(8,128)(2,1)S(1)}, bf16[512,128]{1,0:T(8,128)(2,1)S(1)}, u32[]{:S(2)}, u32[]{:S(2)}) collective-permute-start(bf16[512,128]{1,0:T(8,128)(2,1)S(1)} %slice.28), channel_id=1, source_target_pairs={{0,16},{16,0},{1,17},{17,1},{2,18},{18,2},{3,19},{19,3},{4,20},{20... | collective-permute-start | bytes 393224 | tf_op jit(solution)/shard_map/ppermute | solution.py:23
  58.5 8.5 %collective-permute-start.11 = (bf16[256,128]{1,0:T(8,128)(2,1)S(1)}, bf16[256,128]{1,0:T(8,128)(2,1)S(1)}, u32[]{:S(2)}, u32[]{:S(2)}) collective-permute-start(bf16[256,128]{1,0:T(8,128)(2,1)S(1)} %get-tuple-element.44), channel_id=1, source_target_pairs={{0,2},{2,4},{4,6},{6,0},{1,3},{3,5},{5,7},{7,1},{8,10},{10,12},{12... | collective-permute-start | bytes 196616 | tf_op jit(solution)/shard_map/ppermute | solution.py:23
  60.7 6.3 %collective-permute-start.12 = (bf16[256,128]{1,0:T(8,128)(2,1)S(1)}, bf16[256,128]{1,0:T(8,128)(2,1)S(1)}, u32[]{:S(2)}, u32[]{:S(2)}) collective-permute-start(bf16[256,128]{1,0:T(8,128)(2,1)S(1)} %get-tuple-element.45), channel_id=1, source_target_pairs={{0,4},{2,6},{4,0},{6,2},{1,5},{3,7},{5,1},{7,3},{8,12},{10,14},{12... | collective-permute-start | bytes 196616 | tf_op jit(solution)/shard_map/ppermute | solution.py:23
  60.7 6.3 %collective-permute-start.13 = (bf16[256,128]{1,0:T(8,128)(2,1)S(1)}, bf16[256,128]{1,0:T(8,128)(2,1)S(1)}, u32[]{:S(2)}, u32[]{:S(2)}) collective-permute-start(bf16[256,128]{1,0:T(8,128)(2,1)S(1)} %get-tuple-element.46), channel_id=1, source_target_pairs={{0,6},{2,0},{4,2},{6,4},{1,7},{3,1},{5,3},{7,5},{8,14},{10,8},{12,... | collective-permute-start | bytes 196616 | tf_op jit(solution)/shard_map/ppermute | solution.py:23
  62.8 4.2 %collective-permute-start.27 = (bf16[512,128]{1,0:T(8,128)(2,1)S(1)}, bf16[512,128]{1,0:T(8,128)(2,1)S(1)}, u32[]{:S(2)}, u32[]{:S(2)}) collective-permute-start(bf16[512,128]{1,0:T(8,128)(2,1)S(1)} %slice.29), channel_id=1, source_target_pairs={{0,1},{1,0},{2,3},{3,2},{4,5},{5,4},{6,7},{7,6},{8,9},{9,8},{10,11... | collective-permute-start | bytes 393224 | tf_op jit(solution)/shard_map/ppermute | solution.py:23
  67.1 8.1 %collective-permute-start.14 = (bf16[256,128]{1,0:T(8,128)(2,1)S(1)}, bf16[256,128]{1,0:T(8,128)(2,1)S(1)}, u32[]{:S(2)}, u32[]{:S(2)}) collective-permute-start(bf16[256,128]{1,0:T(8,128)(2,1)S(1)} %get-tuple-element.52), channel_id=1, source_target_pairs={{0,2},{2,4},{4,6},{6,0},{1,3},{3,5},{5,7},{7,1},{8,10},{10,12},{12... | collective-permute-start | bytes 196616 | tf_op jit(solution)/shard_map/ppermute | solution.py:23
  67.1 8.0 %collective-permute-start.15 = (bf16[256,128]{1,0:T(8,128)(2,1)S(1)}, bf16[256,128]{1,0:T(8,128)(2,1)S(1)}, u32[]{:S(2)}, u32[]{:S(2)}) collective-permute-start(bf16[256,128]{1,0:T(8,128)(2,1)S(1)} %get-tuple-element.52), channel_id=1, source_target_pairs={{0,4},{2,6},{4,0},{6,2},{1,5},{3,7},{5,1},{7,3},{8,12},{10,14},{12... | collective-permute-start | bytes 196616 | tf_op jit(solution)/shard_map/ppermute | solution.py:23
  68.6 6.6 %collective-permute-start.16 = (bf16[256,128]{1,0:T(8,128)(2,1)S(1)}, bf16[256,128]{1,0:T(8,128)(2,1)S(1)}, u32[]{:S(2)}, u32[]{:S(2)}) collective-permute-start(bf16[256,128]{1,0:T(8,128)(2,1)S(1)} %get-tuple-element.52), channel_id=1, source_target_pairs={{0,6},{2,0},{4,2},{6,4},{1,7},{3,1},{5,3},{7,5},{8,14},{10,8},{12,... | collective-permute-start | bytes 196616 | tf_op jit(solution)/shard_map/ppermute | solution.py:23
  70.4 16.2 %collective-permute-start.28 = (bf16[3072,128]{1,0:T(8,128)(2,1)S(1)}, bf16[3072,128]{1,0:T(8,128)(2,1)S(1)}, u32[]{:S(2)}, u32[]{:S(2)}) collective-permute-start(bf16[3072,128]{1,0:T(8,128)(2,1)S(1)} %constant_dynamic-update-slice_fusion.4), channel_id=1, source_target_pairs={{0,8},{8,0},{1,9},{9,1},{2,10},{10,2},{3,11},{11,3},{4,12},{12,4},... | collective-permute-start | bytes 2359304 | tf_op jit(solution)/shard_map/ppermute | solution.py:23
  75.2 5.6 %collective-permute-start.17 = (bf16[1024,128]{1,0:T(8,128)(2,1)S(1)}, bf16[1024,128]{1,0:T(8,128)(2,1)S(1)}, u32[]{:S(2)}, u32[]{:S(2)}) collective-permute-start(bf16[1024,128]{1,0:T(8,128)(2,1)S(1)} %pad_maximum_fusion.refs_2_), channel_id=1, source_target_pairs={{0,1},{1,0},{2,3},{3,2},{4,5},{5,4},{6,7},{7,6},{8,9},{9,8},{10,11... | collective-permute-start | bytes 786440 | tf_op jit(solution)/shard_map/ppermute | solution.py:23
  76.7 5.5 %collective-permute-start.19 = (bf16[1024,128]{1,0:T(8,128)(2,1)S(1)}, bf16[1024,128]{1,0:T(8,128)(2,1)S(1)}, u32[]{:S(2)}, u32[]{:S(2)}) collective-permute-start(bf16[1024,128]{1,0:T(8,128)(2,1)S(1)} %pad_maximum_fusion.refs_2_), channel_id=1, source_target_pairs={{0,16},{16,0},{1,17},{17,1},{2,18},{18,2},{3,19},{19,3},{4,20},{20... | collective-permute-start | bytes 786440 | tf_op jit(solution)/shard_map/ppermute | solution.py:23
  82.2 10.3 %collective-permute-start.30 = (bf16[4096,128]{1,0:T(8,128)(2,1)S(1)}, bf16[4096,128]{1,0:T(8,128)(2,1)S(1)}, u32[]{:S(2)}, u32[]{:S(2)}) collective-permute-start(bf16[4096,128]{1,0:T(8,128)(2,1)S(1)} %constant_dynamic-update-slice_fusion.10), channel_id=1, source_target_pairs={{0,8},{8,0},{1,9},{9,1},{2,10},{10,2},{3,11},{11,3},{4,12},{12,4},... | collective-permute-start | bytes 3145736 | tf_op jit(solution)/shard_map/ppermute | solution.py:23
  85.7 5.3 %collective-permute-start.18 = (bf16[512,128]{1,0:T(8,128)(2,1)S(1)}, bf16[512,128]{1,0:T(8,128)(2,1)S(1)}, u32[]{:S(2)}, u32[]{:S(2)}) collective-permute-start(bf16[512,128]{1,0:T(8,128)(2,1)S(1)} %slice.26), channel_id=1, source_target_pairs={{0,16},{16,0},{1,17},{17,1},{2,18},{18,2},{3,19},{19,3},{4,20},{20... | collective-permute-start | bytes 393224 | tf_op jit(solution)/shard_map/ppermute | solution.py:23
  86.5 4.9 %collective-permute-start.20 = (bf16[512,128]{1,0:T(8,128)(2,1)S(1)}, bf16[512,128]{1,0:T(8,128)(2,1)S(1)}, u32[]{:S(2)}, u32[]{:S(2)}) collective-permute-start(bf16[512,128]{1,0:T(8,128)(2,1)S(1)} %slice.27), channel_id=1, source_target_pairs={{0,1},{1,0},{2,3},{3,2},{4,5},{5,4},{6,7},{7,6},{8,9},{9,8},{10,11... | collective-permute-start | bytes 393224 | tf_op jit(solution)/shard_map/ppermute | solution.py:23
  91.4 3.4 %collective-permute-start.29 = (bf16[1024,128]{1,0:T(8,128)(2,1)S(1)}, bf16[1024,128]{1,0:T(8,128)(2,1)S(1)}, u32[]{:S(2)}, u32[]{:S(2)}) collective-permute-start(bf16[1024,128]{1,0:T(8,128)(2,1)S(1)} %pad_maximum_fusion.1), channel_id=1, source_target_pairs={{0,8},{8,0},{1,9},{9,1},{2,10},{10,2},{3,11},{11,3},{4,12},{12,4},... | collective-permute-start | bytes 786440 | tf_op jit(solution)/shard_map/ppermute | solution.py:23

commit v14 on v12

--- a/solution.py
+++ b/solution.py
@@ -162,8 +162,8 @@
 
 
 def terms_kernel(share, chunk, rows, decks, where_ref, turned, phi, *refs):
-    *out_refs, own, even, odd = refs
-    quads = (even, odd)
+    out_refs = [ref for ref in refs if len(ref.shape) == 2]
+    own, *quads = refs[len(out_refs) :]
     outs = len(out_refs)
     width, count = turned.shape[2:]
     base = (member(where_ref, rows, (0, 0, 0)) * CHUNKS + chunk) * share
@@ -173,18 +173,13 @@
         mode = base + lax.rem(i + first, share)
         for b in range(3):
             own[b, i] = jnp.broadcast_to(phi[b, pl.ds(mode, 1), :], (TILE, count))
-    units = [(group, a) for group in range(share // together) for a in range(3)]
-    totals = {}
-    for turn in range(len(units) + 1):
-        if turn < len(units):
-            group, a = units[turn]
-            quad = quads[turn % 2]
+    for group in range(share // together):
+        modes = range(group * together, (group + 1) * together)
+        quad = quads[group % len(quads)]
+        for a in range(3):
             for start in range(0, count, LANES):
                 lanes = slice(start, start + LANES)
-                spread = [
-                    [own[b, group * together + i, :, lanes] for b in range(3)]
-                    for i in range(together)
-                ]
+                spread = [[own[b, mode, :, lanes] for b in range(3)] for mode in modes]
                 for k in range(0, width, TILE):
                     slope = [
                         turned[1 + a, b, k : k + TILE, lanes].astype(jnp.float32) for b in range(3)
@@ -192,16 +187,13 @@
                     for i, row in enumerate(spread):
                         value = row[0] * slope[0] + row[1] * slope[1] + row[2] * slope[2]
                         at = i * width + k
-                        quad[at : at + TILE, lanes] = value.astype(jnp.bfloat16)
-        if turn > 0:
-            group, a = units[turn - 1]
-            value = lax.dot_general(
-                turned[0, a], quads[(turn - 1) % 2][...], TURNED, preferred_element_type=jnp.float32
-            )
-            totals[group] = totals[group] + value if a else value
-    for group, total in totals.items():
-        for i in range(together):
-            start = (group * together + i) * width
+                        quad[a, at : at + TILE, lanes] = value.astype(jnp.bfloat16)
+        total = sum(
+            lax.dot_general(turned[0, a], quad[a], TURNED, preferred_element_type=jnp.float32)
+            for a in range(3)
+        )
+        for i, mode in enumerate(modes):
+            start = mode * width
             out_ref = out_refs[start * outs // (share * width)]
             start = start % (share * width // outs)
             out_ref[start : start + width, :] = total[:, i * width : (i + 1) * width].astype(
@@ -216,7 +208,7 @@
     results = [((share * width // outs, width), t) for t in dtypes]
     scratch = [((3, share, TILE, count), jnp.float32)]
     together = min(4, share)
-    scratch += [((together * width, count), jnp.bfloat16)] * 2
+    scratch += [((3, together * width, count), jnp.bfloat16)] * min(2, share // together)
     inputs = [(v.shape, v.dtype) for v in (turned, phi)]
     return pl.pallas_call(
         functools.partial(terms_kernel, share, chunk, rows, decks),

time: 87.3 us -> 86.3 us (0.989)
  Pallas kernels: 25.9 us -> 25 us
    pallas_call x2, Pallas kernels: 12.4 us -> 11.5 us  [plane_terms(): pl.pallas_call(functools.partial(terms_kernel, share, chunk, rows, decks)...]
  transfers between devices with their start and end apart: 31 -> 31, of which waited for: 13 -> 13; matrix products, arithmetic and copies ran while one was open for 1% -> 1% of each run, Pallas kernels for 15% -> 14%
where the time goes in v14:
time: 86.3 us; the launch traced here: 86.1 us
  starting transfers between devices  42.9 us (50%)
  Pallas kernels  25 us (29%)
  waiting for transfers between devices  14.5 us (17%)
  other arithmetic  2.93 us (3%)
    ppermute x29, starting transfers between devices, rotate(): lax.ppermute(value, axis, [(i, (i + by) % count) for i in range(count)])  35.1 us
    ppermute x29, waiting for transfers between devices, rotate(): lax.ppermute(value, axis, [(i, (i + by) % count) for i in range(count)])  14.5 us
    pallas_call x2, Pallas kernels, plane_terms(): pl.pallas_call(functools.partial(terms_kernel, share, chunk, rows, decks)...  11.5 us
    pallas_call x4, Pallas kernels, put(): pl.pallas_call(functools.partial(place_kernel, (rows, decks, line, runs),...  8.01 us
    ppermute x1, starting transfers between devices, spread_near(): got[r, 1] = lax.ppermute(piece, DIAGONAL, pairs)  7.13 us
    pallas_call x1, Pallas kernels, plane_slopes(): pl.pallas_call(functools.partial(slopes_kernel, sizes, offsets), out_shap...  5.49 us
  transfers between devices with their start and end apart: 31, of which 13 were waited for; matrix products, arithmetic and copies ran while one was open for 1% of the time, Pallas kernels for 14%

profile of v14, /device:TPU:1, one launch (start us, length us, event | category | flops | bytes accessed | tf_op | source)
XLA Modules:
  0.0 86.1 jit_solution(8298891960358768927)
XLA Ops:
  0.0 1.0 %broadcast_select_fusion = bf16[2,10,3,2,128]{4,3,2,1,0:T(2,128)(2,1)S(1)} fusion(pred[]{:T(512)S(6)} %eq.3, bf16[2,10,3,8,128]{4,3,2,1,0:T(8,128)(2,1)} %bitcast.17), kind=kLoop, calls=%fused_computation.5 | loop fusion | flops 15360 | bytes 92161 | tf_op jit(solution)/shard_map/jit(_where)/select_n | solution.py:285
  3.5 7.1 %collective-permute-start.6 = (bf16[2,40,8,128]{3,2,1,0:T(8,128)(2,1)S(1)}, bf16[2,40,8,128]{3,2,1,0:T(8,128)(2,1)S(1)}, u32[]{:S(2)}, u32[]{:S(2)}) collective-permute-start(bf16[2,40,8,128]{3,2,1,0:T(8,128)(2,1)S(1)} %pad_maximum_fusion.2.refs_0_), channel_id=1, source_target_pairs={{0,17},{1,16},{16,1},{17,0},{2,19},{3,18},{18,3},{19,2},{4,21},{5,... | collective-permute-start | bytes 491528 | tf_op jit(solution)/shard_map/ppermute | solution.py:314
  11.0 2.4 %collective-permute-start.1 = (bf16[2,40,8,128]{3,2,1,0:T(8,128)(2,1)S(1)}, bf16[2,40,8,128]{3,2,1,0:T(8,128)(2,1)S(1)}, u32[]{:S(2)}, u32[]{:S(2)}) collective-permute-start(bf16[2,40,8,128]{3,2,1,0:T(8,128)(2,1)S(1)} %pad_maximum_fusion.2.refs_0_), channel_id=1, source_target_pairs={{0,8},{8,0},{1,9},{9,1},{2,10},{10,2},{3,11},{11,3},{4,12},{12,4},... | collective-permute-start | bytes 491528 | tf_op jit(solution)/shard_map/ppermute | solution.py:23
  13.4 3.8 %collective-permute-start.7 = (bf16[2,40,8,128]{3,2,1,0:T(8,128)(2,1)S(1)}, bf16[2,40,8,128]{3,2,1,0:T(8,128)(2,1)S(1)}, u32[]{:S(2)}, u32[]{:S(2)}) collective-permute-start(bf16[2,40,8,128]{3,2,1,0:T(8,128)(2,1)S(1)} %collective-permute-done.6.refs_6_), channel_id=1, source_target_pairs={{0,8},{8,0},{1,9},{9,1},{2,10},{10,2},{3,11},{11,3},{4,12},{12,4},... | collective-permute-start | bytes 491528 | tf_op jit(solution)/shard_map/ppermute | solution.py:23
  17.9 1.4 %collective-permute-start.5 = (bf16[2,40,8,128]{3,2,1,0:T(8,128)(2,1)S(1)}, bf16[2,40,8,128]{3,2,1,0:T(8,128)(2,1)S(1)}, u32[]{:S(2)}, u32[]{:S(2)}) collective-permute-start(bf16[2,40,8,128]{3,2,1,0:T(8,128)(2,1)S(1)} %collective-permute-done.4.refs_4_), channel_id=1, source_target_pairs={{0,8},{8,0},{1,9},{9,1},{2,10},{10,2},{3,11},{11,3},{4,12},{12,4},... | collective-permute-start | bytes 491528 | tf_op jit(solution)/shard_map/ppermute | solution.py:23
  20.7 5.5 %shard_map.28 = (bf16[4,3,128,1280]{3,2,1,0:T(8,128)(2,1)S(1)}, f32[3,128,1280]{2,1,0:T(8,128)S(1)}) custom-call(s32[4]{0:T(128)S(1)} %pad_add_fusion.where_ref, bf16[2,40,8,128]{3,2,1,0:T(8,128)(2,1)S(1)} %pad_maximum_fusion.2.refs_0_, bf16[2,40,8,128]{3,2,1,0:T(8,128)(2,1)S(1)} %collective-permute-done.1.refs_1_, ...), custom_call_target="tpu_custom_call" | custom-call | flops 503316480 | bytes 4194304 | tf_op jit(solution)/shard_map/pallas_call | solution.py:151
  26.2 5.7 %shard_map.29 = (f32[256,128]{1,0:T(8,128)S(1)}, bf16[256,128]{1,0:T(8,128)(2,1)S(1)}, bf16[256,128]{1,0:T(8,128)(2,1)S(1)}, bf16[256,128]{1,0:T(8,128)(2,1)S(1)}) custom-call(s32[4]{0:T(128)S(1)} %pad_add_fusion.where_ref, bf16[4,3,128,1280]{3,2,1,0:T(8,128)(2,1)S(1)} %get-tuple-element.32.turned, f32[3,128,1280]{2,1,0:T(8,128)S(1)} %get-tuple-element.33.phi), custom_call_target="tpu_custom_call" | custom-call | flops 1006632960 | bytes 4194304 | tf_op jit(solution)/shard_map/pallas_call | solution.py:213
  31.9 1.5 %collective-permute-start.8 = (bf16[256,128]{1,0:T(8,128)(2,1)S(1)}, bf16[256,128]{1,0:T(8,128)(2,1)S(1)}, u32[]{:S(2)}, u32[]{:S(2)}) collective-permute-start(bf16[256,128]{1,0:T(8,128)(2,1)S(1)} %get-tuple-element.35), channel_id=1, source_target_pairs={{0,2},{2,4},{4,6},{6,0},{1,3},{3,5},{5,7},{7,1},{8,10},{10,12},{12... | collective-permute-start | bytes 196616 | tf_op jit(solution)/shard_map/ppermute | solution.py:23
  33.5 2.0 %collective-permute-start.9 = (bf16[256,128]{1,0:T(8,128)(2,1)S(1)}, bf16[256,128]{1,0:T(8,128)(2,1)S(1)}, u32[]{:S(2)}, u32[]{:S(2)}) collective-permute-start(bf16[256,128]{1,0:T(8,128)(2,1)S(1)} %get-tuple-element.36), channel_id=1, source_target_pairs={{0,4},{2,6},{4,0},{6,2},{1,5},{3,7},{5,1},{7,3},{8,12},{10,14},{12... | collective-permute-start | bytes 196616 | tf_op jit(solution)/shard_map/ppermute | solution.py:23
  35.5 1.3 %collective-permute-start.10 = (bf16[256,128]{1,0:T(8,128)(2,1)S(1)}, bf16[256,128]{1,0:T(8,128)(2,1)S(1)}, u32[]{:S(2)}, u32[]{:S(2)}) collective-permute-start(bf16[256,128]{1,0:T(8,128)(2,1)S(1)} %get-tuple-element.37), channel_id=1, source_target_pairs={{0,6},{2,0},{4,2},{6,4},{1,7},{3,1},{5,3},{7,5},{8,14},{10,8},{12,... | collective-permute-start | bytes 196616 | tf_op jit(solution)/shard_map/ppermute | solution.py:23
  36.9 5.7 %shard_map.30 = (f32[256,128]{1,0:T(8,128)S(1)}, bf16[256,128]{1,0:T(8,128)(2,1)S(1)}, bf16[256,128]{1,0:T(8,128)(2,1)S(1)}, bf16[256,128]{1,0:T(8,128)(2,1)S(1)}) custom-call(s32[4]{0:T(128)S(1)} %pad_add_fusion.where_ref, bf16[4,3,128,1280]{3,2,1,0:T(8,128)(2,1)S(1)} %get-tuple-element.32.turned, f32[3,128,1280]{2,1,0:T(8,128)S(1)} %get-tuple-element.33.phi), custom_call_target="tpu_custom_call" | custom-call | flops 1006632960 | bytes 4194304 | tf_op jit(solution)/shard_map/pallas_call | solution.py:213
  42.9 1.1 %collective-permute-start.20 = (bf16[256,128]{1,0:T(8,128)(2,1)S(1)}, bf16[256,128]{1,0:T(8,128)(2,1)S(1)}, u32[]{:S(2)}, u32[]{:S(2)}) collective-permute-start(bf16[256,128]{1,0:T(8,128)(2,1)S(1)} %add_convert_fusion.1), channel_id=1, source_target_pairs={{0,4},{2,6},{4,0},{6,2},{1,5},{3,7},{5,1},{7,3},{8,12},{10,14},{12... | collective-permute-start | bytes 196616 | tf_op jit(solution)/shard_map/ppermute | solution.py:23
  44.2 1.3 %collective-permute-start.11 = (bf16[256,128]{1,0:T(8,128)(2,1)S(1)}, bf16[256,128]{1,0:T(8,128)(2,1)S(1)}, u32[]{:S(2)}, u32[]{:S(2)}) collective-permute-start(bf16[256,128]{1,0:T(8,128)(2,1)S(1)} %get-tuple-element.48), channel_id=1, source_target_pairs={{0,2},{2,4},{4,6},{6,0},{1,3},{3,5},{5,7},{7,1},{8,10},{10,12},{12... | collective-permute-start | bytes 196616 | tf_op jit(solution)/shard_map/ppermute | solution.py:23
  45.6 2.0 %collective-permute-start.12 = (bf16[256,128]{1,0:T(8,128)(2,1)S(1)}, bf16[256,128]{1,0:T(8,128)(2,1)S(1)}, u32[]{:S(2)}, u32[]{:S(2)}) collective-permute-start(bf16[256,128]{1,0:T(8,128)(2,1)S(1)} %get-tuple-element.49), channel_id=1, source_target_pairs={{0,4},{2,6},{4,0},{6,2},{1,5},{3,7},{5,1},{7,3},{8,12},{10,14},{12... | collective-permute-start | bytes 196616 | tf_op jit(solution)/shard_map/ppermute | solution.py:23
  47.6 1.4 %collective-permute-done.19 = bf16[256,128]{1,0:T(8,128)(2,1)S(1)} collective-permute-done((bf16[256,128]{1,0:T(8,128)(2,1)S(1)}, bf16[256,128]{1,0:T(8,128)(2,1)S(1)}, u32[]{:S(2)}, u32[]{:S(2)}) %collective-permute-start.19) | collective-permute-done | bytes 65568 | tf_op jit(solution)/shard_map/ppermute | solution.py:23
  49.0 2.0 %collective-permute-start.13 = (bf16[256,128]{1,0:T(8,128)(2,1)S(1)}, bf16[256,128]{1,0:T(8,128)(2,1)S(1)}, u32[]{:S(2)}, u32[]{:S(2)}) collective-permute-start(bf16[256,128]{1,0:T(8,128)(2,1)S(1)} %get-tuple-element.50), channel_id=1, source_target_pairs={{0,6},{2,0},{4,2},{6,4},{1,7},{3,1},{5,3},{7,5},{8,14},{10,8},{12,... | collective-permute-start | bytes 196616 | tf_op jit(solution)/shard_map/ppermute | solution.py:23
  51.1 2.7 %collective-permute-start.23 = (bf16[1024,128]{1,0:T(8,128)(2,1)S(1)}, bf16[1024,128]{1,0:T(8,128)(2,1)S(1)}, u32[]{:S(2)}, u32[]{:S(2)}) collective-permute-start(bf16[1024,128]{1,0:T(8,128)(2,1)S(1)} %get-tuple-element.62.refs_0_), channel_id=1, source_target_pairs={{0,16},{16,0},{1,17},{17,1},{2,18},{18,2},{3,19},{19,3},{4,20},{20... | collective-permute-start | bytes 786440 | tf_op jit(solution)/shard_map/ppermute | solution.py:23
  53.9 1.1 %collective-permute-done.12 = bf16[256,128]{1,0:T(8,128)(2,1)S(1)} collective-permute-done((bf16[256,128]{1,0:T(8,128)(2,1)S(1)}, bf16[256,128]{1,0:T(8,128)(2,1)S(1)}, u32[]{:S(2)}, u32[]{:S(2)}) %collective-permute-start.12) | collective-permute-done | bytes 65568 | tf_op jit(solution)/shard_map/ppermute | solution.py:23
  55.0 2.5 %collective-permute-start.16 = (bf16[256,128]{1,0:T(8,128)(2,1)S(1)}, bf16[256,128]{1,0:T(8,128)(2,1)S(1)}, u32[]{:S(2)}, u32[]{:S(2)}) collective-permute-start(bf16[256,128]{1,0:T(8,128)(2,1)S(1)} %get-tuple-element.60), channel_id=1, source_target_pairs={{0,6},{2,0},{4,2},{6,4},{1,7},{3,1},{5,3},{7,5},{8,14},{10,8},{12,... | collective-permute-start | bytes 196616 | tf_op jit(solution)/shard_map/ppermute | solution.py:23
  58.9 3.1 %collective-permute-done.15 = bf16[256,128]{1,0:T(8,128)(2,1)S(1)} collective-permute-done((bf16[256,128]{1,0:T(8,128)(2,1)S(1)}, bf16[256,128]{1,0:T(8,128)(2,1)S(1)}, u32[]{:S(2)}, u32[]{:S(2)}) %collective-permute-start.15) | collective-permute-done | bytes 65568 | tf_op jit(solution)/shard_map/ppermute | solution.py:23
  62.0 1.1 %collective-permute-done.14 = bf16[256,128]{1,0:T(8,128)(2,1)S(1)} collective-permute-done((bf16[256,128]{1,0:T(8,128)(2,1)S(1)}, bf16[256,128]{1,0:T(8,128)(2,1)S(1)}, u32[]{:S(2)}, u32[]{:S(2)}) %collective-permute-start.14) | collective-permute-done | bytes 65568 | tf_op jit(solution)/shard_map/ppermute | solution.py:23
  63.1 1.4 %collective-permute-start.18 = (bf16[1024,128]{1,0:T(8,128)(2,1)S(1)}, bf16[1024,128]{1,0:T(8,128)(2,1)S(1)}, u32[]{:S(2)}, u32[]{:S(2)}) collective-permute-start(bf16[1024,128]{1,0:T(8,128)(2,1)S(1)} %pad_maximum_fusion.refs_3_), channel_id=1, source_target_pairs={{0,16},{16,0},{1,17},{17,1},{2,18},{18,2},{3,19},{19,3},{4,20},{20... | collective-permute-start | bytes 786440 | tf_op jit(solution)/shard_map/ppermute | solution.py:23
  64.9 1.1 %collective-permute-start.27 = (bf16[512,128]{1,0:T(8,128)(2,1)S(1)}, bf16[512,128]{1,0:T(8,128)(2,1)S(1)}, u32[]{:S(2)}, u32[]{:S(2)}) collective-permute-start(bf16[512,128]{1,0:T(8,128)(2,1)S(1)} %slice.29), channel_id=1, source_target_pairs={{0,1},{1,0},{2,3},{3,2},{4,5},{5,4},{6,7},{7,6},{8,9},{9,8},{10,11... | collective-permute-start | bytes 393224 | tf_op jit(solution)/shard_map/ppermute | solution.py:23
  66.3 1.8 %shard_map.31.refs_6_ = f32[16384,128]{1,0:T(8,128)} custom-call(s32[4]{0:T(128)S(1)} %pad_add_fusion.where_ref, bf16[1024,128]{1,0:T(8,128)(2,1)S(1)} %get-tuple-element.62.refs_0_, bf16[1024,128]{1,0:T(8,128)(2,1)S(1)} %collective-permute-done.22.refs_1_, bf16[1024,128]{1,0:T(8,128)(2,1)S(1)} %collective-permute-done.23.refs_2_), custom_call_target="tpu_custom_call" | custom-call | bytes 2359296 | tf_op jit(solution)/shard_map/pallas_call | solution.py:264
  68.4 1.6 %collective-permute-done.17.refs_4_ = bf16[1024,128]{1,0:T(8,128)(2,1)S(1)} collective-permute-done((bf16[1024,128]{1,0:T(8,128)(2,1)S(1)}, bf16[1024,128]{1,0:T(8,128)(2,1)S(1)}, u32[]{:S(2)}, u32[]{:S(2)}) %collective-permute-start.17) | collective-permute-done | bytes 262176 | tf_op jit(solution)/shard_map/ppermute | solution.py:23
  70.0 1.5 %collective-permute-done.26.refs_0_ = bf16[512,128]{1,0:T(8,128)(2,1)S(1)} collective-permute-done((bf16[512,128]{1,0:T(8,128)(2,1)S(1)}, bf16[512,128]{1,0:T(8,128)(2,1)S(1)}, u32[]{:S(2)}, u32[]{:S(2)}) %collective-permute-start.26) | collective-permute-done | bytes 131104 | tf_op jit(solution)/shard_map/ppermute | solution.py:23
  72.3 3.8 %collective-permute-start.28 = (bf16[4096,128]{1,0:T(8,128)(2,1)S(1)}, bf16[4096,128]{1,0:T(8,128)(2,1)S(1)}, u32[]{:S(2)}, u32[]{:S(2)}) collective-permute-start(bf16[4096,128]{1,0:T(8,128)(2,1)S(1)} %constant_dynamic-update-slice_fusion.4), channel_id=1, source_target_pairs={{0,8},{8,0},{1,9},{9,1},{2,10},{10,2},{3,11},{11,3},{4,12},{12,4},... | collective-permute-start | bytes 3145736 | tf_op jit(solution)/shard_map/ppermute | solution.py:23
  76.5 1.1 %collective-permute-start.25 = (bf16[512,128]{1,0:T(8,128)(2,1)S(1)}, bf16[512,128]{1,0:T(8,128)(2,1)S(1)}, u32[]{:S(2)}, u32[]{:S(2)}) collective-permute-start(bf16[512,128]{1,0:T(8,128)(2,1)S(1)} %slice.27), channel_id=1, source_target_pairs={{0,1},{1,0},{2,3},{3,2},{4,5},{5,4},{6,7},{7,6},{8,9},{9,8},{10,11... | collective-permute-start | bytes 393224 | tf_op jit(solution)/shard_map/ppermute | solution.py:23
  78.4 2.8 %shard_map.32.refs_3_ = f32[16384,128]{1,0:T(8,128)} custom-call(s32[4]{0:T(128)S(1)} %pad_add_fusion.where_ref, bf16[512,128]{1,0:T(8,128)(2,1)S(1)} %collective-permute-done.26.refs_0_, bf16[512,128]{1,0:T(8,128)(2,1)S(1)} %collective-permute-done.27.refs_1_, ...), custom_call_target="tpu_custom_call", output_to_operand_aliasing={{}: (7, {})} | custom-call | bytes 6291456 | tf_op jit(solution)/shard_map/pallas_call | solution.py:264
  81.2 1.3 %collective-permute-start.29 = (bf16[1024,128]{1,0:T(8,128)(2,1)S(1)}, bf16[1024,128]{1,0:T(8,128)(2,1)S(1)}, u32[]{:S(2)}, u32[]{:S(2)}) collective-permute-start(bf16[1024,128]{1,0:T(8,128)(2,1)S(1)} %pad_maximum_fusion.1), channel_id=1, source_target_pairs={{0,8},{8,0},{1,9},{9,1},{2,10},{10,2},{3,11},{11,3},{4,12},{12,4},... | collective-permute-start | bytes 786440 | tf_op jit(solution)/shard_map/ppermute | solution.py:23
  82.5 2.0 %shard_map.33.refs_1_ = f32[16384,128]{1,0:T(8,128)} custom-call(s32[4]{0:T(128)S(1)} %pad_add_fusion.where_ref, bf16[3072,128]{1,0:T(8,128)(2,1)S(1)} %collective-permute-done.30.refs_0_, bf16[512,128]{1,0:T(8,128)(2,1)S(1)} %collective-permute-done.24.refs_1_, ...), custom_call_target="tpu_custom_call", output_to_operand_aliasing={{}: (4, {})} | custom-call | bytes 3145728 | tf_op jit(solution)/shard_map/pallas_call | solution.py:264
  84.5 1.4 %shard_map.34 = f32[16384,128]{1,0:T(8,128)} custom-call(s32[4]{0:T(128)S(1)} %pad_add_fusion.where_ref, bf16[1024,128]{1,0:T(8,128)(2,1)S(1)} %collective-permute-done.29.refs_0_, f32[16384,128]{1,0:T(8,128)} %shard_map.33.refs_1_), custom_call_target="tpu_custom_call", output_to_operand_aliasing={{}: (2, {})} | custom-call | bytes 786432 | tf_op jit(solution)/shard_map/pallas_call | solution.py:264
  (67 shorter events, 9.8 us)
Async XLA Ops:
  1.0 1.5 %collective-permute-start = (bf16[2,10,3,2,128]{4,3,2,1,0:T(2,128)(2,1)S(1)}, bf16[2,10,3,2,128]{4,3,2,1,0:T(2,128)(2,1)S(1)}, u32[]{:S(2)}, u32[]{:S(2)}) collective-permute-start(bf16[2,10,3,2,128]{4,3,2,1,0:T(2,128)(2,1)S(1)} %broadcast_select_fusion), channel_id=1, source_target_pairs={{1,2},{3,4},{5,6},{2,1},{4,3},{6,5},{9,10},{11,12},{13,14},{10,9},... | collective-permute-start | bytes 92168 | tf_op jit(solution)/shard_map/ppermute | solution.py:287
  3.5 9.9 %collective-permute-start.6 = (bf16[2,40,8,128]{3,2,1,0:T(8,128)(2,1)S(1)}, bf16[2,40,8,128]{3,2,1,0:T(8,128)(2,1)S(1)}, u32[]{:S(2)}, u32[]{:S(2)}) collective-permute-start(bf16[2,40,8,128]{3,2,1,0:T(8,128)(2,1)S(1)} %pad_maximum_fusion.2.refs_0_), channel_id=1, source_target_pairs={{0,17},{1,16},{16,1},{17,0},{2,19},{3,18},{18,3},{19,2},{4,21},{5,... | collective-permute-start | bytes 491528 | tf_op jit(solution)/shard_map/ppermute | solution.py:314
  10.6 7.2 %collective-permute-start.4 = (bf16[2,40,8,128]{3,2,1,0:T(8,128)(2,1)S(1)}, bf16[2,40,8,128]{3,2,1,0:T(8,128)(2,1)S(1)}, u32[]{:S(2)}, u32[]{:S(2)}) collective-permute-start(bf16[2,40,8,128]{3,2,1,0:T(8,128)(2,1)S(1)} %pad_maximum_fusion.2.refs_0_), channel_id=1, source_target_pairs={{0,16},{16,0},{1,17},{17,1},{2,18},{18,2},{3,19},{19,3},{4,20},{20... | collective-permute-start | bytes 491528 | tf_op jit(solution)/shard_map/ppermute | solution.py:23
  10.9 8.4 %collective-permute-start.2 = (bf16[2,40,8,128]{3,2,1,0:T(8,128)(2,1)S(1)}, bf16[2,40,8,128]{3,2,1,0:T(8,128)(2,1)S(1)}, u32[]{:S(2)}, u32[]{:S(2)}) collective-permute-start(bf16[2,40,8,128]{3,2,1,0:T(8,128)(2,1)S(1)} %pad_maximum_fusion.2.refs_0_), channel_id=1, source_target_pairs={{0,1},{1,0},{2,3},{3,2},{4,5},{5,4},{6,7},{7,6},{8,9},{9,8},{10,11... | collective-permute-start | bytes 491528 | tf_op jit(solution)/shard_map/ppermute | solution.py:23
  11.0 8.4 %collective-permute-start.1 = (bf16[2,40,8,128]{3,2,1,0:T(8,128)(2,1)S(1)}, bf16[2,40,8,128]{3,2,1,0:T(8,128)(2,1)S(1)}, u32[]{:S(2)}, u32[]{:S(2)}) collective-permute-start(bf16[2,40,8,128]{3,2,1,0:T(8,128)(2,1)S(1)} %pad_maximum_fusion.2.refs_0_), channel_id=1, source_target_pairs={{0,8},{8,0},{1,9},{9,1},{2,10},{10,2},{3,11},{11,3},{4,12},{12,4},... | collective-permute-start | bytes 491528 | tf_op jit(solution)/shard_map/ppermute | solution.py:23
  13.4 6.0 %collective-permute-start.7 = (bf16[2,40,8,128]{3,2,1,0:T(8,128)(2,1)S(1)}, bf16[2,40,8,128]{3,2,1,0:T(8,128)(2,1)S(1)}, u32[]{:S(2)}, u32[]{:S(2)}) collective-permute-start(bf16[2,40,8,128]{3,2,1,0:T(8,128)(2,1)S(1)} %collective-permute-done.6.refs_6_), channel_id=1, source_target_pairs={{0,8},{8,0},{1,9},{9,1},{2,10},{10,2},{3,11},{11,3},{4,12},{12,4},... | collective-permute-start | bytes 491528 | tf_op jit(solution)/shard_map/ppermute | solution.py:23
  17.9 2.5 %collective-permute-start.5 = (bf16[2,40,8,128]{3,2,1,0:T(8,128)(2,1)S(1)}, bf16[2,40,8,128]{3,2,1,0:T(8,128)(2,1)S(1)}, u32[]{:S(2)}, u32[]{:S(2)}) collective-permute-start(bf16[2,40,8,128]{3,2,1,0:T(8,128)(2,1)S(1)} %collective-permute-done.4.refs_4_), channel_id=1, source_target_pairs={{0,8},{8,0},{1,9},{9,1},{2,10},{10,2},{3,11},{11,3},{4,12},{12,4},... | collective-permute-start | bytes 491528 | tf_op jit(solution)/shard_map/ppermute | solution.py:23
  19.3 1.4 %collective-permute-start.3 = (bf16[2,40,8,128]{3,2,1,0:T(8,128)(2,1)S(1)}, bf16[2,40,8,128]{3,2,1,0:T(8,128)(2,1)S(1)}, u32[]{:S(2)}, u32[]{:S(2)}) collective-permute-start(bf16[2,40,8,128]{3,2,1,0:T(8,128)(2,1)S(1)} %collective-permute-done.2.refs_2_), channel_id=1, source_target_pairs={{0,8},{8,0},{1,9},{9,1},{2,10},{10,2},{3,11},{11,3},{4,12},{12,4},... | collective-permute-start | bytes 491528 | tf_op jit(solution)/shard_map/ppermute | solution.py:23
  31.9 10.7 %collective-permute-start.8 = (bf16[256,128]{1,0:T(8,128)(2,1)S(1)}, bf16[256,128]{1,0:T(8,128)(2,1)S(1)}, u32[]{:S(2)}, u32[]{:S(2)}) collective-permute-start(bf16[256,128]{1,0:T(8,128)(2,1)S(1)} %get-tuple-element.35), channel_id=1, source_target_pairs={{0,2},{2,4},{4,6},{6,0},{1,3},{3,5},{5,7},{7,1},{8,10},{10,12},{12... | collective-permute-start | bytes 196616 | tf_op jit(solution)/shard_map/ppermute | solution.py:23
  33.5 9.1 %collective-permute-start.9 = (bf16[256,128]{1,0:T(8,128)(2,1)S(1)}, bf16[256,128]{1,0:T(8,128)(2,1)S(1)}, u32[]{:S(2)}, u32[]{:S(2)}) collective-permute-start(bf16[256,128]{1,0:T(8,128)(2,1)S(1)} %get-tuple-element.36), channel_id=1, source_target_pairs={{0,4},{2,6},{4,0},{6,2},{1,5},{3,7},{5,1},{7,3},{8,12},{10,14},{12... | collective-permute-start | bytes 196616 | tf_op jit(solution)/shard_map/ppermute | solution.py:23
  35.5 7.1 %collective-permute-start.10 = (bf16[256,128]{1,0:T(8,128)(2,1)S(1)}, bf16[256,128]{1,0:T(8,128)(2,1)S(1)}, u32[]{:S(2)}, u32[]{:S(2)}) collective-permute-start(bf16[256,128]{1,0:T(8,128)(2,1)S(1)} %get-tuple-element.37), channel_id=1, source_target_pairs={{0,6},{2,0},{4,2},{6,4},{1,7},{3,1},{5,3},{7,5},{8,14},{10,8},{12,... | collective-permute-start | bytes 196616 | tf_op jit(solution)/shard_map/ppermute | solution.py:23
  42.7 8.4 %collective-permute-start.21 = (bf16[256,128]{1,0:T(8,128)(2,1)S(1)}, bf16[256,128]{1,0:T(8,128)(2,1)S(1)}, u32[]{:S(2)}, u32[]{:S(2)}) collective-permute-start(bf16[256,128]{1,0:T(8,128)(2,1)S(1)} %add_convert_fusion.1), channel_id=1, source_target_pairs={{0,6},{2,0},{4,2},{6,4},{1,7},{3,1},{5,3},{7,5},{8,14},{10,8},{12,... | collective-permute-start | bytes 196616 | tf_op jit(solution)/shard_map/ppermute | solution.py:23
  42.9 8.2 %collective-permute-start.20 = (bf16[256,128]{1,0:T(8,128)(2,1)S(1)}, bf16[256,128]{1,0:T(8,128)(2,1)S(1)}, u32[]{:S(2)}, u32[]{:S(2)}) collective-permute-start(bf16[256,128]{1,0:T(8,128)(2,1)S(1)} %add_convert_fusion.1), channel_id=1, source_target_pairs={{0,4},{2,6},{4,0},{6,2},{1,5},{3,7},{5,1},{7,3},{8,12},{10,14},{12... | collective-permute-start | bytes 196616 | tf_op jit(solution)/shard_map/ppermute | solution.py:23
  44.0 5.0 %collective-permute-start.19 = (bf16[256,128]{1,0:T(8,128)(2,1)S(1)}, bf16[256,128]{1,0:T(8,128)(2,1)S(1)}, u32[]{:S(2)}, u32[]{:S(2)}) collective-permute-start(bf16[256,128]{1,0:T(8,128)(2,1)S(1)} %add_convert_fusion.1), channel_id=1, source_target_pairs={{0,2},{2,4},{4,6},{6,0},{1,3},{3,5},{5,7},{7,1},{8,10},{10,12},{12... | collective-permute-start | bytes 196616 | tf_op jit(solution)/shard_map/ppermute | solution.py:23
  44.2 9.7 %collective-permute-start.11 = (bf16[256,128]{1,0:T(8,128)(2,1)S(1)}, bf16[256,128]{1,0:T(8,128)(2,1)S(1)}, u32[]{:S(2)}, u32[]{:S(2)}) collective-permute-start(bf16[256,128]{1,0:T(8,128)(2,1)S(1)} %get-tuple-element.48), channel_id=1, source_target_pairs={{0,2},{2,4},{4,6},{6,0},{1,3},{3,5},{5,7},{7,1},{8,10},{10,12},{12... | collective-permute-start | bytes 196616 | tf_op jit(solution)/shard_map/ppermute | solution.py:23
  45.6 9.4 %collective-permute-start.12 = (bf16[256,128]{1,0:T(8,128)(2,1)S(1)}, bf16[256,128]{1,0:T(8,128)(2,1)S(1)}, u32[]{:S(2)}, u32[]{:S(2)}) collective-permute-start(bf16[256,128]{1,0:T(8,128)(2,1)S(1)} %get-tuple-element.49), channel_id=1, source_target_pairs={{0,4},{2,6},{4,0},{6,2},{1,5},{3,7},{5,1},{7,3},{8,12},{10,14},{12... | collective-permute-start | bytes 196616 | tf_op jit(solution)/shard_map/ppermute | solution.py:23
  49.0 6.0 %collective-permute-start.13 = (bf16[256,128]{1,0:T(8,128)(2,1)S(1)}, bf16[256,128]{1,0:T(8,128)(2,1)S(1)}, u32[]{:S(2)}, u32[]{:S(2)}) collective-permute-start(bf16[256,128]{1,0:T(8,128)(2,1)S(1)} %get-tuple-element.50), channel_id=1, source_target_pairs={{0,6},{2,0},{4,2},{6,4},{1,7},{3,1},{5,3},{7,5},{8,14},{10,8},{12,... | collective-permute-start | bytes 196616 | tf_op jit(solution)/shard_map/ppermute | solution.py:23
  51.1 13.7 %collective-permute-start.23 = (bf16[1024,128]{1,0:T(8,128)(2,1)S(1)}, bf16[1024,128]{1,0:T(8,128)(2,1)S(1)}, u32[]{:S(2)}, u32[]{:S(2)}) collective-permute-start(bf16[1024,128]{1,0:T(8,128)(2,1)S(1)} %get-tuple-element.62.refs_0_), channel_id=1, source_target_pairs={{0,16},{16,0},{1,17},{17,1},{2,18},{18,2},{3,19},{19,3},{4,20},{20... | collective-permute-start | bytes 786440 | tf_op jit(solution)/shard_map/ppermute | solution.py:23
  53.9 12.1 %collective-permute-start.22 = (bf16[1024,128]{1,0:T(8,128)(2,1)S(1)}, bf16[1024,128]{1,0:T(8,128)(2,1)S(1)}, u32[]{:S(2)}, u32[]{:S(2)}) collective-permute-start(bf16[1024,128]{1,0:T(8,128)(2,1)S(1)} %get-tuple-element.62.refs_0_), channel_id=1, source_target_pairs={{0,1},{1,0},{2,3},{3,2},{4,5},{5,4},{6,7},{7,6},{8,9},{9,8},{10,11... | collective-permute-start | bytes 786440 | tf_op jit(solution)/shard_map/ppermute | solution.py:23
  55.0 3.8 %collective-permute-start.16 = (bf16[256,128]{1,0:T(8,128)(2,1)S(1)}, bf16[256,128]{1,0:T(8,128)(2,1)S(1)}, u32[]{:S(2)}, u32[]{:S(2)}) collective-permute-start(bf16[256,128]{1,0:T(8,128)(2,1)S(1)} %get-tuple-element.60), channel_id=1, source_target_pairs={{0,6},{2,0},{4,2},{6,4},{1,7},{3,1},{5,3},{7,5},{8,14},{10,8},{12,... | collective-permute-start | bytes 196616 | tf_op jit(solution)/shard_map/ppermute | solution.py:23
  57.5 4.4 %collective-permute-start.15 = (bf16[256,128]{1,0:T(8,128)(2,1)S(1)}, bf16[256,128]{1,0:T(8,128)(2,1)S(1)}, u32[]{:S(2)}, u32[]{:S(2)}) collective-permute-start(bf16[256,128]{1,0:T(8,128)(2,1)S(1)} %get-tuple-element.60), channel_id=1, source_target_pairs={{0,4},{2,6},{4,0},{6,2},{1,5},{3,7},{5,1},{7,3},{8,12},{10,14},{12... | collective-permute-start | bytes 196616 | tf_op jit(solution)/shard_map/ppermute | solution.py:23
  57.9 5.1 %collective-permute-start.14 = (bf16[256,128]{1,0:T(8,128)(2,1)S(1)}, bf16[256,128]{1,0:T(8,128)(2,1)S(1)}, u32[]{:S(2)}, u32[]{:S(2)}) collective-permute-start(bf16[256,128]{1,0:T(8,128)(2,1)S(1)} %get-tuple-element.60), channel_id=1, source_target_pairs={{0,2},{2,4},{4,6},{6,0},{1,3},{3,5},{5,7},{7,1},{8,10},{10,12},{12... | collective-permute-start | bytes 196616 | tf_op jit(solution)/shard_map/ppermute | solution.py:23
  63.1 5.3 %collective-permute-start.18 = (bf16[1024,128]{1,0:T(8,128)(2,1)S(1)}, bf16[1024,128]{1,0:T(8,128)(2,1)S(1)}, u32[]{:S(2)}, u32[]{:S(2)}) collective-permute-start(bf16[1024,128]{1,0:T(8,128)(2,1)S(1)} %pad_maximum_fusion.refs_3_), channel_id=1, source_target_pairs={{0,16},{16,0},{1,17},{17,1},{2,18},{18,2},{3,19},{19,3},{4,20},{20... | collective-permute-start | bytes 786440 | tf_op jit(solution)/shard_map/ppermute | solution.py:23
  64.5 5.5 %collective-permute-start.17 = (bf16[1024,128]{1,0:T(8,128)(2,1)S(1)}, bf16[1024,128]{1,0:T(8,128)(2,1)S(1)}, u32[]{:S(2)}, u32[]{:S(2)}) collective-permute-start(bf16[1024,128]{1,0:T(8,128)(2,1)S(1)} %pad_maximum_fusion.refs_3_), channel_id=1, source_target_pairs={{0,1},{1,0},{2,3},{3,2},{4,5},{5,4},{6,7},{7,6},{8,9},{9,8},{10,11... | collective-permute-start | bytes 786440 | tf_op jit(solution)/shard_map/ppermute | solution.py:23
  64.9 7.4 %collective-permute-start.27 = (bf16[512,128]{1,0:T(8,128)(2,1)S(1)}, bf16[512,128]{1,0:T(8,128)(2,1)S(1)}, u32[]{:S(2)}, u32[]{:S(2)}) collective-permute-start(bf16[512,128]{1,0:T(8,128)(2,1)S(1)} %slice.29), channel_id=1, source_target_pairs={{0,1},{1,0},{2,3},{3,2},{4,5},{5,4},{6,7},{7,6},{8,9},{9,8},{10,11... | collective-permute-start | bytes 393224 | tf_op jit(solution)/shard_map/ppermute | solution.py:23
  66.0 5.5 %collective-permute-start.26 = (bf16[512,128]{1,0:T(8,128)(2,1)S(1)}, bf16[512,128]{1,0:T(8,128)(2,1)S(1)}, u32[]{:S(2)}, u32[]{:S(2)}) collective-permute-start(bf16[512,128]{1,0:T(8,128)(2,1)S(1)} %slice.28), channel_id=1, source_target_pairs={{0,16},{16,0},{1,17},{17,1},{2,18},{18,2},{3,19},{19,3},{4,20},{20... | collective-permute-start | bytes 393224 | tf_op jit(solution)/shard_map/ppermute | solution.py:23
  72.3 6.1 %collective-permute-start.28 = (bf16[4096,128]{1,0:T(8,128)(2,1)S(1)}, bf16[4096,128]{1,0:T(8,128)(2,1)S(1)}, u32[]{:S(2)}, u32[]{:S(2)}) collective-permute-start(bf16[4096,128]{1,0:T(8,128)(2,1)S(1)} %constant_dynamic-update-slice_fusion.4), channel_id=1, source_target_pairs={{0,8},{8,0},{1,9},{9,1},{2,10},{10,2},{3,11},{11,3},{4,12},{12,4},... | collective-permute-start | bytes 3145736 | tf_op jit(solution)/shard_map/ppermute | solution.py:23
  76.2 6.3 %collective-permute-start.30 = (bf16[3072,128]{1,0:T(8,128)(2,1)S(1)}, bf16[3072,128]{1,0:T(8,128)(2,1)S(1)}, u32[]{:S(2)}, u32[]{:S(2)}) collective-permute-start(bf16[3072,128]{1,0:T(8,128)(2,1)S(1)} %constant_dynamic-update-slice_fusion.12), channel_id=1, source_target_pairs={{0,8},{8,0},{1,9},{9,1},{2,10},{10,2},{3,11},{11,3},{4,12},{12,4},... | collective-permute-start | bytes 2359304 | tf_op jit(solution)/shard_map/ppermute | solution.py:23
  76.3 4.9 %collective-permute-start.24 = (bf16[512,128]{1,0:T(8,128)(2,1)S(1)}, bf16[512,128]{1,0:T(8,128)(2,1)S(1)}, u32[]{:S(2)}, u32[]{:S(2)}) collective-permute-start(bf16[512,128]{1,0:T(8,128)(2,1)S(1)} %slice.26), channel_id=1, source_target_pairs={{0,16},{16,0},{1,17},{17,1},{2,18},{18,2},{3,19},{19,3},{4,20},{20... | collective-permute-start | bytes 393224 | tf_op jit(solution)/shard_map/ppermute | solution.py:23
  76.5 4.7 %collective-permute-start.25 = (bf16[512,128]{1,0:T(8,128)(2,1)S(1)}, bf16[512,128]{1,0:T(8,128)(2,1)S(1)}, u32[]{:S(2)}, u32[]{:S(2)}) collective-permute-start(bf16[512,128]{1,0:T(8,128)(2,1)S(1)} %slice.27), channel_id=1, source_target_pairs={{0,1},{1,0},{2,3},{3,2},{4,5},{5,4},{6,7},{7,6},{8,9},{9,8},{10,11... | collective-permute-start | bytes 393224 | tf_op jit(solution)/shard_map/ppermute | solution.py:23
  81.2 3.3 %collective-permute-start.29 = (bf16[1024,128]{1,0:T(8,128)(2,1)S(1)}, bf16[1024,128]{1,0:T(8,128)(2,1)S(1)}, u32[]{:S(2)}, u32[]{:S(2)}) collective-permute-start(bf16[1024,128]{1,0:T(8,128)(2,1)S(1)} %pad_maximum_fusion.1), channel_id=1, source_target_pairs={{0,8},{8,0},{1,9},{9,1},{2,10},{10,2},{3,11},{11,3},{4,12},{12,4},... | collective-permute-start | bytes 786440 | tf_op jit(solution)/shard_map/ppermute | solution.py:23

commit v15 on v14

--- a/solution.py
+++ b/solution.py
@@ -21,6 +21,12 @@
 def rotate(value, axis, by=1):
     count = lax.axis_size(axis)
     return lax.ppermute(value, axis, [(i, (i + by) % count) for i in range(count)])
+
+
+def swap(value, by):
+    count = lax.axis_size("deck")
+    assert count & (count - 1) == 0
+    return lax.ppermute(value, "deck", [(i, i ^ by) for i in range(count)])
 
 
 def member(where, rows, offsets):
@@ -167,10 +173,12 @@
     outs = len(out_refs)
     width, count = turned.shape[2:]
     base = (member(where_ref, rows, (0, 0, 0)) * CHUNKS + chunk) * share
-    first = where_ref[3] * (share // decks) if outs > 1 else 0
+    each = share // decks if outs > 1 else share
     together = min(4, share)
     for i in range(share):
-        mode = base + lax.rem(i + first, share)
+        mode = base + i
+        if outs > 1:
+            mode = base + lax.bitwise_xor(where_ref[3], i // each) * each + i % each
         for b in range(3):
             own[b, i] = jnp.broadcast_to(phi[b, pl.ds(mode, 1), :], (TILE, count))
     for group in range(share // together):
@@ -240,7 +248,7 @@
 
         lax.fori_loop(0, line // step, widen, 0)
         start = (member(where_ref, rows, offsets) * CHUNKS + chunk) * decks * line
-        start = start + lax.rem(where_ref[3] - d + decks, decks) * line
+        start = start + lax.bitwise_xor(where_ref[3], d) * line
         to = pl.ds(pl.multiple_of(start, line), line)
         copies.append(
             pltpu.make_async_copy(wide.at[done : done + line], out_ref.at[to], sems.at[n])
@@ -325,7 +333,7 @@
 
 def parts_over_decks(terms, decks):
     if len(terms) > 1:
-        return [terms[0]] + [rotate(terms[r], "deck", r) for r in range(1, decks)]
+        return [terms[0]] + [swap(terms[r], r) for r in range(1, decks)]
     width = terms[0].shape[1]
     return list(lax.all_to_all(terms[0].reshape(decks, -1, width), "deck", 0, 0))
 
@@ -364,7 +372,7 @@
             mine, later = lax.optimization_barrier((mine, terms[n + 1]))
             terms[n + 1] = list(later)
         pieces.append(
-            jnp.concatenate([mine] + [rotate(mine, "deck", r) for r in range(1, decks)], axis=0)
+            jnp.concatenate([mine] + [swap(mine, r) for r in range(1, decks)], axis=0)
         )
 
     def join(chosen):

time: 86.3 us -> 85.8 us (level)
  waiting for transfers between devices: 14.5 us -> 10.2 us
  starting transfers between devices: 42.9 us -> 46.7 us
    ppermute x0 -> x12, starting transfers between devices: none -> 16.1 us  [swap(): return lax.ppermute(value, 'deck', [(i, i ^ by) for i in range(count)])]
    ppermute x29 -> x17, starting transfers between devices: 35.1 us -> 22.9 us  [rotate(): lax.ppermute(value, axis, [(i, (i + by) % count) for i in range(count)])]
    ppermute x29 -> x17, waiting for transfers between devices: 14.5 us -> 5.13 us  [rotate(): lax.ppermute(value, axis, [(i, (i + by) % count) for i in range(count)])]
    ppermute x0 -> x12, waiting for transfers between devices: none -> 5.11 us  [swap(): return lax.ppermute(value, 'deck', [(i, i ^ by) for i in range(count)])]
  transfers between devices with their start and end apart: 31 -> 31, of which waited for: 13 -> 14; matrix products, arithmetic and copies ran while one was open for 1% -> 1% of each run, Pallas kernels for 14% -> 14%
where the time goes in v15:
time: 85.8 us; the launch traced here: 85.5 us
  starting transfers between devices  46.7 us (54%)
  Pallas kernels  25 us (29%)
  waiting for transfers between devices  10.2 us (12%)
  other arithmetic  2.93 us (3%)
    ppermute x17, starting transfers between devices, rotate(): lax.ppermute(value, axis, [(i, (i + by) % count) for i in range(count)])  22.9 us
    ppermute x12, starting transfers between devices, swap(): return lax.ppermute(value, 'deck', [(i, i ^ by) for i in range(count)])  16.1 us
    pallas_call x2, Pallas kernels, plane_terms(): pl.pallas_call(functools.partial(terms_kernel, share, chunk, rows, decks)...  11.5 us
    pallas_call x4, Pallas kernels, put(): pl.pallas_call(functools.partial(place_kernel, (rows, decks, line, runs),...  8 us
    ppermute x1, starting transfers between devices, spread_near(): got[r, 1] = lax.ppermute(piece, DIAGONAL, pairs)  7.13 us
    pallas_call x1, Pallas kernels, plane_slopes(): pl.pallas_call(functools.partial(slopes_kernel, sizes, offsets), out_shap...  5.49 us
    ppermute x17, waiting for transfers between devices, rotate(): lax.ppermute(value, axis, [(i, (i + by) % count) for i in range(count)])  5.13 us
    ppermute x12, waiting for transfers between devices, swap(): return lax.ppermute(value, 'deck', [(i, i ^ by) for i in range(count)])  5.11 us
  transfers between devices with their start and end apart: 31, of which 14 were waited for; matrix products, arithmetic and copies ran while one was open for 1% of the time, Pallas kernels for 14%

profile of v15, /device:TPU:1, one launch (start us, length us, event | category | flops | bytes accessed | tf_op | source)
XLA Modules:
  0.0 85.5 jit_solution(16388994168309142637)
XLA Ops:
  0.0 1.0 %broadcast_select_fusion = bf16[2,10,3,2,128]{4,3,2,1,0:T(2,128)(2,1)S(1)} fusion(pred[]{:T(512)S(6)} %eq.3, bf16[2,10,3,8,128]{4,3,2,1,0:T(8,128)(2,1)} %bitcast.17), kind=kLoop, calls=%fused_computation.5 | loop fusion | flops 15360 | bytes 92161 | tf_op jit(solution)/shard_map/jit(_where)/select_n | solution.py:293
  2.6 0.9 %pad_maximum_fusion.2.refs_0_ = bf16[2,40,8,128]{3,2,1,0:T(8,128)(2,1)S(1)} fusion(bf16[2,9,8,128]{3,2,1,0:T(8,128)(2,1)S(1)} %bitcast.19, bf16[2,1,8,128]{3,2,1,0:T(8,128)(2,1)S(1)} %fusion.7, bf16[2,30,8,128]{3,2,1,0:T(8,128)(2,1)} %bitcast.18), kind=kLoop, calls=%fused_computation.2 | loop fusion | flops 163840 | bytes 327680 | tf_op jit(solution)/shard_map/concatenate | solution.py:313
  3.5 7.1 %collective-permute-start.6 = (bf16[2,40,8,128]{3,2,1,0:T(8,128)(2,1)S(1)}, bf16[2,40,8,128]{3,2,1,0:T(8,128)(2,1)S(1)}, u32[]{:S(2)}, u32[]{:S(2)}) collective-permute-start(bf16[2,40,8,128]{3,2,1,0:T(8,128)(2,1)S(1)} %pad_maximum_fusion.2.refs_0_), channel_id=1, source_target_pairs={{0,17},{1,16},{16,1},{17,0},{2,19},{3,18},{18,3},{19,2},{4,21},{5,... | collective-permute-start | bytes 491528 | tf_op jit(solution)/shard_map/ppermute | solution.py:322
  11.0 2.4 %collective-permute-start.1 = (bf16[2,40,8,128]{3,2,1,0:T(8,128)(2,1)S(1)}, bf16[2,40,8,128]{3,2,1,0:T(8,128)(2,1)S(1)}, u32[]{:S(2)}, u32[]{:S(2)}) collective-permute-start(bf16[2,40,8,128]{3,2,1,0:T(8,128)(2,1)S(1)} %pad_maximum_fusion.2.refs_0_), channel_id=1, source_target_pairs={{0,8},{8,0},{1,9},{9,1},{2,10},{10,2},{3,11},{11,3},{4,12},{12,4},... | collective-permute-start | bytes 491528 | tf_op jit(solution)/shard_map/ppermute | solution.py:23
  13.4 3.8 %collective-permute-start.7 = (bf16[2,40,8,128]{3,2,1,0:T(8,128)(2,1)S(1)}, bf16[2,40,8,128]{3,2,1,0:T(8,128)(2,1)S(1)}, u32[]{:S(2)}, u32[]{:S(2)}) collective-permute-start(bf16[2,40,8,128]{3,2,1,0:T(8,128)(2,1)S(1)} %collective-permute-done.6.refs_6_), channel_id=1, source_target_pairs={{0,8},{8,0},{1,9},{9,1},{2,10},{10,2},{3,11},{11,3},{4,12},{12,4},... | collective-permute-start | bytes 491528 | tf_op jit(solution)/shard_map/ppermute | solution.py:23
  17.9 1.4 %collective-permute-start.5 = (bf16[2,40,8,128]{3,2,1,0:T(8,128)(2,1)S(1)}, bf16[2,40,8,128]{3,2,1,0:T(8,128)(2,1)S(1)}, u32[]{:S(2)}, u32[]{:S(2)}) collective-permute-start(bf16[2,40,8,128]{3,2,1,0:T(8,128)(2,1)S(1)} %collective-permute-done.4.refs_4_), channel_id=1, source_target_pairs={{0,8},{8,0},{1,9},{9,1},{2,10},{10,2},{3,11},{11,3},{4,12},{12,4},... | collective-permute-start | bytes 491528 | tf_op jit(solution)/shard_map/ppermute | solution.py:23
  19.4 0.9 %collective-permute-done.5.refs_5_ = bf16[2,40,8,128]{3,2,1,0:T(8,128)(2,1)S(1)} collective-permute-done((bf16[2,40,8,128]{3,2,1,0:T(8,128)(2,1)S(1)}, bf16[2,40,8,128]{3,2,1,0:T(8,128)(2,1)S(1)}, u32[]{:S(2)}, u32[]{:S(2)}) %collective-permute-start.5) | collective-permute-done | bytes 163872 | tf_op jit(solution)/shard_map/ppermute | solution.py:23
  20.7 5.5 %shard_map.28 = (bf16[4,3,128,1280]{3,2,1,0:T(8,128)(2,1)S(1)}, f32[3,128,1280]{2,1,0:T(8,128)S(1)}) custom-call(s32[4]{0:T(128)S(1)} %pad_add_fusion.where_ref, bf16[2,40,8,128]{3,2,1,0:T(8,128)(2,1)S(1)} %pad_maximum_fusion.2.refs_0_, bf16[2,40,8,128]{3,2,1,0:T(8,128)(2,1)S(1)} %collective-permute-done.1.refs_1_, ...), custom_call_target="tpu_custom_call" | custom-call | flops 503316480 | bytes 4194304 | tf_op jit(solution)/shard_map/pallas_call | solution.py:157
  26.2 5.7 %shard_map.29 = (f32[256,128]{1,0:T(8,128)S(1)}, bf16[256,128]{1,0:T(8,128)(2,1)S(1)}, bf16[256,128]{1,0:T(8,128)(2,1)S(1)}, bf16[256,128]{1,0:T(8,128)(2,1)S(1)}) custom-call(s32[4]{0:T(128)S(1)} %pad_add_fusion.where_ref, bf16[4,3,128,1280]{3,2,1,0:T(8,128)(2,1)S(1)} %get-tuple-element.32.turned, f32[3,128,1280]{2,1,0:T(8,128)S(1)} %get-tuple-element.33.phi), custom_call_target="tpu_custom_call" | custom-call | flops 1006632960 | bytes 4194304 | tf_op jit(solution)/shard_map/pallas_call | solution.py:221
  32.0 1.6 %collective-permute-start.8 = (bf16[256,128]{1,0:T(8,128)(2,1)S(1)}, bf16[256,128]{1,0:T(8,128)(2,1)S(1)}, u32[]{:S(2)}, u32[]{:S(2)}) collective-permute-start(bf16[256,128]{1,0:T(8,128)(2,1)S(1)} %get-tuple-element.35), channel_id=1, source_target_pairs={{0,2},{2,0},{4,6},{6,4},{1,3},{3,1},{5,7},{7,5},{8,10},{10,8},{12,... | collective-permute-start | bytes 196616 | tf_op jit(solution)/shard_map/ppermute | solution.py:29
  33.5 2.0 %collective-permute-start.9 = (bf16[256,128]{1,0:T(8,128)(2,1)S(1)}, bf16[256,128]{1,0:T(8,128)(2,1)S(1)}, u32[]{:S(2)}, u32[]{:S(2)}) collective-permute-start(bf16[256,128]{1,0:T(8,128)(2,1)S(1)} %get-tuple-element.36), channel_id=1, source_target_pairs={{0,4},{2,6},{4,0},{6,2},{1,5},{3,7},{5,1},{7,3},{8,12},{10,14},{12... | collective-permute-start | bytes 196616 | tf_op jit(solution)/shard_map/ppermute | solution.py:29
  35.7 5.7 %shard_map.30 = (f32[256,128]{1,0:T(8,128)S(1)}, bf16[256,128]{1,0:T(8,128)(2,1)S(1)}, bf16[256,128]{1,0:T(8,128)(2,1)S(1)}, bf16[256,128]{1,0:T(8,128)(2,1)S(1)}) custom-call(s32[4]{0:T(128)S(1)} %pad_add_fusion.where_ref, bf16[4,3,128,1280]{3,2,1,0:T(8,128)(2,1)S(1)} %get-tuple-element.32.turned, f32[3,128,1280]{2,1,0:T(8,128)S(1)} %get-tuple-element.33.phi), custom_call_target="tpu_custom_call" | custom-call | flops 1006632960 | bytes 4194304 | tf_op jit(solution)/shard_map/pallas_call | solution.py:221
  41.5 3.2 %collective-permute-start.21 = (bf16[256,128]{1,0:T(8,128)(2,1)S(1)}, bf16[256,128]{1,0:T(8,128)(2,1)S(1)}, u32[]{:S(2)}, u32[]{:S(2)}) collective-permute-start(bf16[256,128]{1,0:T(8,128)(2,1)S(1)} %add_convert_fusion.1), channel_id=1, source_target_pairs={{0,6},{2,4},{4,2},{6,0},{1,7},{3,5},{5,3},{7,1},{8,14},{10,12},{12... | collective-permute-start | bytes 196616 | tf_op jit(solution)/shard_map/ppermute | solution.py:29
  45.1 1.0 %collective-permute-start.11 = (bf16[256,128]{1,0:T(8,128)(2,1)S(1)}, bf16[256,128]{1,0:T(8,128)(2,1)S(1)}, u32[]{:S(2)}, u32[]{:S(2)}) collective-permute-start(bf16[256,128]{1,0:T(8,128)(2,1)S(1)} %get-tuple-element.48), channel_id=1, source_target_pairs={{0,2},{2,0},{4,6},{6,4},{1,3},{3,1},{5,7},{7,5},{8,10},{10,8},{12,... | collective-permute-start | bytes 196616 | tf_op jit(solution)/shard_map/ppermute | solution.py:29
  46.2 2.4 %collective-permute-start.12 = (bf16[256,128]{1,0:T(8,128)(2,1)S(1)}, bf16[256,128]{1,0:T(8,128)(2,1)S(1)}, u32[]{:S(2)}, u32[]{:S(2)}) collective-permute-start(bf16[256,128]{1,0:T(8,128)(2,1)S(1)} %get-tuple-element.49), channel_id=1, source_target_pairs={{0,4},{2,6},{4,0},{6,2},{1,5},{3,7},{5,1},{7,3},{8,12},{10,14},{12... | collective-permute-start | bytes 196616 | tf_op jit(solution)/shard_map/ppermute | solution.py:29
  48.7 1.7 %collective-permute-start.13 = (bf16[256,128]{1,0:T(8,128)(2,1)S(1)}, bf16[256,128]{1,0:T(8,128)(2,1)S(1)}, u32[]{:S(2)}, u32[]{:S(2)}) collective-permute-start(bf16[256,128]{1,0:T(8,128)(2,1)S(1)} %get-tuple-element.50), channel_id=1, source_target_pairs={{0,6},{2,4},{4,2},{6,0},{1,7},{3,5},{5,3},{7,1},{8,14},{10,12},{12... | collective-permute-start | bytes 196616 | tf_op jit(solution)/shard_map/ppermute | solution.py:29
  50.5 1.6 %collective-permute-start.23 = (bf16[1024,128]{1,0:T(8,128)(2,1)S(1)}, bf16[1024,128]{1,0:T(8,128)(2,1)S(1)}, u32[]{:S(2)}, u32[]{:S(2)}) collective-permute-start(bf16[1024,128]{1,0:T(8,128)(2,1)S(1)} %get-tuple-element.62.refs_0_), channel_id=1, source_target_pairs={{0,16},{16,0},{1,17},{17,1},{2,18},{18,2},{3,19},{19,3},{4,20},{20... | collective-permute-start | bytes 786440 | tf_op jit(solution)/shard_map/ppermute | solution.py:23
  52.6 1.7 %collective-permute-done.13 = bf16[256,128]{1,0:T(8,128)(2,1)S(1)} collective-permute-done((bf16[256,128]{1,0:T(8,128)(2,1)S(1)}, bf16[256,128]{1,0:T(8,128)(2,1)S(1)}, u32[]{:S(2)}, u32[]{:S(2)}) %collective-permute-start.13) | collective-permute-done | bytes 65568 | tf_op jit(solution)/shard_map/ppermute | solution.py:29
  54.4 1.8 %collective-permute-start.16 = (bf16[256,128]{1,0:T(8,128)(2,1)S(1)}, bf16[256,128]{1,0:T(8,128)(2,1)S(1)}, u32[]{:S(2)}, u32[]{:S(2)}) collective-permute-start(bf16[256,128]{1,0:T(8,128)(2,1)S(1)} %get-tuple-element.60), channel_id=1, source_target_pairs={{0,6},{2,4},{4,2},{6,0},{1,7},{3,5},{5,3},{7,1},{8,14},{10,12},{12... | collective-permute-start | bytes 196616 | tf_op jit(solution)/shard_map/ppermute | solution.py:29
  56.2 0.9 %collective-permute-start.15 = (bf16[256,128]{1,0:T(8,128)(2,1)S(1)}, bf16[256,128]{1,0:T(8,128)(2,1)S(1)}, u32[]{:S(2)}, u32[]{:S(2)}) collective-permute-start(bf16[256,128]{1,0:T(8,128)(2,1)S(1)} %get-tuple-element.60), channel_id=1, source_target_pairs={{0,4},{2,6},{4,0},{6,2},{1,5},{3,7},{5,1},{7,3},{8,12},{10,14},{12... | collective-permute-start | bytes 196616 | tf_op jit(solution)/shard_map/ppermute | solution.py:29
  57.1 0.9 %collective-permute-start.14 = (bf16[256,128]{1,0:T(8,128)(2,1)S(1)}, bf16[256,128]{1,0:T(8,128)(2,1)S(1)}, u32[]{:S(2)}, u32[]{:S(2)}) collective-permute-start(bf16[256,128]{1,0:T(8,128)(2,1)S(1)} %get-tuple-element.60), channel_id=1, source_target_pairs={{0,2},{2,0},{4,6},{6,4},{1,3},{3,1},{5,7},{7,5},{8,10},{10,8},{12,... | collective-permute-start | bytes 196616 | tf_op jit(solution)/shard_map/ppermute | solution.py:29
  58.0 1.4 %collective-permute-done.16 = bf16[256,128]{1,0:T(8,128)(2,1)S(1)} collective-permute-done((bf16[256,128]{1,0:T(8,128)(2,1)S(1)}, bf16[256,128]{1,0:T(8,128)(2,1)S(1)}, u32[]{:S(2)}, u32[]{:S(2)}) %collective-permute-start.16) | collective-permute-done | bytes 65568 | tf_op jit(solution)/shard_map/ppermute | solution.py:29
  59.4 1.0 %collective-permute-done.15 = bf16[256,128]{1,0:T(8,128)(2,1)S(1)} collective-permute-done((bf16[256,128]{1,0:T(8,128)(2,1)S(1)}, bf16[256,128]{1,0:T(8,128)(2,1)S(1)}, u32[]{:S(2)}, u32[]{:S(2)}) %collective-permute-start.15) | collective-permute-done | bytes 65568 | tf_op jit(solution)/shard_map/ppermute | solution.py:29
  62.4 1.1 %collective-permute-start.27 = (bf16[512,128]{1,0:T(8,128)(2,1)S(1)}, bf16[512,128]{1,0:T(8,128)(2,1)S(1)}, u32[]{:S(2)}, u32[]{:S(2)}) collective-permute-start(bf16[512,128]{1,0:T(8,128)(2,1)S(1)} %slice.29), channel_id=1, source_target_pairs={{0,1},{1,0},{2,3},{3,2},{4,5},{5,4},{6,7},{7,6},{8,9},{9,8},{10,11... | collective-permute-start | bytes 393224 | tf_op jit(solution)/shard_map/ppermute | solution.py:23
  63.5 0.9 %collective-permute-start.26 = (bf16[512,128]{1,0:T(8,128)(2,1)S(1)}, bf16[512,128]{1,0:T(8,128)(2,1)S(1)}, u32[]{:S(2)}, u32[]{:S(2)}) collective-permute-start(bf16[512,128]{1,0:T(8,128)(2,1)S(1)} %slice.28), channel_id=1, source_target_pairs={{0,16},{16,0},{1,17},{17,1},{2,18},{18,2},{3,19},{19,3},{4,20},{20... | collective-permute-start | bytes 393224 | tf_op jit(solution)/shard_map/ppermute | solution.py:23
  64.5 1.8 %shard_map.31.refs_6_ = f32[16384,128]{1,0:T(8,128)} custom-call(s32[4]{0:T(128)S(1)} %pad_add_fusion.where_ref, bf16[1024,128]{1,0:T(8,128)(2,1)S(1)} %get-tuple-element.62.refs_0_, bf16[1024,128]{1,0:T(8,128)(2,1)S(1)} %collective-permute-done.22.refs_1_, bf16[1024,128]{1,0:T(8,128)(2,1)S(1)} %collective-permute-done.23.refs_2_), custom_call_target="tpu_custom_call" | custom-call | bytes 2359296 | tf_op jit(solution)/shard_map/pallas_call | solution.py:272
  68.6 6.1 %collective-permute-start.28 = (bf16[4096,128]{1,0:T(8,128)(2,1)S(1)}, bf16[4096,128]{1,0:T(8,128)(2,1)S(1)}, u32[]{:S(2)}, u32[]{:S(2)}) collective-permute-start(bf16[4096,128]{1,0:T(8,128)(2,1)S(1)} %constant_dynamic-update-slice_fusion.4), channel_id=1, source_target_pairs={{0,8},{8,0},{1,9},{9,1},{2,10},{10,2},{3,11},{11,3},{4,12},{12,4},... | collective-permute-start | bytes 3145736 | tf_op jit(solution)/shard_map/ppermute | solution.py:23
  75.0 1.2 %collective-permute-start.24 = (bf16[512,128]{1,0:T(8,128)(2,1)S(1)}, bf16[512,128]{1,0:T(8,128)(2,1)S(1)}, u32[]{:S(2)}, u32[]{:S(2)}) collective-permute-start(bf16[512,128]{1,0:T(8,128)(2,1)S(1)} %slice.26), channel_id=1, source_target_pairs={{0,16},{16,0},{1,17},{17,1},{2,18},{18,2},{3,19},{19,3},{4,20},{20... | collective-permute-start | bytes 393224 | tf_op jit(solution)/shard_map/ppermute | solution.py:23
  77.0 2.8 %shard_map.32.refs_3_ = f32[16384,128]{1,0:T(8,128)} custom-call(s32[4]{0:T(128)S(1)} %pad_add_fusion.where_ref, bf16[512,128]{1,0:T(8,128)(2,1)S(1)} %collective-permute-done.26.refs_0_, bf16[512,128]{1,0:T(8,128)(2,1)S(1)} %collective-permute-done.27.refs_1_, ...), custom_call_target="tpu_custom_call", output_to_operand_aliasing={{}: (7, {})} | custom-call | bytes 6291456 | tf_op jit(solution)/shard_map/pallas_call | solution.py:272
  80.5 1.7 %collective-permute-start.29 = (bf16[1024,128]{1,0:T(8,128)(2,1)S(1)}, bf16[1024,128]{1,0:T(8,128)(2,1)S(1)}, u32[]{:S(2)}, u32[]{:S(2)}) collective-permute-start(bf16[1024,128]{1,0:T(8,128)(2,1)S(1)} %pad_maximum_fusion.1), channel_id=1, source_target_pairs={{0,8},{8,0},{1,9},{9,1},{2,10},{10,2},{3,11},{11,3},{4,12},{12,4},... | collective-permute-start | bytes 786440 | tf_op jit(solution)/shard_map/ppermute | solution.py:23
  82.1 2.0 %shard_map.33.refs_1_ = f32[16384,128]{1,0:T(8,128)} custom-call(s32[4]{0:T(128)S(1)} %pad_add_fusion.where_ref, bf16[3072,128]{1,0:T(8,128)(2,1)S(1)} %collective-permute-done.30.refs_0_, bf16[512,128]{1,0:T(8,128)(2,1)S(1)} %collective-permute-done.24.refs_1_, ...), custom_call_target="tpu_custom_call", output_to_operand_aliasing={{}: (4, {})} | custom-call | bytes 3145728 | tf_op jit(solution)/shard_map/pallas_call | solution.py:272
  84.2 1.4 %shard_map.34 = f32[16384,128]{1,0:T(8,128)} custom-call(s32[4]{0:T(128)S(1)} %pad_add_fusion.where_ref, bf16[1024,128]{1,0:T(8,128)(2,1)S(1)} %collective-permute-done.29.refs_0_, f32[16384,128]{1,0:T(8,128)} %shard_map.33.refs_1_), custom_call_target="tpu_custom_call", output_to_operand_aliasing={{}: (2, {})} | custom-call | bytes 786432 | tf_op jit(solution)/shard_map/pallas_call | solution.py:272
  (67 shorter events, 10.6 us)
Async XLA Ops:
  1.0 1.5 %collective-permute-start = (bf16[2,10,3,2,128]{4,3,2,1,0:T(2,128)(2,1)S(1)}, bf16[2,10,3,2,128]{4,3,2,1,0:T(2,128)(2,1)S(1)}, u32[]{:S(2)}, u32[]{:S(2)}) collective-permute-start(bf16[2,10,3,2,128]{4,3,2,1,0:T(2,128)(2,1)S(1)} %broadcast_select_fusion), channel_id=1, source_target_pairs={{1,2},{3,4},{5,6},{2,1},{4,3},{6,5},{9,10},{11,12},{13,14},{10,9},... | collective-permute-start | bytes 92168 | tf_op jit(solution)/shard_map/ppermute | solution.py:295
  3.5 9.9 %collective-permute-start.6 = (bf16[2,40,8,128]{3,2,1,0:T(8,128)(2,1)S(1)}, bf16[2,40,8,128]{3,2,1,0:T(8,128)(2,1)S(1)}, u32[]{:S(2)}, u32[]{:S(2)}) collective-permute-start(bf16[2,40,8,128]{3,2,1,0:T(8,128)(2,1)S(1)} %pad_maximum_fusion.2.refs_0_), channel_id=1, source_target_pairs={{0,17},{1,16},{16,1},{17,0},{2,19},{3,18},{18,3},{19,2},{4,21},{5,... | collective-permute-start | bytes 491528 | tf_op jit(solution)/shard_map/ppermute | solution.py:322
  10.6 7.2 %collective-permute-start.4 = (bf16[2,40,8,128]{3,2,1,0:T(8,128)(2,1)S(1)}, bf16[2,40,8,128]{3,2,1,0:T(8,128)(2,1)S(1)}, u32[]{:S(2)}, u32[]{:S(2)}) collective-permute-start(bf16[2,40,8,128]{3,2,1,0:T(8,128)(2,1)S(1)} %pad_maximum_fusion.2.refs_0_), channel_id=1, source_target_pairs={{0,16},{16,0},{1,17},{17,1},{2,18},{18,2},{3,19},{19,3},{4,20},{20... | collective-permute-start | bytes 491528 | tf_op jit(solution)/shard_map/ppermute | solution.py:23
  10.9 8.4 %collective-permute-start.2 = (bf16[2,40,8,128]{3,2,1,0:T(8,128)(2,1)S(1)}, bf16[2,40,8,128]{3,2,1,0:T(8,128)(2,1)S(1)}, u32[]{:S(2)}, u32[]{:S(2)}) collective-permute-start(bf16[2,40,8,128]{3,2,1,0:T(8,128)(2,1)S(1)} %pad_maximum_fusion.2.refs_0_), channel_id=1, source_target_pairs={{0,1},{1,0},{2,3},{3,2},{4,5},{5,4},{6,7},{7,6},{8,9},{9,8},{10,11... | collective-permute-start | bytes 491528 | tf_op jit(solution)/shard_map/ppermute | solution.py:23
  11.0 8.4 %collective-permute-start.1 = (bf16[2,40,8,128]{3,2,1,0:T(8,128)(2,1)S(1)}, bf16[2,40,8,128]{3,2,1,0:T(8,128)(2,1)S(1)}, u32[]{:S(2)}, u32[]{:S(2)}) collective-permute-start(bf16[2,40,8,128]{3,2,1,0:T(8,128)(2,1)S(1)} %pad_maximum_fusion.2.refs_0_), channel_id=1, source_target_pairs={{0,8},{8,0},{1,9},{9,1},{2,10},{10,2},{3,11},{11,3},{4,12},{12,4},... | collective-permute-start | bytes 491528 | tf_op jit(solution)/shard_map/ppermute | solution.py:23
  13.4 6.0 %collective-permute-start.7 = (bf16[2,40,8,128]{3,2,1,0:T(8,128)(2,1)S(1)}, bf16[2,40,8,128]{3,2,1,0:T(8,128)(2,1)S(1)}, u32[]{:S(2)}, u32[]{:S(2)}) collective-permute-start(bf16[2,40,8,128]{3,2,1,0:T(8,128)(2,1)S(1)} %collective-permute-done.6.refs_6_), channel_id=1, source_target_pairs={{0,8},{8,0},{1,9},{9,1},{2,10},{10,2},{3,11},{11,3},{4,12},{12,4},... | collective-permute-start | bytes 491528 | tf_op jit(solution)/shard_map/ppermute | solution.py:23
  17.9 2.5 %collective-permute-start.5 = (bf16[2,40,8,128]{3,2,1,0:T(8,128)(2,1)S(1)}, bf16[2,40,8,128]{3,2,1,0:T(8,128)(2,1)S(1)}, u32[]{:S(2)}, u32[]{:S(2)}) collective-permute-start(bf16[2,40,8,128]{3,2,1,0:T(8,128)(2,1)S(1)} %collective-permute-done.4.refs_4_), channel_id=1, source_target_pairs={{0,8},{8,0},{1,9},{9,1},{2,10},{10,2},{3,11},{11,3},{4,12},{12,4},... | collective-permute-start | bytes 491528 | tf_op jit(solution)/shard_map/ppermute | solution.py:23
  19.3 1.4 %collective-permute-start.3 = (bf16[2,40,8,128]{3,2,1,0:T(8,128)(2,1)S(1)}, bf16[2,40,8,128]{3,2,1,0:T(8,128)(2,1)S(1)}, u32[]{:S(2)}, u32[]{:S(2)}) collective-permute-start(bf16[2,40,8,128]{3,2,1,0:T(8,128)(2,1)S(1)} %collective-permute-done.2.refs_2_), channel_id=1, source_target_pairs={{0,8},{8,0},{1,9},{9,1},{2,10},{10,2},{3,11},{11,3},{4,12},{12,4},... | collective-permute-start | bytes 491528 | tf_op jit(solution)/shard_map/ppermute | solution.py:23
  32.0 9.5 %collective-permute-start.8 = (bf16[256,128]{1,0:T(8,128)(2,1)S(1)}, bf16[256,128]{1,0:T(8,128)(2,1)S(1)}, u32[]{:S(2)}, u32[]{:S(2)}) collective-permute-start(bf16[256,128]{1,0:T(8,128)(2,1)S(1)} %get-tuple-element.35), channel_id=1, source_target_pairs={{0,2},{2,0},{4,6},{6,4},{1,3},{3,1},{5,7},{7,5},{8,10},{10,8},{12,... | collective-permute-start | bytes 196616 | tf_op jit(solution)/shard_map/ppermute | solution.py:29
  33.5 8.0 %collective-permute-start.9 = (bf16[256,128]{1,0:T(8,128)(2,1)S(1)}, bf16[256,128]{1,0:T(8,128)(2,1)S(1)}, u32[]{:S(2)}, u32[]{:S(2)}) collective-permute-start(bf16[256,128]{1,0:T(8,128)(2,1)S(1)} %get-tuple-element.36), channel_id=1, source_target_pairs={{0,4},{2,6},{4,0},{6,2},{1,5},{3,7},{5,1},{7,3},{8,12},{10,14},{12... | collective-permute-start | bytes 196616 | tf_op jit(solution)/shard_map/ppermute | solution.py:29
  35.6 5.9 %collective-permute-start.10 = (bf16[256,128]{1,0:T(8,128)(2,1)S(1)}, bf16[256,128]{1,0:T(8,128)(2,1)S(1)}, u32[]{:S(2)}, u32[]{:S(2)}) collective-permute-start(bf16[256,128]{1,0:T(8,128)(2,1)S(1)} %get-tuple-element.37), channel_id=1, source_target_pairs={{0,6},{2,4},{4,2},{6,0},{1,7},{3,5},{5,3},{7,1},{8,14},{10,12},{12... | collective-permute-start | bytes 196616 | tf_op jit(solution)/shard_map/ppermute | solution.py:29
  41.5 9.0 %collective-permute-start.21 = (bf16[256,128]{1,0:T(8,128)(2,1)S(1)}, bf16[256,128]{1,0:T(8,128)(2,1)S(1)}, u32[]{:S(2)}, u32[]{:S(2)}) collective-permute-start(bf16[256,128]{1,0:T(8,128)(2,1)S(1)} %add_convert_fusion.1), channel_id=1, source_target_pairs={{0,6},{2,4},{4,2},{6,0},{1,7},{3,5},{5,3},{7,1},{8,14},{10,12},{12... | collective-permute-start | bytes 196616 | tf_op jit(solution)/shard_map/ppermute | solution.py:29
  44.7 5.7 %collective-permute-start.20 = (bf16[256,128]{1,0:T(8,128)(2,1)S(1)}, bf16[256,128]{1,0:T(8,128)(2,1)S(1)}, u32[]{:S(2)}, u32[]{:S(2)}) collective-permute-start(bf16[256,128]{1,0:T(8,128)(2,1)S(1)} %add_convert_fusion.1), channel_id=1, source_target_pairs={{0,4},{2,6},{4,0},{6,2},{1,5},{3,7},{5,1},{7,3},{8,12},{10,14},{12... | collective-permute-start | bytes 196616 | tf_op jit(solution)/shard_map/ppermute | solution.py:29
  44.7 4.0 %collective-permute-start.19 = (bf16[256,128]{1,0:T(8,128)(2,1)S(1)}, bf16[256,128]{1,0:T(8,128)(2,1)S(1)}, u32[]{:S(2)}, u32[]{:S(2)}) collective-permute-start(bf16[256,128]{1,0:T(8,128)(2,1)S(1)} %add_convert_fusion.1), channel_id=1, source_target_pairs={{0,2},{2,0},{4,6},{6,4},{1,3},{3,1},{5,7},{7,5},{8,10},{10,8},{12,... | collective-permute-start | bytes 196616 | tf_op jit(solution)/shard_map/ppermute | solution.py:29
  45.1 7.5 %collective-permute-start.11 = (bf16[256,128]{1,0:T(8,128)(2,1)S(1)}, bf16[256,128]{1,0:T(8,128)(2,1)S(1)}, u32[]{:S(2)}, u32[]{:S(2)}) collective-permute-start(bf16[256,128]{1,0:T(8,128)(2,1)S(1)} %get-tuple-element.48), channel_id=1, source_target_pairs={{0,2},{2,0},{4,6},{6,4},{1,3},{3,1},{5,7},{7,5},{8,10},{10,8},{12,... | collective-permute-start | bytes 196616 | tf_op jit(solution)/shard_map/ppermute | solution.py:29
  46.2 6.5 %collective-permute-start.12 = (bf16[256,128]{1,0:T(8,128)(2,1)S(1)}, bf16[256,128]{1,0:T(8,128)(2,1)S(1)}, u32[]{:S(2)}, u32[]{:S(2)}) collective-permute-start(bf16[256,128]{1,0:T(8,128)(2,1)S(1)} %get-tuple-element.49), channel_id=1, source_target_pairs={{0,4},{2,6},{4,0},{6,2},{1,5},{3,7},{5,1},{7,3},{8,12},{10,14},{12... | collective-permute-start | bytes 196616 | tf_op jit(solution)/shard_map/ppermute | solution.py:29
  48.7 5.6 %collective-permute-start.13 = (bf16[256,128]{1,0:T(8,128)(2,1)S(1)}, bf16[256,128]{1,0:T(8,128)(2,1)S(1)}, u32[]{:S(2)}, u32[]{:S(2)}) collective-permute-start(bf16[256,128]{1,0:T(8,128)(2,1)S(1)} %get-tuple-element.50), channel_id=1, source_target_pairs={{0,6},{2,4},{4,2},{6,0},{1,7},{3,5},{5,3},{7,1},{8,14},{10,12},{12... | collective-permute-start | bytes 196616 | tf_op jit(solution)/shard_map/ppermute | solution.py:29
  50.5 11.9 %collective-permute-start.23 = (bf16[1024,128]{1,0:T(8,128)(2,1)S(1)}, bf16[1024,128]{1,0:T(8,128)(2,1)S(1)}, u32[]{:S(2)}, u32[]{:S(2)}) collective-permute-start(bf16[1024,128]{1,0:T(8,128)(2,1)S(1)} %get-tuple-element.62.refs_0_), channel_id=1, source_target_pairs={{0,16},{16,0},{1,17},{17,1},{2,18},{18,2},{3,19},{19,3},{4,20},{20... | collective-permute-start | bytes 786440 | tf_op jit(solution)/shard_map/ppermute | solution.py:23
  52.1 11.4 %collective-permute-start.22 = (bf16[1024,128]{1,0:T(8,128)(2,1)S(1)}, bf16[1024,128]{1,0:T(8,128)(2,1)S(1)}, u32[]{:S(2)}, u32[]{:S(2)}) collective-permute-start(bf16[1024,128]{1,0:T(8,128)(2,1)S(1)} %get-tuple-element.62.refs_0_), channel_id=1, source_target_pairs={{0,1},{1,0},{2,3},{3,2},{4,5},{5,4},{6,7},{7,6},{8,9},{9,8},{10,11... | collective-permute-start | bytes 786440 | tf_op jit(solution)/shard_map/ppermute | solution.py:23
  54.4 5.0 %collective-permute-start.16 = (bf16[256,128]{1,0:T(8,128)(2,1)S(1)}, bf16[256,128]{1,0:T(8,128)(2,1)S(1)}, u32[]{:S(2)}, u32[]{:S(2)}) collective-permute-start(bf16[256,128]{1,0:T(8,128)(2,1)S(1)} %get-tuple-element.60), channel_id=1, source_target_pairs={{0,6},{2,4},{4,2},{6,0},{1,7},{3,5},{5,3},{7,1},{8,14},{10,12},{12... | collective-permute-start | bytes 196616 | tf_op jit(solution)/shard_map/ppermute | solution.py:29
  56.2 4.1 %collective-permute-start.15 = (bf16[256,128]{1,0:T(8,128)(2,1)S(1)}, bf16[256,128]{1,0:T(8,128)(2,1)S(1)}, u32[]{:S(2)}, u32[]{:S(2)}) collective-permute-start(bf16[256,128]{1,0:T(8,128)(2,1)S(1)} %get-tuple-element.60), channel_id=1, source_target_pairs={{0,4},{2,6},{4,0},{6,2},{1,5},{3,7},{5,1},{7,3},{8,12},{10,14},{12... | collective-permute-start | bytes 196616 | tf_op jit(solution)/shard_map/ppermute | solution.py:29
  57.1 4.1 %collective-permute-start.14 = (bf16[256,128]{1,0:T(8,128)(2,1)S(1)}, bf16[256,128]{1,0:T(8,128)(2,1)S(1)}, u32[]{:S(2)}, u32[]{:S(2)}) collective-permute-start(bf16[256,128]{1,0:T(8,128)(2,1)S(1)} %get-tuple-element.60), channel_id=1, source_target_pairs={{0,2},{2,0},{4,6},{6,4},{1,3},{3,1},{5,7},{7,5},{8,10},{10,8},{12,... | collective-permute-start | bytes 196616 | tf_op jit(solution)/shard_map/ppermute | solution.py:29
  61.2 5.3 %collective-permute-start.18 = (bf16[1024,128]{1,0:T(8,128)(2,1)S(1)}, bf16[1024,128]{1,0:T(8,128)(2,1)S(1)}, u32[]{:S(2)}, u32[]{:S(2)}) collective-permute-start(bf16[1024,128]{1,0:T(8,128)(2,1)S(1)} %pad_maximum_fusion.refs_3_), channel_id=1, source_target_pairs={{0,16},{16,0},{1,17},{17,1},{2,18},{18,2},{3,19},{19,3},{4,20},{20... | collective-permute-start | bytes 786440 | tf_op jit(solution)/shard_map/ppermute | solution.py:23
  61.9 5.2 %collective-permute-start.17 = (bf16[1024,128]{1,0:T(8,128)(2,1)S(1)}, bf16[1024,128]{1,0:T(8,128)(2,1)S(1)}, u32[]{:S(2)}, u32[]{:S(2)}) collective-permute-start(bf16[1024,128]{1,0:T(8,128)(2,1)S(1)} %pad_maximum_fusion.refs_3_), channel_id=1, source_target_pairs={{0,1},{1,0},{2,3},{3,2},{4,5},{5,4},{6,7},{7,6},{8,9},{9,8},{10,11... | collective-permute-start | bytes 786440 | tf_op jit(solution)/shard_map/ppermute | solution.py:23
  62.4 6.2 %collective-permute-start.27 = (bf16[512,128]{1,0:T(8,128)(2,1)S(1)}, bf16[512,128]{1,0:T(8,128)(2,1)S(1)}, u32[]{:S(2)}, u32[]{:S(2)}) collective-permute-start(bf16[512,128]{1,0:T(8,128)(2,1)S(1)} %slice.29), channel_id=1, source_target_pairs={{0,1},{1,0},{2,3},{3,2},{4,5},{5,4},{6,7},{7,6},{8,9},{9,8},{10,11... | collective-permute-start | bytes 393224 | tf_op jit(solution)/shard_map/ppermute | solution.py:23
  63.5 4.4 %collective-permute-start.26 = (bf16[512,128]{1,0:T(8,128)(2,1)S(1)}, bf16[512,128]{1,0:T(8,128)(2,1)S(1)}, u32[]{:S(2)}, u32[]{:S(2)}) collective-permute-start(bf16[512,128]{1,0:T(8,128)(2,1)S(1)} %slice.28), channel_id=1, source_target_pairs={{0,16},{16,0},{1,17},{17,1},{2,18},{18,2},{3,19},{19,3},{4,20},{20... | collective-permute-start | bytes 393224 | tf_op jit(solution)/shard_map/ppermute | solution.py:23
  68.6 8.4 %collective-permute-start.28 = (bf16[4096,128]{1,0:T(8,128)(2,1)S(1)}, bf16[4096,128]{1,0:T(8,128)(2,1)S(1)}, u32[]{:S(2)}, u32[]{:S(2)}) collective-permute-start(bf16[4096,128]{1,0:T(8,128)(2,1)S(1)} %constant_dynamic-update-slice_fusion.4), channel_id=1, source_target_pairs={{0,8},{8,0},{1,9},{9,1},{2,10},{10,2},{3,11},{11,3},{4,12},{12,4},... | collective-permute-start | bytes 3145736 | tf_op jit(solution)/shard_map/ppermute | solution.py:23
  74.9 7.3 %collective-permute-start.30 = (bf16[3072,128]{1,0:T(8,128)(2,1)S(1)}, bf16[3072,128]{1,0:T(8,128)(2,1)S(1)}, u32[]{:S(2)}, u32[]{:S(2)}) collective-permute-start(bf16[3072,128]{1,0:T(8,128)(2,1)S(1)} %constant_dynamic-update-slice_fusion.12), channel_id=1, source_target_pairs={{0,8},{8,0},{1,9},{9,1},{2,10},{10,2},{3,11},{11,3},{4,12},{12,4},... | collective-permute-start | bytes 2359304 | tf_op jit(solution)/shard_map/ppermute | solution.py:23
  75.0 4.9 %collective-permute-start.24 = (bf16[512,128]{1,0:T(8,128)(2,1)S(1)}, bf16[512,128]{1,0:T(8,128)(2,1)S(1)}, u32[]{:S(2)}, u32[]{:S(2)}) collective-permute-start(bf16[512,128]{1,0:T(8,128)(2,1)S(1)} %slice.26), channel_id=1, source_target_pairs={{0,16},{16,0},{1,17},{17,1},{2,18},{18,2},{3,19},{19,3},{4,20},{20... | collective-permute-start | bytes 393224 | tf_op jit(solution)/shard_map/ppermute | solution.py:23
  76.1 4.3 %collective-permute-start.25 = (bf16[512,128]{1,0:T(8,128)(2,1)S(1)}, bf16[512,128]{1,0:T(8,128)(2,1)S(1)}, u32[]{:S(2)}, u32[]{:S(2)}) collective-permute-start(bf16[512,128]{1,0:T(8,128)(2,1)S(1)} %slice.27), channel_id=1, source_target_pairs={{0,1},{1,0},{2,3},{3,2},{4,5},{5,4},{6,7},{7,6},{8,9},{9,8},{10,11... | collective-permute-start | bytes 393224 | tf_op jit(solution)/shard_map/ppermute | solution.py:23
  80.5 3.7 %collective-permute-start.29 = (bf16[1024,128]{1,0:T(8,128)(2,1)S(1)}, bf16[1024,128]{1,0:T(8,128)(2,1)S(1)}, u32[]{:S(2)}, u32[]{:S(2)}) collective-permute-start(bf16[1024,128]{1,0:T(8,128)(2,1)S(1)} %pad_maximum_fusion.1), channel_id=1, source_target_pairs={{0,8},{8,0},{1,9},{9,1},{2,10},{10,2},{3,11},{11,3},{4,12},{12,4},... | collective-permute-start | bytes 786440 | tf_op jit(solution)/shard_map/ppermute | solution.py:23

commit v16 on v15

--- a/solution.py
+++ b/solution.py
@@ -371,9 +371,7 @@
         if n < CHUNKS - 1:
             mine, later = lax.optimization_barrier((mine, terms[n + 1]))
             terms[n + 1] = list(later)
-        pieces.append(
-            jnp.concatenate([mine] + [swap(mine, r) for r in range(1, decks)], axis=0)
-        )
+        pieces.append([mine] + [swap(mine, r) for r in range(1, decks)])
 
     def join(chosen):
         return chosen[0][0], sum((ps for _, ps, _ in chosen), []), jnp.concatenate(
@@ -385,12 +383,15 @@
 
     result = None
     waiting = []
-    for n, piece in enumerate(pieces):
+    for n, runs in enumerate(pieces):
+        piece = jnp.concatenate(runs, axis=0)
         across = rotate(piece, "side")
         along = [rotate(piece, "row", r) for r in range(1, rows)]
         near = [(n, [((0, 0, 0), every)], piece), (n, [((0, 0, 1), every)], across)]
         near += [(n, [((r, 0, 0), every)], v) for r, v in enumerate(along, 1)]
         halves = [across[: half * line]] + [v[half * line :] for v in along]
+        if n < CHUNKS - 1:
+            halves, pieces[n + 1][0] = lax.optimization_barrier((halves, pieces[n + 1][0]))
         if n > 0:
             result = put_all(result, waiting)
             halves, result = lax.optimization_barrier((halves, result))

time: 85.8 us -> 85.8 us (level)
  transfers between devices with their start and end apart: 31 -> 31, of which waited for: 14 -> 10; matrix products, arithmetic and copies ran while one was open for 1% -> 1% of each run, Pallas kernels for 14% -> 14%
where the time goes in v16:
time: 85.8 us; the launch traced here: 85.6 us
  starting transfers between devices  46.6 us (54%)
  Pallas kernels  25 us (29%)
  waiting for transfers between devices  10.4 us (12%)
  other arithmetic  2.91 us (3%)
    ppermute x17, starting transfers between devices, rotate(): lax.ppermute(value, axis, [(i, (i + by) % count) for i in range(count)])  22.7 us
    ppermute x12, starting transfers between devices, swap(): return lax.ppermute(value, 'deck', [(i, i ^ by) for i in range(count)])  16.1 us
    pallas_call x2, Pallas kernels, plane_terms(): pl.pallas_call(functools.partial(terms_kernel, share, chunk, rows, decks)...  11.5 us
    pallas_call x4, Pallas kernels, put(): pl.pallas_call(functools.partial(place_kernel, (rows, decks, line, runs),...  8 us
    ppermute x1, starting transfers between devices, spread_near(): got[r, 1] = lax.ppermute(piece, DIAGONAL, pairs)  7.13 us
    pallas_call x1, Pallas kernels, plane_slopes(): pl.pallas_call(functools.partial(slopes_kernel, sizes, offsets), out_shap...  5.49 us
    ppermute x17, waiting for transfers between devices, rotate(): lax.ppermute(value, axis, [(i, (i + by) % count) for i in range(count)])  5.33 us
    ppermute x12, waiting for transfers between devices, swap(): return lax.ppermute(value, 'deck', [(i, i ^ by) for i in range(count)])  5.05 us
  transfers between devices with their start and end apart: 31, of which 10 were waited for; matrix products, arithmetic and copies ran while one was open for 1% of the time, Pallas kernels for 14%

profile of v16, /device:TPU:1, one launch (start us, length us, event | category | flops | bytes accessed | tf_op | source)
XLA Modules:
  0.0 85.6 jit_solution(1652804134638996141)
XLA Ops:
  0.0 1.0 %broadcast_select_fusion = bf16[2,10,3,2,128]{4,3,2,1,0:T(2,128)(2,1)S(1)} fusion(pred[]{:T(512)S(6)} %eq.3, bf16[2,10,3,8,128]{4,3,2,1,0:T(8,128)(2,1)} %bitcast.17), kind=kLoop, calls=%fused_computation.4 | loop fusion | flops 15360 | bytes 92161 | tf_op jit(solution)/shard_map/jit(_where)/select_n | solution.py:293
  2.6 0.9 %pad_maximum_fusion.1.refs_0_ = bf16[2,40,8,128]{3,2,1,0:T(8,128)(2,1)S(1)} fusion(bf16[2,9,8,128]{3,2,1,0:T(8,128)(2,1)S(1)} %bitcast.19, bf16[2,1,8,128]{3,2,1,0:T(8,128)(2,1)S(1)} %fusion.7, bf16[2,30,8,128]{3,2,1,0:T(8,128)(2,1)} %bitcast.18), kind=kLoop, calls=%fused_computation.1 | loop fusion | flops 163840 | bytes 327680 | tf_op jit(solution)/shard_map/concatenate | solution.py:313
  3.5 7.1 %collective-permute-start.6 = (bf16[2,40,8,128]{3,2,1,0:T(8,128)(2,1)S(1)}, bf16[2,40,8,128]{3,2,1,0:T(8,128)(2,1)S(1)}, u32[]{:S(2)}, u32[]{:S(2)}) collective-permute-start(bf16[2,40,8,128]{3,2,1,0:T(8,128)(2,1)S(1)} %pad_maximum_fusion.1.refs_0_), channel_id=1, source_target_pairs={{0,17},{1,16},{16,1},{17,0},{2,19},{3,18},{18,3},{19,2},{4,21},{5,... | collective-permute-start | bytes 491528 | tf_op jit(solution)/shard_map/ppermute | solution.py:322
  11.0 2.4 %collective-permute-start.1 = (bf16[2,40,8,128]{3,2,1,0:T(8,128)(2,1)S(1)}, bf16[2,40,8,128]{3,2,1,0:T(8,128)(2,1)S(1)}, u32[]{:S(2)}, u32[]{:S(2)}) collective-permute-start(bf16[2,40,8,128]{3,2,1,0:T(8,128)(2,1)S(1)} %pad_maximum_fusion.1.refs_0_), channel_id=1, source_target_pairs={{0,8},{8,0},{1,9},{9,1},{2,10},{10,2},{3,11},{11,3},{4,12},{12,4},... | collective-permute-start | bytes 491528 | tf_op jit(solution)/shard_map/ppermute | solution.py:23
  13.4 3.8 %collective-permute-start.7 = (bf16[2,40,8,128]{3,2,1,0:T(8,128)(2,1)S(1)}, bf16[2,40,8,128]{3,2,1,0:T(8,128)(2,1)S(1)}, u32[]{:S(2)}, u32[]{:S(2)}) collective-permute-start(bf16[2,40,8,128]{3,2,1,0:T(8,128)(2,1)S(1)} %collective-permute-done.6.refs_6_), channel_id=1, source_target_pairs={{0,8},{8,0},{1,9},{9,1},{2,10},{10,2},{3,11},{11,3},{4,12},{12,4},... | collective-permute-start | bytes 491528 | tf_op jit(solution)/shard_map/ppermute | solution.py:23
  17.9 1.4 %collective-permute-start.5 = (bf16[2,40,8,128]{3,2,1,0:T(8,128)(2,1)S(1)}, bf16[2,40,8,128]{3,2,1,0:T(8,128)(2,1)S(1)}, u32[]{:S(2)}, u32[]{:S(2)}) collective-permute-start(bf16[2,40,8,128]{3,2,1,0:T(8,128)(2,1)S(1)} %collective-permute-done.4.refs_4_), channel_id=1, source_target_pairs={{0,8},{8,0},{1,9},{9,1},{2,10},{10,2},{3,11},{11,3},{4,12},{12,4},... | collective-permute-start | bytes 491528 | tf_op jit(solution)/shard_map/ppermute | solution.py:23
  19.4 0.9 %collective-permute-done.5.refs_5_ = bf16[2,40,8,128]{3,2,1,0:T(8,128)(2,1)S(1)} collective-permute-done((bf16[2,40,8,128]{3,2,1,0:T(8,128)(2,1)S(1)}, bf16[2,40,8,128]{3,2,1,0:T(8,128)(2,1)S(1)}, u32[]{:S(2)}, u32[]{:S(2)}) %collective-permute-start.5) | collective-permute-done | bytes 163872 | tf_op jit(solution)/shard_map/ppermute | solution.py:23
  20.7 5.5 %shard_map.28 = (bf16[4,3,128,1280]{3,2,1,0:T(8,128)(2,1)S(1)}, f32[3,128,1280]{2,1,0:T(8,128)S(1)}) custom-call(s32[4]{0:T(128)S(1)} %pad_add_fusion.where_ref, bf16[2,40,8,128]{3,2,1,0:T(8,128)(2,1)S(1)} %pad_maximum_fusion.1.refs_0_, bf16[2,40,8,128]{3,2,1,0:T(8,128)(2,1)S(1)} %collective-permute-done.1.refs_1_, ...), custom_call_target="tpu_custom_call" | custom-call | flops 503316480 | bytes 4194304 | tf_op jit(solution)/shard_map/pallas_call | solution.py:157
  26.2 5.7 %shard_map.29 = (f32[256,128]{1,0:T(8,128)S(1)}, bf16[256,128]{1,0:T(8,128)(2,1)S(1)}, bf16[256,128]{1,0:T(8,128)(2,1)S(1)}, bf16[256,128]{1,0:T(8,128)(2,1)S(1)}) custom-call(s32[4]{0:T(128)S(1)} %pad_add_fusion.where_ref, bf16[4,3,128,1280]{3,2,1,0:T(8,128)(2,1)S(1)} %get-tuple-element.35.turned, f32[3,128,1280]{2,1,0:T(8,128)S(1)} %get-tuple-element.36.phi), custom_call_target="tpu_custom_call" | custom-call | flops 1006632960 | bytes 4194304 | tf_op jit(solution)/shard_map/pallas_call | solution.py:221
  32.0 1.6 %collective-permute-start.8 = (bf16[256,128]{1,0:T(8,128)(2,1)S(1)}, bf16[256,128]{1,0:T(8,128)(2,1)S(1)}, u32[]{:S(2)}, u32[]{:S(2)}) collective-permute-start(bf16[256,128]{1,0:T(8,128)(2,1)S(1)} %get-tuple-element.38), channel_id=1, source_target_pairs={{0,2},{2,0},{4,6},{6,4},{1,3},{3,1},{5,7},{7,5},{8,10},{10,8},{12,... | collective-permute-start | bytes 196616 | tf_op jit(solution)/shard_map/ppermute | solution.py:29
  33.5 2.0 %collective-permute-start.9 = (bf16[256,128]{1,0:T(8,128)(2,1)S(1)}, bf16[256,128]{1,0:T(8,128)(2,1)S(1)}, u32[]{:S(2)}, u32[]{:S(2)}) collective-permute-start(bf16[256,128]{1,0:T(8,128)(2,1)S(1)} %get-tuple-element.39), channel_id=1, source_target_pairs={{0,4},{2,6},{4,0},{6,2},{1,5},{3,7},{5,1},{7,3},{8,12},{10,14},{12... | collective-permute-start | bytes 196616 | tf_op jit(solution)/shard_map/ppermute | solution.py:29
  35.7 5.7 %shard_map.30 = (f32[256,128]{1,0:T(8,128)S(1)}, bf16[256,128]{1,0:T(8,128)(2,1)S(1)}, bf16[256,128]{1,0:T(8,128)(2,1)S(1)}, bf16[256,128]{1,0:T(8,128)(2,1)S(1)}) custom-call(s32[4]{0:T(128)S(1)} %pad_add_fusion.where_ref, bf16[4,3,128,1280]{3,2,1,0:T(8,128)(2,1)S(1)} %get-tuple-element.35.turned, f32[3,128,1280]{2,1,0:T(8,128)S(1)} %get-tuple-element.36.phi), custom_call_target="tpu_custom_call" | custom-call | flops 1006632960 | bytes 4194304 | tf_op jit(solution)/shard_map/pallas_call | solution.py:221
  41.5 3.2 %collective-permute-start.13 = (bf16[256,128]{1,0:T(8,128)(2,1)S(1)}, bf16[256,128]{1,0:T(8,128)(2,1)S(1)}, u32[]{:S(2)}, u32[]{:S(2)}) collective-permute-start(bf16[256,128]{1,0:T(8,128)(2,1)S(1)} %add_convert_fusion.1), channel_id=1, source_target_pairs={{0,6},{2,4},{4,2},{6,0},{1,7},{3,5},{5,3},{7,1},{8,14},{10,12},{12... | collective-permute-start | bytes 196616 | tf_op jit(solution)/shard_map/ppermute | solution.py:29
  45.1 1.0 %collective-permute-start.16 = (bf16[256,128]{1,0:T(8,128)(2,1)S(1)}, bf16[256,128]{1,0:T(8,128)(2,1)S(1)}, u32[]{:S(2)}, u32[]{:S(2)}) collective-permute-start(bf16[256,128]{1,0:T(8,128)(2,1)S(1)} %get-tuple-element.52), channel_id=1, source_target_pairs={{0,2},{2,0},{4,6},{6,4},{1,3},{3,1},{5,7},{7,5},{8,10},{10,8},{12,... | collective-permute-start | bytes 196616 | tf_op jit(solution)/shard_map/ppermute | solution.py:29
  46.2 2.4 %collective-permute-start.17 = (bf16[256,128]{1,0:T(8,128)(2,1)S(1)}, bf16[256,128]{1,0:T(8,128)(2,1)S(1)}, u32[]{:S(2)}, u32[]{:S(2)}) collective-permute-start(bf16[256,128]{1,0:T(8,128)(2,1)S(1)} %get-tuple-element.53), channel_id=1, source_target_pairs={{0,4},{2,6},{4,0},{6,2},{1,5},{3,7},{5,1},{7,3},{8,12},{10,14},{12... | collective-permute-start | bytes 196616 | tf_op jit(solution)/shard_map/ppermute | solution.py:29
  48.7 1.7 %collective-permute-start.18 = (bf16[256,128]{1,0:T(8,128)(2,1)S(1)}, bf16[256,128]{1,0:T(8,128)(2,1)S(1)}, u32[]{:S(2)}, u32[]{:S(2)}) collective-permute-start(bf16[256,128]{1,0:T(8,128)(2,1)S(1)} %get-tuple-element.54), channel_id=1, source_target_pairs={{0,6},{2,4},{4,2},{6,0},{1,7},{3,5},{5,3},{7,1},{8,14},{10,12},{12... | collective-permute-start | bytes 196616 | tf_op jit(solution)/shard_map/ppermute | solution.py:29
  50.5 1.6 %collective-permute-start.15 = (bf16[1024,128]{1,0:T(8,128)(2,1)S(1)}, bf16[1024,128]{1,0:T(8,128)(2,1)S(1)}, u32[]{:S(2)}, u32[]{:S(2)}) collective-permute-start(bf16[1024,128]{1,0:T(8,128)(2,1)S(1)} %get-tuple-element.74.refs_0_), channel_id=1, source_target_pairs={{0,16},{16,0},{1,17},{17,1},{2,18},{18,2},{3,19},{19,3},{4,20},{20... | collective-permute-start | bytes 786440 | tf_op jit(solution)/shard_map/ppermute | solution.py:23
  52.6 1.7 %collective-permute-done.18 = bf16[256,128]{1,0:T(8,128)(2,1)S(1)} collective-permute-done((bf16[256,128]{1,0:T(8,128)(2,1)S(1)}, bf16[256,128]{1,0:T(8,128)(2,1)S(1)}, u32[]{:S(2)}, u32[]{:S(2)}) %collective-permute-start.18) | collective-permute-done | bytes 65568 | tf_op jit(solution)/shard_map/ppermute | solution.py:29
  54.4 1.8 %collective-permute-start.21 = (bf16[256,128]{1,0:T(8,128)(2,1)S(1)}, bf16[256,128]{1,0:T(8,128)(2,1)S(1)}, u32[]{:S(2)}, u32[]{:S(2)}) collective-permute-start(bf16[256,128]{1,0:T(8,128)(2,1)S(1)} %add_convert_fusion), channel_id=1, source_target_pairs={{0,6},{2,4},{4,2},{6,0},{1,7},{3,5},{5,3},{7,1},{8,14},{10,12},{12... | collective-permute-start | bytes 196616 | tf_op jit(solution)/shard_map/ppermute | solution.py:29
  56.2 0.9 %collective-permute-start.20 = (bf16[256,128]{1,0:T(8,128)(2,1)S(1)}, bf16[256,128]{1,0:T(8,128)(2,1)S(1)}, u32[]{:S(2)}, u32[]{:S(2)}) collective-permute-start(bf16[256,128]{1,0:T(8,128)(2,1)S(1)} %add_convert_fusion), channel_id=1, source_target_pairs={{0,4},{2,6},{4,0},{6,2},{1,5},{3,7},{5,1},{7,3},{8,12},{10,14},{12... | collective-permute-start | bytes 196616 | tf_op jit(solution)/shard_map/ppermute | solution.py:29
  57.1 0.9 %collective-permute-start.19 = (bf16[256,128]{1,0:T(8,128)(2,1)S(1)}, bf16[256,128]{1,0:T(8,128)(2,1)S(1)}, u32[]{:S(2)}, u32[]{:S(2)}) collective-permute-start(bf16[256,128]{1,0:T(8,128)(2,1)S(1)} %add_convert_fusion), channel_id=1, source_target_pairs={{0,2},{2,0},{4,6},{6,4},{1,3},{3,1},{5,7},{7,5},{8,10},{10,8},{12,... | collective-permute-start | bytes 196616 | tf_op jit(solution)/shard_map/ppermute | solution.py:29
  58.0 3.2 %collective-permute-done.19 = bf16[256,128]{1,0:T(8,128)(2,1)S(1)} collective-permute-done((bf16[256,128]{1,0:T(8,128)(2,1)S(1)}, bf16[256,128]{1,0:T(8,128)(2,1)S(1)}, u32[]{:S(2)}, u32[]{:S(2)}) %collective-permute-start.19) | collective-permute-done | bytes 65568 | tf_op jit(solution)/shard_map/ppermute | solution.py:29
  61.3 0.7 collective-permute-start.23
  63.1 1.2 %collective-permute-start.27 = (bf16[512,128]{1,0:T(8,128)(2,1)S(1)}, bf16[512,128]{1,0:T(8,128)(2,1)S(1)}, u32[]{:S(2)}, u32[]{:S(2)}) collective-permute-start(bf16[512,128]{1,0:T(8,128)(2,1)S(1)} %slice.27), channel_id=1, source_target_pairs={{0,1},{1,0},{2,3},{3,2},{4,5},{5,4},{6,7},{7,6},{8,9},{9,8},{10,11... | collective-permute-start | bytes 393224 | tf_op jit(solution)/shard_map/ppermute | solution.py:23
  64.4 1.8 %shard_map.31.refs_6_ = f32[16384,128]{1,0:T(8,128)} custom-call(s32[4]{0:T(128)S(1)} %pad_add_fusion.where_ref, bf16[1024,128]{1,0:T(8,128)(2,1)S(1)} %get-tuple-element.74.refs_0_, bf16[1024,128]{1,0:T(8,128)(2,1)S(1)} %collective-permute-done.14.refs_1_, bf16[1024,128]{1,0:T(8,128)(2,1)S(1)} %collective-permute-done.15.refs_2_), custom_call_target="tpu_custom_call" | custom-call | bytes 2359296 | tf_op jit(solution)/shard_map/pallas_call | solution.py:272
  66.2 1.8 %collective-permute-done.26.refs_0_ = bf16[512,128]{1,0:T(8,128)(2,1)S(1)} collective-permute-done((bf16[512,128]{1,0:T(8,128)(2,1)S(1)}, bf16[512,128]{1,0:T(8,128)(2,1)S(1)}, u32[]{:S(2)}, u32[]{:S(2)}) %collective-permute-start.26) | collective-permute-done | bytes 131104 | tf_op jit(solution)/shard_map/ppermute | solution.py:23
  68.7 6.1 %collective-permute-start.28 = (bf16[4096,128]{1,0:T(8,128)(2,1)S(1)}, bf16[4096,128]{1,0:T(8,128)(2,1)S(1)}, u32[]{:S(2)}, u32[]{:S(2)}) collective-permute-start(bf16[4096,128]{1,0:T(8,128)(2,1)S(1)} %constant_dynamic-update-slice_fusion.8), channel_id=1, source_target_pairs={{0,8},{8,0},{1,9},{9,1},{2,10},{10,2},{3,11},{11,3},{4,12},{12,4},... | collective-permute-start | bytes 3145736 | tf_op jit(solution)/shard_map/ppermute | solution.py:23
  75.0 1.2 %collective-permute-start.24 = (bf16[512,128]{1,0:T(8,128)(2,1)S(1)}, bf16[512,128]{1,0:T(8,128)(2,1)S(1)}, u32[]{:S(2)}, u32[]{:S(2)}) collective-permute-start(bf16[512,128]{1,0:T(8,128)(2,1)S(1)} %slice.28), channel_id=1, source_target_pairs={{0,16},{16,0},{1,17},{17,1},{2,18},{18,2},{3,19},{19,3},{4,20},{20... | collective-permute-start | bytes 393224 | tf_op jit(solution)/shard_map/ppermute | solution.py:23
  77.1 2.8 %shard_map.32.refs_3_ = f32[16384,128]{1,0:T(8,128)} custom-call(s32[4]{0:T(128)S(1)} %pad_add_fusion.where_ref, bf16[512,128]{1,0:T(8,128)(2,1)S(1)} %collective-permute-done.26.refs_0_, bf16[512,128]{1,0:T(8,128)(2,1)S(1)} %collective-permute-done.27.refs_1_, ...), custom_call_target="tpu_custom_call", output_to_operand_aliasing={{}: (7, {})} | custom-call | bytes 6291456 | tf_op jit(solution)/shard_map/pallas_call | solution.py:272
  80.5 1.7 %collective-permute-start.29 = (bf16[1024,128]{1,0:T(8,128)(2,1)S(1)}, bf16[1024,128]{1,0:T(8,128)(2,1)S(1)}, u32[]{:S(2)}, u32[]{:S(2)}) collective-permute-start(bf16[1024,128]{1,0:T(8,128)(2,1)S(1)} %pad_maximum_fusion), channel_id=1, source_target_pairs={{0,8},{8,0},{1,9},{9,1},{2,10},{10,2},{3,11},{11,3},{4,12},{12,4},... | collective-permute-start | bytes 786440 | tf_op jit(solution)/shard_map/ppermute | solution.py:23
  82.2 2.0 %shard_map.33.refs_1_ = f32[16384,128]{1,0:T(8,128)} custom-call(s32[4]{0:T(128)S(1)} %pad_add_fusion.where_ref, bf16[3072,128]{1,0:T(8,128)(2,1)S(1)} %collective-permute-done.30.refs_0_, bf16[512,128]{1,0:T(8,128)(2,1)S(1)} %collective-permute-done.24.refs_1_, ...), custom_call_target="tpu_custom_call", output_to_operand_aliasing={{}: (4, {})} | custom-call | bytes 3145728 | tf_op jit(solution)/shard_map/pallas_call | solution.py:272
  84.2 1.4 %shard_map.34 = f32[16384,128]{1,0:T(8,128)} custom-call(s32[4]{0:T(128)S(1)} %pad_add_fusion.where_ref, bf16[1024,128]{1,0:T(8,128)(2,1)S(1)} %collective-permute-done.29.refs_0_, f32[16384,128]{1,0:T(8,128)} %shard_map.33.refs_1_), custom_call_target="tpu_custom_call", output_to_operand_aliasing={{}: (2, {})} | custom-call | bytes 786432 | tf_op jit(solution)/shard_map/pallas_call | solution.py:272
  (67 shorter events, 8.1 us)
Async XLA Ops:
  1.0 1.5 %collective-permute-start = (bf16[2,10,3,2,128]{4,3,2,1,0:T(2,128)(2,1)S(1)}, bf16[2,10,3,2,128]{4,3,2,1,0:T(2,128)(2,1)S(1)}, u32[]{:S(2)}, u32[]{:S(2)}) collective-permute-start(bf16[2,10,3,2,128]{4,3,2,1,0:T(2,128)(2,1)S(1)} %broadcast_select_fusion), channel_id=1, source_target_pairs={{1,2},{3,4},{5,6},{2,1},{4,3},{6,5},{9,10},{11,12},{13,14},{10,9},... | collective-permute-start | bytes 92168 | tf_op jit(solution)/shard_map/ppermute | solution.py:295
  3.5 9.9 %collective-permute-start.6 = (bf16[2,40,8,128]{3,2,1,0:T(8,128)(2,1)S(1)}, bf16[2,40,8,128]{3,2,1,0:T(8,128)(2,1)S(1)}, u32[]{:S(2)}, u32[]{:S(2)}) collective-permute-start(bf16[2,40,8,128]{3,2,1,0:T(8,128)(2,1)S(1)} %pad_maximum_fusion.1.refs_0_), channel_id=1, source_target_pairs={{0,17},{1,16},{16,1},{17,0},{2,19},{3,18},{18,3},{19,2},{4,21},{5,... | collective-permute-start | bytes 491528 | tf_op jit(solution)/shard_map/ppermute | solution.py:322
  10.6 7.2 %collective-permute-start.4 = (bf16[2,40,8,128]{3,2,1,0:T(8,128)(2,1)S(1)}, bf16[2,40,8,128]{3,2,1,0:T(8,128)(2,1)S(1)}, u32[]{:S(2)}, u32[]{:S(2)}) collective-permute-start(bf16[2,40,8,128]{3,2,1,0:T(8,128)(2,1)S(1)} %pad_maximum_fusion.1.refs_0_), channel_id=1, source_target_pairs={{0,16},{16,0},{1,17},{17,1},{2,18},{18,2},{3,19},{19,3},{4,20},{20... | collective-permute-start | bytes 491528 | tf_op jit(solution)/shard_map/ppermute | solution.py:23
  10.9 8.4 %collective-permute-start.2 = (bf16[2,40,8,128]{3,2,1,0:T(8,128)(2,1)S(1)}, bf16[2,40,8,128]{3,2,1,0:T(8,128)(2,1)S(1)}, u32[]{:S(2)}, u32[]{:S(2)}) collective-permute-start(bf16[2,40,8,128]{3,2,1,0:T(8,128)(2,1)S(1)} %pad_maximum_fusion.1.refs_0_), channel_id=1, source_target_pairs={{0,1},{1,0},{2,3},{3,2},{4,5},{5,4},{6,7},{7,6},{8,9},{9,8},{10,11... | collective-permute-start | bytes 491528 | tf_op jit(solution)/shard_map/ppermute | solution.py:23
  11.0 8.4 %collective-permute-start.1 = (bf16[2,40,8,128]{3,2,1,0:T(8,128)(2,1)S(1)}, bf16[2,40,8,128]{3,2,1,0:T(8,128)(2,1)S(1)}, u32[]{:S(2)}, u32[]{:S(2)}) collective-permute-start(bf16[2,40,8,128]{3,2,1,0:T(8,128)(2,1)S(1)} %pad_maximum_fusion.1.refs_0_), channel_id=1, source_target_pairs={{0,8},{8,0},{1,9},{9,1},{2,10},{10,2},{3,11},{11,3},{4,12},{12,4},... | collective-permute-start | bytes 491528 | tf_op jit(solution)/shard_map/ppermute | solution.py:23
  13.4 6.0 %collective-permute-start.7 = (bf16[2,40,8,128]{3,2,1,0:T(8,128)(2,1)S(1)}, bf16[2,40,8,128]{3,2,1,0:T(8,128)(2,1)S(1)}, u32[]{:S(2)}, u32[]{:S(2)}) collective-permute-start(bf16[2,40,8,128]{3,2,1,0:T(8,128)(2,1)S(1)} %collective-permute-done.6.refs_6_), channel_id=1, source_target_pairs={{0,8},{8,0},{1,9},{9,1},{2,10},{10,2},{3,11},{11,3},{4,12},{12,4},... | collective-permute-start | bytes 491528 | tf_op jit(solution)/shard_map/ppermute | solution.py:23
  17.9 2.5 %collective-permute-start.5 = (bf16[2,40,8,128]{3,2,1,0:T(8,128)(2,1)S(1)}, bf16[2,40,8,128]{3,2,1,0:T(8,128)(2,1)S(1)}, u32[]{:S(2)}, u32[]{:S(2)}) collective-permute-start(bf16[2,40,8,128]{3,2,1,0:T(8,128)(2,1)S(1)} %collective-permute-done.4.refs_4_), channel_id=1, source_target_pairs={{0,8},{8,0},{1,9},{9,1},{2,10},{10,2},{3,11},{11,3},{4,12},{12,4},... | collective-permute-start | bytes 491528 | tf_op jit(solution)/shard_map/ppermute | solution.py:23
  19.3 1.4 %collective-permute-start.3 = (bf16[2,40,8,128]{3,2,1,0:T(8,128)(2,1)S(1)}, bf16[2,40,8,128]{3,2,1,0:T(8,128)(2,1)S(1)}, u32[]{:S(2)}, u32[]{:S(2)}) collective-permute-start(bf16[2,40,8,128]{3,2,1,0:T(8,128)(2,1)S(1)} %collective-permute-done.2.refs_2_), channel_id=1, source_target_pairs={{0,8},{8,0},{1,9},{9,1},{2,10},{10,2},{3,11},{11,3},{4,12},{12,4},... | collective-permute-start | bytes 491528 | tf_op jit(solution)/shard_map/ppermute | solution.py:23
  32.0 9.5 %collective-permute-start.8 = (bf16[256,128]{1,0:T(8,128)(2,1)S(1)}, bf16[256,128]{1,0:T(8,128)(2,1)S(1)}, u32[]{:S(2)}, u32[]{:S(2)}) collective-permute-start(bf16[256,128]{1,0:T(8,128)(2,1)S(1)} %get-tuple-element.38), channel_id=1, source_target_pairs={{0,2},{2,0},{4,6},{6,4},{1,3},{3,1},{5,7},{7,5},{8,10},{10,8},{12,... | collective-permute-start | bytes 196616 | tf_op jit(solution)/shard_map/ppermute | solution.py:29
  33.5 8.0 %collective-permute-start.9 = (bf16[256,128]{1,0:T(8,128)(2,1)S(1)}, bf16[256,128]{1,0:T(8,128)(2,1)S(1)}, u32[]{:S(2)}, u32[]{:S(2)}) collective-permute-start(bf16[256,128]{1,0:T(8,128)(2,1)S(1)} %get-tuple-element.39), channel_id=1, source_target_pairs={{0,4},{2,6},{4,0},{6,2},{1,5},{3,7},{5,1},{7,3},{8,12},{10,14},{12... | collective-permute-start | bytes 196616 | tf_op jit(solution)/shard_map/ppermute | solution.py:29
  35.6 5.9 %collective-permute-start.10 = (bf16[256,128]{1,0:T(8,128)(2,1)S(1)}, bf16[256,128]{1,0:T(8,128)(2,1)S(1)}, u32[]{:S(2)}, u32[]{:S(2)}) collective-permute-start(bf16[256,128]{1,0:T(8,128)(2,1)S(1)} %get-tuple-element.40), channel_id=1, source_target_pairs={{0,6},{2,4},{4,2},{6,0},{1,7},{3,5},{5,3},{7,1},{8,14},{10,12},{12... | collective-permute-start | bytes 196616 | tf_op jit(solution)/shard_map/ppermute | solution.py:29
  41.5 9.0 %collective-permute-start.13 = (bf16[256,128]{1,0:T(8,128)(2,1)S(1)}, bf16[256,128]{1,0:T(8,128)(2,1)S(1)}, u32[]{:S(2)}, u32[]{:S(2)}) collective-permute-start(bf16[256,128]{1,0:T(8,128)(2,1)S(1)} %add_convert_fusion.1), channel_id=1, source_target_pairs={{0,6},{2,4},{4,2},{6,0},{1,7},{3,5},{5,3},{7,1},{8,14},{10,12},{12... | collective-permute-start | bytes 196616 | tf_op jit(solution)/shard_map/ppermute | solution.py:29
  44.7 5.7 %collective-permute-start.12 = (bf16[256,128]{1,0:T(8,128)(2,1)S(1)}, bf16[256,128]{1,0:T(8,128)(2,1)S(1)}, u32[]{:S(2)}, u32[]{:S(2)}) collective-permute-start(bf16[256,128]{1,0:T(8,128)(2,1)S(1)} %add_convert_fusion.1), channel_id=1, source_target_pairs={{0,4},{2,6},{4,0},{6,2},{1,5},{3,7},{5,1},{7,3},{8,12},{10,14},{12... | collective-permute-start | bytes 196616 | tf_op jit(solution)/shard_map/ppermute | solution.py:29
  44.7 4.0 %collective-permute-start.11 = (bf16[256,128]{1,0:T(8,128)(2,1)S(1)}, bf16[256,128]{1,0:T(8,128)(2,1)S(1)}, u32[]{:S(2)}, u32[]{:S(2)}) collective-permute-start(bf16[256,128]{1,0:T(8,128)(2,1)S(1)} %add_convert_fusion.1), channel_id=1, source_target_pairs={{0,2},{2,0},{4,6},{6,4},{1,3},{3,1},{5,7},{7,5},{8,10},{10,8},{12,... | collective-permute-start | bytes 196616 | tf_op jit(solution)/shard_map/ppermute | solution.py:29
  45.1 7.5 %collective-permute-start.16 = (bf16[256,128]{1,0:T(8,128)(2,1)S(1)}, bf16[256,128]{1,0:T(8,128)(2,1)S(1)}, u32[]{:S(2)}, u32[]{:S(2)}) collective-permute-start(bf16[256,128]{1,0:T(8,128)(2,1)S(1)} %get-tuple-element.52), channel_id=1, source_target_pairs={{0,2},{2,0},{4,6},{6,4},{1,3},{3,1},{5,7},{7,5},{8,10},{10,8},{12,... | collective-permute-start | bytes 196616 | tf_op jit(solution)/shard_map/ppermute | solution.py:29
  46.2 6.5 %collective-permute-start.17 = (bf16[256,128]{1,0:T(8,128)(2,1)S(1)}, bf16[256,128]{1,0:T(8,128)(2,1)S(1)}, u32[]{:S(2)}, u32[]{:S(2)}) collective-permute-start(bf16[256,128]{1,0:T(8,128)(2,1)S(1)} %get-tuple-element.53), channel_id=1, source_target_pairs={{0,4},{2,6},{4,0},{6,2},{1,5},{3,7},{5,1},{7,3},{8,12},{10,14},{12... | collective-permute-start | bytes 196616 | tf_op jit(solution)/shard_map/ppermute | solution.py:29
  48.7 5.6 %collective-permute-start.18 = (bf16[256,128]{1,0:T(8,128)(2,1)S(1)}, bf16[256,128]{1,0:T(8,128)(2,1)S(1)}, u32[]{:S(2)}, u32[]{:S(2)}) collective-permute-start(bf16[256,128]{1,0:T(8,128)(2,1)S(1)} %get-tuple-element.54), channel_id=1, source_target_pairs={{0,6},{2,4},{4,2},{6,0},{1,7},{3,5},{5,3},{7,1},{8,14},{10,12},{12... | collective-permute-start | bytes 196616 | tf_op jit(solution)/shard_map/ppermute | solution.py:29
  50.5 7.5 %collective-permute-start.15 = (bf16[1024,128]{1,0:T(8,128)(2,1)S(1)}, bf16[1024,128]{1,0:T(8,128)(2,1)S(1)}, u32[]{:S(2)}, u32[]{:S(2)}) collective-permute-start(bf16[1024,128]{1,0:T(8,128)(2,1)S(1)} %get-tuple-element.74.refs_0_), channel_id=1, source_target_pairs={{0,16},{16,0},{1,17},{17,1},{2,18},{18,2},{3,19},{19,3},{4,20},{20... | collective-permute-start | bytes 786440 | tf_op jit(solution)/shard_map/ppermute | solution.py:23
  52.1 5.9 %collective-permute-start.14 = (bf16[1024,128]{1,0:T(8,128)(2,1)S(1)}, bf16[1024,128]{1,0:T(8,128)(2,1)S(1)}, u32[]{:S(2)}, u32[]{:S(2)}) collective-permute-start(bf16[1024,128]{1,0:T(8,128)(2,1)S(1)} %get-tuple-element.74.refs_0_), channel_id=1, source_target_pairs={{0,1},{1,0},{2,3},{3,2},{4,5},{5,4},{6,7},{7,6},{8,9},{9,8},{10,11... | collective-permute-start | bytes 786440 | tf_op jit(solution)/shard_map/ppermute | solution.py:23
  54.4 6.9 %collective-permute-start.21 = (bf16[256,128]{1,0:T(8,128)(2,1)S(1)}, bf16[256,128]{1,0:T(8,128)(2,1)S(1)}, u32[]{:S(2)}, u32[]{:S(2)}) collective-permute-start(bf16[256,128]{1,0:T(8,128)(2,1)S(1)} %add_convert_fusion), channel_id=1, source_target_pairs={{0,6},{2,4},{4,2},{6,0},{1,7},{3,5},{5,3},{7,1},{8,14},{10,12},{12... | collective-permute-start | bytes 196616 | tf_op jit(solution)/shard_map/ppermute | solution.py:29
  56.2 5.0 %collective-permute-start.20 = (bf16[256,128]{1,0:T(8,128)(2,1)S(1)}, bf16[256,128]{1,0:T(8,128)(2,1)S(1)}, u32[]{:S(2)}, u32[]{:S(2)}) collective-permute-start(bf16[256,128]{1,0:T(8,128)(2,1)S(1)} %add_convert_fusion), channel_id=1, source_target_pairs={{0,4},{2,6},{4,0},{6,2},{1,5},{3,7},{5,1},{7,3},{8,12},{10,14},{12... | collective-permute-start | bytes 196616 | tf_op jit(solution)/shard_map/ppermute | solution.py:29
  57.1 4.1 %collective-permute-start.19 = (bf16[256,128]{1,0:T(8,128)(2,1)S(1)}, bf16[256,128]{1,0:T(8,128)(2,1)S(1)}, u32[]{:S(2)}, u32[]{:S(2)}) collective-permute-start(bf16[256,128]{1,0:T(8,128)(2,1)S(1)} %add_convert_fusion), channel_id=1, source_target_pairs={{0,2},{2,0},{4,6},{6,4},{1,3},{3,1},{5,7},{7,5},{8,10},{10,8},{12,... | collective-permute-start | bytes 196616 | tf_op jit(solution)/shard_map/ppermute | solution.py:29
  61.3 7.4 %collective-permute-start.23 = (bf16[1024,128]{1,0:T(8,128)(2,1)S(1)}, bf16[1024,128]{1,0:T(8,128)(2,1)S(1)}, u32[]{:S(2)}, u32[]{:S(2)}) collective-permute-start(bf16[1024,128]{1,0:T(8,128)(2,1)S(1)} %get-tuple-element.66.refs_3_), channel_id=1, source_target_pairs={{0,16},{16,0},{1,17},{17,1},{2,18},{18,2},{3,19},{19,3},{4,20},{20... | collective-permute-start | bytes 786440 | tf_op jit(solution)/shard_map/ppermute | solution.py:23
  62.0 6.7 %collective-permute-start.22 = (bf16[1024,128]{1,0:T(8,128)(2,1)S(1)}, bf16[1024,128]{1,0:T(8,128)(2,1)S(1)}, u32[]{:S(2)}, u32[]{:S(2)}) collective-permute-start(bf16[1024,128]{1,0:T(8,128)(2,1)S(1)} %get-tuple-element.66.refs_3_), channel_id=1, source_target_pairs={{0,1},{1,0},{2,3},{3,2},{4,5},{5,4},{6,7},{7,6},{8,9},{9,8},{10,11... | collective-permute-start | bytes 786440 | tf_op jit(solution)/shard_map/ppermute | solution.py:23
  62.5 5.5 %collective-permute-start.26 = (bf16[512,128]{1,0:T(8,128)(2,1)S(1)}, bf16[512,128]{1,0:T(8,128)(2,1)S(1)}, u32[]{:S(2)}, u32[]{:S(2)}) collective-permute-start(bf16[512,128]{1,0:T(8,128)(2,1)S(1)} %slice.26), channel_id=1, source_target_pairs={{0,16},{16,0},{1,17},{17,1},{2,18},{18,2},{3,19},{19,3},{4,20},{20... | collective-permute-start | bytes 393224 | tf_op jit(solution)/shard_map/ppermute | solution.py:23
  63.1 5.5 %collective-permute-start.27 = (bf16[512,128]{1,0:T(8,128)(2,1)S(1)}, bf16[512,128]{1,0:T(8,128)(2,1)S(1)}, u32[]{:S(2)}, u32[]{:S(2)}) collective-permute-start(bf16[512,128]{1,0:T(8,128)(2,1)S(1)} %slice.27), channel_id=1, source_target_pairs={{0,1},{1,0},{2,3},{3,2},{4,5},{5,4},{6,7},{7,6},{8,9},{9,8},{10,11... | collective-permute-start | bytes 393224 | tf_op jit(solution)/shard_map/ppermute | solution.py:23
  68.7 8.4 %collective-permute-start.28 = (bf16[4096,128]{1,0:T(8,128)(2,1)S(1)}, bf16[4096,128]{1,0:T(8,128)(2,1)S(1)}, u32[]{:S(2)}, u32[]{:S(2)}) collective-permute-start(bf16[4096,128]{1,0:T(8,128)(2,1)S(1)} %constant_dynamic-update-slice_fusion.8), channel_id=1, source_target_pairs={{0,8},{8,0},{1,9},{9,1},{2,10},{10,2},{3,11},{11,3},{4,12},{12,4},... | collective-permute-start | bytes 3145736 | tf_op jit(solution)/shard_map/ppermute | solution.py:23
  74.9 7.3 %collective-permute-start.30 = (bf16[3072,128]{1,0:T(8,128)(2,1)S(1)}, bf16[3072,128]{1,0:T(8,128)(2,1)S(1)}, u32[]{:S(2)}, u32[]{:S(2)}) collective-permute-start(bf16[3072,128]{1,0:T(8,128)(2,1)S(1)} %constant_dynamic-update-slice_fusion.16), channel_id=1, source_target_pairs={{0,8},{8,0},{1,9},{9,1},{2,10},{10,2},{3,11},{11,3},{4,12},{12,4},... | collective-permute-start | bytes 2359304 | tf_op jit(solution)/shard_map/ppermute | solution.py:23
  75.0 5.0 %collective-permute-start.24 = (bf16[512,128]{1,0:T(8,128)(2,1)S(1)}, bf16[512,128]{1,0:T(8,128)(2,1)S(1)}, u32[]{:S(2)}, u32[]{:S(2)}) collective-permute-start(bf16[512,128]{1,0:T(8,128)(2,1)S(1)} %slice.28), channel_id=1, source_target_pairs={{0,16},{16,0},{1,17},{17,1},{2,18},{18,2},{3,19},{19,3},{4,20},{20... | collective-permute-start | bytes 393224 | tf_op jit(solution)/shard_map/ppermute | solution.py:23
  76.2 4.3 %collective-permute-start.25 = (bf16[512,128]{1,0:T(8,128)(2,1)S(1)}, bf16[512,128]{1,0:T(8,128)(2,1)S(1)}, u32[]{:S(2)}, u32[]{:S(2)}) collective-permute-start(bf16[512,128]{1,0:T(8,128)(2,1)S(1)} %slice.29), channel_id=1, source_target_pairs={{0,1},{1,0},{2,3},{3,2},{4,5},{5,4},{6,7},{7,6},{8,9},{9,8},{10,11... | collective-permute-start | bytes 393224 | tf_op jit(solution)/shard_map/ppermute | solution.py:23
  80.5 3.7 %collective-permute-start.29 = (bf16[1024,128]{1,0:T(8,128)(2,1)S(1)}, bf16[1024,128]{1,0:T(8,128)(2,1)S(1)}, u32[]{:S(2)}, u32[]{:S(2)}) collective-permute-start(bf16[1024,128]{1,0:T(8,128)(2,1)S(1)} %pad_maximum_fusion), channel_id=1, source_target_pairs={{0,8},{8,0},{1,9},{9,1},{2,10},{10,2},{3,11},{11,3},{4,12},{12,4},... | collective-permute-start | bytes 786440 | tf_op jit(solution)/shard_map/ppermute | solution.py:23
